TPU v7x, 32 devices: a whole 2x2x4 slice. The times are simulated.
32 devices in a mesh: dp: 8 (over y, x, core), tensor: 4 (over z).
Axes of the slice: x: 2, y: 2, z: 4, core: 2. Of those that a mesh axis runs over, the one named last changes fastest.
Arguments:
- tokens_in: bfloat16 [16, 1536, 1280], P('dp', 'tensor'), may hold values from -6 to 6
- cotangent: bfloat16 [16, 1536, 1280], P('dp', 'tensor'), may hold values from -6 to 6
- picture_ids: int32 [16, 1536], P('dp', 'tensor'), may hold values from 0 to 3, as said below
- patch_positions: int32 [2, 16, 1536], P(None, 'dp', 'tensor'), may hold values from 0 to 511, as said below
- qkv_weight: float32 [1280, 3, 1280], P('dp', None, 'tensor'), may hold values from -0.15625 to 0.15625
- out_weight: float32 [1280, 1280], P('tensor', 'dp'), may hold values from -0.75 to 0.75
- up_projection_weight: float32 [1280, 4, 1280], P('dp', None, 'tensor'), may hold values from -0.15625 to 0.15625
- down_weight: float32 [4, 1280, 1280], P(None, 'tensor', 'dp'), may hold values from -0.078125 to 0.078125
- projection_bias_rows: float32 [7, 1280], P(None, 'tensor'), may hold values from -1.8 to 1.8
- norm_vectors: float32 [6, 1280], replicated
- qkv_first: float32 [1280, 3, 1280], P('dp', None, 'tensor'), may hold values from -104.40705 to 104.40705
- out_first: float32 [1280, 1280], P('tensor', 'dp'), may hold values from -20.850058 to 20.850058
- up_first: float32 [1280, 4, 1280], P('dp', None, 'tensor'), may hold values from -31.353468 to 31.353468
- down_first: float32 [4, 1280, 1280], P(None, 'tensor', 'dp'), may hold values from -52.203526 to 52.203526
- bias_first: float32 [7, 1280], P(None, 'tensor'), may hold values from -62.706936 to 62.706936
- vector_first: float32 [6, 1280], replicated, may hold values from -104.40705 to 104.40705
- qkv_second: float32 [1280, 3, 1280], P('dp', None, 'tensor'), may hold values from 1292.6976 to 5160.96
- out_second: float32 [1280, 1280], P('tensor', 'dp'), may hold values from 51.6096 to 206.4384
- up_second: float32 [1280, 4, 1280], P('dp', None, 'tensor'), may hold values from 115.5072 to 466.944
- down_second: float32 [4, 1280, 1280], P(None, 'tensor', 'dp'), may hold values from 324.4032 to 1292.6976
- bias_second: float32 [7, 1280], P(None, 'tensor'), may hold values from 466.944 to 1867.776
- vector_second: float32 [6, 1280], replicated, may hold values from 1292.6976 to 5160.96
Outputs:
- block_out: bfloat16 [16, 1536, 1280], P('dp', 'tensor')
- input_grad: float32 [16, 1536, 1280], P('dp', 'tensor')
- qkv_new: float32 [1280, 3, 1280], P('dp', None, 'tensor')
- qkv_first_new: float32 [1280, 3, 1280], P('dp', None, 'tensor')
- qkv_second_new: float32 [1280, 3, 1280], P('dp', None, 'tensor')
- out_new: float32 [1280, 1280], P('tensor', 'dp')
- out_first_new: float32 [1280, 1280], P('tensor', 'dp')
- out_second_new: float32 [1280, 1280], P('tensor', 'dp')
- up_new: float32 [1280, 4, 1280], P('dp', None, 'tensor')
- up_first_new: float32 [1280, 4, 1280], P('dp', None, 'tensor')
- up_second_new: float32 [1280, 4, 1280], P('dp', None, 'tensor')
- down_new: float32 [4, 1280, 1280], P(None, 'tensor', 'dp')
- down_first_new: float32 [4, 1280, 1280], P(None, 'tensor', 'dp')
- down_second_new: float32 [4, 1280, 1280], P(None, 'tensor', 'dp')
- bias_new: float32 [7, 1280], P(None, 'tensor')
- bias_first_new: float32 [7, 1280], P(None, 'tensor')
- bias_second_new: float32 [7, 1280], P(None, 'tensor')
- vector_new: float32 [6, 1280], replicated
- vector_first_new: float32 [6, 1280], replicated
- vector_second_new: float32 [6, 1280], replicated
Inputs may be any that keep to these rules, and one draw needn't show every extreme that they name: `picture_ids`: each row holds three pictures numbered 1, 2, 3 one after another from its first slot, then padding numbered 0; picture 2 has exactly 1024 patches, pictures 1 and 3 at least 102. `patch_positions`: patch i of a picture of grid width w lies at row i // w and column i % w; each picture has its own width, from 2 to 33, and picture 2 of the first packed row has width 2; padding lies at 0, 0.
All inputs are finite; a program needn't handle non-finite values.
Results may differ from a plain program's by a relative error of at most 0.015.
Values may be sent and summed in bfloat16 or wider, within the bound.
No kernel may reach another device: no remote copies, remote signals or barrier semaphores. Data moves between devices by JAX's collectives and lax.ppermute only.
A program may use at most 256 MiB of HBM per device.

v0:
```python
import jax
import jax.numpy as jnp
from jax import lax
from jax.sharding import PartitionSpec as P

HEAD = 80
STEP = 10


NORM_EPS = 1e-06
BETA_ONE = 0.9
BETA_TWO = 0.95
ADAM_EPS = 1e-08
MATRIX_RATE = 0.03
VECTOR_RATE = 0.2
MATRIX_DECAY = 0.1
GELU_SLOPE = 1.702


def layer_norm(source, gain_vec, offset_vec):
    centre = source - jnp.mean(source, axis=-1, keepdims=True)
    spread = lax.rsqrt(jnp.mean(centre * centre, axis=-1, keepdims=True) + NORM_EPS)
    normed = centre * spread
    return (normed * gain_vec + offset_vec, normed, spread)


def norm_back(gradient, gain_vec, normed, spread):
    scaled = gradient * gain_vec
    return spread * (
        scaled
        - jnp.mean(scaled, axis=-1, keepdims=True)
        - normed * jnp.mean(scaled * normed, axis=-1, keepdims=True)
    )


def rotary_tables(positions):
    quarter = HEAD // 4
    powers = jnp.arange(quarter, dtype=jnp.float32) * (2.0 / (HEAD // 2))
    inverse = jnp.power(10000.0, -powers)
    angles = jnp.concatenate(
        [
            positions[0].astype(jnp.float32)[:, None] * inverse,
            positions[1].astype(jnp.float32)[:, None] * inverse,
        ],
        axis=-1,
    )
    angles = jnp.concatenate([angles, angles], axis=-1)
    return (jnp.cos(angles)[:, None, :], jnp.sin(angles)[:, None, :])


def turn(values, cosine, sine):
    half_size = values.shape[-1] // 2
    swapped = jnp.concatenate([-values[..., half_size:], values[..., :half_size]], axis=-1)
    return values * cosine + swapped * sine


def turn_back(gradient, cosine, sine):
    half_size = gradient.shape[-1] // 2
    shifted = gradient * sine
    turned = jnp.concatenate([shifted[..., half_size:], -shifted[..., :half_size]], axis=-1)
    return gradient * cosine + turned


def quick_gelu(values):
    return values * jax.nn.sigmoid(GELU_SLOPE * values)


def gelu_slope(values):
    sigmoid_v = jax.nn.sigmoid(GELU_SLOPE * values)
    return sigmoid_v + GELU_SLOPE * values * sigmoid_v * (1.0 - sigmoid_v)


def adam_step(weight, gradient, first, second, rate, decay):
    first_new = BETA_ONE * first + (1.0 - BETA_ONE) * gradient
    second_new = BETA_TWO * second + (1.0 - BETA_TWO) * gradient * gradient
    fix_one = 1.0 - BETA_ONE**STEP
    fix_two = 1.0 - BETA_TWO**STEP
    ratio = first_new / fix_one / (jnp.sqrt(second_new / fix_two) + ADAM_EPS)
    return (weight - rate * (ratio + decay * weight), first_new, second_new)


def attend(queries, key_rows, value_rows, allowed):
    scale = queries.shape[-1] ** (-0.5)
    scores = (
        jnp.einsum("qhe,khe->hqk", queries, key_rows, preferred_element_type=jnp.float32) * scale
    )
    scores = jnp.where(allowed[None], scores, -1e30)
    largest = jnp.max(scores, axis=-1, keepdims=True)
    raised = jnp.exp(scores - largest)
    totals = jnp.sum(raised, axis=-1, keepdims=True)
    chances = raised / totals
    mixed = jnp.einsum(
        "hqk,khe->qhe", chances.astype(jnp.bfloat16), value_rows, preferred_element_type=jnp.float32
    )
    return (mixed, (largest + jnp.log(totals))[..., 0])


def attend_back(queries, key_rows, value_rows, allowed, log_totals, grad_mixed):
    scale = queries.shape[-1] ** (-0.5)
    scores = (
        jnp.einsum("qhe,khe->hqk", queries, key_rows, preferred_element_type=jnp.float32) * scale
    )
    scores = jnp.where(allowed[None], scores, -1e30)
    chances = jnp.exp(scores - log_totals[..., None])
    grad_chances = jnp.einsum(
        "qhe,khe->hqk", grad_mixed, value_rows, preferred_element_type=jnp.float32
    )
    centre = jnp.sum(grad_chances * chances, axis=-1, keepdims=True)
    grad_scores = (chances * (grad_chances - centre)).astype(jnp.bfloat16)
    query_grad = (
        jnp.einsum("hqk,khe->qhe", grad_scores, key_rows, preferred_element_type=jnp.float32)
        * scale
    )
    key_grad = (
        jnp.einsum("hqk,qhe->khe", grad_scores, queries, preferred_element_type=jnp.float32) * scale
    )
    value_grad = jnp.einsum(
        "hqk,qhe->khe", chances.astype(jnp.bfloat16), grad_mixed, preferred_element_type=jnp.float32
    )
    return (query_grad, key_grad, value_grad)


def gather_rows(local_rows):
    return lax.all_gather(local_rows, "tensor", axis=0, tiled=True)


def gather_grads(local_rows):
    return lax.all_gather(local_rows, "tensor", axis=0, tiled=True)


def branch_sum(left_rows, right_matrix):
    return lax.psum_scatter(
        jnp.dot(left_rows, right_matrix, preferred_element_type=jnp.float32).astype(jnp.bfloat16),
        "tensor",
        scatter_dimension=0,
        tiled=True,
    ).astype(jnp.float32)


def input_sum(left_rows, right_matrix):
    return lax.psum_scatter(
        lax.dot_general(
            left_rows, right_matrix, (((1,), (1,)), ((), ())), preferred_element_type=jnp.float32
        ).astype(jnp.bfloat16),
        "tensor",
        scatter_dimension=0,
        tiled=True,
    ).astype(jnp.float32)


def body(
    tokens_in,
    cotangent,
    picture_ids,
    patch_positions,
    qkv_weight,
    out_weight,
    up_projection_weight,
    down_weight,
    projection_bias_rows,
    norm_vectors,
    qkv_first,
    out_first,
    up_first,
    down_first,
    bias_first,
    vector_first,
    qkv_second,
    out_second,
    up_second,
    down_second,
    bias_second,
    vector_second,
):
    groups = lax.axis_size("tensor")
    local_rows = tokens_in.shape[1]
    full_rows = local_rows * groups
    model_width = tokens_in.shape[2]
    slice_width = qkv_weight.shape[2]
    feed_groups = up_projection_weight.shape[1]
    local_heads = slice_width // HEAD
    query_block = 512
    all_ids, all_positions = (
        lax.all_gather(picture_ids, "tensor", axis=1, tiled=True),
        lax.all_gather(patch_positions, "tensor", axis=2, tiled=True),
    )

    def fetch_attention():
        return (
            lax.all_gather(qkv_weight.astype(jnp.bfloat16), "dp", axis=0, tiled=True),
            lax.all_gather(out_weight.astype(jnp.bfloat16), "dp", axis=1, tiled=True),
        )

    def fetch_feed():
        return (
            lax.all_gather(up_projection_weight.astype(jnp.bfloat16), "dp", axis=0, tiled=True),
            lax.all_gather(down_weight.astype(jnp.bfloat16), "dp", axis=2, tiled=True),
        )

    def micro_step(totals, inputs):
        rows_in, rows_cot, row_ids, row_positions = inputs
        attention_weights, feed_weights = (fetch_attention(), fetch_feed())
        qkv_full, out_full = attention_weights
        up_complete, down_full = feed_weights
        source = rows_in.astype(jnp.float32)
        cosine, sine = rotary_tables(row_positions)
        first_norm, first_hat, first_scale = layer_norm(source, norm_vectors[0], norm_vectors[1])
        first_full = gather_rows(first_norm.astype(jnp.bfloat16))
        mixed = jnp.einsum("td,dcf->tcf", first_full, qkv_full, preferred_element_type=jnp.float32)
        mixed = mixed + projection_bias_rows[0:3][None]
        queries = turn(mixed[:, 0].reshape(full_rows, local_heads, HEAD), cosine, sine).astype(
            jnp.bfloat16
        )
        key_rows = turn(mixed[:, 1].reshape(full_rows, local_heads, HEAD), cosine, sine).astype(
            jnp.bfloat16
        )
        value_rows = mixed[:, 2].reshape(full_rows, local_heads, HEAD).astype(jnp.bfloat16)
        mixed_list = []
        total_list = []
        for first_row in range(0, full_rows, query_block):
            allowed = row_ids[first_row : first_row + query_block, None] == row_ids[None, :]
            mixed_part, log_part = attend(
                queries[first_row : first_row + query_block], key_rows, value_rows, allowed
            )
            mixed_list.append(mixed_part)
            total_list.append(log_part)
        attended = (
            jnp.concatenate(mixed_list, axis=0).reshape(full_rows, slice_width).astype(jnp.bfloat16)
        )
        log_totals = jnp.concatenate(total_list, axis=1)
        middle = source + branch_sum(attended, out_full) + norm_vectors[4]
        second_norm, second_hat, second_scale = layer_norm(middle, norm_vectors[2], norm_vectors[3])
        second_complete = gather_rows(second_norm.astype(jnp.bfloat16))
        hidden_units = jnp.einsum(
            "sp,piv->siv", second_complete, up_complete, preferred_element_type=jnp.float32
        )
        hidden_units = (hidden_units + projection_bias_rows[3:7][None]).reshape(
            full_rows, feed_groups * slice_width
        )
        active_units = quick_gelu(hidden_units).astype(jnp.bfloat16)
        down_matrix = down_full.reshape(feed_groups * slice_width, model_width)
        result = middle + branch_sum(active_units, down_matrix) + norm_vectors[5]
        attention_weights, feed_weights = (fetch_attention(), fetch_feed())
        qkv_full, out_full = attention_weights
        up_complete, down_full = feed_weights
        down_matrix = down_full.reshape(feed_groups * slice_width, model_width)
        grad_out = rows_cot.astype(jnp.float32)
        grad_full = gather_grads(grad_out.astype(jnp.bfloat16))
        grad_down = jnp.einsum(
            "tk,td->kd", active_units, grad_full, preferred_element_type=jnp.float32
        )
        grad_down = grad_down.reshape(feed_groups, slice_width, model_width)
        grad_active = lax.dot_general(
            grad_full, down_matrix, (((1,), (1,)), ((), ())), preferred_element_type=jnp.float32
        )
        grad_hidden = (grad_active * gelu_slope(hidden_units)).astype(jnp.bfloat16)
        bias_up = jnp.sum(grad_hidden, axis=0, dtype=jnp.float32).reshape(feed_groups, slice_width)
        grad_up = jnp.einsum(
            "td,tk->dk", second_complete, grad_hidden, preferred_element_type=jnp.float32
        )
        grad_up = grad_up.reshape(model_width, feed_groups, slice_width)
        up_matrix = up_complete.reshape(model_width, feed_groups * slice_width)
        grad_second = input_sum(grad_hidden, up_matrix)
        grad_middle = grad_out + norm_back(grad_second, norm_vectors[2], second_hat, second_scale)
        grad_branch = gather_grads(grad_middle.astype(jnp.bfloat16))
        grad_outw = jnp.einsum(
            "tk,td->kd", attended, grad_branch, preferred_element_type=jnp.float32
        )
        grad_attended = lax.dot_general(
            grad_branch, out_full, (((1,), (1,)), ((), ())), preferred_element_type=jnp.float32
        )
        grad_attended = grad_attended.astype(jnp.bfloat16).reshape(full_rows, local_heads, HEAD)
        query_list = []
        grad_keys = jnp.zeros((full_rows, local_heads, HEAD), jnp.float32)
        grad_values = jnp.zeros((full_rows, local_heads, HEAD), jnp.float32)
        for first_row in range(0, full_rows, query_block):
            allowed = row_ids[first_row : first_row + query_block, None] == row_ids[None, :]
            query_grad, key_grad, value_grad = attend_back(
                queries[first_row : first_row + query_block],
                key_rows,
                value_rows,
                allowed,
                log_totals[:, first_row : first_row + query_block],
                grad_attended[first_row : first_row + query_block],
            )
            query_list.append(query_grad)
            grad_keys = grad_keys + key_grad
            grad_values = grad_values + value_grad
        grad_queries = turn_back(jnp.concatenate(query_list, axis=0), cosine, sine)
        grad_keys = turn_back(grad_keys, cosine, sine)
        grad_mixed = jnp.stack([grad_queries, grad_keys, grad_values], axis=1)
        grad_mixed = grad_mixed.reshape(full_rows, 3, slice_width).astype(jnp.bfloat16)
        bias_qkv = jnp.sum(grad_mixed, axis=0, dtype=jnp.float32)
        grad_qkv = jnp.einsum(
            "td,tcf->dcf", first_full, grad_mixed, preferred_element_type=jnp.float32
        )
        grad_first = input_sum(
            grad_mixed.reshape(full_rows, 3 * slice_width),
            qkv_full.reshape(model_width, 3 * slice_width),
        )
        grad_source = grad_middle + norm_back(grad_first, norm_vectors[0], first_hat, first_scale)
        vector_grad = jnp.stack(
            [
                jnp.sum(grad_first * first_hat, axis=0),
                jnp.sum(grad_first, axis=0),
                jnp.sum(grad_second * second_hat, axis=0),
                jnp.sum(grad_second, axis=0),
                jnp.sum(grad_middle, axis=0),
                jnp.sum(grad_out, axis=0),
            ]
        )
        new_totals = (
            totals[0] + grad_qkv,
            totals[1] + grad_outw,
            totals[2] + grad_up,
            totals[3] + grad_down,
            totals[4] + jnp.concatenate([bias_qkv, bias_up], axis=0),
            totals[5] + vector_grad,
        )
        return (new_totals, (result.astype(jnp.bfloat16), grad_source))

    initial = (
        jnp.zeros((model_width, 3, slice_width), jnp.float32),
        jnp.zeros((slice_width, model_width), jnp.float32),
        jnp.zeros((model_width, feed_groups, slice_width), jnp.float32),
        jnp.zeros((feed_groups, slice_width, model_width), jnp.float32),
        jnp.zeros((3 + feed_groups, slice_width), jnp.float32),
        jnp.zeros((6, model_width), jnp.float32),
    )
    totals, outputs = lax.scan(
        micro_step, initial, (tokens_in, cotangent, all_ids, jnp.moveaxis(all_positions, 1, 0))
    )
    block_out, input_grad = outputs
    grad_qkv, grad_outw, grad_up, grad_down = (
        lax.psum_scatter(totals[0], "dp", scatter_dimension=0, tiled=True),
        lax.psum_scatter(totals[1], "dp", scatter_dimension=1, tiled=True),
        lax.psum_scatter(totals[2], "dp", scatter_dimension=0, tiled=True),
        lax.psum_scatter(totals[3], "dp", scatter_dimension=2, tiled=True),
    )
    tensor_index = lax.axis_index("tensor")
    offset = tensor_index * slice_width
    placed = lax.dynamic_update_slice(
        jnp.zeros((3 + feed_groups, model_width), jnp.float32), totals[4], (0, offset)
    )
    summed = lax.psum(jnp.concatenate([placed, totals[5]], axis=0), ("dp", "tensor"))
    grad_bias = lax.dynamic_slice(
        summed[: 3 + feed_groups], (0, offset), (3 + feed_groups, slice_width)
    )
    grad_vector = summed[3 + feed_groups :]
    qkv_new, qkv_first_new, qkv_second_new = adam_step(
        qkv_weight, grad_qkv, qkv_first, qkv_second, MATRIX_RATE, MATRIX_DECAY
    )
    out_new, out_first_new, out_second_new = adam_step(
        out_weight, grad_outw, out_first, out_second, MATRIX_RATE, MATRIX_DECAY
    )
    up_new, up_first_new, up_second_new = adam_step(
        up_projection_weight, grad_up, up_first, up_second, MATRIX_RATE, MATRIX_DECAY
    )
    down_new, down_first_new, down_second_new = adam_step(
        down_weight, grad_down, down_first, down_second, MATRIX_RATE, MATRIX_DECAY
    )
    bias_new, bias_first_new, bias_second_new = adam_step(
        projection_bias_rows, grad_bias, bias_first, bias_second, VECTOR_RATE, 0.0
    )
    vector_new, vector_first_new, vector_second_new = adam_step(
        norm_vectors, grad_vector, vector_first, vector_second, VECTOR_RATE, 0.0
    )
    return (
        block_out,
        input_grad,
        qkv_new,
        qkv_first_new,
        qkv_second_new,
        out_new,
        out_first_new,
        out_second_new,
        up_new,
        up_first_new,
        up_second_new,
        down_new,
        down_first_new,
        down_second_new,
        bias_new,
        bias_first_new,
        bias_second_new,
        vector_new,
        vector_first_new,
        vector_second_new,
    )


def solution(mesh):
    return jax.shard_map(
        body,
        mesh=mesh,
        in_specs=(
            P("dp", "tensor", None),
            P("dp", "tensor", None),
            P("dp", "tensor"),
            P(None, "dp", "tensor"),
            P("dp", None, "tensor"),
            P("tensor", "dp"),
            P("dp", None, "tensor"),
            P(None, "tensor", "dp"),
            P(None, "tensor"),
            P(),
            P("dp", None, "tensor"),
            P("tensor", "dp"),
            P("dp", None, "tensor"),
            P(None, "tensor", "dp"),
            P(None, "tensor"),
            P(),
            P("dp", None, "tensor"),
            P("tensor", "dp"),
            P("dp", None, "tensor"),
            P(None, "tensor", "dp"),
            P(None, "tensor"),
            P(),
        ),
        out_specs=(
            P("dp", "tensor", None),
            P("dp", "tensor", None),
            P("dp", None, "tensor"),
            P("dp", None, "tensor"),
            P("dp", None, "tensor"),
            P("tensor", "dp"),
            P("tensor", "dp"),
            P("tensor", "dp"),
            P("dp", None, "tensor"),
            P("dp", None, "tensor"),
            P("dp", None, "tensor"),
            P(None, "tensor", "dp"),
            P(None, "tensor", "dp"),
            P(None, "tensor", "dp"),
            P(None, "tensor"),
            P(None, "tensor"),
            P(None, "tensor"),
            P(),
            P(),
            P(),
        ),
        check_vma=False,
    )
```

profile of v0, /device:TPU:0, one launch (start us, length us, event | category | flops | bytes accessed | tf_op | source)
XLA Modules:
  0.0 2057.7 jit_solution(1499836925227159668)
XLA Ops:
  9.0 16.4 all_gather.51
  25.3 13.8 all_gather.50
  45.3 1707.0 %while.27 = (s32[]{:T(128)}, f32[1280,3,320]{0,2,1:T(8,128)}, f32[320,1280]{1,0:T(8,128)}, f32[1280,4,320]{0,2,1:T(8,128)}, f32[4,320,1280]{2,1,0:T(8,128)}, /*i...) while((s32[]{:T(128)}, f32[1280,3,320]{0,2,1:T(8,128)}, ...), condition=%wide.region_30.31_spmd.clone, body=%wide.region_0.30_spmd.clone.sunk | while | flops 54673776640 | bytes 1415245440 | solution.py:330
  52.4 14.6 all_gather.69
  72.5 9.6 all-gather.16.cloned.1.call-done
  82.2 78.7 %all-gather.12.cloned.1.call-done = bf16[1536,1280]{1,0:T(8,128)(2,1)} async-done(((bf16[384,1280]{1,0:T(8,128)(2,1)}), bf16[1536,1280]{1,0:T(8,128)(2,1)}) %all-gather.12.cloned.1.call-update) | async-done | bytes 3932176 | tf_op jit(solution)/shard_map/while/body/eval_jaxpr/all_gather | solution.py:124
  160.9 7.3 convolution_add_fusion.9
  174.4 7.8 fusion.299
  219.4 70.2 %reduce-scatter.14.cloned.1.call-done = bf16[384,1280]{1,0:T(8,128)(2,1)} async-done(((bf16[1536,1280]{1,0:T(8,128)(2,1)}), bf16[384,1280]{1,0:T(8,128)(2,1)}) %reduce-scatter.14.cloned.1.call-update) | async-done | bytes 983056 | tf_op jit(solution)/shard_map/while/body/eval_jaxpr/reduce_scatter | solution.py:132
  297.0 30.5 %all-gather.20.cloned.1.call-done = bf16[4,320,1280]{1,2,0:T(8,128)(2,1)} async-done(((bf16[4,320,160]{1,2,0:T(8,128)(2,1)}), bf16[4,320,1280]{1,2,0:T(8,128)(2,1)}) %all-gather.20.cloned.1.call-update) | async-done | bytes 3276816 | tf_op jit(solution)/shard_map/while/body/eval_jaxpr/all_gather | solution.py:197
  333.8 31.3 %all-gather.14.cloned.1.call-done = bf16[1280,4,320]{2,0,1:T(8,128)(2,1)} async-done(((bf16[160,4,320]{2,0,1:T(8,128)(2,1)}), bf16[1280,4,320]{2,0,1:T(8,128)(2,1)}) %all-gather.14.cloned.1.call-update) | async-done | bytes 3276816 | tf_op jit(solution)/shard_map/while/body/eval_jaxpr/all_gather | solution.py:196
  371.0 72.6 %all-gather.18.cloned.1.call-done = bf16[1536,1280]{1,0:T(8,128)(2,1)} async-done(((bf16[384,1280]{1,0:T(8,128)(2,1)}), bf16[1536,1280]{1,0:T(8,128)(2,1)}) %all-gather.18.cloned.1.call-update) | async-done | bytes 3932176 | tf_op jit(solution)/shard_map/while/body/eval_jaxpr/all_gather | solution.py:124
  443.6 10.2 convolution_add_fusion.10
  453.9 9.3 copy.80
  463.1 57.8 %all-gather.22.cloned.1.call-done = bf16[1,1536,1280]{2,1,0:T(8,128)(2,1)} async-done(((bf16[1,384,1280]{2,1,0:T(8,128)(2,1)}), bf16[1,1536,1280]{2,1,0:T(8,128)(2,1)}) %all-gather.22.cloned.1.call-update) | async-done | bytes 3932176 | tf_op jit(solution)/shard_map/while/body/eval_jaxpr/all_gather | solution.py:128
  520.9 11.4 convert_reduce_fusion.12
  534.2 6.7 convolution_convert_fusion.7
  541.0 71.3 %reduce-scatter.16.cloned.1.call-done = bf16[384,1280]{1,0:T(8,128)(2,1)} async-done(((bf16[1536,1280]{1,0:T(8,128)(2,1)}), bf16[384,1280]{1,0:T(8,128)(2,1)}) %reduce-scatter.16.cloned.1.call-update) | async-done | bytes 983056 | tf_op jit(solution)/shard_map/while/body/eval_jaxpr/reduce_scatter | solution.py:141
  622.2 12.9 fusion.320
  635.2 62.5 %all-gather.24.cloned.1.call-done = bf16[1536,1280]{1,0:T(8,128)(2,1)} async-done(((bf16[384,1280]{1,0:T(8,128)(2,1)}), bf16[1536,1280]{1,0:T(8,128)(2,1)}) %all-gather.24.cloned.1.call-update) | async-done | bytes 3932176 | tf_op jit(solution)/shard_map/while/body/eval_jaxpr/all_gather | solution.py:128
  702.3 11.8 multiply_reduce_fusion.11
  715.7 7.3 multiply_convert_fusion.13
  726.0 7.6 multiply_reduce_fusion.9
  733.5 12.7 multiply_convert_fusion.11
  747.9 7.5 multiply_reduce_fusion.10
  755.3 9.4 multiply_convert_fusion.12
  806.6 7.0 fusion.318
  826.0 9.3 fusion.316
  839.0 9.6 select_add_fusion.10
  863.4 21.7 %reduce-scatter.18.cloned.1.call-done = bf16[384,1280]{1,0:T(8,128)(2,1)} async-done(((bf16[1536,1280]{1,0:T(8,128)(2,1)}), bf16[384,1280]{1,0:T(8,128)(2,1)}) %reduce-scatter.18.cloned.1.call-update) | async-done | bytes 983056 | tf_op jit(solution)/shard_map/while/body/eval_jaxpr/reduce_scatter | solution.py:141
  898.5 14.6 all_gather.69
  918.4 10.1 all-gather.16.cloned.1.call-done
  928.5 78.7 %all-gather.12.cloned.1.call-done = bf16[1536,1280]{1,0:T(8,128)(2,1)} async-done(((bf16[384,1280]{1,0:T(8,128)(2,1)}), bf16[1536,1280]{1,0:T(8,128)(2,1)}) %all-gather.12.cloned.1.call-update) | async-done | bytes 3932176 | tf_op jit(solution)/shard_map/while/body/eval_jaxpr/all_gather | solution.py:124
  1007.2 7.3 convolution_add_fusion.9
  1020.8 7.8 fusion.299
  1028.6 12.2 fusion.303
  1076.0 70.2 %reduce-scatter.14.cloned.1.call-done = bf16[384,1280]{1,0:T(8,128)(2,1)} async-done(((bf16[1536,1280]{1,0:T(8,128)(2,1)}), bf16[384,1280]{1,0:T(8,128)(2,1)}) %reduce-scatter.14.cloned.1.call-update) | async-done | bytes 983056 | tf_op jit(solution)/shard_map/while/body/eval_jaxpr/reduce_scatter | solution.py:132
  1153.6 30.5 %all-gather.20.cloned.1.call-done = bf16[4,320,1280]{1,2,0:T(8,128)(2,1)} async-done(((bf16[4,320,160]{1,2,0:T(8,128)(2,1)}), bf16[4,320,1280]{1,2,0:T(8,128)(2,1)}) %all-gather.20.cloned.1.call-update) | async-done | bytes 3276816 | tf_op jit(solution)/shard_map/while/body/eval_jaxpr/all_gather | solution.py:197
  1190.3 31.3 %all-gather.14.cloned.1.call-done = bf16[1280,4,320]{2,0,1:T(8,128)(2,1)} async-done(((bf16[160,4,320]{2,0,1:T(8,128)(2,1)}), bf16[1280,4,320]{2,0,1:T(8,128)(2,1)}) %all-gather.14.cloned.1.call-update) | async-done | bytes 3276816 | tf_op jit(solution)/shard_map/while/body/eval_jaxpr/all_gather | solution.py:196
  1227.6 72.6 %all-gather.18.cloned.1.call-done = bf16[1536,1280]{1,0:T(8,128)(2,1)} async-done(((bf16[384,1280]{1,0:T(8,128)(2,1)}), bf16[1536,1280]{1,0:T(8,128)(2,1)}) %all-gather.18.cloned.1.call-update) | async-done | bytes 3932176 | tf_op jit(solution)/shard_map/while/body/eval_jaxpr/all_gather | solution.py:124
  1300.2 10.2 convolution_add_fusion.10
  1310.4 9.2 copy.80
  1319.7 57.6 %all-gather.22.cloned.1.call-done = bf16[1,1536,1280]{2,1,0:T(8,128)(2,1)} async-done(((bf16[1,384,1280]{2,1,0:T(8,128)(2,1)}), bf16[1,1536,1280]{2,1,0:T(8,128)(2,1)}) %all-gather.22.cloned.1.call-update) | async-done | bytes 3932176 | tf_op jit(solution)/shard_map/while/body/eval_jaxpr/all_gather | solution.py:128
  1377.3 11.4 convert_reduce_fusion.12
  1390.6 6.7 convolution_convert_fusion.7
  1397.4 71.4 %reduce-scatter.16.cloned.1.call-done = bf16[384,1280]{1,0:T(8,128)(2,1)} async-done(((bf16[1536,1280]{1,0:T(8,128)(2,1)}), bf16[384,1280]{1,0:T(8,128)(2,1)}) %reduce-scatter.16.cloned.1.call-update) | async-done | bytes 983056 | tf_op jit(solution)/shard_map/while/body/eval_jaxpr/reduce_scatter | solution.py:141
  1478.6 12.9 fusion.320
  1491.6 62.5 %all-gather.24.cloned.1.call-done = bf16[1536,1280]{1,0:T(8,128)(2,1)} async-done(((bf16[384,1280]{1,0:T(8,128)(2,1)}), bf16[1536,1280]{1,0:T(8,128)(2,1)}) %all-gather.24.cloned.1.call-update) | async-done | bytes 3932176 | tf_op jit(solution)/shard_map/while/body/eval_jaxpr/all_gather | solution.py:128
  1558.7 11.8 multiply_reduce_fusion.11
  1572.2 7.3 multiply_convert_fusion.13
  1582.4 7.6 multiply_reduce_fusion.9
  1589.9 12.6 multiply_convert_fusion.11
  1604.3 7.5 multiply_reduce_fusion.10
  1611.7 9.4 multiply_convert_fusion.12
  1663.1 7.0 fusion.318
  1682.4 9.3 fusion.316
  1698.4 10.6 select_add_fusion.10
  1717.9 7.6 select_add_fusion.8
  1725.5 16.0 reduce-scatter.18.cloned.1.call-done
  1757.6 9.6 copy.72
  1767.3 7.4 copy.70
  1774.8 8.6 copy.73
  1785.3 108.4 %all-reduce.4.cloned.1.call-done = f32[13,1280]{1,0:T(8,128)} async-done(((f32[13,1280]{1,0:T(8,128)}), f32[13,1280]{1,0:T(8,128)}) %all-reduce.4.cloned.1.call-update) | async-done | bytes 66576 | tf_op jit(solution)/shard_map/psum | solution.py:345
  1898.9 139.9 %all-reduce.6.cloned.1.call-done = f32[1280,4,320]{2,1,0:T(4,128)} async-done(((f32[1280,4,320]{2,1,0:T(4,128)}), f32[1280,4,320]{2,1,0:T(4,128)}) %all-reduce.6.cloned.1.call-update) | async-done | bytes 6553616
  (606 shorter events, 377.4 us)
Async XLA Ops:
  8.0 37.3 %copy-start.73 = (f32[7,320]{1,0:T(8,128)S(1)}, f32[7,320]{1,0:T(8,128)}, u32[]{:S(2)}) copy-start(f32[7,320]{1,0:T(8,128)} %param.32) | copy-start | bytes 26884
  8.0 37.3 %copy-start.4 = (bf16[2,384,1280]{2,1,0:T(8,128)(2,1)S(1)}, bf16[2,384,1280]{2,1,0:T(8,128)(2,1)}, u32[]{:S(2)}) copy-start(bf16[2,384,1280]{2,1,0:T(8,128)(2,1)} %param.24) | copy-start | bytes 5898244
  45.3 24.3 %copy-start.49 = (bf16[320,160]{0,1:T(8,128)(2,1)}, bf16[320,160]{0,1:T(8,128)(2,1)S(1)}, u32[]{:S(2)}) copy-start(bf16[320,160]{0,1:T(8,128)(2,1)S(1)} %get-tuple-element.739) | copy-start | bytes 307204 | tf_op jit(solution)/shard_map/while
  45.3 36.8 %all-gather.16.cloned.1.call-start = ((), (), s32[]{:S(2)}) async-start(), calls=%async_computation.14 | async-start | bytes 3317760 | tf_op jit(solution)/shard_map/while/body/eval_jaxpr/all_gather | solution.py:190
  46.1 114.8 %all-gather.12.cloned.1.call-start = ((), (), s32[]{:S(2)}) async-start(), calls=%async_computation.12 | async-start | bytes 4915200 | tf_op jit(solution)/shard_map/while/body/eval_jaxpr/all_gather | solution.py:124
  48.1 24.4 %copy-start.53 = (f32[1280]{0:T(1024)}, f32[1280]{0:T(1024)S(1)}, u32[]{:S(2)}) copy-start(f32[1280]{0:T(1024)S(1)} %get-tuple-element.614) | copy-start | bytes 15364 | tf_op jit(solution)/shard_map/while
  48.1 567.2 %copy-start.46 = (f32[1280]{0:T(1024)}, f32[1280]{0:T(1024)S(1)}, u32[]{:S(2)}) copy-start(f32[1280]{0:T(1024)S(1)} %get-tuple-element.617) | copy-start | bytes 15364 | tf_op jit(solution)/shard_map/while
  48.1 24.4 %copy-start.60 = (f32[384]{0:T(512)}, f32[384]{0:T(512)S(1)}, u32[]{:S(2)}) copy-start(f32[384]{0:T(512)S(1)} %broadcast_multiply_fusion.16) | copy-start | bytes 4612 | tf_op jit(solution)/shard_map/while
  50.0 239.6 %reduce-scatter.14.cloned.1.call-start = ((), (), s32[]{:S(2)}) async-start(), calls=%async_computation.15 | async-start | bytes 4915200 | tf_op jit(solution)/shard_map/while/body/eval_jaxpr/reduce_scatter | solution.py:132
  69.7 100.3 %copy-start.18 = (f32[1536,80]{0,1:T(8,128)}, f32[1536,80]{0,1:T(8,128)S(1)}, u32[]{:S(2)}) copy-start(f32[1536,80]{0,1:T(8,128)S(1)} %get-tuple-element.626) | copy-start | bytes 1474564 | tf_op jit(solution)/shard_map/while
  171.6 29.6 %copy-start.7 = (bf16[1536,4,80]{0,2,1:T(8,128)(2,1)}, bf16[1536,4,80]{0,2,1:T(8,128)(2,1)S(1)}, u32[]{:S(2)}) copy-start(bf16[1536,4,80]{0,2,1:T(8,128)(2,1)S(1)} %get-tuple-element.630) | copy-start | bytes 2949124 | tf_op jit(solution)/shard_map/while
  218.2 109.3 %all-gather.20.cloned.1.call-start = ((), (), s32[]{:S(2)}) async-start(), calls=%async_computation.17 | async-start | bytes 4423680 | tf_op jit(solution)/shard_map/while/body/eval_jaxpr/all_gather | solution.py:197
  218.8 146.3 %all-gather.14.cloned.1.call-start = ((), (), s32[]{:S(2)}) async-start(), calls=%async_computation.13 | async-start | bytes 4423680 | tf_op jit(solution)/shard_map/while/body/eval_jaxpr/all_gather | solution.py:196
  219.4 224.3 %all-gather.18.cloned.1.call-start = ((), (), s32[]{:S(2)}) async-start(), calls=%async_computation.16 | async-start | bytes 4915200 | tf_op jit(solution)/shard_map/while/body/eval_jaxpr/all_gather | solution.py:124
  294.6 226.3 %all-gather.22.cloned.1.call-start = ((), (), s32[]{:S(2)}) async-start(), calls=%async_computation.18 | async-start | bytes 4915200 | tf_op jit(solution)/shard_map/while/body/eval_jaxpr/all_gather | solution.py:128
  297.0 315.4 %reduce-scatter.16.cloned.1.call-start = ((), (), s32[]{:S(2)}) async-start(), calls=%async_computation.19 | async-start | bytes 4915200 | tf_op jit(solution)/shard_map/while/body/eval_jaxpr/reduce_scatter | solution.py:141
  541.0 156.8 %all-gather.24.cloned.1.call-start = ((), (), s32[]{:S(2)}) async-start(), calls=%async_computation.20 | async-start | bytes 4915200 | tf_op jit(solution)/shard_map/while/body/eval_jaxpr/all_gather | solution.py:128
  620.8 227.9 %reduce-scatter.20.cloned.1.call-start = ((), (), s32[]{:S(2)}) async-start(), calls=%async_computation.22 | async-start | bytes 4915200 | tf_op jit(solution)/shard_map/while/body/eval_jaxpr/reduce_scatter | solution.py:132
  635.1 62.6 %copy-start.43 = (bf16[320,1280]{0,1:T(8,128)(2,1)S(1)}, bf16[320,1280]{0,1:T(8,128)(2,1)}, u32[]{:S(2)}) copy-start(bf16[320,1280]{0,1:T(8,128)(2,1)} %all_gather.69) | copy-start | bytes 2457604 | tf_op jit(solution)/shard_map/while
  635.1 67.1 %copy-start.13 = (bf16[1536,1,320]{0,2,1:T(8,128)(2,1)S(1)}, bf16[1536,1,320]{0,2,1:T(8,128)(2,1)}, u32[]{:S(2)}) copy-start(bf16[1536,1,320]{0,2,1:T(8,128)(2,1)} %slice.316) | copy-start | bytes 2949124 | tf_op jit(solution)/shard_map/while
  635.1 249.9 %reduce-scatter.18.cloned.1.call-start = ((), (), s32[]{:S(2)}) async-start(), calls=%async_computation.21 | async-start | bytes 4915200 | tf_op jit(solution)/shard_map/while/body/eval_jaxpr/reduce_scatter | solution.py:141
  857.4 27.6 %copy-start.54 = (f32[1280]{0:T(1024)S(1)}, f32[1280]{0:T(1024)}, u32[]{:S(2)}) copy-start(f32[1280]{0:T(1024)} %copy-done.53) | copy-start | bytes 15364 | tf_op jit(solution)/shard_map/while
  857.4 27.6 %copy-start.61 = (f32[384]{0:T(512)S(1)}, f32[384]{0:T(512)}, u32[]{:S(2)}) copy-start(f32[384]{0:T(512)} %copy-done.60) | copy-start | bytes 4612 | tf_op jit(solution)/shard_map/while
  857.4 27.6 %copy-start.70 = (f32[384]{0:T(512)S(1)}, f32[384]{0:T(512)}, u32[]{:S(2)}) copy-start(f32[384]{0:T(512)} %copy-done.69) | copy-start | bytes 4612 | tf_op jit(solution)/shard_map/while
  857.4 29.8 %copy-start.72 = (f32[1,1280]{1,0:T(1,128)S(1)}, f32[1,1280]{1,0:T(1,128)}, u32[]{:S(2)}) copy-start(f32[1,1280]{1,0:T(1,128)} %stack.67) | copy-start | bytes 15364 | tf_op jit(solution)/shard_map/while
  857.5 29.9 %copy-start.58 = (f32[6,1280]{1,0:T(8,128)S(1)}, f32[6,1280]{1,0:T(8,128)}, u32[]{:S(2)}) copy-start(f32[6,1280]{1,0:T(8,128)} %get-tuple-element.705) | copy-start | bytes 92164 | tf_op jit(solution)/shard_map/while
  863.4 27.8 %copy-start.45 = (bf16[160,3,320]{2,0,1:T(8,128)(2,1)S(1)}, bf16[160,3,320]{2,0,1:T(8,128)(2,1)}, u32[]{:S(2)}) copy-start(bf16[160,3,320]{2,0,1:T(8,128)(2,1)} %copy-done.44) | copy-start | bytes 921604 | tf_op jit(solution)/shard_map/while
  863.4 27.8 %copy-start.50 = (bf16[320,160]{0,1:T(8,128)(2,1)S(1)}, bf16[320,160]{0,1:T(8,128)(2,1)}, u32[]{:S(2)}) copy-start(bf16[320,160]{0,1:T(8,128)(2,1)} %copy-done.49) | copy-start | bytes 307204 | tf_op jit(solution)/shard_map/while
  863.4 27.8 %copy-start.74 = (f32[7,320]{1,0:T(8,128)S(1)}, f32[7,320]{1,0:T(8,128)}, u32[]{:S(2)}) copy-start(f32[7,320]{1,0:T(8,128)} %get-tuple-element.851) | copy-start | bytes 26884 | tf_op jit(solution)/shard_map/while
  891.4 24.4 %copy-start.49 = (bf16[320,160]{0,1:T(8,128)(2,1)}, bf16[320,160]{0,1:T(8,128)(2,1)S(1)}, u32[]{:S(2)}) copy-start(bf16[320,160]{0,1:T(8,128)(2,1)S(1)} %get-tuple-element.739) | copy-start | bytes 307204 | tf_op jit(solution)/shard_map/while
  891.4 37.1 %all-gather.16.cloned.1.call-start = ((), (), s32[]{:S(2)}) async-start(), calls=%async_computation.14 | async-start | bytes 3317760 | tf_op jit(solution)/shard_map/while/body/eval_jaxpr/all_gather | solution.py:190
  892.2 115.0 %all-gather.12.cloned.1.call-start = ((), (), s32[]{:S(2)}) async-start(), calls=%async_computation.12 | async-start | bytes 4915200 | tf_op jit(solution)/shard_map/while/body/eval_jaxpr/all_gather | solution.py:124
  894.2 24.1 %copy-start.53 = (f32[1280]{0:T(1024)}, f32[1280]{0:T(1024)S(1)}, u32[]{:S(2)}) copy-start(f32[1280]{0:T(1024)S(1)} %get-tuple-element.614) | copy-start | bytes 15364 | tf_op jit(solution)/shard_map/while
  894.2 577.5 %copy-start.46 = (f32[1280]{0:T(1024)}, f32[1280]{0:T(1024)S(1)}, u32[]{:S(2)}) copy-start(f32[1280]{0:T(1024)S(1)} %get-tuple-element.617) | copy-start | bytes 15364 | tf_op jit(solution)/shard_map/while
  894.2 24.1 %copy-start.60 = (f32[384]{0:T(512)}, f32[384]{0:T(512)S(1)}, u32[]{:S(2)}) copy-start(f32[384]{0:T(512)S(1)} %broadcast_multiply_fusion.16) | copy-start | bytes 4612 | tf_op jit(solution)/shard_map/while
  896.1 250.1 %reduce-scatter.14.cloned.1.call-start = ((), (), s32[]{:S(2)}) async-start(), calls=%async_computation.15 | async-start | bytes 4915200 | tf_op jit(solution)/shard_map/while/body/eval_jaxpr/reduce_scatter | solution.py:132
  915.8 100.5 %copy-start.18 = (f32[1536,80]{0,1:T(8,128)}, f32[1536,80]{0,1:T(8,128)S(1)}, u32[]{:S(2)}) copy-start(f32[1536,80]{0,1:T(8,128)S(1)} %get-tuple-element.626) | copy-start | bytes 1474564 | tf_op jit(solution)/shard_map/while
  1018.0 39.8 %copy-start.7 = (bf16[1536,4,80]{0,2,1:T(8,128)(2,1)}, bf16[1536,4,80]{0,2,1:T(8,128)(2,1)S(1)}, u32[]{:S(2)}) copy-start(bf16[1536,4,80]{0,2,1:T(8,128)(2,1)S(1)} %get-tuple-element.630) | copy-start | bytes 2949124 | tf_op jit(solution)/shard_map/while
  1074.7 109.3 %all-gather.20.cloned.1.call-start = ((), (), s32[]{:S(2)}) async-start(), calls=%async_computation.17 | async-start | bytes 4423680 | tf_op jit(solution)/shard_map/while/body/eval_jaxpr/all_gather | solution.py:197
  1075.3 146.3 %all-gather.14.cloned.1.call-start = ((), (), s32[]{:S(2)}) async-start(), calls=%async_computation.13 | async-start | bytes 4423680 | tf_op jit(solution)/shard_map/while/body/eval_jaxpr/all_gather | solution.py:196
  1075.9 224.3 %all-gather.18.cloned.1.call-start = ((), (), s32[]{:S(2)}) async-start(), calls=%async_computation.16 | async-start | bytes 4915200 | tf_op jit(solution)/shard_map/while/body/eval_jaxpr/all_gather | solution.py:124
  1151.2 226.1 %all-gather.22.cloned.1.call-start = ((), (), s32[]{:S(2)}) async-start(), calls=%async_computation.18 | async-start | bytes 4915200 | tf_op jit(solution)/shard_map/while/body/eval_jaxpr/all_gather | solution.py:128
  1153.5 315.2 %reduce-scatter.16.cloned.1.call-start = ((), (), s32[]{:S(2)}) async-start(), calls=%async_computation.19 | async-start | bytes 4915200 | tf_op jit(solution)/shard_map/while/body/eval_jaxpr/reduce_scatter | solution.py:141
  1397.3 156.8 %all-gather.24.cloned.1.call-start = ((), (), s32[]{:S(2)}) async-start(), calls=%async_computation.20 | async-start | bytes 4915200 | tf_op jit(solution)/shard_map/while/body/eval_jaxpr/all_gather | solution.py:128
  1477.2 231.9 %reduce-scatter.20.cloned.1.call-start = ((), (), s32[]{:S(2)}) async-start(), calls=%async_computation.22 | async-start | bytes 4915200 | tf_op jit(solution)/shard_map/while/body/eval_jaxpr/reduce_scatter | solution.py:132
  1491.5 62.6 %copy-start.43 = (bf16[320,1280]{0,1:T(8,128)(2,1)S(1)}, bf16[320,1280]{0,1:T(8,128)(2,1)}, u32[]{:S(2)}) copy-start(bf16[320,1280]{0,1:T(8,128)(2,1)} %all_gather.69) | copy-start | bytes 2457604 | tf_op jit(solution)/shard_map/while
  1491.5 67.1 %copy-start.13 = (bf16[1536,1,320]{0,2,1:T(8,128)(2,1)S(1)}, bf16[1536,1,320]{0,2,1:T(8,128)(2,1)}, u32[]{:S(2)}) copy-start(bf16[1536,1,320]{0,2,1:T(8,128)(2,1)} %slice.316) | copy-start | bytes 2949124 | tf_op jit(solution)/shard_map/while
  1491.6 249.9 %reduce-scatter.18.cloned.1.call-start = ((), (), s32[]{:S(2)}) async-start(), calls=%async_computation.21 | async-start | bytes 4915200 | tf_op jit(solution)/shard_map/while/body/eval_jaxpr/reduce_scatter | solution.py:141
  1717.9 25.8 %copy-start.72 = (f32[1,1280]{1,0:T(1,128)S(1)}, f32[1,1280]{1,0:T(1,128)}, u32[]{:S(2)}) copy-start(f32[1,1280]{1,0:T(1,128)} %stack.67) | copy-start | bytes 15364 | tf_op jit(solution)/shard_map/while
  1717.9 25.9 %copy-start.58 = (f32[6,1280]{1,0:T(8,128)S(1)}, f32[6,1280]{1,0:T(8,128)}, u32[]{:S(2)}) copy-start(f32[6,1280]{1,0:T(8,128)} %get-tuple-element.705) | copy-start | bytes 92164 | tf_op jit(solution)/shard_map/while
  1752.3 141.4 %all-reduce.4.cloned.1.call-start = ((), (), s32[]{:S(2)}) async-start(), calls=%async_computation.10 | async-start | bytes 163840 | tf_op jit(solution)/shard_map/psum | solution.py:345
  1754.7 142.1 %reduce-scatter.10.cloned.1.call-start = ((), (), s32[]{:S(2)}) async-start(), calls=%async_computation.8 | async-start | bytes 2211840 | tf_op jit(solution)/shard_map/reduce_scatter | solution.py:336
  1757.6 281.2 %all-reduce.6.cloned.1.call-start = ((), (), s32[]{:S(2)}) async-start(), calls=%async_computation.11 | async-start | bytes 15728640
  1767.3 276.1 %reduce-scatter.8.cloned.1.call-start = ((), (), s32[]{:S(2)}) async-start(), calls=%async_computation.7 | async-start | bytes 6635520 | tf_op jit(solution)/shard_map/reduce_scatter | solution.py:335
  1774.8 271.9 %reduce-scatter.12.cloned.1.call-start = ((), (), s32[]{:S(2)}) async-start(), calls=%async_computation.9 | async-start | bytes 8847360 | tf_op jit(solution)/shard_map/reduce_scatter | solution.py:338
  1783.5 111.1 %copy-start.80 = (f32[7,320]{1,0:T(8,128)S(1)}, f32[7,320]{1,0:T(8,128)}, u32[]{:S(2)}) copy-start(f32[7,320]{1,0:T(8,128)} %param.38) | copy-start | bytes 26884
  1783.5 111.1 %copy-start.81 = (f32[7,320]{1,0:T(8,128)S(1)}, f32[7,320]{1,0:T(8,128)}, u32[]{:S(2)}) copy-start(f32[7,320]{1,0:T(8,128)} %param.44) | copy-start | bytes 26884
  1783.5 111.8 %copy-start.78 = (f32[6,1280]{1,0:T(8,128)S(1)}, f32[6,1280]{1,0:T(8,128)}, u32[]{:S(2)}) copy-start(f32[6,1280]{1,0:T(8,128)} %param.39) | copy-start | bytes 92164
  1783.5 111.8 %copy-start.79 = (f32[6,1280]{1,0:T(8,128)S(1)}, f32[6,1280]{1,0:T(8,128)}, u32[]{:S(2)}) copy-start(f32[6,1280]{1,0:T(8,128)} %param.45) | copy-start | bytes 92164
  1783.5 113.3 %copy-start.64 = (f32[320,160]{0,1:T(8,128)S(1)}, f32[320,160]{0,1:T(8,128)}, u32[]{:S(2)}) copy-start(f32[320,160]{0,1:T(8,128)} %param.29) | copy-start | bytes 614404
  1783.5 113.3 %copy-start.77 = (f32[320,160]{0,1:T(8,128)S(1)}, f32[320,160]{0,1:T(8,128)}, u32[]{:S(2)}) copy-start(f32[320,160]{0,1:T(8,128)} %param.35) | copy-start | bytes 614404
  1783.5 255.3 %copy-start.51 = (f32[160,4,320]{2,1,0:T(4,128)S(1)}, f32[160,4,320]{2,1,0:T(4,128)}, u32[]{:S(2)}) copy-start(f32[160,4,320]{2,1,0:T(4,128)} %param.30) | copy-start | bytes 2457604
  1783.5 255.3 %copy-start.62 = (f32[160,4,320]{2,1,0:T(4,128)S(1)}, f32[160,4,320]{2,1,0:T(4,128)}, u32[]{:S(2)}) copy-start(f32[160,4,320]{2,1,0:T(4,128)} %param.36) | copy-start | bytes 2457604
  1896.8 146.5 %copy-start.55 = (f32[160,3,320]{2,0,1:T(8,128)S(1)}, f32[160,3,320]{2,0,1:T(8,128)}, u32[]{:S(2)}) copy-start(f32[160,3,320]{2,0,1:T(8,128)} %param.28) | copy-start | bytes 1843204
  (139 other events, 909.9 us)
Sparse Core Ops, SparseCore 0:
  48.2 33.8 all-gather.15
  84.4 76.4 all-gather.11
  218.3 71.2 reduce-scatter.13
  291.5 35.9 all-gather.19
  329.4 35.6 all-gather.13
  367.2 76.4 all-gather.17
  445.9 74.9 all-gather.21
  541.1 71.2 reduce-scatter.15
  620.9 76.7 all-gather.23
  700.0 71.2 reduce-scatter.19
  813.8 71.1 reduce-scatter.17
  894.0 34.4 all-gather.15
  930.8 76.4 all-gather.11
  1074.9 71.2 reduce-scatter.13
  1148.1 35.9 all-gather.19
  1186.0 35.6 all-gather.13
  1223.7 76.4 all-gather.17
  1302.3 74.9 all-gather.21
  1397.5 71.2 reduce-scatter.15
  1477.3 76.7 all-gather.23
  1556.6 71.2 reduce-scatter.19
  1670.2 71.2 reduce-scatter.17
  1758.9 40.6 reduce-scatter.9
  1803.3 59.7 reduce-scatter.7
  1866.6 75.9 reduce-scatter.11
Sparse Core Ops, SparseCore 1:
  1759.9 133.8 all-reduce.3
  1897.3 141.4 all-reduce.5
where the time goes:
time: 2060 us
  waiting for transfers between devices  1260 us (61%)
  matrix products  368 us (18%)
  other arithmetic  209 us (10%)
  local copies, waits for them, and re-layouts  139 us (7%)
  blocking collectives  59.3 us (3%)
    all_gather x4, waiting for transfers between devices, gather_rows(): return lax.all_gather(local_rows, 'tensor', axis=0, tiled=True)  303 us
    all_gather x4, waiting for transfers between devices, gather_grads(): return lax.all_gather(local_rows, 'tensor', axis=0, tiled=True)  240 us
    reduce_scatter x4, waiting for transfers between devices, input_sum(): lax.psum_scatter(lax.dot_general(left_rows, right_matrix, (((1,), (1,)),...  180 us
    reduce_scatter x4, waiting for transfers between devices, branch_sum(): lax.psum_scatter(jnp.dot(left_rows, right_matrix, preferred_element_type=...  140 us
    unnamed x6, waiting for transfers between devices  140 us
    psum x1, waiting for transfers between devices, body(): lax.psum(jnp.concatenate([placed, totals[5]], axis=0), ('dp', 'tensor'))  108 us
    all_gather x2, waiting for transfers between devices, fetch_feed(): lax.all_gather(up_projection_weight.astype(jnp.bfloat16), 'dp', axis=0, t...  62.6 us
    all_gather x2, waiting for transfers between devices, fetch_feed(): lax.all_gather(down_weight.astype(jnp.bfloat16), 'dp', axis=2, tiled=True)  60.9 us
  transfers between devices with their start and end apart: 27, of which 22 were waited for; matrix products, arithmetic and copies ran while one was open for 24% of the time, Pallas kernels for 0%

commit v1 on v0

v1 whole, which is shorter than its diff:
```python
import functools

import jax
import jax.numpy as jnp
from jax import lax
from jax.experimental import pallas as pl
from jax.experimental.pallas import tpu as pltpu
from jax.sharding import Mesh, PartitionSpec as P

HEAD = 80
HALF = HEAD // 2
STEP = 10
MIDDLE = 1024

NORM_EPS = 1e-06
BETA_ONE = 0.9
BETA_TWO = 0.95
ADAM_EPS = 1e-08
MATRIX_RATE = 0.03
VECTOR_RATE = 0.2
MATRIX_DECAY = 0.1
GELU_SLOPE = 1.702
LOG2E = 1.4426950408889634
LN2 = 0.6931471805599453

BF = jnp.bfloat16
F32 = jnp.float32


def dot(left, right, left_dim, right_dim):
    return lax.dot_general(
        left, right, (((left_dim,), (right_dim,)), ((), ())), preferred_element_type=F32
    )


def normalise(source):
    centre = source - jnp.mean(source, axis=-1, keepdims=True)
    spread = lax.rsqrt(jnp.mean(centre * centre, axis=-1, keepdims=True) + NORM_EPS)
    return centre * spread, spread


def norm_back(gradient, gain_vec, normed, spread):
    scaled = gradient * gain_vec
    return spread * (
        scaled
        - jnp.mean(scaled, axis=-1, keepdims=True)
        - normed * jnp.mean(scaled * normed, axis=-1, keepdims=True)
    )


def adam_step(weight, gradient, first, second, rate, decay):
    first_new = BETA_ONE * first + (1.0 - BETA_ONE) * gradient
    second_new = BETA_TWO * second + (1.0 - BETA_TWO) * gradient * gradient
    fix_one = 1.0 - BETA_ONE**STEP
    fix_two = 1.0 - BETA_TWO**STEP
    ratio = first_new / fix_one / (jnp.sqrt(second_new / fix_two) + ADAM_EPS)
    return (weight - rate * (ratio + decay * weight), first_new, second_new)


NEAR = [(0, 1), (1, 0), (2, 3), (3, 2)]
MIDS = [(1, 2), (2, 1)]
OUTER = [(1, 0), (2, 3)]
INNER = [(0, 1), (3, 2)]


def after(value, *earlier):
    return lax.optimization_barrier((value, *earlier))[0]


def move(value, axis, pairs, *earlier):
    return lax.ppermute(after(value, *earlier) if earlier else value, axis, pairs)


def swap_core(value, *earlier):
    return move(value, "c", [(0, 1), (1, 0)], *earlier)


def swap_bit(value, bit, count, *earlier):
    return move(value, "g", [(i, i ^ (1 << bit)) for i in range(count)], *earlier)


class Gather:
    def __init__(self, block, order, g, count):
        self.rows, self.columns = block.shape
        self.order, self.g, self.count = list(order), g, count
        self.bits = len(self.order)
        self.current = block.reshape((1,) * self.bits + block.shape)

    def step(self, *earlier):
        if not self.order:
            return self.current
        bit = self.order.pop(0)
        other = swap_bit(self.current, bit, self.count, *earlier)
        axis = self.bits - 1 - bit
        upper = ((self.g >> bit) & 1) == 1
        mine = self.current
        self.current = jnp.concatenate(
            [jnp.where(upper, other, mine), jnp.where(upper, mine, other)], axis=axis
        )
        return other

    def finish(self, *earlier):
        last = self.step(*earlier)
        while self.order:
            last = self.step()
        return last

    def whole(self):
        return self.current.reshape(self.count * self.rows, self.columns)


def scatter_g(full, order, g, count, *earlier):
    bits = len(order)
    rows = full.shape[0] // count
    current = full.reshape((2,) * bits + (rows, full.shape[1]))
    for bit in order:
        axis = bits - 1 - bit
        mine = (g >> bit) & 1
        sent = lax.dynamic_slice_in_dim(current, 1 - mine, 1, axis).astype(BF)
        kept = lax.dynamic_slice_in_dim(current, mine, 1, axis)
        current = kept.astype(F32) + swap_bit(sent, bit, count, *earlier).astype(F32)
        earlier = ()
    return current.reshape(rows, full.shape[1])


def row_moves(step):
    moves = []
    for c in range(2):
        for z in range(4):
            place = z ^ step
            moves.append((c * 4 + z, (place >> 1) * 4 + 2 * c + (place & 1)))
    return moves


def rows_in(local, c, z, *earlier):
    _, size, width = local.shape
    part = size // 2
    pieces = []
    for step in range(4):
        place = z ^ step
        sent = lax.dynamic_slice(local, (place & 1, (place >> 1) * part, 0), (1, part, width))
        pieces.append(move(sent, ("c", "z"), row_moves(step), *earlier))
    own = jnp.concatenate(pieces, axis=0)
    both = jnp.stack([own, swap_core(own)])
    place = 2 * c + (z & 1)
    blocks = []
    for k in range(4):
        for h in range(2):
            which = h ^ c
            blocks.append(
                lax.dynamic_slice(both, (which, k ^ place ^ (2 * which), 0, 0), (1, 1, part, width)).reshape(
                    part, width
                )
            )
    return jnp.concatenate(blocks, axis=0)


def rows_out(turned, start, c, z, *earlier):
    rows, width = turned.shape
    part = rows // 8
    place = 2 * c + (z & 1)
    longer = jnp.concatenate([turned, turned[:part]], axis=0)
    pieces = []
    for step in range(4):
        k = place ^ step
        first = lax.rem(k * 2 * part + c * part - start + rows, rows)
        sent = lax.dynamic_slice(longer, (first, 0), (part, width))
        back = [(b, a) for a, b in row_moves(step)]
        pieces.append(move(sent, ("c", "z"), back, *earlier))
    stacked = jnp.stack(pieces)
    blocks = []
    for j in range(2):
        for h in range(2):
            blocks.append(
                lax.dynamic_slice(stacked, (z ^ (2 * h + j), 0, 0), (1, part, width)).reshape(part, width)
            )
    return jnp.concatenate(blocks, axis=0).reshape(2, 2 * part, width), pieces


def add_up(value, count):
    value = value + swap_core(value)
    for bit in range(count.bit_length() - 1):
        value = value + swap_bit(value, bit, count)
    for distance in (1, 2):
        value = value + lax.ppermute(value, "z", [(i, i ^ distance) for i in range(4)])
    return value


SEGMENTS = ((0, MIDDLE, False), (MIDDLE, None, True))


def attend_kernel(q_ref, k_ref, v_ref, cos_ref, sin_ref, mask_ref, qt_ref, kt_ref, vt_ref, ot_ref, lse_ref, *, block):
    cosine, sine = cos_ref[...], sin_ref[...]

    def turn(source, factor):
        first, second = source[:HALF], source[HALF:]
        return (
            jnp.concatenate([first * cosine - second * sine, second * cosine + first * sine], axis=0) * factor
        ).astype(BF)

    rows = q_ref.shape[1]
    qt = turn(q_ref[...], LOG2E * HEAD ** (-0.5))
    kt = turn(k_ref[...], 1.0)
    vt = v_ref[...].astype(BF)
    qt_ref[0] = qt
    kt_ref[0] = kt
    vt_ref[0] = vt
    for first, last, masked in ((0, MIDDLE, False), (MIDDLE, rows, True)):
        keys = kt[:, first:last]
        values = vt[:, first:last]
        for at in range(first, last, block):
            scores = dot(keys, qt[:, at : at + block], 0, 0)
            if masked:
                scores = scores + mask_ref[:, at - first : at - first + block]
            largest = jnp.max(scores, axis=0, keepdims=True)
            raised = jnp.exp2(scores - largest)
            total = jnp.sum(raised, axis=0, keepdims=True)
            mixed = dot(values, raised.astype(BF), 1, 0)
            ot_ref[:, at : at + block] = (mixed / total).astype(BF)
            lse_ref[0, :, at : at + block] = largest + jnp.log2(total)


def attend_back_kernel(qt_ref, kt_ref, vt_ref, ot_ref, dot_ref, lse_ref, cos_ref, sin_ref, mask_ref, dq_ref, dk_ref, dv_ref, *, block):
    cosine, sine = cos_ref[...], sin_ref[...]

    def turn_back(grad, factor):
        first, second = grad[:HALF] * factor, grad[HALF:] * factor
        return jnp.concatenate([first * cosine + second * sine, second * cosine - first * sine], axis=0).astype(BF)

    rows = cos_ref.shape[1]
    qt, kt, vt, dot_ = qt_ref[0], kt_ref[0], vt_ref[0], dot_ref[...]
    delta = jnp.sum(dot_.astype(F32) * ot_ref[...].astype(F32), axis=0, keepdims=True)
    lse = lse_ref[0]
    queries = qt.astype(F32).T.astype(BF)
    grads = dot_.astype(F32).T.astype(BF)
    dq_parts, dk_parts, dv_parts = [], [], []
    for first, last, masked in ((0, MIDDLE, False), (MIDDLE, rows, True)):
        keys = kt[:, first:last]
        values = vt[:, first:last]
        dk = dv = None
        for at in range(first, last, block):
            sl = slice(at, at + block)
            scores = dot(keys, qt[:, sl], 0, 0)
            if masked:
                scores = scores + mask_ref[:, at - first : at - first + block]
            chances = jnp.exp2(scores - lse[:, sl])
            grad_chances = dot(values, dot_[:, sl], 0, 0)
            grad_scores = (chances * (grad_chances - delta[:, sl])).astype(BF)
            dv_part = dot(chances.astype(BF), grads[sl], 1, 0)
            dk_part = dot(grad_scores, queries[sl], 1, 0)
            dv = dv_part if dv is None else dv + dv_part
            dk = dk_part if dk is None else dk + dk_part
            dq_parts.append(dot(keys, grad_scores, 1, 0))
        dk_parts.append(dk.T)
        dv_parts.append(dv.T)
    dq_ref[0] = turn_back(jnp.concatenate(dq_parts, axis=1), HEAD ** (-0.5))
    dk_ref[0] = turn_back(jnp.concatenate(dk_parts, axis=1), LN2)
    dv_ref[0] = jnp.concatenate(dv_parts, axis=1).astype(BF)


def attend(mixed, cosine, sine, mask):
    rows = mixed.shape[1]
    heads = 4
    once = lambda shape: pl.BlockSpec(shape, lambda h: (0, 0))
    part = lambda which: pl.BlockSpec((HEAD, rows), lambda h: ((h // 2) * 8 + 2 * which + h % 2, 0))
    each = pl.BlockSpec((1, HEAD, rows), lambda h: (h, 0, 0))
    return pl.pallas_call(
        functools.partial(attend_kernel, block=256),
        grid=(heads,),
        in_specs=[part(0), part(1), part(2), once(cosine.shape), once(sine.shape), once(mask.shape)],
        out_specs=[
            each,
            each,
            each,
            pl.BlockSpec((HEAD, rows), lambda h: (h, 0)),
            pl.BlockSpec((1, 1, rows), lambda h: (h, 0, 0)),
        ],
        out_shape=[jax.ShapeDtypeStruct((heads, HEAD, rows), BF)] * 3
        + [
            jax.ShapeDtypeStruct((heads * HEAD, rows), BF),
            jax.ShapeDtypeStruct((heads, 1, rows), F32),
        ],
        compiler_params=pltpu.CompilerParams(vmem_limit_bytes=40 * 2**20),
        cost_estimate=pl.CostEstimate(flops=heads * 4 * 1310720 * 256, bytes_accessed=16 * 2**20, transcendentals=heads * 1310720),
        name="attend",
    )(mixed, mixed, mixed, cosine, sine, mask)


def attend_back(saved, grad_mixed, cosine, sine, mask):
    qt, kt, vt, mixed, lse = saved
    heads, _, rows = qt.shape
    once = lambda shape: pl.BlockSpec(shape, lambda h: (0, 0))
    each = pl.BlockSpec((1, HEAD, rows), lambda h: (h, 0, 0))
    flat = pl.BlockSpec((HEAD, rows), lambda h: (h, 0))
    return pl.pallas_call(
        functools.partial(attend_back_kernel, block=256),
        grid=(heads,),
        in_specs=[
            each,
            each,
            each,
            flat,
            flat,
            pl.BlockSpec((1, 1, rows), lambda h: (h, 0, 0)),
            once(cosine.shape),
            once(sine.shape),
            once(mask.shape),
        ],
        out_specs=[each, each, each],
        out_shape=[jax.ShapeDtypeStruct((heads, HEAD, rows), BF)] * 3,
        compiler_params=pltpu.CompilerParams(vmem_limit_bytes=50 * 2**20),
        cost_estimate=pl.CostEstimate(flops=heads * 10 * 1310720 * 256, bytes_accessed=16 * 2**20, transcendentals=heads * 1310720),
        name="attend_back",
    )(qt, kt, vt, mixed, grad_mixed, lse, cosine, sine, mask)


def body(
    tokens_in,
    cotangent,
    picture_ids,
    patch_positions,
    qkv_weight,
    out_weight,
    up_projection_weight,
    down_weight,
    projection_bias_rows,
    norm_vectors,
    qkv_first,
    out_first,
    up_first,
    down_first,
    bias_first,
    vector_first,
    qkv_second,
    out_second,
    up_second,
    down_second,
    bias_second,
    vector_second,
):
    count = lax.axis_size("g")
    bits = count.bit_length() - 1
    g, c, z = lax.axis_index("g"), lax.axis_index("c"), lax.axis_index("z")
    is_mid = (z == 1) | (z == 2)
    low_core = c == 0
    d_local = qkv_weight.shape[0]
    width = tokens_in.shape[2]
    part_rows = tokens_in.shape[1]
    inner = 640
    forth, back = tuple(range(bits)), tuple(reversed(range(bits)))

    with jax.named_scope("small"):
        bias_half = jnp.where(
            low_core,
            jnp.concatenate([projection_bias_rows[0:3, :160].reshape(480), projection_bias_rows[3:5].reshape(640)]),
            jnp.concatenate([projection_bias_rows[0:3, 160:].reshape(480), projection_bias_rows[5:7].reshape(640)]),
        )
        counted = jnp.concatenate([picture_ids[None], patch_positions], axis=0).astype(F32)
        small = jnp.concatenate([bias_half, counted.reshape(3 * 2 * part_rows)])[None]
        relative = jnp.concatenate(
            [small] + [lax.ppermute(small, "z", [(i, i ^ d) for i in range(4)]) for d in (1, 2, 3)], axis=0
        )
        biases = relative[:, :1120]
        bias_near = biases[:2]
        bias_far = jnp.where(is_mid, biases[2:][::-1], biases[2:])
        counted = relative[:, 1120:].reshape(4, 3, 2, part_rows)
        counted = jnp.where((z & 1) == 0, counted[:, :, 0], counted[:, :, 1])
        counted = jnp.concatenate([lax.dynamic_slice_in_dim(counted, k ^ z, 1, 0) for k in range(4)], axis=0)
        counted = jnp.where((z >> 1) == c, counted, swap_core(counted))
        counted = jnp.moveaxis(counted, 1, 0).reshape(3, 4 * part_rows)

    with jax.named_scope("pack"):
        qkv_low = qkv_weight.astype(BF).reshape(d_local, 3, 2, 160)
        out_low = out_weight.astype(BF).T.reshape(d_local, 1, 2, 160)
        first_low = jnp.concatenate([qkv_low, out_low], axis=1)
        up_low = up_projection_weight.astype(BF)
        down_low = jnp.transpose(down_weight.astype(BF), (2, 0, 1))
        halves = [
            jnp.concatenate(
                [
                    first_low[:, :, h].reshape(d_local, inner),
                    up_low[:, 2 * h : 2 * h + 2].reshape(d_local, inner),
                    down_low[:, 2 * h : 2 * h + 2].reshape(d_local, inner),
                ],
                axis=1,
            )
            for h in range(2)
        ]
        keep = jnp.where(low_core, halves[0], halves[1])
        other = swap_core(jnp.where(low_core, halves[1], halves[0]))
        shard = jnp.concatenate([jnp.where(low_core, keep, other), jnp.where(low_core, other, keep)], axis=0)
        shard_q, shard_u, shard_d = [shard[:, i * inner : (i + 1) * inner] for i in range(3)]

    def near_z(own, *earlier):
        partner = move(own, "z", NEAR, *earlier)
        return jnp.concatenate([own, partner], axis=-1)

    def far_of(mid, end):
        return jnp.where(is_mid, mid, end)

    with jax.named_scope("rows_x"):
        source = rows_in(tokens_in, c, z)
    with jax.named_scope("gq"):
        near_q = near_z(shard_q)
        mid_q = move(near_q, "z", MIDS)
        qa = Gather(near_q, forth, g, count)
        qax = qa.step()
        end_q = move(mid_q, "z", OUTER)
    with jax.named_scope("gu"):
        near_u = near_z(shard_u, near_q)
        mid_u = move(near_u, "z", MIDS)
        ua = Gather(near_u, forth, g, count)
        uax = ua.step(near_q)
        end_u = move(mid_u, "z", OUTER, end_q)
    with jax.named_scope("gq"):
        qay = qa.finish()
        qb = Gather(far_of(mid_q, end_q), back, g, count)
        qby = qb.step(uax)
        qbx = qb.finish(uax)
    with jax.named_scope("gd"):
        near_d = near_z(shard_d, near_u)
        mid_d = move(near_d, "z", MIDS, mid_u)
        da = Gather(near_d, forth, g, count)
        dax = da.step(qax)
        end_d = move(mid_d, "z", OUTER, end_u)
    with jax.named_scope("gu"):
        uay = ua.finish(qay)
        ub = Gather(far_of(mid_u, end_u), back, g, count)
        uby = ub.step(qby)
        ubx = ub.finish(dax)
    with jax.named_scope("gd"):
        day = da.finish(uby)
        db = Gather(far_of(mid_d, end_d), back, g, count)
        dby = db.step(uay)
        dbx = db.finish(qbx)
    with jax.named_scope("rows_g"):
        grad_rows = rows_in(cotangent, c, z, end_u)

    first_wa, first_wb = qa.whole(), qb.whole()
    up_wa, up_wb = ua.whole(), ub.whole()
    down_wa, down_wb = da.whole(), db.whole()

    rows = source.shape[0]
    start = jnp.sum((counted[0] == 1).astype(jnp.int32))
    turned = lambda value: jnp.roll(value, -start, axis=0)
    counted = jnp.roll(counted, -start, axis=1)
    source = turned(source).astype(F32)
    grad_rows = turned(grad_rows)
    ids = counted[0, MIDDLE:]
    mask = jnp.where(ids[:, None] == ids[None, :], 0.0, -1e30).astype(F32)
    powers = jnp.arange(HEAD // 4, dtype=F32) * (2.0 / (HEAD // 2))
    inverse = jnp.power(10000.0, -powers)
    angles = jnp.concatenate([inverse[:, None] * counted[1][None], inverse[:, None] * counted[2][None]], axis=0)
    cosine, sine = jnp.cos(angles), jnp.sin(angles)

    hat_one, scale_one = normalise(source)
    a_one = (hat_one * norm_vectors[0] + norm_vectors[1]).astype(BF)

    def qkv_bias(pair):
        zero = jnp.zeros((160,), F32)
        return jnp.concatenate([pair[0, :480], zero, pair[1, :480], zero])

    saved = []
    for weight, bias, earlier in ((first_wa, bias_near, (dax, qby)), (first_wb, bias_far, (uby,))):
        mixed = dot(after(weight, *earlier), a_one, 0, 1) + qkv_bias(bias)[:, None]
        saved.append(attend(mixed, cosine, sine, mask))

    def out_part(weight):
        return jnp.concatenate([weight[:, 480:640], weight[:, 1120:1280]], axis=1)

    def qkv_part(weight):
        return jnp.concatenate([weight[:, :480], weight[:, 640:1120]], axis=1)

    out_wa, out_wb = out_part(first_wa), out_part(first_wb)
    branch = (dot(saved[0][3], out_wa, 0, 1) + dot(after(saved[1][3], grad_rows, uay), out_wb, 0, 1)).astype(BF)
    middle = source + (branch.astype(F32) + swap_core(branch).astype(F32)) + norm_vectors[4]
    hat_two, scale_two = normalise(middle)
    a_two = (hat_two * norm_vectors[2] + norm_vectors[3]).astype(BF)

    def up_bias(pair):
        return pair[:, 480:].reshape(1280)

    active, slopes = [], []
    for weight, bias, earlier in ((up_wa, bias_near, (dby,)), (up_wb, bias_far, (day,))):
        hidden = dot(a_two, after(weight, *earlier), 1, 0) + up_bias(bias)
        gate = jax.nn.sigmoid(GELU_SLOPE * hidden)
        active.append((hidden * gate).astype(BF))
        slopes.append((gate + GELU_SLOPE * hidden * gate * (1.0 - gate)).astype(BF))
    feed = (dot(active[0], down_wa, 1, 1) + dot(active[1], down_wb, 1, 1)).astype(BF)
    result = middle + (feed.astype(F32) + swap_core(feed).astype(F32)) + norm_vectors[5]
    with jax.named_scope("rows_out"):
        block_out, out_pieces = rows_out(result.astype(BF), start, c, z)

    def give(near, far, *earlier):
        far = scatter_g(far, forth, g, count, *earlier)
        near = scatter_g(near, back, g, count, *earlier)
        far = far + lax.ppermute(far.astype(BF), "z", INNER).astype(F32)
        near = near + lax.ppermute(far.astype(BF), "z", MIDS).astype(F32)
        own = near[:, :inner] + lax.ppermute(near[:, inner:].astype(BF), "z", NEAR).astype(F32)
        upper, lower = own[:d_local], own[d_local:]
        keep = jnp.where(low_core, upper, lower)
        other = swap_core(jnp.where(low_core, lower, upper).astype(BF)).astype(F32)
        return jnp.stack([jnp.where(low_core, keep, other), jnp.where(low_core, other, keep)], axis=1)

    with jax.named_scope("sd"):
        grad_down = give(*[dot(grad_rows, a, 0, 0).astype(BF) for a in active], day, dbx)
    grad_hidden = [
        (dot(grad_rows, w, 1, 0) * s.astype(F32)).astype(BF) for w, s in ((down_wa, slopes[0]), (down_wb, slopes[1]))
    ]
    bias_up = [jnp.sum(v, axis=0, dtype=F32) for v in grad_hidden]
    with jax.named_scope("su"):
        grad_up = give(*[dot(a_two, v, 0, 0).astype(BF) for v in grad_hidden])
    part = (dot(grad_hidden[0], up_wa, 1, 1) + dot(grad_hidden[1], up_wb, 1, 1)).astype(BF)
    grad_second = part.astype(F32) + swap_core(part).astype(F32)
    grad_out = grad_rows.astype(F32)
    grad_middle = grad_out + norm_back(grad_second, norm_vectors[2], hat_two, scale_two)
    grad_branch = grad_middle.astype(BF)
    grad_mixed, grad_outw = [None, None], [None, None]
    for i, weight, earlier in ((1, out_wb, ()), (0, out_wa, tuple(out_pieces))):
        grad_outw[i] = dot(grad_branch, saved[i][3], 0, 1).astype(BF)
        grad_att = dot(weight, grad_branch, 0, 1).astype(BF)
        if earlier:
            grad_att = after(grad_att, *earlier)
        dq, dk, dv = attend_back(saved[i], grad_att, cosine, sine, mask)
        joined = jnp.stack([v.reshape(2, 160, rows) for v in (dq, dk, dv)], axis=1)
        grad_mixed[i] = joined.reshape(960, rows)
    bias_qkv = [jnp.sum(v, axis=1, dtype=F32) for v in grad_mixed]
    part = (
        dot(grad_mixed[0], qkv_part(first_wa), 0, 1) + dot(grad_mixed[1], qkv_part(first_wb), 0, 1)
    ).astype(BF)
    grad_first_full = []
    for v, o in zip(grad_mixed, grad_outw):
        gq = dot(a_one, v, 0, 1).astype(BF)
        grad_first_full.append(jnp.concatenate([gq[:, :480], o[:, :160], gq[:, 480:], o[:, 160:]], axis=1))
    with jax.named_scope("sq"):
        grad_first = give(*grad_first_full)
    grad_norm = part.astype(F32) + swap_core(part).astype(F32)
    grad_source = grad_middle + norm_back(grad_norm, norm_vectors[0], hat_one, scale_one)
    with jax.named_scope("rows_dx"):
        input_grad, _ = rows_out(grad_source.astype(BF), start, c, z)
        input_grad = input_grad.astype(F32)

    def own_half(value):
        return jnp.where(low_core, value[: rows // 2], value[rows // 2 :])

    vector_grad = jnp.stack(
        [
            jnp.sum(own_half(v), axis=0)
            for v in (grad_norm * hat_one, grad_norm, grad_second * hat_two, grad_second, grad_middle, grad_out)
        ]
    )
    far_zero = jnp.where(z < 2, 2, 1)
    far_one = jnp.where(z < 2, 3, 0)
    placed = jnp.zeros((7, 4, 320), F32)
    for index, place in enumerate((z, z ^ 1, far_zero, far_one)):
        qkv_sum = bias_qkv[index // 2].reshape(2, 3, 1, 160)[index % 2]
        up_sum = bias_up[index // 2].reshape(2, 2, 1, 320)[index % 2]
        placed = lax.dynamic_update_slice(placed, qkv_sum, (0, place, c * 160))
        placed = lax.dynamic_update_slice(placed, up_sum, (3 + 2 * c, place, 0))
    with jax.named_scope("vectors"):
        summed = add_up(jnp.concatenate([placed.reshape(7, 4 * 320), vector_grad], axis=0), count)
    grad_bias = lax.dynamic_slice(summed, (0, z * 320), (7, 320))
    grad_vector = summed[7:]

    first_split = grad_first.reshape(d_local, 2, 4, 160)
    grad_qkv = jnp.moveaxis(first_split[:, :, :3], 1, 2).reshape(d_local, 3, 320)
    grad_o = first_split[:, :, 3].reshape(d_local, 320).T
    grad_up = grad_up.reshape(d_local, 4, 320)
    grad_down = jnp.transpose(grad_down.reshape(d_local, 4, 320), (1, 2, 0))
    outputs = [block_out, input_grad]
    for weight, grad, first, second, rate, decay in (
        (qkv_weight, grad_qkv, qkv_first, qkv_second, MATRIX_RATE, MATRIX_DECAY),
        (out_weight, grad_o, out_first, out_second, MATRIX_RATE, MATRIX_DECAY),
        (up_projection_weight, grad_up, up_first, up_second, MATRIX_RATE, MATRIX_DECAY),
        (down_weight, grad_down, down_first, down_second, MATRIX_RATE, MATRIX_DECAY),
        (projection_bias_rows, grad_bias, bias_first, bias_second, VECTOR_RATE, 0.0),
        (norm_vectors, grad_vector, vector_first, vector_second, VECTOR_RATE, 0.0),
    ):
        outputs.extend(adam_step(weight, grad, first, second, rate, decay))
    return tuple(outputs)


def solution(mesh):
    devices = mesh.devices.reshape(mesh.shape["dp"] // 2, 2, mesh.shape["tensor"])
    own_mesh = Mesh(devices, ("g", "c", "z"))
    rows = P(("g", "c"), "z", None)
    in_weights = (P(("g", "c"), None, "z"), P("z", ("g", "c")), P(("g", "c"), None, "z"), P(None, "z", ("g", "c")))
    vectors = (P(None, "z"), P())
    params = in_weights + vectors
    out_specs = [rows, rows]
    for spec in params:
        out_specs.extend([spec] * 3)
    return jax.shard_map(
        body,
        mesh=own_mesh,
        in_specs=(rows, rows, P(("g", "c"), "z"), P(None, ("g", "c"), "z")) + params * 3,
        out_specs=tuple(out_specs),
        check_vma=False,
    )
```

time: 2060 us -> 957 us (0.46)
  waiting for transfers between devices: 1260 us -> 331 us
  matrix products: 368 us -> 153 us
  starting transfers between devices: 1.14 us -> 122 us
  Pallas kernels: 0 us -> 61.9 us
  blocking collectives: 59.3 us -> 0 us
  local copies, waits for them, and re-layouts: 139 us -> 96.5 us
  other arithmetic: 209 us -> 175 us
    all_gather x14 -> x0, waiting for transfers between devices: 686 us -> none  [the longest x4 303 us: gather_rows(): return lax.all_gather(local_rows, 'tensor', axis=0, tiled=True)]
    ppermute x0 -> x77, waiting for transfers between devices: none -> 331 us  [the longest x63 259 us: move(): lax.ppermute(after(value, *earlier) if earlier else value, axis, pairs)]
    reduce_scatter x11 -> x0, waiting for transfers between devices: 321 us -> none  [the longest x4 180 us: input_sum(): lax.psum_scatter(lax.dot_general(left_rows, right_matrix, (((1,), (1,)),...]
    dot_general x60 -> x24, matrix products: 368 us -> 153 us  [dot(): lax.dot_general(left, right, (((left_dim,), (right_dim,)), ((), ())), pre...]
    unnamed x6 -> x0, waiting for transfers between devices: 140 us -> none
    ppermute x0 -> x77, starting transfers between devices: none -> 122 us  [the longest x63 85.1 us: move(): lax.ppermute(after(value, *earlier) if earlier else value, axis, pairs)]
    psum x1 -> x0, waiting for transfers between devices: 108 us -> none  [body(): lax.psum(jnp.concatenate([placed, totals[5]], axis=0), ('dp', 'tensor'))]
    while x328 -> x0, local copies, waits for them, and re-layouts: 63.7 us -> none
  transfers between devices with their start and end apart: 27 -> 77, of which waited for: 22 -> 27; matrix products, arithmetic and copies ran while one was open for 24% -> 36% of each run, Pallas kernels for 0% -> 7%
where the time goes in v1:
time: 957 us; the launch traced here: 947 us
  waiting for transfers between devices  331 us (35%)
  other arithmetic  175 us (18%)
  matrix products  153 us (16%)
  starting transfers between devices  122 us (13%)
  local copies, waits for them, and re-layouts  96.5 us (10%)
  Pallas kernels  61.9 us (6%)
    ppermute x63, waiting for transfers between devices, move(): lax.ppermute(after(value, *earlier) if earlier else value, axis, pairs)  259 us
    dot_general x24, matrix products, dot(): lax.dot_general(left, right, (((left_dim,), (right_dim,)), ((), ())), pre...  153 us
    ppermute x63, starting transfers between devices, move(): lax.ppermute(after(value, *earlier) if earlier else value, axis, pairs)  85.1 us
    ppermute x3, waiting for transfers between devices, give(): far = far + lax.ppermute(far.astype(BF), 'z', INNER).astype(F32)  38 us
    ppermute x2, waiting for transfers between devices, add_up(): lax.ppermute(value, 'z', [(i, i ^ distance) for i in range(4)])  33.9 us
    pallas_call x2, Pallas kernels, attend_back(): pl.pallas_call(functools.partial(attend_back_kernel, block=256), grid=(he...  32 us
    pallas_call x2, Pallas kernels, attend(): pl.pallas_call(functools.partial(attend_kernel, block=256), grid=(heads,)...  30 us
    unnamed x330, local copies, waits for them, and re-layouts  22.3 us
  transfers between devices with their start and end apart: 77, of which 27 were waited for; matrix products, arithmetic and copies ran while one was open for 36% of the time, Pallas kernels for 7%

profile of v1, /device:TPU:0, one launch (start us, length us, event | category | flops | bytes accessed | tf_op | source)
XLA Modules:
  0.0 946.8 jit_solution(11330700699266670884)
XLA Ops:
  3.5 5.1 collective-permute-start.7
  30.4 5.3 collective-permute-start
  48.5 16.2 %collective-permute-done.10 = bf16[320,640]{1,0:T(8,128)(2,1)S(1)} collective-permute-done((bf16[320,640]{1,0:T(8,128)(2,1)S(1)}, bf16[320,640]{1,0:T(8,128)(2,1)S(1)}, u32[]{:S(2)}, u32[]{:S(2)}) %collective-permute-start.10) | collective-permute-done | bytes 409632 | tf_op jit(solution)/shard_map/gq/ppermute | solution.py:71
  67.1 5.9 collective-permute-done.2
  79.7 3.7 collective-permute-start.4
  100.0 11.2 %collective-permute-done.18 = bf16[1,1,320,1280]{3,2,1,0:T(8,128)(2,1)S(1)} collective-permute-done((bf16[1,1,320,1280]{3,2,1,0:T(8,128)(2,1)}, bf16[1,1,320,1280]{3,2,1,0:T(8,128)(2,1)S(1)}, u32[]{:S(2)}, u32[]{:S(2)}) %collective-permute-start.18) | collective-permute-done | bytes 819232 | tf_op jit(solution)/shard_map/gu/ppermute | solution.py:71
  124.9 22.2 %collective-permute-done.17 = bf16[320,1280]{1,0:T(8,128)(2,1)S(1)} collective-permute-done((bf16[320,1280]{1,0:T(8,128)(2,1)S(1)}, bf16[320,1280]{1,0:T(8,128)(2,1)S(1)}, u32[]{:S(2)}, u32[]{:S(2)}) %collective-permute-start.17) | collective-permute-done | bytes 819232 | tf_op jit(solution)/shard_map/gq/ppermute | solution.py:71
  152.8 16.2 %collective-permute-done.22 = bf16[320,1280]{1,0:T(8,128)(2,1)S(1)} collective-permute-done((bf16[320,1280]{1,0:T(8,128)(2,1)S(1)}, bf16[320,1280]{1,0:T(8,128)(2,1)S(1)}, u32[]{:S(2)}, u32[]{:S(2)}) %collective-permute-start.22) | collective-permute-done | bytes 819232 | tf_op jit(solution)/shard_map/gu/ppermute | solution.py:71
  174.4 5.6 collective-permute-start.24
  180.0 3.5 collective-permute-start.25
  183.6 6.4 convolution_add_fusion.6.q_ref.k_ref.v_ref
  190.0 14.9 %attend.2 = (bf16[4,80,1536]{2,1,0:T(8,128)(2,1)S(1)}, bf16[4,80,1536]{2,1,0:T(8,128)(2,1)S(1)}, bf16[4,80,1536]{2,1,0:T(8,128)(2,1)S(1)}, bf16[320,1536]{1,0:T(8,128)(2,1)S(1)}, f32[4,1,1536]{2,1,0:T(1,128)S(1)}) custom-call(f32[1280,1536]{1,0:T(8,128)S(1)} %convolution_add_fusion.6.q_ref.k_ref.v_ref, ...), custom_call_target="tpu_custom_call" | custom-call | flops 5368709120 | bytes 16777216 | tf_op jit(solution)/shard_map/attend/pallas_call | solution.py:267
  206.8 5.5 fusion.68
  219.2 8.9 collective-permute-done.27
  235.9 14.2 %collective-permute-done.20 = bf16[2,1,320,1280]{3,2,1,0:T(8,128)(2,1)S(1)} collective-permute-done((bf16[2,1,320,1280]{3,2,1,0:T(8,128)(2,1)S(1)}, bf16[2,1,320,1280]{3,2,1,0:T(8,128)(2,1)S(1)}, u32[]{:S(2)}, u32[]{:S(2)}) %collective-permute-start.20) | collective-permute-done | bytes 1638432 | tf_op jit(solution)/shard_map/gq/ppermute | solution.py:71
  254.5 6.4 convolution_add_fusion.5.q_ref.k_ref.v_ref
  260.9 15.1 %attend.3 = (bf16[4,80,1536]{2,1,0:T(8,128)(2,1)S(1)}, bf16[4,80,1536]{2,1,0:T(8,128)(2,1)S(1)}, bf16[4,80,1536]{2,1,0:T(8,128)(2,1)S(1)}, bf16[320,1536]{1,0:T(8,128)(2,1)S(1)}, f32[4,1,1536]{2,1,0:T(1,128)S(1)}) custom-call(f32[1280,1536]{1,0:T(8,128)S(1)} %convolution_add_fusion.5.q_ref.k_ref.v_ref, ...), custom_call_target="tpu_custom_call" | custom-call | flops 5368709120 | bytes 16777216 | tf_op jit(solution)/shard_map/attend/pallas_call | solution.py:267
  279.5 3.8 fusion.116
  285.2 9.5 fusion.104
  297.3 4.6 collective-permute-start.30
  315.4 29.6 %collective-permute-done.36 = bf16[2,1,320,1280]{3,2,1,0:T(8,128)(2,1)S(1)} collective-permute-done((bf16[2,1,320,1280]{3,2,1,0:T(8,128)(2,1)S(1)}, bf16[2,1,320,1280]{3,2,1,0:T(8,128)(2,1)S(1)}, u32[]{:S(2)}, u32[]{:S(2)}) %collective-permute-start.36) | collective-permute-done | bytes 1638432 | tf_op jit(solution)/shard_map/gd/ppermute | solution.py:71
  349.2 5.2 fusion.113
  359.6 6.3 multiply_convert_fusion
  365.9 7.0 convolution_convert_fusion
  372.9 7.4 fusion.131
  380.3 7.0 convert_reduce_fusion.1
  387.3 7.3 convolution_convert_fusion.2
  394.6 7.4 fusion.132
  402.0 5.3 convolution_add_fusion.4
  407.3 6.3 convolution_convert_fusion.1
  416.4 8.7 convert_reduce_fusion.2
  426.5 8.3 convolution_convert_fusion.3
  440.8 12.3 %fusion.16 = bf16[1536,1280]{1,0:T(8,128)(2,1)} fusion(f32[1536,1280]{1,0:T(8,128)} %fusion.131, bf16[1280,1280]{1,0:T(8,128)(2,1)} %bitcast.290, f32[1536,1280]{1,0:T(8,128)} %copy-done.146), kind=kOutput, calls=%fused_computation.56 | convolution fusion | flops 5048893440 | bytes 22937600 | tf_op jit(solution)/shard_map/dot_general | solution.py:31
  454.9 10.1 %fusion.17 = bf16[1536,1280]{1,0:T(8,128)(2,1)S(1)} fusion(f32[1536,1280]{1,0:T(8,128)} %fusion.132, bf16[1536,1280]{1,0:T(8,128)(2,1)} %get-tuple-element.329, bf16[1280,1280]{1,0:T(8,128)(2,1)S(1)} %bitcast.289), kind=kOutput, calls=%fused_computation.57 | convolution fusion | flops 5037096960 | bytes 19005440 | tf_op jit(solution)/shard_map/dot_general | solution.py:31
  465.0 13.8 %collective-permute-done.58 = bf16[2,1,320,1280]{3,2,1,0:T(8,128)(2,1)S(1)} collective-permute-done((bf16[2,1,320,1280]{3,2,1,0:T(8,128)(2,1)S(1)}, bf16[2,1,320,1280]{3,2,1,0:T(8,128)(2,1)S(1)}, u32[]{:S(2)}, u32[]{:S(2)}) %collective-permute-start.58) | collective-permute-done | bytes 1638432 | tf_op jit(solution)/shard_map/su/ppermute | solution.py:71
  479.3 34.2 %collective-permute-done.66 = bf16[2,1,320,1280]{3,2,1,0:T(8,128)(2,1)S(1)} collective-permute-done((bf16[2,1,320,1280]{3,2,1,0:T(8,128)(2,1)S(1)}, bf16[2,1,320,1280]{3,2,1,0:T(8,128)(2,1)S(1)}, u32[]{:S(2)}, u32[]{:S(2)}) %collective-permute-start.66) | collective-permute-done | bytes 1638432 | tf_op jit(solution)/shard_map/sd/ppermute | solution.py:71
  518.9 15.7 %collective-permute-done.59 = bf16[1,1,320,1280]{3,2,1,0:T(8,128)(2,1)S(1)} collective-permute-done((bf16[1,1,320,1280]{3,2,1,0:T(8,128)(2,1)S(1)}, bf16[1,1,320,1280]{3,2,1,0:T(8,128)(2,1)S(1)}, u32[]{:S(2)}, u32[]{:S(2)}) %collective-permute-start.59) | collective-permute-done | bytes 819232 | tf_op jit(solution)/shard_map/su/ppermute | solution.py:71
  535.4 15.5 %collective-permute-done.67 = bf16[1,1,320,1280]{3,2,1,0:T(8,128)(2,1)S(1)} collective-permute-done((bf16[1,1,320,1280]{3,2,1,0:T(8,128)(2,1)S(1)}, bf16[1,1,320,1280]{3,2,1,0:T(8,128)(2,1)S(1)}, u32[]{:S(2)}, u32[]{:S(2)}) %collective-permute-start.67) | collective-permute-done | bytes 819232 | tf_op jit(solution)/shard_map/sd/ppermute | solution.py:71
  559.8 12.3 %collective-permute-done.60 = bf16[320,1280]{1,0:T(8,128)(2,1)S(1)} collective-permute-done((bf16[320,1280]{1,0:T(8,128)(2,1)S(1)}, bf16[320,1280]{1,0:T(8,128)(2,1)S(1)}, u32[]{:S(2)}, u32[]{:S(2)}) %collective-permute-start.60) | collective-permute-done | bytes 819232 | tf_op jit(solution)/shard_map/su/ppermute | solution.py:497
  573.9 12.6 %collective-permute-done.68 = bf16[320,1280]{1,0:T(8,128)(2,1)S(1)} collective-permute-done((bf16[320,1280]{1,0:T(8,128)(2,1)S(1)}, bf16[320,1280]{1,0:T(8,128)(2,1)S(1)}, u32[]{:S(2)}, u32[]{:S(2)}) %collective-permute-start.68) | collective-permute-done | bytes 819232 | tf_op jit(solution)/shard_map/sd/ppermute | solution.py:497
  594.5 16.4 %fusion.112 = (bf16[1536,1280]{1,0:T(8,128)(2,1)}, f32[1536,1280]{1,0:T(8,128)}, f32[1536,1280]{1,0:T(8,128)}, f32[1536,1280]{1,0:T(8,128)}, bf16[1536,1280]{1,0:T(8,128)(2,1)}) fusion(f32[1536]{0:T(1024)S(1)} %broadcast_multiply_fusion.4, f32[1536,1280]{1,0:T(8,128)S(1)} %bitcast.242, f32[1536]{0:T(1024)S(1)} %copy-done.108, ...), kind=kLoop, calls=%fused_computation.429 | loop fusion | flops 39321600 | bytes 59017216 | tf_op jit(solution)/shard_map/convert_element_type | solution.py:517
  611.0 5.3 convolution_convert_fusion.8.dot_ref
  624.3 16.2 %attend_back.3 = (bf16[4,80,1536]{2,1,0:T(8,128)(2,1)S(1)}, bf16[4,80,1536]{2,1,0:T(8,128)(2,1)S(1)}, bf16[4,80,1536]{2,1,0:T(8,128)(2,1)S(1)}) custom-call(bf16[4,80,1536]{2,1,0:T(8,128)(2,1)} %copy-done.8, bf16[4,80,1536]{2,1,0:T(8,128)(2,1)} %copy-done.9, bf16[4,80,1536]{2,1,0:T(8,128)(2,1)} %copy-done.10, bf16[320,1536]{1,0:T(8,128)(2,1)} %copy-done.3, ...), custom_call_target="tpu_custom_call" | custom-call | flops 13421772800 | bytes 16777216 | tf_op jit(solution)/shard_map/attend_back/pallas_call | solution.py:295
  643.5 4.2 fusion.25
  654.2 4.4 convolution_convert_fusion.4
  660.6 5.8 copy.140
  670.7 5.4 collective-permute-start.39
  678.4 3.7 collective-permute-start.41
  690.1 8.0 collective-permute-done.40
  698.2 10.5 %collective-permute-done.41 = bf16[192,1280]{1,0:T(8,128)(2,1)S(1)} collective-permute-done((bf16[192,1280]{1,0:T(8,128)(2,1)S(1)}, bf16[192,1280]{1,0:T(8,128)(2,1)S(1)}, u32[]{:S(2)}, u32[]{:S(2)}) %collective-permute-start.41) | collective-permute-done | bytes 491552 | tf_op jit(solution)/shard_map/rows_out/ppermute | solution.py:71
  709.5 15.8 %attend_back.2 = (bf16[4,80,1536]{2,1,0:T(8,128)(2,1)S(1)}, bf16[4,80,1536]{2,1,0:T(8,128)(2,1)S(1)}, bf16[4,80,1536]{2,1,0:T(8,128)(2,1)S(1)}) custom-call(bf16[4,80,1536]{2,1,0:T(8,128)(2,1)} %copy-done.5, bf16[4,80,1536]{2,1,0:T(8,128)(2,1)} %copy-done.6, bf16[4,80,1536]{2,1,0:T(8,128)(2,1)} %copy-done.7, bf16[320,1536]{1,0:T(8,128)(2,1)} %copy-done.1, ...), custom_call_target="tpu_custom_call" | custom-call | flops 13421772800 | bytes 16777216 | tf_op jit(solution)/shard_map/attend_back/pallas_call | solution.py:295
  727.8 6.3 convolution_convert_fusion.5
  743.5 8.1 fusion.30
  751.7 8.1 fusion.15
  774.0 20.2 %collective-permute-done.51 = bf16[1,1,320,1280]{3,2,1,0:T(8,128)(2,1)} collective-permute-done((bf16[1,1,320,1280]{3,2,1,0:T(8,128)(2,1)}, bf16[1,1,320,1280]{3,2,1,0:T(8,128)(2,1)}, u32[]{:S(2)}, u32[]{:S(2)}) %collective-permute-start.51) | collective-permute-done | bytes 819232 | tf_op jit(solution)/shard_map/sq/ppermute | solution.py:71
  800.3 13.1 %collective-permute-done.52 = bf16[320,1280]{1,0:T(8,128)(2,1)S(1)} collective-permute-done((bf16[320,1280]{1,0:T(8,128)(2,1)S(1)}, bf16[320,1280]{1,0:T(8,128)(2,1)S(1)}, u32[]{:S(2)}, u32[]{:S(2)}) %collective-permute-start.52) | collective-permute-done | bytes 819232 | tf_op jit(solution)/shard_map/sq/ppermute | solution.py:497
  822.3 5.3 multiply_subtract_fusion.1
  830.6 17.3 %collective-permute-start.54 = (bf16[320,640]{1,0:T(8,128)(2,1)S(1)}, bf16[320,640]{1,0:T(8,128)(2,1)}, u32[]{:S(2)}, u32[]{:S(2)}) collective-permute-start(bf16[320,640]{1,0:T(8,128)(2,1)S(1)} %slice.606), channel_id=1, source_target_pairs={{0,1},{1,0},{2,3},{3,2},{4,5},{5,4},{6,7},{7,6},{8,9},{9,8},{10,11... | collective-permute-start | bytes 1228808 | tf_op jit(solution)/shard_map/sq/ppermute | solution.py:499
  847.9 8.3 multiply_reduce_fusion.2
  856.2 4.4 fusion.24
  860.6 7.5 convert_add_fusion.1
  869.9 3.8 multiply_subtract_fusion
  886.7 5.2 collective-permute-start.44
  904.3 33.9 %collective-permute-done.76 = f32[13,1280]{1,0:T(8,128)} collective-permute-done((f32[13,1280]{1,0:T(8,128)}, f32[13,1280]{1,0:T(8,128)}, u32[]{:S(2)}, u32[]{:S(2)}) %collective-permute-start.76) | collective-permute-done | bytes 66592 | tf_op jit(solution)/shard_map/vectors/ppermute | solution.py:185
  (707 shorter events, 285.4 us)
Async XLA Ops:
  3.5 26.2 %collective-permute-start.7 = (f32[1,3424]{1,0:T(1,128)S(1)}, f32[1,3424]{1,0:T(1,128)S(1)}, u32[]{:S(2)}, u32[]{:S(2)}) collective-permute-start(f32[1,3424]{1,0:T(1,128)S(1)} %broadcast_in_dim.15), channel_id=1, source_target_pairs={{0,3},{1,2},{2,1},{3,0},{4,7},{5,6},{6,5},{7,4},{8,11},{9,10},{10,... | collective-permute-start | bytes 41096 | tf_op jit(solution)/shard_map/small/ppermute | solution.py:361
  8.6 21.8 %collective-permute-start.6 = (f32[1,3424]{1,0:T(1,128)S(1)}, f32[1,3424]{1,0:T(1,128)S(1)}, u32[]{:S(2)}, u32[]{:S(2)}) collective-permute-start(f32[1,3424]{1,0:T(1,128)S(1)} %broadcast_in_dim.15), channel_id=1, source_target_pairs={{0,2},{1,3},{2,0},{3,1},{4,6},{5,7},{6,4},{7,5},{8,10},{9,11},{10,... | collective-permute-start | bytes 41096 | tf_op jit(solution)/shard_map/small/ppermute | solution.py:361
  8.6 27.4 %collective-permute-start.5 = (f32[1,3424]{1,0:T(1,128)S(1)}, f32[1,3424]{1,0:T(1,128)}, u32[]{:S(2)}, u32[]{:S(2)}) collective-permute-start(f32[1,3424]{1,0:T(1,128)S(1)} %broadcast_in_dim.15), channel_id=1, source_target_pairs={{0,1},{1,0},{2,3},{3,2},{4,5},{5,4},{6,7},{7,6},{8,9},{9,8},{10,11... | collective-permute-start | bytes 41096 | tf_op jit(solution)/shard_map/small/ppermute | solution.py:361
  24.7 18.0 %collective-permute-start.9 = (bf16[160,1920]{1,0:T(8,128)(2,1)}, bf16[160,1920]{1,0:T(8,128)(2,1)}, u32[]{:S(2)}, u32[]{:S(2)}) collective-permute-start(bf16[160,1920]{1,0:T(8,128)(2,1)} %broadcast_select_fusion.26), channel_id=1, source_target_pairs={{0,4},{4,0},{1,5},{5,1},{2,6},{6,2},{3,7},{7,3},{8,12},{12,8},{9,1... | collective-permute-start | bytes 1843208 | tf_op jit(solution)/shard_map/pack/ppermute | solution.py:71
  26.0 53.6 %collective-permute-start.3 = (bf16[1,192,1280]{2,1,0:T(8,128)(2,1)}, bf16[1,192,1280]{2,1,0:T(8,128)(2,1)S(1)}, u32[]{:S(2)}, u32[]{:S(2)}) collective-permute-start(bf16[1,192,1280]{2,1,0:T(8,128)(2,1)} %get-tuple-element.259), channel_id=1, source_target_pairs={{0,5},{1,4},{2,1},{3,0},{4,7},{5,6},{6,3},{7,2},{8,13},{9,12},{10,... | collective-permute-start | bytes 1474568 | tf_op jit(solution)/shard_map/rows_x/ppermute | solution.py:71
  29.7 36.3 %collective-permute-start.1 = (bf16[1,192,1280]{2,1,0:T(8,128)(2,1)}, bf16[1,192,1280]{2,1,0:T(8,128)(2,1)}, u32[]{:S(2)}, u32[]{:S(2)}) collective-permute-start(bf16[1,192,1280]{2,1,0:T(8,128)(2,1)} %get-tuple-element.260), channel_id=1, source_target_pairs={{0,1},{1,0},{2,5},{3,4},{4,3},{5,2},{6,7},{7,6},{8,9},{9,8},{10,13... | collective-permute-start | bytes 1474568 | tf_op jit(solution)/shard_map/rows_x/ppermute | solution.py:71
  30.4 16.7 %collective-permute-start = (bf16[1,192,1280]{2,1,0:T(8,128)(2,1)}, bf16[1,192,1280]{2,1,0:T(8,128)(2,1)}, u32[]{:S(2)}, u32[]{:S(2)}) collective-permute-start(bf16[1,192,1280]{2,1,0:T(8,128)(2,1)} %get-tuple-element.261), channel_id=1, source_target_pairs={{0,0},{1,1},{2,4},{3,5},{4,2},{5,3},{6,6},{7,7},{8,8},{9,9},{10,12... | collective-permute-start | bytes 1474568 | tf_op jit(solution)/shard_map/rows_x/ppermute | solution.py:71
  40.6 32.5 %collective-permute-start.2 = (bf16[1,192,1280]{2,1,0:T(8,128)(2,1)}, bf16[1,192,1280]{2,1,0:T(8,128)(2,1)}, u32[]{:S(2)}, u32[]{:S(2)}) collective-permute-start(bf16[1,192,1280]{2,1,0:T(8,128)(2,1)} %get-tuple-element.262), channel_id=1, source_target_pairs={{0,4},{1,5},{2,0},{3,1},{4,6},{5,7},{6,2},{7,3},{8,12},{9,13},{10,... | collective-permute-start | bytes 1474568 | tf_op jit(solution)/shard_map/rows_x/ppermute | solution.py:71
  44.8 19.9 %collective-permute-start.10 = (bf16[320,640]{1,0:T(8,128)(2,1)S(1)}, bf16[320,640]{1,0:T(8,128)(2,1)S(1)}, u32[]{:S(2)}, u32[]{:S(2)}) collective-permute-start(bf16[320,640]{1,0:T(8,128)(2,1)S(1)} %get-tuple-element.278), channel_id=1, source_target_pairs={{0,1},{1,0},{2,3},{3,2},{4,5},{5,4},{6,7},{7,6},{8,9},{9,8},{10,11... | collective-permute-start | bytes 1228808 | tf_op jit(solution)/shard_map/gq/ppermute | solution.py:71
  74.1 19.5 %collective-permute-start.11 = (bf16[1,1,320,1280]{3,2,1,0:T(8,128)(2,1)}, bf16[1,1,320,1280]{3,2,1,0:T(8,128)(2,1)}, u32[]{:S(2)}, u32[]{:S(2)}) collective-permute-start(bf16[1,1,320,1280]{3,2,1,0:T(8,128)(2,1)} %get-tuple-element.297), channel_id=1, source_target_pairs={{0,8},{8,0},{16,24},{24,16},{1,9},{9,1},{17,25},{25,17},{2,10},{10... | collective-permute-start | bytes 2457608 | tf_op jit(solution)/shard_map/gq/ppermute | solution.py:71
  79.7 35.0 %collective-permute-start.4 = (bf16[4,192,1280]{2,1,0:T(8,128)(2,1)S(1)}, bf16[4,192,1280]{2,1,0:T(8,128)(2,1)}, u32[]{:S(2)}, u32[]{:S(2)}) collective-permute-start(bf16[4,192,1280]{2,1,0:T(8,128)(2,1)S(1)} %constant_dynamic-update-slice_fusion), channel_id=1, source_target_pairs={{0,4},{4,0},{1,5},{5,1},{2,6},{6,2},{3,7},{7,3},{8,12},{12,8},{9,1... | collective-permute-start | bytes 5898248 | tf_op jit(solution)/shard_map/rows_x/ppermute | solution.py:71
  89.8 21.4 %collective-permute-start.18 = (bf16[1,1,320,1280]{3,2,1,0:T(8,128)(2,1)}, bf16[1,1,320,1280]{3,2,1,0:T(8,128)(2,1)S(1)}, u32[]{:S(2)}, u32[]{:S(2)}) collective-permute-start(bf16[1,1,320,1280]{3,2,1,0:T(8,128)(2,1)} %get-tuple-element.67), channel_id=1, source_target_pairs={{0,8},{8,0},{16,24},{24,16},{1,9},{9,1},{17,25},{25,17},{2,10},{10... | collective-permute-start | bytes 2457608 | tf_op jit(solution)/shard_map/gu/ppermute | solution.py:71
  93.6 56.5 %collective-permute-start.15 = (bf16[1,1,320,1280]{3,2,1,0:T(8,128)(2,1)S(1)}, bf16[1,1,320,1280]{3,2,1,0:T(8,128)(2,1)S(1)}, u32[]{:S(2)}, u32[]{:S(2)}) collective-permute-start(bf16[1,1,320,1280]{3,2,1,0:T(8,128)(2,1)S(1)} %get-tuple-element.66), channel_id=1, source_target_pairs={{0,8},{8,0},{16,24},{24,16},{1,9},{9,1},{17,25},{25,17},{2,10},{10... | collective-permute-start | bytes 2457608 | tf_op jit(solution)/shard_map/gd/ppermute | solution.py:71
  97.1 72.7 %collective-permute-start.12 = (bf16[1,2,320,1280]{3,2,1,0:T(8,128)(2,1)S(1)}, bf16[1,2,320,1280]{3,2,1,0:T(8,128)(2,1)S(1)}, u32[]{:S(2)}, u32[]{:S(2)}) collective-permute-start(bf16[1,2,320,1280]{3,2,1,0:T(8,128)(2,1)S(1)} %pad_maximum_fusion.14), channel_id=1, source_target_pairs={{0,16},{8,24},{16,0},{24,8},{1,17},{9,25},{17,1},{25,9},{2,18},{10... | collective-permute-start | bytes 4915208 | tf_op jit(solution)/shard_map/gq/ppermute | solution.py:71
  98.7 48.5 %collective-permute-start.17 = (bf16[320,1280]{1,0:T(8,128)(2,1)S(1)}, bf16[320,1280]{1,0:T(8,128)(2,1)S(1)}, u32[]{:S(2)}, u32[]{:S(2)}) collective-permute-start(bf16[320,1280]{1,0:T(8,128)(2,1)S(1)} %collective-permute-done.16), channel_id=1, source_target_pairs={{1,0},{2,3},{5,4},{6,7},{9,8},{10,11},{13,12},{14,15},{17,16},{18,... | collective-permute-start | bytes 2457608 | tf_op jit(solution)/shard_map/gq/ppermute | solution.py:71
  111.2 61.8 %collective-permute-start.31 = (bf16[320,1280]{1,0:T(8,128)(2,1)S(1)}, bf16[320,1280]{1,0:T(8,128)(2,1)}, u32[]{:S(2)}, u32[]{:S(2)}) collective-permute-start(bf16[320,1280]{1,0:T(8,128)(2,1)S(1)} %get-tuple-element.82), channel_id=1, source_target_pairs={{1,2},{2,1},{5,6},{6,5},{9,10},{10,9},{13,14},{14,13},{17,18},{18,... | collective-permute-start | bytes 2457608 | tf_op jit(solution)/shard_map/gd/ppermute | solution.py:71
  147.2 21.9 %collective-permute-start.19 = (bf16[1,1,320,1280]{3,2,1,0:T(8,128)(2,1)S(1)}, bf16[1,1,320,1280]{3,2,1,0:T(8,128)(2,1)S(1)}, u32[]{:S(2)}, u32[]{:S(2)}) collective-permute-start(bf16[1,1,320,1280]{3,2,1,0:T(8,128)(2,1)S(1)} %select_bitcast_fusion.2), channel_id=1, source_target_pairs={{0,16},{8,24},{16,0},{24,8},{1,17},{9,25},{17,1},{25,9},{2,18},{10... | collective-permute-start | bytes 2457608 | tf_op jit(solution)/shard_map/gq/ppermute | solution.py:71
  148.8 20.3 %collective-permute-start.22 = (bf16[320,1280]{1,0:T(8,128)(2,1)S(1)}, bf16[320,1280]{1,0:T(8,128)(2,1)S(1)}, u32[]{:S(2)}, u32[]{:S(2)}) collective-permute-start(bf16[320,1280]{1,0:T(8,128)(2,1)S(1)} %collective-permute-done.21), channel_id=1, source_target_pairs={{1,0},{2,3},{5,4},{6,7},{9,8},{10,11},{13,12},{14,15},{17,16},{18,... | collective-permute-start | bytes 2457608 | tf_op jit(solution)/shard_map/gu/ppermute | solution.py:71
  169.2 58.9 %collective-permute-start.23 = (bf16[1,1,320,1280]{3,2,1,0:T(8,128)(2,1)S(1)}, bf16[1,1,320,1280]{3,2,1,0:T(8,128)(2,1)}, u32[]{:S(2)}, u32[]{:S(2)}) collective-permute-start(bf16[1,1,320,1280]{3,2,1,0:T(8,128)(2,1)S(1)} %select_bitcast_fusion.1), channel_id=1, source_target_pairs={{0,16},{8,24},{16,0},{24,8},{1,17},{9,25},{17,1},{25,9},{2,18},{10... | collective-permute-start | bytes 2457608 | tf_op jit(solution)/shard_map/gu/ppermute | solution.py:71
  173.0 59.2 %collective-permute-start.32 = (bf16[320,1280]{1,0:T(8,128)(2,1)}, bf16[320,1280]{1,0:T(8,128)(2,1)}, u32[]{:S(2)}, u32[]{:S(2)}) collective-permute-start(bf16[320,1280]{1,0:T(8,128)(2,1)} %collective-permute-done.31), channel_id=1, source_target_pairs={{1,0},{2,3},{5,4},{6,7},{9,8},{10,11},{13,12},{14,15},{17,16},{18,... | collective-permute-start | bytes 2457608 | tf_op jit(solution)/shard_map/gd/ppermute | solution.py:71
  174.3 42.2 %collective-permute-start.26 = (bf16[1,192,1280]{2,1,0:T(8,128)(2,1)S(1)}, bf16[1,192,1280]{2,1,0:T(8,128)(2,1)}, u32[]{:S(2)}, u32[]{:S(2)}) collective-permute-start(bf16[1,192,1280]{2,1,0:T(8,128)(2,1)S(1)} %copy-done.94), channel_id=1, source_target_pairs={{0,4},{1,5},{2,0},{3,1},{4,6},{5,7},{6,2},{7,3},{8,12},{9,13},{10,... | collective-permute-start | bytes 1474568 | tf_op jit(solution)/shard_map/rows_g/ppermute | solution.py:71
  174.4 38.1 %collective-permute-start.24 = (bf16[1,192,1280]{2,1,0:T(8,128)(2,1)}, bf16[1,192,1280]{2,1,0:T(8,128)(2,1)}, u32[]{:S(2)}, u32[]{:S(2)}) collective-permute-start(bf16[1,192,1280]{2,1,0:T(8,128)(2,1)} %get-tuple-element.76), channel_id=1, source_target_pairs={{0,0},{1,1},{2,4},{3,5},{4,2},{5,3},{6,6},{7,7},{8,8},{9,9},{10,12... | collective-permute-start | bytes 1474568 | tf_op jit(solution)/shard_map/rows_g/ppermute | solution.py:71
  180.0 33.9 %collective-permute-start.25 = (bf16[1,192,1280]{2,1,0:T(8,128)(2,1)}, bf16[1,192,1280]{2,1,0:T(8,128)(2,1)}, u32[]{:S(2)}, u32[]{:S(2)}) collective-permute-start(bf16[1,192,1280]{2,1,0:T(8,128)(2,1)} %get-tuple-element.77), channel_id=1, source_target_pairs={{0,1},{1,0},{2,5},{3,4},{4,3},{5,2},{6,7},{7,6},{8,9},{9,8},{10,13... | collective-permute-start | bytes 1474568 | tf_op jit(solution)/shard_map/rows_g/ppermute | solution.py:71
  213.9 36.1 %collective-permute-start.20 = (bf16[2,1,320,1280]{3,2,1,0:T(8,128)(2,1)S(1)}, bf16[2,1,320,1280]{3,2,1,0:T(8,128)(2,1)S(1)}, u32[]{:S(2)}, u32[]{:S(2)}) collective-permute-start(bf16[2,1,320,1280]{3,2,1,0:T(8,128)(2,1)S(1)} %pad_maximum_fusion.15), channel_id=1, source_target_pairs={{0,8},{8,0},{16,24},{24,16},{1,9},{9,1},{17,25},{25,17},{2,10},{10... | collective-permute-start | bytes 4915208 | tf_op jit(solution)/shard_map/gq/ppermute | solution.py:71
  216.6 36.4 %collective-permute-start.29 = (bf16[1,2,320,1280]{3,2,1,0:T(8,128)(2,1)S(1)}, bf16[1,2,320,1280]{3,2,1,0:T(8,128)(2,1)S(1)}, u32[]{:S(2)}, u32[]{:S(2)}) collective-permute-start(bf16[1,2,320,1280]{3,2,1,0:T(8,128)(2,1)S(1)} %copy-done.81), channel_id=1, source_target_pairs={{0,16},{8,24},{16,0},{24,8},{1,17},{9,25},{17,1},{25,9},{2,18},{10... | collective-permute-start | bytes 4915208 | tf_op jit(solution)/shard_map/gu/ppermute | solution.py:71
  228.1 55.5 %collective-permute-start.28 = (bf16[4,192,1280]{2,1,0:T(8,128)(2,1)S(1)}, bf16[4,192,1280]{2,1,0:T(8,128)(2,1)S(1)}, u32[]{:S(2)}, u32[]{:S(2)}) collective-permute-start(bf16[4,192,1280]{2,1,0:T(8,128)(2,1)S(1)} %constant_dynamic-update-slice_fusion.10), channel_id=1, source_target_pairs={{0,4},{4,0},{1,5},{5,1},{2,6},{6,2},{3,7},{7,3},{8,12},{12,8},{9,1... | collective-permute-start | bytes 5898248 | tf_op jit(solution)/shard_map/rows_g/ppermute | solution.py:71
  230.8 80.9 %collective-permute-start.34 = (bf16[1,2,320,1280]{3,2,1,0:T(8,128)(2,1)}, bf16[1,2,320,1280]{3,2,1,0:T(8,128)(2,1)}, u32[]{:S(2)}, u32[]{:S(2)}) collective-permute-start(bf16[1,2,320,1280]{3,2,1,0:T(8,128)(2,1)} %pad_maximum_fusion.17), channel_id=1, source_target_pairs={{0,16},{8,24},{16,0},{24,8},{1,17},{9,25},{17,1},{25,9},{2,18},{10... | collective-permute-start | bytes 4915208 | tf_op jit(solution)/shard_map/gd/ppermute | solution.py:71
  232.3 75.8 %collective-permute-start.35 = (bf16[2,1,320,1280]{3,2,1,0:T(8,128)(2,1)}, bf16[2,1,320,1280]{3,2,1,0:T(8,128)(2,1)}, u32[]{:S(2)}, u32[]{:S(2)}) collective-permute-start(bf16[2,1,320,1280]{3,2,1,0:T(8,128)(2,1)} %pad_maximum_fusion.18), channel_id=1, source_target_pairs={{0,8},{8,0},{16,24},{24,16},{1,9},{9,1},{17,25},{25,17},{2,10},{10... | collective-permute-start | bytes 4915208 | tf_op jit(solution)/shard_map/gu/ppermute | solution.py:71
  253.0 52.8 %collective-permute-start.33 = (bf16[1,1,320,1280]{3,2,1,0:T(8,128)(2,1)}, bf16[1,1,320,1280]{3,2,1,0:T(8,128)(2,1)}, u32[]{:S(2)}, u32[]{:S(2)}) collective-permute-start(bf16[1,1,320,1280]{3,2,1,0:T(8,128)(2,1)} %select_bitcast_fusion), channel_id=1, source_target_pairs={{0,16},{8,24},{16,0},{24,8},{1,17},{9,25},{17,1},{25,9},{2,18},{10... | collective-permute-start | bytes 2457608 | tf_op jit(solution)/shard_map/gd/ppermute | solution.py:71
  297.3 50.0 %collective-permute-start.30 = (bf16[1536,1280]{1,0:T(8,128)(2,1)S(1)}, bf16[1536,1280]{1,0:T(8,128)(2,1)S(1)}, u32[]{:S(2)}, u32[]{:S(2)}) collective-permute-start(bf16[1536,1280]{1,0:T(8,128)(2,1)S(1)} %fusion.20), channel_id=1, source_target_pairs={{0,4},{4,0},{1,5},{5,1},{2,6},{6,2},{3,7},{7,3},{8,12},{12,8},{9,1... | collective-permute-start | bytes 11796488 | tf_op jit(solution)/shard_map/ppermute | solution.py:71
  307.5 37.6 %collective-permute-start.36 = (bf16[2,1,320,1280]{3,2,1,0:T(8,128)(2,1)S(1)}, bf16[2,1,320,1280]{3,2,1,0:T(8,128)(2,1)S(1)}, u32[]{:S(2)}, u32[]{:S(2)}) collective-permute-start(bf16[2,1,320,1280]{3,2,1,0:T(8,128)(2,1)S(1)} %pad_maximum_fusion.19), channel_id=1, source_target_pairs={{0,8},{8,0},{16,24},{24,16},{1,9},{9,1},{17,25},{25,17},{2,10},{10... | collective-permute-start | bytes 4915208 | tf_op jit(solution)/shard_map/gd/ppermute | solution.py:71
  415.0 100.4 %collective-permute-start.64 = (bf16[1,2,320,1280]{3,2,1,0:T(8,128)(2,1)}, bf16[1,2,320,1280]{3,2,1,0:T(8,128)(2,1)}, u32[]{:S(2)}, u32[]{:S(2)}) collective-permute-start(bf16[1,2,320,1280]{3,2,1,0:T(8,128)(2,1)} %constant_dynamic-slice_fusion.2), channel_id=1, source_target_pairs={{0,16},{8,24},{16,0},{24,8},{1,17},{9,25},{17,1},{25,9},{2,18},{10... | collective-permute-start | bytes 4915208 | tf_op jit(solution)/shard_map/sd/ppermute | solution.py:71
  436.6 117.1 %collective-permute-start.56 = (bf16[1,2,320,1280]{3,2,1,0:T(8,128)(2,1)S(1)}, bf16[1,2,320,1280]{3,2,1,0:T(8,128)(2,1)}, u32[]{:S(2)}, u32[]{:S(2)}) collective-permute-start(bf16[1,2,320,1280]{3,2,1,0:T(8,128)(2,1)S(1)} %constant_dynamic-slice_fusion.4), channel_id=1, source_target_pairs={{0,16},{8,24},{16,0},{24,8},{1,17},{9,25},{17,1},{25,9},{2,18},{10... | collective-permute-start | bytes 4915208 | tf_op jit(solution)/shard_map/su/ppermute | solution.py:71
  440.1 38.7 %collective-permute-start.58 = (bf16[2,1,320,1280]{3,2,1,0:T(8,128)(2,1)S(1)}, bf16[2,1,320,1280]{3,2,1,0:T(8,128)(2,1)S(1)}, u32[]{:S(2)}, u32[]{:S(2)}) collective-permute-start(bf16[2,1,320,1280]{3,2,1,0:T(8,128)(2,1)S(1)} %constant_dynamic-slice_fusion.3), channel_id=1, source_target_pairs={{0,8},{8,0},{16,24},{24,16},{1,9},{9,1},{17,25},{25,17},{2,10},{10... | collective-permute-start | bytes 4915208 | tf_op jit(solution)/shard_map/su/ppermute | solution.py:71
  453.2 60.3 %collective-permute-start.66 = (bf16[2,1,320,1280]{3,2,1,0:T(8,128)(2,1)S(1)}, bf16[2,1,320,1280]{3,2,1,0:T(8,128)(2,1)S(1)}, u32[]{:S(2)}, u32[]{:S(2)}) collective-permute-start(bf16[2,1,320,1280]{3,2,1,0:T(8,128)(2,1)S(1)} %constant_dynamic-slice_fusion.1), channel_id=1, source_target_pairs={{0,8},{8,0},{16,24},{24,16},{1,9},{9,1},{17,25},{25,17},{2,10},{10... | collective-permute-start | bytes 4915208 | tf_op jit(solution)/shard_map/sd/ppermute | solution.py:71
  454.8 139.7 %collective-permute-start.37 = (bf16[1536,1280]{1,0:T(8,128)(2,1)}, bf16[1536,1280]{1,0:T(8,128)(2,1)}, u32[]{:S(2)}, u32[]{:S(2)}) collective-permute-start(bf16[1536,1280]{1,0:T(8,128)(2,1)} %fusion.16), channel_id=1, source_target_pairs={{0,4},{4,0},{1,5},{5,1},{2,6},{6,2},{3,7},{7,3},{8,12},{12,8},{9,1... | collective-permute-start | bytes 11796488 | tf_op jit(solution)/shard_map/ppermute | solution.py:71
  478.8 110.4 %collective-permute-start.42 = (bf16[1536,1280]{1,0:T(8,128)(2,1)S(1)}, bf16[1536,1280]{1,0:T(8,128)(2,1)S(1)}, u32[]{:S(2)}, u32[]{:S(2)}) collective-permute-start(bf16[1536,1280]{1,0:T(8,128)(2,1)S(1)} %fusion.17), channel_id=1, source_target_pairs={{0,4},{4,0},{1,5},{5,1},{2,6},{6,2},{3,7},{7,3},{8,12},{12,8},{9,1... | collective-permute-start | bytes 11796488 | tf_op jit(solution)/shard_map/ppermute | solution.py:71
  513.5 21.2 %collective-permute-start.59 = (bf16[1,1,320,1280]{3,2,1,0:T(8,128)(2,1)S(1)}, bf16[1,1,320,1280]{3,2,1,0:T(8,128)(2,1)S(1)}, u32[]{:S(2)}, u32[]{:S(2)}) collective-permute-start(bf16[1,1,320,1280]{3,2,1,0:T(8,128)(2,1)S(1)} %dynamic-slice_convert_fusion.2), channel_id=1, source_target_pairs={{0,16},{8,24},{16,0},{24,8},{1,17},{9,25},{17,1},{25,9},{2,18},{10... | collective-permute-start | bytes 2457608 | tf_op jit(solution)/shard_map/su/ppermute | solution.py:71
  515.4 35.5 %collective-permute-start.67 = (bf16[1,1,320,1280]{3,2,1,0:T(8,128)(2,1)S(1)}, bf16[1,1,320,1280]{3,2,1,0:T(8,128)(2,1)S(1)}, u32[]{:S(2)}, u32[]{:S(2)}) collective-permute-start(bf16[1,1,320,1280]{3,2,1,0:T(8,128)(2,1)S(1)} %dynamic-slice_convert_fusion), channel_id=1, source_target_pairs={{0,16},{8,24},{16,0},{24,8},{1,17},{9,25},{17,1},{25,9},{2,18},{10... | collective-permute-start | bytes 2457608 | tf_op jit(solution)/shard_map/sd/ppermute | solution.py:71
  534.6 143.8 %collective-permute-start.65 = (bf16[1,1,320,1280]{3,2,1,0:T(8,128)(2,1)}, bf16[1,1,320,1280]{3,2,1,0:T(8,128)(2,1)}, u32[]{:S(2)}, u32[]{:S(2)}) collective-permute-start(bf16[1,1,320,1280]{3,2,1,0:T(8,128)(2,1)} %dynamic-slice_convert_fusion.1), channel_id=1, source_target_pairs={{0,8},{8,0},{16,24},{24,16},{1,9},{9,1},{17,25},{25,17},{2,10},{10... | collective-permute-start | bytes 2457608 | tf_op jit(solution)/shard_map/sd/ppermute | solution.py:71
  550.9 21.2 %collective-permute-start.60 = (bf16[320,1280]{1,0:T(8,128)(2,1)S(1)}, bf16[320,1280]{1,0:T(8,128)(2,1)S(1)}, u32[]{:S(2)}, u32[]{:S(2)}) collective-permute-start(bf16[320,1280]{1,0:T(8,128)(2,1)S(1)} %bitcast_convert_fusion.1), channel_id=1, source_target_pairs={{0,1},{3,2},{4,5},{7,6},{8,9},{11,10},{12,13},{15,14},{16,17},{19,... | collective-permute-start | bytes 2457608 | tf_op jit(solution)/shard_map/su/ppermute | solution.py:497
  553.7 32.8 %collective-permute-start.68 = (bf16[320,1280]{1,0:T(8,128)(2,1)S(1)}, bf16[320,1280]{1,0:T(8,128)(2,1)S(1)}, u32[]{:S(2)}, u32[]{:S(2)}) collective-permute-start(bf16[320,1280]{1,0:T(8,128)(2,1)S(1)} %bitcast_convert_fusion), channel_id=1, source_target_pairs={{0,1},{3,2},{4,5},{7,6},{8,9},{11,10},{12,13},{15,14},{16,17},{19,... | collective-permute-start | bytes 2457608 | tf_op jit(solution)/shard_map/sd/ppermute | solution.py:497
  572.1 98.6 %collective-permute-start.57 = (bf16[1,1,320,1280]{3,2,1,0:T(8,128)(2,1)}, bf16[1,1,320,1280]{3,2,1,0:T(8,128)(2,1)S(1)}, u32[]{:S(2)}, u32[]{:S(2)}) collective-permute-start(bf16[1,1,320,1280]{3,2,1,0:T(8,128)(2,1)} %dynamic-slice_convert_fusion.3), channel_id=1, source_target_pairs={{0,8},{8,0},{16,24},{24,16},{1,9},{9,1},{17,25},{25,17},{2,10},{10... | collective-permute-start | bytes 2457608 | tf_op jit(solution)/shard_map/su/ppermute | solution.py:71
  586.5 89.6 %collective-permute-start.61 = (bf16[320,1280]{1,0:T(8,128)(2,1)}, bf16[320,1280]{1,0:T(8,128)(2,1)}, u32[]{:S(2)}, u32[]{:S(2)}) collective-permute-start(bf16[320,1280]{1,0:T(8,128)(2,1)} %fusion.38), channel_id=1, source_target_pairs={{1,2},{2,1},{5,6},{6,5},{9,10},{10,9},{13,14},{14,13},{17,18},{18,... | collective-permute-start | bytes 2457608 | tf_op jit(solution)/shard_map/su/ppermute | solution.py:498
  589.3 92.9 %collective-permute-start.69 = (bf16[320,1280]{1,0:T(8,128)(2,1)}, bf16[320,1280]{1,0:T(8,128)(2,1)}, u32[]{:S(2)}, u32[]{:S(2)}) collective-permute-start(bf16[320,1280]{1,0:T(8,128)(2,1)} %fusion.37), channel_id=1, source_target_pairs={{1,2},{2,1},{5,6},{6,5},{9,10},{10,9},{13,14},{14,13},{17,18},{18,... | collective-permute-start | bytes 2457608 | tf_op jit(solution)/shard_map/sd/ppermute | solution.py:498
  652.4 32.8 %collective-permute-start.38 = (bf16[192,1280]{1,0:T(8,128)(2,1)}, bf16[192,1280]{1,0:T(8,128)(2,1)S(1)}, u32[]{:S(2)}, u32[]{:S(2)}) collective-permute-start(bf16[192,1280]{1,0:T(8,128)(2,1)} %get-tuple-element.219), channel_id=1, source_target_pairs={{0,0},{1,1},{4,2},{5,3},{2,4},{3,5},{6,6},{7,7},{8,8},{9,9},{12,10... | collective-permute-start | bytes 1474568 | tf_op jit(solution)/shard_map/rows_out/ppermute | solution.py:71
  670.7 17.0 %collective-permute-start.39 = (bf16[192,1280]{1,0:T(8,128)(2,1)S(1)}, bf16[192,1280]{1,0:T(8,128)(2,1)S(1)}, u32[]{:S(2)}, u32[]{:S(2)}) collective-permute-start(bf16[192,1280]{1,0:T(8,128)(2,1)S(1)} %copy-done.104), channel_id=1, source_target_pairs={{1,0},{0,1},{5,2},{4,3},{3,4},{2,5},{7,6},{6,7},{9,8},{8,9},{13,10... | collective-permute-start | bytes 1474568 | tf_op jit(solution)/shard_map/rows_out/ppermute | solution.py:71
  676.1 22.1 %collective-permute-start.40 = (bf16[192,1280]{1,0:T(8,128)(2,1)S(1)}, bf16[192,1280]{1,0:T(8,128)(2,1)S(1)}, u32[]{:S(2)}, u32[]{:S(2)}) collective-permute-start(bf16[192,1280]{1,0:T(8,128)(2,1)S(1)} %copy-done.103), channel_id=1, source_target_pairs={{4,0},{5,1},{0,2},{1,3},{6,4},{7,5},{2,6},{3,7},{12,8},{13,9},{8,1... | collective-permute-start | bytes 1474568 | tf_op jit(solution)/shard_map/rows_out/ppermute | solution.py:71
  678.4 30.3 %collective-permute-start.41 = (bf16[192,1280]{1,0:T(8,128)(2,1)S(1)}, bf16[192,1280]{1,0:T(8,128)(2,1)S(1)}, u32[]{:S(2)}, u32[]{:S(2)}) collective-permute-start(bf16[192,1280]{1,0:T(8,128)(2,1)S(1)} %get-tuple-element.222), channel_id=1, source_target_pairs={{5,0},{4,1},{1,2},{0,3},{7,4},{6,5},{3,6},{2,7},{13,8},{12,9},{9,1... | collective-permute-start | bytes 1474568 | tf_op jit(solution)/shard_map/rows_out/ppermute | solution.py:71
  682.1 81.0 %collective-permute-start.50 = (bf16[2,1,320,1280]{3,2,1,0:T(8,128)(2,1)}, bf16[2,1,320,1280]{3,2,1,0:T(8,128)(2,1)}, u32[]{:S(2)}, u32[]{:S(2)}) collective-permute-start(bf16[2,1,320,1280]{3,2,1,0:T(8,128)(2,1)} %constant_dynamic-slice_fusion.5), channel_id=1, source_target_pairs={{0,8},{8,0},{16,24},{24,16},{1,9},{9,1},{17,25},{25,17},{2,10},{10... | collective-permute-start | bytes 4915208 | tf_op jit(solution)/shard_map/sq/ppermute | solution.py:71
  685.3 76.1 %collective-permute-start.62 = (bf16[320,640]{1,0:T(8,128)(2,1)}, bf16[320,640]{1,0:T(8,128)(2,1)}, u32[]{:S(2)}, u32[]{:S(2)}) collective-permute-start(bf16[320,640]{1,0:T(8,128)(2,1)} %slice.605), channel_id=1, source_target_pairs={{0,1},{1,0},{2,3},{3,2},{4,5},{5,4},{6,7},{7,6},{8,9},{9,8},{10,11... | collective-permute-start | bytes 1228808 | tf_op jit(solution)/shard_map/su/ppermute | solution.py:499
  687.6 78.9 %collective-permute-start.70 = (bf16[320,640]{1,0:T(8,128)(2,1)}, bf16[320,640]{1,0:T(8,128)(2,1)}, u32[]{:S(2)}, u32[]{:S(2)}) collective-permute-start(bf16[320,640]{1,0:T(8,128)(2,1)} %slice.604), channel_id=1, source_target_pairs={{0,1},{1,0},{2,3},{3,2},{4,5},{5,4},{6,7},{7,6},{8,9},{9,8},{10,11... | collective-permute-start | bytes 1228808 | tf_op jit(solution)/shard_map/sd/ppermute | solution.py:499
  742.0 54.8 %collective-permute-start.48 = (bf16[1,2,320,1280]{3,2,1,0:T(8,128)(2,1)}, bf16[1,2,320,1280]{3,2,1,0:T(8,128)(2,1)}, u32[]{:S(2)}, u32[]{:S(2)}) collective-permute-start(bf16[1,2,320,1280]{3,2,1,0:T(8,128)(2,1)} %constant_dynamic-slice_fusion.6), channel_id=1, source_target_pairs={{0,16},{8,24},{16,0},{24,8},{1,17},{9,25},{17,1},{25,9},{2,18},{10... | collective-permute-start | bytes 4915208 | tf_op jit(solution)/shard_map/sq/ppermute | solution.py:71
  759.8 88.1 %collective-permute-start.43 = (bf16[1536,1280]{1,0:T(8,128)(2,1)}, bf16[1536,1280]{1,0:T(8,128)(2,1)}, u32[]{:S(2)}, u32[]{:S(2)}) collective-permute-start(bf16[1536,1280]{1,0:T(8,128)(2,1)} %fusion.15), channel_id=1, source_target_pairs={{0,4},{4,0},{1,5},{5,1},{2,6},{6,2},{3,7},{7,3},{8,12},{12,8},{9,1... | collective-permute-start | bytes 11796488 | tf_op jit(solution)/shard_map/ppermute | solution.py:71
  765.9 28.2 %collective-permute-start.51 = (bf16[1,1,320,1280]{3,2,1,0:T(8,128)(2,1)}, bf16[1,1,320,1280]{3,2,1,0:T(8,128)(2,1)}, u32[]{:S(2)}, u32[]{:S(2)}) collective-permute-start(bf16[1,1,320,1280]{3,2,1,0:T(8,128)(2,1)} %dynamic-slice_convert_fusion.4), channel_id=1, source_target_pairs={{0,16},{8,24},{16,0},{24,8},{1,17},{9,25},{17,1},{25,9},{2,18},{10... | collective-permute-start | bytes 2457608 | tf_op jit(solution)/shard_map/sq/ppermute | solution.py:71
  769.2 48.1 %collective-permute-start.71 = (bf16[160,640]{1,0:T(8,128)(2,1)}, bf16[160,640]{1,0:T(8,128)(2,1)S(1)}, u32[]{:S(2)}, u32[]{:S(2)}) collective-permute-start(bf16[160,640]{1,0:T(8,128)(2,1)} %select_convert_fusion), channel_id=1, source_target_pairs={{0,4},{4,0},{1,5},{5,1},{2,6},{6,2},{3,7},{7,3},{8,12},{12,8},{9,1... | collective-permute-start | bytes 614408 | tf_op jit(solution)/shard_map/sd/ppermute | solution.py:71
  795.5 17.9 %collective-permute-start.52 = (bf16[320,1280]{1,0:T(8,128)(2,1)S(1)}, bf16[320,1280]{1,0:T(8,128)(2,1)S(1)}, u32[]{:S(2)}, u32[]{:S(2)}) collective-permute-start(bf16[320,1280]{1,0:T(8,128)(2,1)S(1)} %bitcast_convert_fusion.2), channel_id=1, source_target_pairs={{0,1},{3,2},{4,5},{7,6},{8,9},{11,10},{12,13},{15,14},{16,17},{19,... | collective-permute-start | bytes 2457608 | tf_op jit(solution)/shard_map/sq/ppermute | solution.py:497
  799.8 27.8 %collective-permute-start.49 = (bf16[1,1,320,1280]{3,2,1,0:T(8,128)(2,1)}, bf16[1,1,320,1280]{3,2,1,0:T(8,128)(2,1)}, u32[]{:S(2)}, u32[]{:S(2)}) collective-permute-start(bf16[1,1,320,1280]{3,2,1,0:T(8,128)(2,1)} %dynamic-slice_convert_fusion.5), channel_id=1, source_target_pairs={{0,8},{8,0},{16,24},{24,16},{1,9},{9,1},{17,25},{25,17},{2,10},{10... | collective-permute-start | bytes 2457608 | tf_op jit(solution)/shard_map/sq/ppermute | solution.py:71
  830.6 43.9 %collective-permute-start.54 = (bf16[320,640]{1,0:T(8,128)(2,1)S(1)}, bf16[320,640]{1,0:T(8,128)(2,1)}, u32[]{:S(2)}, u32[]{:S(2)}) collective-permute-start(bf16[320,640]{1,0:T(8,128)(2,1)S(1)} %slice.606), channel_id=1, source_target_pairs={{0,1},{1,0},{2,3},{3,2},{4,5},{5,4},{6,7},{7,6},{8,9},{9,8},{10,11... | collective-permute-start | bytes 1228808 | tf_op jit(solution)/shard_map/sq/ppermute | solution.py:499
  886.7 53.9 %collective-permute-start.44 = (bf16[192,1280]{1,0:T(8,128)(2,1)}, bf16[192,1280]{1,0:T(8,128)(2,1)}, u32[]{:S(2)}, u32[]{:S(2)}) collective-permute-start(bf16[192,1280]{1,0:T(8,128)(2,1)} %get-tuple-element.215), channel_id=1, source_target_pairs={{0,0},{1,1},{4,2},{5,3},{2,4},{3,5},{6,6},{7,7},{8,8},{9,9},{12,10... | collective-permute-start | bytes 1474568 | tf_op jit(solution)/shard_map/rows_dx/ppermute | solution.py:71
  891.9 48.6 %collective-permute-start.45 = (bf16[192,1280]{1,0:T(8,128)(2,1)}, bf16[192,1280]{1,0:T(8,128)(2,1)}, u32[]{:S(2)}, u32[]{:S(2)}) collective-permute-start(bf16[192,1280]{1,0:T(8,128)(2,1)} %get-tuple-element.216), channel_id=1, source_target_pairs={{1,0},{0,1},{5,2},{4,3},{3,4},{2,5},{7,6},{6,7},{9,8},{8,9},{13,10... | collective-permute-start | bytes 1474568 | tf_op jit(solution)/shard_map/rows_dx/ppermute | solution.py:71
  893.7 46.9 %collective-permute-start.46 = (bf16[192,1280]{1,0:T(8,128)(2,1)}, bf16[192,1280]{1,0:T(8,128)(2,1)}, u32[]{:S(2)}, u32[]{:S(2)}) collective-permute-start(bf16[192,1280]{1,0:T(8,128)(2,1)} %get-tuple-element.217), channel_id=1, source_target_pairs={{4,0},{5,1},{0,2},{1,3},{6,4},{7,5},{2,6},{3,7},{12,8},{13,9},{8,1... | collective-permute-start | bytes 1474568 | tf_op jit(solution)/shard_map/rows_dx/ppermute | solution.py:71
  893.7 46.9 %collective-permute-start.47 = (bf16[192,1280]{1,0:T(8,128)(2,1)S(1)}, bf16[192,1280]{1,0:T(8,128)(2,1)}, u32[]{:S(2)}, u32[]{:S(2)}) collective-permute-start(bf16[192,1280]{1,0:T(8,128)(2,1)S(1)} %get-tuple-element.218), channel_id=1, source_target_pairs={{5,0},{4,1},{1,2},{0,3},{7,4},{6,5},{3,6},{2,7},{13,8},{12,9},{9,1... | collective-permute-start | bytes 1474568 | tf_op jit(solution)/shard_map/rows_dx/ppermute | solution.py:71
  896.1 42.1 %collective-permute-start.76 = (f32[13,1280]{1,0:T(8,128)}, f32[13,1280]{1,0:T(8,128)}, u32[]{:S(2)}, u32[]{:S(2)}) collective-permute-start(f32[13,1280]{1,0:T(8,128)} %add.676), channel_id=1, source_target_pairs={{0,2},{1,3},{2,0},{3,1},{4,6},{5,7},{6,4},{7,5},{8,10},{9,11},{10,... | collective-permute-start | bytes 199688 | tf_op jit(solution)/shard_map/vectors/ppermute | solution.py:185
  (172 other events, 3348.8 us)

commit v2 on v1

v2 whole, which is shorter than its diff:
```python
import functools

import jax
import jax.numpy as jnp
from jax import lax
from jax.experimental import pallas as pl
from jax.experimental.pallas import tpu as pltpu
from jax.sharding import Mesh, PartitionSpec as P

HEAD = 80
HALF = HEAD // 2
STEP = 10
MIDDLE = 1024

NORM_EPS = 1e-06
BETA_ONE = 0.9
BETA_TWO = 0.95
ADAM_EPS = 1e-08
MATRIX_RATE = 0.03
VECTOR_RATE = 0.2
MATRIX_DECAY = 0.1
GELU_SLOPE = 1.702
LOG2E = 1.4426950408889634
LN2 = 0.6931471805599453

BF = jnp.bfloat16
F32 = jnp.float32


def dot(left, right, left_dim, right_dim):
    return lax.dot_general(
        left, right, (((left_dim,), (right_dim,)), ((), ())), preferred_element_type=F32
    )


def normalise(source):
    centre = source - jnp.mean(source, axis=-1, keepdims=True)
    spread = lax.rsqrt(jnp.mean(centre * centre, axis=-1, keepdims=True) + NORM_EPS)
    return centre * spread, spread


def norm_back(gradient, gain_vec, normed, spread):
    scaled = gradient * gain_vec
    return spread * (
        scaled
        - jnp.mean(scaled, axis=-1, keepdims=True)
        - normed * jnp.mean(scaled * normed, axis=-1, keepdims=True)
    )


def adam_step(weight, gradient, first, second, rate, decay):
    first_new = BETA_ONE * first + (1.0 - BETA_ONE) * gradient
    second_new = BETA_TWO * second + (1.0 - BETA_TWO) * gradient * gradient
    fix_one = 1.0 - BETA_ONE**STEP
    fix_two = 1.0 - BETA_TWO**STEP
    ratio = first_new / fix_one / (jnp.sqrt(second_new / fix_two) + ADAM_EPS)
    return (weight - rate * (ratio + decay * weight), first_new, second_new)


NEAR = [(0, 1), (1, 0), (2, 3), (3, 2)]
MIDS = [(1, 2), (2, 1)]
OUTER = [(1, 0), (2, 3)]
INNER = [(0, 1), (3, 2)]


def after(value, *earlier):
    return lax.optimization_barrier((value, *earlier))[0]


def move(value, axis, pairs, *earlier):
    return lax.ppermute(after(value, *earlier) if earlier else value, axis, pairs)


def swap_core(value, *earlier):
    return move(value, "c", [(0, 1), (1, 0)], *earlier)


def swap_bit(value, bit, count, *earlier):
    return move(value, "g", [(i, i ^ (1 << bit)) for i in range(count)], *earlier)


class Gather:
    def __init__(self, block, order, g, count):
        self.rows, self.columns = block.shape
        self.order, self.g, self.count = list(order), g, count
        self.bits = len(self.order)
        self.current = block.reshape((1,) * self.bits + block.shape)
        self.other = None

    def take(self, *earlier):
        if self.other is None:
            return
        other = after(self.other, *earlier) if earlier else self.other
        upper = ((self.g >> self.bit) & 1) == 1
        mine = self.current
        self.current = jnp.concatenate(
            [jnp.where(upper, other, mine), jnp.where(upper, mine, other)], axis=self.bits - 1 - self.bit
        )
        self.other = None

    def step(self, *earlier):
        self.take()
        if self.order:
            self.bit = self.order.pop(0)
            self.other = swap_bit(self.current, self.bit, self.count, *earlier)
            return self.other
        return self.current

    def finish(self, *earlier):
        last = self.step(*earlier)
        while self.order:
            last = self.step()
        return last

    def whole(self):
        self.take()
        return self.current.reshape(self.count * self.rows, self.columns)


class Scatter:
    def __init__(self, full, order, g, count):
        self.rows, self.columns = full.shape[0] // count, full.shape[1]
        self.order, self.g, self.count = list(order), g, count
        self.bits = len(self.order)
        self.terms = [full.reshape((2,) * self.bits + (self.rows, self.columns))]

    def sliced(self, place, axis):
        return [lax.dynamic_slice_in_dim(v, place, 1, axis) for v in self.terms]

    def total(self, terms):
        out = terms[0].astype(F32)
        for term in terms[1:]:
            out = out + term.astype(F32)
        return out

    def send(self, *earlier):
        bit = self.order.pop(0)
        axis = self.bits - 1 - bit
        mine = (self.g >> bit) & 1
        sent = self.total(self.sliced(1 - mine, axis)).astype(BF)
        self.kept = self.sliced(mine, axis)
        self.got = swap_bit(sent, bit, self.count, *earlier)
        return self.got

    def add(self, *earlier):
        self.terms = self.kept + [after(self.got, *earlier) if earlier else self.got]
        while len(self.order) > 1:
            self.send()
            self.terms = self.kept + [self.got]

    def whole(self):
        return self.total(self.terms).reshape(self.rows, self.columns)


def row_moves(step):
    moves = []
    for c in range(2):
        for z in range(4):
            moves.append((c * 4 + z, (z >> 1) * 4 + 2 * c + ((z & 1) ^ step)))
    return moves


class RowsIn:
    def __init__(self, local, z):
        self.local, self.odd = local, (z & 1) == 1
        self.pieces = []

    def send(self, *earlier):
        step = len(self.pieces)
        sent = jnp.where(self.odd, self.local[1 - step], self.local[step])
        self.sent = sent
        self.pieces.append(move(sent, ("c", "z"), row_moves(step), *earlier))
        return self.pieces[-1]

    def half(self, *earlier):
        first, second = [after(v, *earlier) if earlier else v for v in self.pieces]
        return jnp.concatenate(
            [jnp.where(self.odd, second, first), jnp.where(self.odd, first, second)], axis=0
        )


def rows_out(turned, start, c, z):
    rows, width = turned.shape
    part = rows // 4
    odd = z & 1
    longer = jnp.concatenate([turned, turned[:part]], axis=0)
    pieces = []
    for step in range(2):
        first = lax.rem((2 * c + (odd ^ step)) * part - start + rows, rows)
        sent = lax.dynamic_slice(longer, (first, 0), (part, width))
        pieces.append(lax.ppermute(sent, ("c", "z"), [(b, a) for a, b in row_moves(step)]))
    first, second = pieces
    return jnp.stack([jnp.where(odd == 1, second, first), jnp.where(odd == 1, first, second)]), pieces


def turn_rows(start, upper, lower, vectors=None):
    half, width = upper.shape
    rows = 2 * half
    block = 256
    more = block + 16

    def kernel(start_ref, up_ref, low_ref, *refs):
        wide = refs[-1]
        for at in range(0, half, block):
            wide[at : at + block] = up_ref[at : at + block].astype(F32)
            wide[half + at : half + at + block] = low_ref[at : at + block].astype(F32)
        wide[rows : rows + more] = up_ref[:more].astype(F32)

        @pl.loop(0, rows // block)
        def _(i):
            at = i * block
            first = lax.rem(at + start_ref[0], rows)
            low = lax.rem(first, 8)
            value = wide[pl.ds(pl.multiple_of(first - low, 8), more)]
            value = pltpu.roll(value, lax.rem(more - low, more), 0)[:block]
            into = pl.ds(pl.multiple_of(at, block), block)
            if vectors is None:
                refs[0][into] = value.astype(BF)
            else:
                refs[1][into] = value.astype(BF)
                refs[2][into] = first_norm_step(value, refs[0][...])[0].astype(BF)

    outs = 1 if vectors is None else 2
    extra = [] if vectors is None else [vectors]
    return pl.pallas_call(
        kernel,
        in_specs=[pl.BlockSpec(memory_space=pltpu.SMEM)]
        + [pl.BlockSpec(memory_space=pltpu.VMEM)] * (2 + len(extra)),
        out_specs=[pl.BlockSpec(memory_space=pltpu.VMEM)] * outs,
        out_shape=[jax.ShapeDtypeStruct((rows, width), BF)] * outs,
        scratch_shapes=[pltpu.VMEM((rows + more, width), F32)],
        compiler_params=pltpu.CompilerParams(vmem_limit_bytes=40 * 2**20),
        cost_estimate=FREE,
        name="turn_rows",
    )(start[None], upper, lower, *extra)


def add_up(value, count):
    value = value + swap_core(value)
    for bit in range(count.bit_length() - 1):
        value = value + swap_bit(value, bit, count)
    for distance in (1, 2):
        value = value + lax.ppermute(value, "z", [(i, i ^ distance) for i in range(4)])
    return value


SEGMENTS = ((0, MIDDLE, False), (MIDDLE, None, True))


def attend_kernel(q_ref, k_ref, v_ref, cos_ref, sin_ref, mask_ref, qt_ref, kt_ref, vt_ref, ot_ref, lse_ref, *, block):
    cosine, sine = cos_ref[...], sin_ref[...]

    def turn(source, factor):
        first, second = source[:HALF], source[HALF:]
        return (
            jnp.concatenate([first * cosine - second * sine, second * cosine + first * sine], axis=0) * factor
        ).astype(BF)

    rows = q_ref.shape[1]
    qt = turn(q_ref[...], LOG2E * HEAD ** (-0.5))
    kt = turn(k_ref[...], 1.0)
    vt = v_ref[...].astype(BF)
    qt_ref[0] = qt
    kt_ref[0] = kt
    vt_ref[0] = vt
    for first, last, masked in ((0, MIDDLE, False), (MIDDLE, rows, True)):
        keys = kt[:, first:last]
        values = vt[:, first:last]
        for at in range(first, last, block):
            scores = dot(keys, qt[:, at : at + block], 0, 0)
            if masked:
                scores = scores + mask_ref[:, at - first : at - first + block]
            largest = jnp.max(scores, axis=0, keepdims=True)
            raised = jnp.exp2(scores - largest)
            total = jnp.sum(raised, axis=0, keepdims=True)
            mixed = dot(values, raised.astype(BF), 1, 0)
            ot_ref[:, at : at + block] = (mixed / total).astype(BF)
            lse_ref[0, :, at : at + block] = largest + jnp.log2(total)


def attend_back_kernel(qt_ref, kt_ref, vt_ref, ot_ref, dot_ref, lse_ref, cos_ref, sin_ref, mask_ref, dq_ref, dk_ref, dv_ref, *, block):
    cosine, sine = cos_ref[...], sin_ref[...]

    def turn_back(grad, factor):
        first, second = grad[:HALF] * factor, grad[HALF:] * factor
        return jnp.concatenate([first * cosine + second * sine, second * cosine - first * sine], axis=0).astype(BF)

    rows = cos_ref.shape[1]
    qt, kt, vt, dot_ = qt_ref[0], kt_ref[0], vt_ref[0], dot_ref[...]
    delta = jnp.sum(dot_.astype(F32) * ot_ref[...].astype(F32), axis=0, keepdims=True)
    lse = lse_ref[0]
    queries = qt.astype(F32).T.astype(BF)
    grads = dot_.astype(F32).T.astype(BF)
    dq_parts, dk_parts, dv_parts = [], [], []
    for first, last, masked in ((0, MIDDLE, False), (MIDDLE, rows, True)):
        keys = kt[:, first:last]
        values = vt[:, first:last]
        dk = dv = None
        for at in range(first, last, block):
            sl = slice(at, at + block)
            scores = dot(keys, qt[:, sl], 0, 0)
            if masked:
                scores = scores + mask_ref[:, at - first : at - first + block]
            chances = jnp.exp2(scores - lse[:, sl])
            grad_chances = dot(values, dot_[:, sl], 0, 0)
            grad_scores = (chances * (grad_chances - delta[:, sl])).astype(BF)
            dv_part = dot(chances.astype(BF), grads[sl], 1, 0)
            dk_part = dot(grad_scores, queries[sl], 1, 0)
            dv = dv_part if dv is None else dv + dv_part
            dk = dk_part if dk is None else dk + dk_part
            dq_parts.append(dot(keys, grad_scores, 1, 0))
        dk_parts.append(dk.T)
        dv_parts.append(dv.T)
    dq_ref[0] = turn_back(jnp.concatenate(dq_parts, axis=1), HEAD ** (-0.5))
    dk_ref[0] = turn_back(jnp.concatenate(dk_parts, axis=1), LN2)
    dv_ref[0] = jnp.concatenate(dv_parts, axis=1).astype(BF)


def attend(mixed, cosine, sine, mask):
    rows = mixed.shape[1]
    heads = 4
    once = lambda shape: pl.BlockSpec(shape, lambda h: (0, 0))
    part = lambda which: pl.BlockSpec((HEAD, rows), lambda h: ((h // 2) * 8 + 2 * which + h % 2, 0))
    each = pl.BlockSpec((1, HEAD, rows), lambda h: (h, 0, 0))
    return pl.pallas_call(
        functools.partial(attend_kernel, block=256),
        grid=(heads,),
        in_specs=[part(0), part(1), part(2), once(cosine.shape), once(sine.shape), once(mask.shape)],
        out_specs=[
            each,
            each,
            each,
            pl.BlockSpec((HEAD, rows), lambda h: (h, 0)),
            pl.BlockSpec((1, 1, rows), lambda h: (h, 0, 0)),
        ],
        out_shape=[jax.ShapeDtypeStruct((heads, HEAD, rows), BF)] * 3
        + [
            jax.ShapeDtypeStruct((heads * HEAD, rows), BF),
            jax.ShapeDtypeStruct((heads, 1, rows), F32),
        ],
        compiler_params=pltpu.CompilerParams(vmem_limit_bytes=40 * 2**20),
        cost_estimate=FREE,
        name="attend",
    )(mixed, mixed, mixed, cosine, sine, mask)


def attend_back(saved, grad_mixed, cosine, sine, mask):
    qt, kt, vt, mixed, lse = saved
    heads, _, rows = qt.shape
    once = lambda shape: pl.BlockSpec(shape, lambda h: (0, 0))
    each = pl.BlockSpec((1, HEAD, rows), lambda h: (h, 0, 0))
    flat = pl.BlockSpec((HEAD, rows), lambda h: (h, 0))
    return pl.pallas_call(
        functools.partial(attend_back_kernel, block=256),
        grid=(heads,),
        in_specs=[
            each,
            each,
            each,
            flat,
            flat,
            pl.BlockSpec((1, 1, rows), lambda h: (h, 0, 0)),
            once(cosine.shape),
            once(sine.shape),
            once(mask.shape),
        ],
        out_specs=[each, each, each],
        out_shape=[jax.ShapeDtypeStruct((heads, HEAD, rows), BF)] * 3,
        compiler_params=pltpu.CompilerParams(vmem_limit_bytes=50 * 2**20),
        cost_estimate=FREE,
        name="attend_back",
    )(qt, kt, vt, mixed, grad_mixed, lse, cosine, sine, mask)


FREE = pl.CostEstimate(flops=0, bytes_accessed=0, transcendentals=0)
BLOCK = 256


def params(mib=48):
    return pltpu.CompilerParams(vmem_limit_bytes=mib * 2**20, dimension_semantics=("arbitrary",))


def whole(shape):
    return pl.BlockSpec(shape, lambda i: (0,) * len(shape))


def rows_of(width, block=BLOCK):
    return pl.BlockSpec((block, width), lambda i: (i, 0))


def columns_of(height, block=BLOCK):
    return pl.BlockSpec((height, block), lambda i: (0, i))


def product(name, pairs, outs, finish, extras=(), block=None):
    size = pairs[0][0].shape[1 - pairs[0][1]]
    block = block or (640 if size % 640 == 0 else 512 if size % 512 == 0 else BLOCK)
    in_specs, operands = [], []
    for left, left_dim, right, _ in pairs:
        in_specs.append(rows_of(left.shape[1], block) if left_dim == 1 else columns_of(left.shape[0], block))
        in_specs.append(whole(right.shape))
        operands.extend([left, right])
    for value in extras:
        in_specs.append(rows_of(value.shape[1], block) if value.shape[0] == size else whole(value.shape))
        operands.append(value)
    out_specs, out_shape = [], []
    for out in outs:
        if len(out) == 2:
            out_specs.append(rows_of(out[0], block))
            out_shape.append(jax.ShapeDtypeStruct((size, out[0]), out[1]))
        else:
            out_specs.append(whole((1, out[0])))
            out_shape.append(jax.ShapeDtypeStruct((1, out[0]), F32))

    def kernel(*refs):
        total = None
        for i, (_, left_dim, _, right_dim) in enumerate(pairs):
            term = dot(refs[2 * i][...], refs[2 * i + 1][...], left_dim, right_dim)
            total = term if total is None else total + term
        at = 2 * len(pairs)
        values = finish(total, *[r[...] for r in refs[at : at + len(extras)]])
        store(values, refs[at + len(extras) :], outs)

    return pl.pallas_call(
        kernel,
        grid=(size // block,),
        in_specs=in_specs,
        out_specs=out_specs,
        out_shape=out_shape,
        compiler_params=params(),
        cost_estimate=FREE,
        name=name,
    )(*operands)


def store(values, refs, outs):
    for value, ref, out in zip(values, refs, outs):
        if len(out) == 2:
            ref[...] = value.astype(out[1])
        else:
            summed = jnp.sum(value, axis=0, keepdims=True)

            @pl.when(pl.program_id(0) == 0)
            def _():
                ref[...] = summed

            @pl.when(pl.program_id(0) > 0)
            def _():
                ref[...] += summed


def by_rows(name, inputs, outs, step, block=256):
    size = inputs[0].shape[0]
    in_specs = [rows_of(v.shape[1], block) if v.shape[0] == size else whole(v.shape) for v in inputs]
    out_specs, out_shape = [], []
    for out in outs:
        if len(out) == 2:
            out_specs.append(rows_of(out[0], block))
            out_shape.append(jax.ShapeDtypeStruct((size, out[0]), out[1]))
        else:
            out_specs.append(whole((1, out[0])))
            out_shape.append(jax.ShapeDtypeStruct((1, out[0]), F32))

    def kernel(*refs):
        values = step(*[r[...] for r in refs[: len(inputs)]])
        store(values, refs[len(inputs) :], outs)

    return pl.pallas_call(
        kernel,
        grid=(size // block,),
        in_specs=in_specs,
        out_specs=out_specs,
        out_shape=out_shape,
        compiler_params=params(),
        cost_estimate=FREE,
        name=name,
    )(*inputs)


def first_norm_step(source, vectors):
    hat, _ = normalise(source.astype(F32))
    return (hat * vectors[0:1] + vectors[1:2],)


def second_norm_step(source, part, other, vectors):
    middle = source.astype(F32) + (part.astype(F32) + other.astype(F32)) + vectors[4:5]
    hat, _ = normalise(middle)
    return middle, hat * vectors[2:3] + vectors[3:4]


def second_back_step(part, other, middle, grad_out, vectors):
    grad = part.astype(F32) + other.astype(F32)
    hat, scale = normalise(middle.astype(F32))
    out = grad_out.astype(F32)
    grad_middle = out + norm_back(grad, vectors[2:3], hat, scale)
    return grad_middle, grad_middle, grad * hat, grad, grad_middle, out


def first_back_step(part, other, source, grad_middle, vectors):
    grad = part.astype(F32) + other.astype(F32)
    hat, scale = normalise(source.astype(F32))
    return grad_middle.astype(F32) + norm_back(grad, vectors[0:1], hat, scale), grad * hat, grad


def result_step(middle, part, other, vectors):
    return (middle.astype(F32) + (part.astype(F32) + other.astype(F32)) + vectors[5:6],)


def hidden_step(total, bias):
    hidden = total + bias
    gate = 1.0 / (1.0 + jnp.exp(-GELU_SLOPE * hidden))
    return hidden * gate, gate + GELU_SLOPE * hidden * gate * (1.0 - gate)


def hidden_back_step(total, slope):
    grad = (total * slope.astype(F32)).astype(BF)
    return grad, grad.astype(F32)


def feed_back(grad_rows, down, up, slopes):
    size, width = grad_rows.shape
    hidden = slopes[0].shape[1]

    def kernel(g_ref, da_ref, db_ref, ua_ref, ub_ref, sa_ref, sb_ref, ha_ref, hb_ref, part_ref, suma_ref, sumb_ref):
        total = None
        for d_ref, u_ref, s_ref, h_ref, sum_ref in (
            (da_ref, ua_ref, sa_ref, ha_ref, suma_ref),
            (db_ref, ub_ref, sb_ref, hb_ref, sumb_ref),
        ):
            grad = (dot(g_ref[...], d_ref[...], 1, 0) * s_ref[...].astype(F32)).astype(BF)
            h_ref[...] = grad
            store((grad.astype(F32),), (sum_ref,), ((hidden,),))
            term = dot(grad, u_ref[...], 1, 1)
            total = term if total is None else total + term
        part_ref[...] = total.astype(BF)

    weight = whole((width, hidden))
    return pl.pallas_call(
        kernel,
        grid=(size // 512,),
        in_specs=[rows_of(width, 512)] + [weight] * 4 + [rows_of(hidden, 512)] * 2,
        out_specs=[rows_of(hidden, 512)] * 2 + [rows_of(width, 512)] + [whole((1, hidden))] * 2,
        out_shape=[jax.ShapeDtypeStruct((size, hidden), BF)] * 2
        + [jax.ShapeDtypeStruct((size, width), BF)]
        + [jax.ShapeDtypeStruct((1, hidden), F32)] * 2,
        compiler_params=params(60),
        cost_estimate=FREE,
        name="feed_back",
    )(grad_rows, *down, *up, *slopes)


def second_norm_back(part, other, middle, grad_rows, vectors, outs):
    size, width = part.shape
    inner = outs[0].shape[1]

    def kernel(p_ref, o_ref, m_ref, g_ref, v_ref, wa_ref, wb_ref, branch_ref, da_ref, db_ref, *sums):
        _, grad_middle, *terms = second_back_step(p_ref[...], o_ref[...], m_ref[...], g_ref[...], v_ref[...])
        branch = grad_middle.astype(BF)
        branch_ref[...] = branch
        for w_ref, d_ref in ((wa_ref, da_ref), (wb_ref, db_ref)):
            d_ref[...] = dot(w_ref[...], branch, 0, 1).astype(BF)
        store(terms, sums, ((width,),) * 4)

    return pl.pallas_call(
        kernel,
        grid=(size // BLOCK,),
        in_specs=[rows_of(width)] * 4 + [whole(vectors.shape)] + [whole((width, inner))] * 2,
        out_specs=[rows_of(width)] + [columns_of(inner)] * 2 + [whole((1, width))] * 4,
        out_shape=[jax.ShapeDtypeStruct((size, width), BF)]
        + [jax.ShapeDtypeStruct((inner, size), BF)] * 2
        + [jax.ShapeDtypeStruct((1, width), F32)] * 4,
        compiler_params=params(),
        cost_estimate=FREE,
        name="norm_two_back",
    )(part, other, middle, grad_rows, vectors, *outs)


def first_grads(a_one, grad_branch, grad_mixed, mixed, inner):
    rows, width = a_one.shape

    def kernel(a_ref, g_ref, m_ref, o_ref, out_ref):
        for slot in range(2):
            at = slot * inner
            out_ref[:, at : at + 480] = dot(a_ref[...], m_ref[slot * 480 : (slot + 1) * 480], 0, 1).astype(BF)
            out_ref[:, at + 480 : at + 640] = dot(g_ref[...], o_ref[slot * 160 : (slot + 1) * 160], 0, 1).astype(BF)

    return pl.pallas_call(
        kernel,
        grid=(width // BLOCK,),
        in_specs=[columns_of(rows), columns_of(rows), whole(grad_mixed.shape), whole(mixed.shape)],
        out_specs=rows_of(2 * inner),
        out_shape=jax.ShapeDtypeStruct((width, 2 * inner), BF),
        compiler_params=params(),
        cost_estimate=FREE,
        name="first_grads",
    )(a_one, grad_branch, grad_mixed, mixed)


def pack(core, qkv, out, up, down, inner):
    rows = out.shape[0]

    def kernel(core_ref, qkv_ref, out_ref, up_ref, down_ref, keep_ref, give_ref):
        for ref, mine in ((keep_ref, core_ref[0]), (give_ref, 1 - core_ref[0])):
            low = mine == 0
            for i in range(3):
                value = qkv_ref[i]
                ref[:, i * 160 : (i + 1) * 160] = jnp.where(low, value[:, :160], value[:, 160:]).astype(BF)
            value = out_ref[...]
            ref[:, 480:640] = jnp.where(low, value[:, :160], value[:, 160:]).astype(BF)
            for j in range(2):
                ref[:, inner + j * 320 : inner + (j + 1) * 320] = jnp.where(
                    low, up_ref[:, j], up_ref[:, j + 2]
                ).astype(BF)
                ref[:, 2 * inner + j * 320 : 2 * inner + (j + 1) * 320] = jnp.where(
                    low, down_ref[j], down_ref[j + 2]
                ).astype(BF)

    return pl.pallas_call(
        kernel,
        in_specs=[pl.BlockSpec(memory_space=pltpu.SMEM)] + [pl.BlockSpec(memory_space=pltpu.VMEM)] * 4,
        out_specs=[pl.BlockSpec(memory_space=pltpu.VMEM)] * 2,
        out_shape=[jax.ShapeDtypeStruct((rows, 3 * inner), BF)] * 2,
        compiler_params=pltpu.CompilerParams(vmem_limit_bytes=40 * 2**20),
        cost_estimate=FREE,
        name="pack",
    )(core, qkv, out, up, down)


def body(
    tokens_in,
    cotangent,
    picture_ids,
    patch_positions,
    qkv_weight,
    out_weight,
    up_projection_weight,
    down_weight,
    projection_bias_rows,
    norm_vectors,
    qkv_first,
    out_first,
    up_first,
    down_first,
    bias_first,
    vector_first,
    qkv_second,
    out_second,
    up_second,
    down_second,
    bias_second,
    vector_second,
):
    count = lax.axis_size("g")
    bits = count.bit_length() - 1
    g, c, z = lax.axis_index("g"), lax.axis_index("c"), lax.axis_index("z")
    is_mid = (z == 1) | (z == 2)
    low_core = c == 0
    d_local = qkv_weight.shape[0]
    width = tokens_in.shape[2]
    part_rows = tokens_in.shape[1]
    inner = 640
    forth, back = tuple(range(bits)), tuple(reversed(range(bits)))

    with jax.named_scope("small"):
        bias_half = jnp.where(
            low_core,
            jnp.concatenate([projection_bias_rows[0:3, :160].reshape(480), projection_bias_rows[3:5].reshape(640)]),
            jnp.concatenate([projection_bias_rows[0:3, 160:].reshape(480), projection_bias_rows[5:7].reshape(640)]),
        )
        counted = jnp.concatenate([picture_ids[None], patch_positions], axis=0).astype(F32)
        small = jnp.concatenate([bias_half, counted.reshape(3 * 2 * part_rows)])[None]
        smalls = [lax.ppermute(small, "z", [(i, i ^ d) for i in range(4)]) for d in (1, 2, 3)]
        relative = jnp.concatenate([small] + smalls, axis=0)
        biases = relative[:, :1120]
        bias_near = biases[:2]
        bias_far = jnp.where(is_mid, biases[2:][::-1], biases[2:])
        counted = relative[:, 1120:].reshape(4, 3, 2, part_rows)
        counted = jnp.where((z & 1) == 0, counted[:, :, 0], counted[:, :, 1])
        counted = jnp.concatenate([lax.dynamic_slice_in_dim(counted, k ^ z, 1, 0) for k in range(4)], axis=0)
        counted = jnp.where((z >> 1) == c, counted, swap_core(counted))
        counted = jnp.moveaxis(counted, 1, 0).reshape(3, 4 * part_rows)

    rows_x, rows_g = RowsIn(tokens_in, z), RowsIn(cotangent, z)
    with jax.named_scope("rows_x"):
        r0, r1 = rows_x.send(), rows_x.send()

    with jax.named_scope("pack"):
        keep, give_away = pack(
            after(c[None].astype(jnp.int32), rows_x.sent),
            jnp.transpose(qkv_weight, (1, 0, 2)),
            out_weight.T,
            up_projection_weight,
            jnp.transpose(down_weight, (0, 2, 1)),
            inner,
        )
        other = swap_core(give_away)
        shard = jnp.concatenate([jnp.where(low_core, keep, other), jnp.where(low_core, other, keep)], axis=0)
        shard_q, shard_u, shard_d = [shard[:, i * inner : (i + 1) * inner] for i in range(3)]

    def pair(first, second):
        return jnp.concatenate([first, second], axis=-1)

    def along(value, distance, *earlier):
        return move(value, "z", [(i, i ^ distance) for i in range(4)], *earlier)

    def gather(block, order):
        return Gather(block, order, g, count)

    def far_of(two, three):
        return jnp.where(is_mid, pair(three, two), pair(two, three))

    def far_of(mid, end):
        return jnp.where(is_mid, mid, end)

    start = jnp.sum((counted[0] == 1).astype(jnp.int32))

    def halves_of(rows_half, *earlier):
        own = rows_half.half(*earlier)
        other = swap_core(own)
        return jnp.where(low_core, own, other), jnp.where(low_core, other, own)

    with jax.named_scope("near"):
        near_q = along(shard_q, 1)
        near_u = along(shard_u, 1)
        near_d = along(shard_d, 1, near_q)
    with jax.named_scope("far"):
        two_q = along(shard_q, 2, near_u)
        three_q = along(shard_q, 3, near_d)
    qa, ua, da = gather(pair(shard_q, near_q), forth), gather(pair(shard_u, near_u), back), gather(pair(shard_d, near_d), forth)
    with jax.named_scope("gx"):
        qax = qa.step()
        dax = da.step(qax)
    with jax.named_scope("gy"):
        uay = ua.step()
        qay = qa.finish(uay)
    with jax.named_scope("gx"):
        uax = ua.finish(dax)
    two_q, three_q = after(two_q, dax, qax, uay), after(three_q, dax, qax, uay)
    qb = gather(jnp.where(is_mid, pair(three_q, two_q), pair(two_q, three_q)), back)
    with jax.named_scope("rows_x"):
        source, a_one = turn_rows(start, *halves_of(rows_x, near_u), norm_vectors)
    qa.take(a_one)
    with jax.named_scope("far"):
        mid_u = move(pair(shard_u, near_u), "z", MIDS, two_q, three_q, dax, uay)
        end_u = move(mid_u, "z", OUTER, qay)
        mid_d = move(pair(shard_d, near_d), "z", MIDS, mid_u, qay)
    with jax.named_scope("gy"):
        qby = qb.step(qay)

    first_wa = qa.whole()

    rows = source.shape[0]
    counted = jnp.roll(counted, -start, axis=1)
    ids = counted[0, MIDDLE:]
    mask = jnp.where(ids[:, None] == ids[None, :], 0.0, -1e30).astype(F32)
    powers = jnp.arange(HEAD // 4, dtype=F32) * (2.0 / (HEAD // 2))
    inverse = jnp.power(10000.0, -powers)
    angles = jnp.concatenate([inverse[:, None] * counted[1][None], inverse[:, None] * counted[2][None]], axis=0)
    cosine, sine = jnp.cos(angles), jnp.sin(angles)

    def qkv_bias(pair):
        zero = jnp.zeros((160,), F32)
        return jnp.concatenate([pair[0, :480], zero, pair[1, :480], zero])

    mixed = dot(after(first_wa, mid_u), a_one, 0, 1) + qkv_bias(bias_near)[:, None]
    saved = [attend(mixed, cosine, sine, mask)]
    done = saved[0][3]
    qb.take(done)
    ua.take(done)
    with jax.named_scope("far"):
        end_d = move(mid_d, "z", OUTER, end_u, qby, done)
    with jax.named_scope("gx"):
        qbx = qb.finish(uax)
    with jax.named_scope("gy"):
        day = da.finish(qby)
    with jax.named_scope("rows_g"):
        rows_g.send(end_d, qby)
        rows_g.send(end_d, qby)
    ub, db = gather(far_of(mid_u, end_u), forth), gather(far_of(mid_d, end_d), back)
    with jax.named_scope("gx"):
        ubx = ub.step(qbx)
    with jax.named_scope("gy"):
        dby = db.step(day)
    first_wb = qb.whole()
    mixed = dot(after(first_wb, day), a_one, 0, 1) + qkv_bias(bias_far)[:, None]
    saved.append(attend(mixed, cosine, sine, mask))
    done = saved[1][3]
    ub.take(done)
    db.take(done)
    with jax.named_scope("gy"):
        uby = ub.finish(dby)
    with jax.named_scope("gx"):
        dbx = db.finish(ubx)
    with jax.named_scope("rows_g"):
        (grad_rows,) = turn_rows(start, *halves_of(rows_g, ubx, dby, done))

    def out_part(weight):
        return jnp.concatenate([weight[:, 480:640], weight[:, 1120:1280]], axis=1)

    def qkv_part(weight):
        return jnp.concatenate([weight[:, :480], weight[:, 640:1120]], axis=1)

    out_wa, out_wb = out_part(first_wa), out_part(first_wb)
    qkv_wa, qkv_wb = qkv_part(first_wa), qkv_part(first_wb)
    same = lambda total: (total,)
    (branch,) = product(
        "out_product",
        [(saved[0][3], 0, out_wa, 1), (saved[1][3], 0, out_wb, 1)],
        [(width, BF)],
        same,
    )
    middle, a_two = by_rows(
        "norm_two",
        [source, branch, swap_core(branch), norm_vectors],
        [(width, BF), (width, BF)],
        second_norm_step,
    )

    def feed_forward(weight, bias):
        return product(
            "up_product",
            [(a_two, 1, weight, 0)],
            [(2 * inner, BF), (2 * inner, BF)],
            hidden_step,
            [bias[:, 480:].reshape(1, 2 * inner)],
        )

    def down_grads(value):
        return product("down_grads", [(grad_rows, 0, value, 0)], [(2 * inner, BF)], same)[0]

    up_wa, down_wa = ua.whole(), da.whole()
    active_a, slope_a = feed_forward(up_wa, bias_near)
    grads_d_near = down_grads(active_a)
    ub.take(grads_d_near, qkv_wa, qkv_wb)
    db.take(grads_d_near)
    up_wb, down_wb = ub.whole(), db.whole()
    active_b, slope_b = feed_forward(up_wb, bias_far)
    grads_d_far = down_grads(active_b)
    active, slopes = (active_a, active_b), (slope_a, slope_b)

    def both_halves(own):
        upper, lower = own[:d_local], own[d_local:]
        keep = jnp.where(low_core, upper, lower)
        other = swap_core(jnp.where(low_core, lower, upper).astype(BF)).astype(F32)
        return jnp.stack([jnp.where(low_core, keep, other), jnp.where(low_core, other, keep)], axis=1)

    class SumZ:
        def __init__(self, near, far, *earlier):
            low_part, high_part = far[:, :inner].astype(BF), far[:, inner:].astype(BF)
            two, three = jnp.where(is_mid, high_part, low_part), jnp.where(is_mid, low_part, high_part)
            self.own = near[:, :inner]
            self.moved = [
                along(value, distance, *earlier)
                for distance, value in ((2, two), (3, three), (1, near[:, inner:].astype(BF)))
            ]

        def take(self, *earlier):
            for value in self.moved:
                self.own = self.own + (after(value, *earlier) if earlier else value).astype(F32)

        def whole(self, *earlier):
            return both_halves(after(self.own, *earlier) if earlier else self.own)

    grads_d = [grads_d_near, grads_d_far]
    with jax.named_scope("sd"):
        near_d, far_d = Scatter(grads_d[0], back, g, count), Scatter(grads_d[1], forth, g, count)
        one_d = [far_d.send(day, dbx), near_d.send(day, dbx)]
    *grad_hidden, part_u, sum_a, sum_b = feed_back(
        after(grad_rows, *grads_d), (down_wa, down_wb), (up_wa, up_wb), slopes
    )
    bias_up = [sum_a, sum_b]

    def up_grads(value, *earlier):
        return product("up_grads", [(after(a_two, *earlier), 0, value, 0)], [(2 * inner, BF)], same)[0]

    grads_u_far = up_grads(grad_hidden[1], part_u)
    with jax.named_scope("sd"):
        far_d.add(grads_u_far)
        near_d.add(grads_u_far)
        sent_d = [far_d.send(), near_d.send()]
    part_u_other = swap_core(part_u, *one_d, grads_u_far)
    (feed,) = product(
        "down_product",
        [(active[0], 1, down_wa, 1), (after(active[1], grads_u_far, *one_d), 1, down_wb, 1)],
        [(width, BF)],
        same,
    )
    feed_other = swap_core(feed)
    grads_u_near = up_grads(grad_hidden[0], feed)
    grad_branch, *grad_atts, sums_0, sums_1, sums_2, sums_3 = second_norm_back(
        part_u, part_u_other, after(middle, grads_u_near, feed_other), grad_rows, norm_vectors, (out_wa, out_wb)
    )
    sums_two = [sums_0, sums_1, sums_2, sums_3]
    with jax.named_scope("sd"):
        far_d.add(grad_branch)
        near_d.add(grad_branch)
    with jax.named_scope("su"):
        near_u, far_u = Scatter(grads_u_near, back, g, count), Scatter(grads_u_far, forth, g, count)
        one_u = [far_u.send(*sent_d, grad_branch), near_u.send(*sent_d, grad_branch)]

    def attention_back(i, *earlier):
        dq, dk, dv = attend_back(saved[i], after(grad_atts[i], *earlier), cosine, sine, mask)
        return jnp.stack([v.reshape(2, 160, rows) for v in (dq, dk, dv)], axis=1).reshape(960, rows)

    with jax.named_scope("sd"):
        line_d = SumZ(near_d.whole(), far_d.whole())
    mixed_far = attention_back(1, *sent_d)
    (result,) = by_rows(
        "result", [after(middle, mixed_far), feed, feed_other, norm_vectors], [(width, BF)], result_step
    )
    with jax.named_scope("sd"):
        line_d.take(result)
    with jax.named_scope("rows_out"):
        block_out, out_pieces = rows_out(after(result, *line_d.moved), start, c, z)
    grads_far = first_grads(a_one, after(grad_branch, result), mixed_far, saved[1][3], inner)
    with jax.named_scope("su"):
        far_u.add(grads_far)
        near_u.add(grads_far)
        sent_u = [far_u.send(), near_u.send()]
    mixed_near = attention_back(0, *one_u, grads_far)
    with jax.named_scope("su"):
        far_u.add(mixed_near)
        near_u.add(mixed_near)
        line_u = SumZ(near_u.whole(), far_u.whole())
    (part,) = product(
        "qkv_back",
        [(after(mixed_near, *sent_u), 0, qkv_wa, 1), (mixed_far, 0, qkv_wb, 1)],
        [(width, BF)],
        same,
    )
    part_other = swap_core(part, *out_pieces)
    grads_near = first_grads(a_one, after(grad_branch, part, *out_pieces), mixed_near, saved[0][3], inner)
    with jax.named_scope("sq"):
        near_q, far_q = Scatter(grads_near, back, g, count), Scatter(grads_far, forth, g, count)
        one_q = [far_q.send(grads_near), near_q.send(grads_near)]
    bias_qkv = [jnp.sum(v, axis=1, dtype=F32) for v in (mixed_near, mixed_far)]
    grad_source, *sums_one = by_rows(
        "norm_back",
        [part, part_other, after(source, grads_near), grad_branch, norm_vectors],
        [(width, BF), (width,), (width,)],
        first_back_step,
    )
    with jax.named_scope("su"):
        line_u.take(grad_source)
    with jax.named_scope("rows_dx"):
        input_grad, dx_pieces = rows_out(grad_source, start, c, z)
        input_grad = input_grad.astype(F32)
    with jax.named_scope("sq"):
        far_q.add(grad_source)
        near_q.add(grad_source)
        sent_q = [far_q.send(), near_q.send()]
        far_q.add(*dx_pieces)
        near_q.add(*dx_pieces)
        line_q = SumZ(near_q.whole(), far_q.whole())
        line_q.take()
        grad_first = line_q.whole()
    with jax.named_scope("sd"):
        grad_down = line_d.whole(*dx_pieces)
    with jax.named_scope("su"):
        grad_up = line_u.whole(*dx_pieces)

    vector_grad = 0.5 * jnp.concatenate(sums_one + sums_two, axis=0)
    bias_up = [after(v, *sent_q) for v in bias_up]
    far_zero = jnp.where(z < 2, 2, 1)
    far_one = jnp.where(z < 2, 3, 0)
    placed = jnp.zeros((7, 4, 320), F32)
    for index, place in enumerate((z, z ^ 1, far_zero, far_one)):
        qkv_sum = bias_qkv[index // 2].reshape(2, 3, 1, 160)[index % 2]
        up_sum = bias_up[index // 2].reshape(2, 2, 1, 320)[index % 2]
        placed = lax.dynamic_update_slice(placed, qkv_sum, (0, place, c * 160))
        placed = lax.dynamic_update_slice(placed, up_sum, (3 + 2 * c, place, 0))
    with jax.named_scope("vectors"):
        summed = add_up(
            after(jnp.concatenate([placed.reshape(7, 4 * 320), vector_grad], axis=0), *sent_q), count
        )
    grad_bias = lax.dynamic_slice(summed, (0, z * 320), (7, 320))
    grad_vector = summed[7:]

    first_split = grad_first.reshape(d_local, 2, 4, 160)
    grad_qkv = jnp.moveaxis(first_split[:, :, :3], 1, 2).reshape(d_local, 3, 320)
    grad_o = first_split[:, :, 3].reshape(d_local, 320).T
    grad_up = grad_up.reshape(d_local, 4, 320)
    grad_down = jnp.transpose(grad_down.reshape(d_local, 4, 320), (1, 2, 0))
    outputs = [block_out, input_grad]
    for weight, grad, first, second, rate, decay in (
        (qkv_weight, grad_qkv, qkv_first, qkv_second, MATRIX_RATE, MATRIX_DECAY),
        (out_weight, grad_o, out_first, out_second, MATRIX_RATE, MATRIX_DECAY),
        (up_projection_weight, grad_up, up_first, up_second, MATRIX_RATE, MATRIX_DECAY),
        (down_weight, grad_down, down_first, down_second, MATRIX_RATE, MATRIX_DECAY),
        (projection_bias_rows, grad_bias, bias_first, bias_second, VECTOR_RATE, 0.0),
        (norm_vectors, grad_vector, vector_first, vector_second, VECTOR_RATE, 0.0),
    ):
        outputs.extend(adam_step(weight, grad, first, second, rate, decay))
    return tuple(outputs)


def solution(mesh):
    devices = mesh.devices.reshape(mesh.shape["dp"] // 2, 2, mesh.shape["tensor"])
    own_mesh = Mesh(devices, ("g", "c", "z"))
    rows = P(("g", "c"), "z", None)
    in_weights = (P(("g", "c"), None, "z"), P("z", ("g", "c")), P(("g", "c"), None, "z"), P(None, "z", ("g", "c")))
    vectors = (P(None, "z"), P())
    params = in_weights + vectors
    out_specs = [rows, rows]
    for spec in params:
        out_specs.extend([spec] * 3)
    return jax.shard_map(
        body,
        mesh=own_mesh,
        in_specs=(rows, rows, P(("g", "c"), "z"), P(None, ("g", "c"), "z")) + params * 3,
        out_specs=tuple(out_specs),
        check_vma=False,
    )
```

time: 957 us -> 711 us (0.74)
  Pallas kernels: 61.9 us -> 260 us
  waiting for transfers between devices: 331 us -> 137 us
  matrix products: 153 us -> 12.4 us
  other arithmetic: 175 us -> 118 us
  local copies, waits for them, and re-layouts: 96.5 us -> 47.6 us
    pallas_call x0 -> x19, Pallas kernels: none -> 198 us  [the longest x9 87.8 us: product(): pl.pallas_call(kernel, grid=(size // block,), in_specs=in_specs, out_spec...]
    ppermute x63 -> x60, waiting for transfers between devices: 259 us -> 106 us  [move(): lax.ppermute(after(value, *earlier) if earlier else value, axis, pairs)]
    dot_general x24 -> x2, matrix products: 153 us -> 12.4 us  [dot(): lax.dot_general(left, right, (((left_dim,), (right_dim,)), ((), ())), pre...]
    ppermute x9 -> x4, waiting for transfers between devices: 38 us -> 2.86 us  [rows_out(): lax.ppermute(sent, ('c', 'z'), [(b, a) for a, b in row_moves(step)])]
    reduce_sum x12 -> x2, other arithmetic: 34 us -> 3.22 us  [body(): bias_qkv = [jnp.sum(v, axis=1, dtype=F32) for v in (mixed_near, mixed_far)]]
    convert_element_type x14 -> x9, other arithmetic: 36.2 us -> 13.4 us  [the longest x6 12.6 us: send(): sent = self.total(self.sliced(1 - mine, axis)).astype(BF)]
    ppermute x9 -> x4, starting transfers between devices: 30.5 us -> 11.4 us  [rows_out(): lax.ppermute(sent, ('c', 'z'), [(b, a) for a, b in row_moves(step)])]
    add x13 -> x3, other arithmetic: 24 us -> 5.37 us  [take(): self.own + (after(value, *earlier) if earlier else value).astype(F32)]
  transfers between devices with their start and end apart: 77 -> 69, of which waited for: 27 -> 20; matrix products, arithmetic and copies ran while one was open for 36% -> 21% of each run, Pallas kernels for 7% -> 35%
where the time goes in v2:
time: 711 us; the launch traced here: 700 us
  Pallas kernels  260 us (37%)
  waiting for transfers between devices  137 us (19%)
  starting transfers between devices  121 us (17%)
  other arithmetic  118 us (17%)
  local copies, waits for them, and re-layouts  47.6 us (7%)
  matrix products  12.4 us (2%)
    ppermute x60, waiting for transfers between devices, move(): lax.ppermute(after(value, *earlier) if earlier else value, axis, pairs)  106 us
    ppermute x60, starting transfers between devices, move(): lax.ppermute(after(value, *earlier) if earlier else value, axis, pairs)  99.2 us
    pallas_call x9, Pallas kernels, product(): pl.pallas_call(kernel, grid=(size // block,), in_specs=in_specs, out_spec...  87.8 us
    pallas_call x1, Pallas kernels, feed_back(): pl.pallas_call(kernel, grid=(size // 512,), in_specs=[rows_of(width, 512)...  34.2 us
    pallas_call x2, Pallas kernels, attend_back(): pl.pallas_call(functools.partial(attend_back_kernel, block=256), grid=(he...  31.6 us
    pallas_call x2, Pallas kernels, attend(): pl.pallas_call(functools.partial(attend_kernel, block=256), grid=(heads,)...  29.8 us
    ppermute x2, waiting for transfers between devices, add_up(): lax.ppermute(value, 'z', [(i, i ^ distance) for i in range(4)])  28.9 us
    pallas_call x3, Pallas kernels, by_rows(): pl.pallas_call(kernel, grid=(size // block,), in_specs=in_specs, out_spec...  26.7 us
  transfers between devices with their start and end apart: 69, of which 20 were waited for; matrix products, arithmetic and copies ran while one was open for 21% of the time, Pallas kernels for 35%

profile of v2, /device:TPU:0, one launch (start us, length us, event | category | flops | bytes accessed | tf_op | source)
XLA Modules:
  0.0 699.7 jit_solution(5157357043628422936)
XLA Ops:
  3.5 3.1 collective-permute-start
  6.6 2.6 collective-permute-start.1
  9.2 2.7 select_bitcast_fusion.7
  14.8 3.1 collective-permute-start.5
  29.0 30.1 %collective-permute-done.9 = bf16[320,640]{1,0:T(8,128)(2,1)S(1)} collective-permute-done((bf16[320,640]{1,0:T(8,128)(2,1)S(1)}, bf16[320,640]{1,0:T(8,128)(2,1)S(1)}, u32[]{:S(2)}, u32[]{:S(2)}) %collective-permute-start.9) | collective-permute-done | bytes 409632 | tf_op jit(solution)/shard_map/near/ppermute | solution.py:71
  61.1 6.5 collective-permute-done.6
  73.2 3.3 collective-permute-done.14
  82.3 4.4 collective-permute-done.11
  91.4 9.4 %collective-permute-done.15 = bf16[1,1,320,1280]{3,2,1,0:T(8,128)(2,1)S(1)} collective-permute-done((bf16[1,1,320,1280]{3,2,1,0:T(8,128)(2,1)S(1)}, bf16[1,1,320,1280]{3,2,1,0:T(8,128)(2,1)S(1)}, u32[]{:S(2)}, u32[]{:S(2)}) %collective-permute-start.15) | collective-permute-done | bytes 819232 | tf_op jit(solution)/shard_map/gx/ppermute | solution.py:71
  107.8 7.9 %turn_rows.2 = (bf16[1536,1280]{1,0:T(8,128)(2,1)S(1)}, bf16[1536,1280]{1,0:T(8,128)(2,1)S(1)}) custom-call(s32[1]{0:T(128)} %bitcast.6.start_ref, bf16[768,1280]{1,0:T(8,128)(2,1)S(1)} %get-tuple-element.335.up_ref, bf16[768,1280]{1,0:T(8,128)(2,1)S(1)} %get-tuple-element.334.low_ref, f32[6,1280]{1,0:T(8,128)S(1)} %copy-done.33), custom_call_target="tpu_custom_call" | custom-call | tf_op jit(solution)/shard_map/rows_x/turn_rows/pallas_call | solution.py:225
  117.6 4.7 collective-permute-done.12
  126.6 6.2 convolution_add_fusion.1.q_ref.k_ref.v_ref
  133.4 14.9 %attend.2 = (bf16[4,80,1536]{2,1,0:T(8,128)(2,1)S(1)}, bf16[4,80,1536]{2,1,0:T(8,128)(2,1)S(1)}, bf16[4,80,1536]{2,1,0:T(8,128)(2,1)S(1)}, bf16[320,1536]{1,0:T(8,128)(2,1)S(1)}, f32[4,1,1536]{2,1,0:T(1,128)S(1)}) custom-call(f32[1280,1536]{1,0:T(8,128)S(1)} %convolution_add_fusion.1.q_ref.k_ref.v_ref, ...), custom_call_target="tpu_custom_call" | custom-call | tf_op jit(solution)/shard_map/attend/pallas_call | solution.py:325
  155.2 2.5 pad_maximum_fusion.8.refs_1_
  158.1 2.5 select_bitcast_fusion.9
  160.6 14.8 %collective-permute-done.25 = bf16[320,1280]{1,0:T(8,128)(2,1)S(1)} collective-permute-done((bf16[320,1280]{1,0:T(8,128)(2,1)}, bf16[320,1280]{1,0:T(8,128)(2,1)S(1)}, u32[]{:S(2)}, u32[]{:S(2)}) %collective-permute-start.25) | collective-permute-done | bytes 819232 | tf_op jit(solution)/shard_map/far/ppermute | solution.py:71
  175.4 8.9 %collective-permute-start.29 = (bf16[384,1280]{1,0:T(8,128)(2,1)}, bf16[384,1280]{1,0:T(8,128)(2,1)}, u32[]{:S(2)}, u32[]{:S(2)}) collective-permute-start(bf16[384,1280]{1,0:T(8,128)(2,1)} %get-tuple-element.176), channel_id=1, source_target_pairs={{0,0},{1,1},{2,4},{3,5},{4,2},{5,3},{6,6},{7,7},{8,8},{9,9},{10,12... | collective-permute-start | bytes 2949128 | tf_op jit(solution)/shard_map/rows_g/ppermute | solution.py:71
  188.8 3.5 broadcast_select_fusion.7
  193.8 6.2 convolution_add_fusion.q_ref.k_ref.v_ref
  200.4 14.9 %attend.3 = (bf16[4,80,1536]{2,1,0:T(8,128)(2,1)S(1)}, bf16[4,80,1536]{2,1,0:T(8,128)(2,1)S(1)}, bf16[4,80,1536]{2,1,0:T(8,128)(2,1)S(1)}, bf16[320,1536]{1,0:T(8,128)(2,1)S(1)}, f32[4,1,1536]{2,1,0:T(1,128)S(1)}) custom-call(f32[1280,1536]{1,0:T(8,128)S(1)} %convolution_add_fusion.q_ref.k_ref.v_ref, f32[1280,1536]{1,0:T(8,128)S(1)} %convolution_add_fusion.q_ref.k_ref.v_ref, ...), custom_call_target="tpu_custom_call" | custom-call | tf_op jit(solution)/shard_map/attend/pallas_call | solution.py:325
  217.4 6.1 out_product.1.refs_1_
  225.8 2.8 broadcast_select_fusion.17
  232.5 2.5 pad_maximum_fusion.9.refs_3_
  239.6 4.8 turn_rows.3.refs_0_.g_ref
  246.3 8.9 %norm_two.1 = (bf16[1536,1280]{1,0:T(8,128)(2,1)S(1)}, bf16[1536,1280]{1,0:T(8,128)(2,1)}) custom-call(bf16[1536,1280]{1,0:T(8,128)(2,1)} %copy-done.8, bf16[1536,1280]{1,0:T(8,128)(2,1)} %out_product.1.refs_1_, bf16[1536,1280]{1,0:T(8,128)(2,1)} %collective-permute-done.22.refs_2_, f32[6,1280]{1,0:T(8,128)S(1)} %copy-done.33), custom_call_target="tpu_custom_call" | custom-call | tf_op jit(solution)/shard_map/norm_two/pallas_call | solution.py:468
  257.2 10.5 %up_product.2 = (bf16[1536,1280]{1,0:T(8,128)(2,1)}, bf16[1536,1280]{1,0:T(8,128)(2,1)}) custom-call(bf16[1536,1280]{1,0:T(8,128)(2,1)} %get-tuple-element.198.refs_0_, bf16[1280,1280]{1,0:T(8,128)(2,1)S(1)} %bitcast.150, f32[1,1280]{1,0:T(1,128)S(1)} %bitcast.182), custom_call_target="tpu_custom_call" | custom-call | tf_op jit(solution)/shard_map/up_product/pallas_call | solution.py:424
  267.7 8.2 %down_grads.2 = bf16[1280,1280]{1,0:T(8,128)(2,1)S(1)} custom-call(bf16[1536,1280]{1,0:T(8,128)(2,1)} %copy-done, bf16[1536,1280]{1,0:T(8,128)(2,1)} %get-tuple-element.180.refs_1_.refs_0_), custom_call_target="tpu_custom_call" | custom-call | tf_op jit(solution)/shard_map/down_grads/pallas_call | solution.py:424
  275.9 2.8 broadcast_select_fusion.13
  279.1 11.4 %up_product.3 = (bf16[1536,1280]{1,0:T(8,128)(2,1)}, bf16[1536,1280]{1,0:T(8,128)(2,1)}) custom-call(bf16[1536,1280]{1,0:T(8,128)(2,1)} %get-tuple-element.198.refs_0_, bf16[1280,1280]{1,0:T(8,128)(2,1)S(1)} %bitcast.152, f32[1,1280]{1,0:T(1,128)S(1)} %bitcast.181), custom_call_target="tpu_custom_call" | custom-call | tf_op jit(solution)/shard_map/up_product/pallas_call | solution.py:424
  290.5 8.5 %down_grads.3 = bf16[1280,1280]{1,0:T(8,128)(2,1)S(1)} custom-call(bf16[1536,1280]{1,0:T(8,128)(2,1)} %copy-done, bf16[1536,1280]{1,0:T(8,128)(2,1)} %get-tuple-element.197.refs_1_.refs_2_), custom_call_target="tpu_custom_call" | custom-call | tf_op jit(solution)/shard_map/down_grads/pallas_call | solution.py:424
  310.1 34.2 %feed_back.1 = (bf16[1536,1280]{1,0:T(8,128)(2,1)}, bf16[1536,1280]{1,0:T(8,128)(2,1)}, bf16[1536,1280]{1,0:T(8,128)(2,1)}, f32[1,1280]{1,0:T(1,128)}, f32[1,1280]{1,0:T(1,128)}) custom-call(bf16[1536,1280]{1,0:T(8,128)(2,1)} %copy-done, bf16[1280,1280]{1,0:T(8,128)(2,1)} %bitcast.154, bf16[1280,1280]{1,0:T(8,128)(2,1)} %bitcast.183, ...), custom_call_target="tpu_custom_call" | custom-call | tf_op jit(solution)/shard_map/feed_back/pallas_call | solution.py:538
  344.3 8.4 %up_grads.2 = bf16[1280,1280]{1,0:T(8,128)(2,1)S(1)} custom-call(bf16[1536,1280]{1,0:T(8,128)(2,1)} %get-tuple-element.198.refs_0_, bf16[1536,1280]{1,0:T(8,128)(2,1)} %get-tuple-element.195.refs_1_), custom_call_target="tpu_custom_call" | custom-call | tf_op jit(solution)/shard_map/up_grads/pallas_call | solution.py:424
  352.8 15.1 %down_product.1.refs_1_ = bf16[1536,1280]{1,0:T(8,128)(2,1)} custom-call(bf16[1536,1280]{1,0:T(8,128)(2,1)} %get-tuple-element.180.refs_1_.refs_0_, bf16[1280,1280]{1,0:T(8,128)(2,1)S(1)} %bitcast.155, bf16[1536,1280]{1,0:T(8,128)(2,1)} %get-tuple-element.197.refs_1_.refs_2_, bf16[1280,1280]{1,0:T(8,128)(2,1)} %bitcast.184), custom_call_target="tpu_custom_call" | custom-call | tf_op jit(solution)/shard_map/down_product/pallas_call | solution.py:424
  375.0 8.2 %up_grads.3 = bf16[1280,1280]{1,0:T(8,128)(2,1)S(1)} custom-call(bf16[1536,1280]{1,0:T(8,128)(2,1)} %get-tuple-element.198.refs_0_, bf16[1536,1280]{1,0:T(8,128)(2,1)} %get-tuple-element.199.refs_1_), custom_call_target="tpu_custom_call" | custom-call | tf_op jit(solution)/shard_map/up_grads/pallas_call | solution.py:424
  386.2 14.9 %norm_two_back.1 = (bf16[1536,1280]{1,0:T(8,128)(2,1)}, bf16[320,1536]{1,0:T(8,128)(2,1)S(1)}, bf16[320,1536]{1,0:T(8,128)(2,1)S(1)}, f32[1,1280]{1,0:T(1,128)S(...) custom-call(bf16[1536,1280]{1,0:T(8,128)(2,1)} %get-tuple-element.196.p_ref, ...), custom_call_target="tpu_custom_call" | custom-call | tf_op jit(solution)/shard_map/norm_two_back/pallas_call | solution.py:564
  405.9 8.7 %collective-permute-start.41 = (bf16[320,640]{1,0:T(8,128)(2,1)}, bf16[320,640]{1,0:T(8,128)(2,1)}, u32[]{:S(2)}, u32[]{:S(2)}) collective-permute-start(bf16[320,640]{1,0:T(8,128)(2,1)} %slice.472), channel_id=1, source_target_pairs={{0,1},{1,0},{2,3},{3,2},{4,5},{5,4},{6,7},{7,6},{8,9},{9,8},{10,11... | collective-permute-start | bytes 1228808 | tf_op jit(solution)/shard_map/sd/ppermute | solution.py:71
  422.9 15.8 %attend_back.2 = (bf16[4,80,1536]{2,1,0:T(8,128)(2,1)S(1)}, bf16[4,80,1536]{2,1,0:T(8,128)(2,1)S(1)}, bf16[4,80,1536]{2,1,0:T(8,128)(2,1)S(1)}) custom-call(bf16[4,80,1536]{2,1,0:T(8,128)(2,1)} %copy-done.40, bf16[4,80,1536]{2,1,0:T(8,128)(2,1)} %copy-done.41, bf16[4,80,1536]{2,1,0:T(8,128)(2,1)} %copy-done.42, bf16[320,1536]{1,0:T(8,128)(2,1)} %copy-done.17, ...), custom_call_target="tpu_custom_call" | custom-call | tf_op jit(solution)/shard_map/attend_back/pallas_call | solution.py:353
  440.1 7.3 %result.1 = bf16[1536,1280]{1,0:T(8,128)(2,1)S(1)} custom-call(bf16[1536,1280]{1,0:T(8,128)(2,1)} %copy-done.9, bf16[1536,1280]{1,0:T(8,128)(2,1)} %down_product.1.refs_1_, bf16[1536,1280]{1,0:T(8,128)(2,1)} %collective-permute-done.36.refs_2_, f32[6,1280]{1,0:T(8,128)S(1)} %copy-done.35), custom_call_target="tpu_custom_call" | custom-call | tf_op jit(solution)/shard_map/result/pallas_call | solution.py:468
  447.4 10.0 %first_grads.2 = bf16[1280,1280]{1,0:T(8,128)(2,1)} custom-call(bf16[1536,1280]{1,0:T(8,128)(2,1)} %copy-done.7, bf16[1536,1280]{1,0:T(8,128)(2,1)} %get-tuple-element.230.g_ref.refs_3_, bf16[960,1536]{1,0:T(8,128)(2,1)S(1)} %bitcast.156, bf16[320,1536]{1,0:T(8,128)(2,1)S(1)} %copy-done.18), custom_call_target="tpu_custom_call" | custom-call | tf_op jit(solution)/shard_map/first_grads/pallas_call | solution.py:587
  457.6 2.8 fusion.7
  462.9 2.5 add_convert_fusion.4
  469.8 15.8 %attend_back.3 = (bf16[4,80,1536]{2,1,0:T(8,128)(2,1)S(1)}, bf16[4,80,1536]{2,1,0:T(8,128)(2,1)S(1)}, bf16[4,80,1536]{2,1,0:T(8,128)(2,1)S(1)}) custom-call(bf16[4,80,1536]{2,1,0:T(8,128)(2,1)} %copy-done.37, bf16[4,80,1536]{2,1,0:T(8,128)(2,1)} %copy-done.38, bf16[4,80,1536]{2,1,0:T(8,128)(2,1)} %copy-done.39, bf16[320,1536]{1,0:T(8,128)(2,1)} %copy-done.15, ...), custom_call_target="tpu_custom_call" | custom-call | tf_op jit(solution)/shard_map/attend_back/pallas_call | solution.py:353
  489.2 11.4 %qkv_back.1.refs_0_ = bf16[1536,1280]{1,0:T(8,128)(2,1)} custom-call(bf16[960,1536]{1,0:T(8,128)(2,1)} %bitcast.158, bf16[1280,960]{1,0:T(8,128)(2,1)S(1)} %copy-done.13, bf16[960,1536]{1,0:T(8,128)(2,1)} %bitcast.157, bf16[1280,960]{1,0:T(8,128)(2,1)S(1)} %copy-done.14), custom_call_target="tpu_custom_call" | custom-call | tf_op jit(solution)/shard_map/qkv_back/pallas_call | solution.py:424
  500.6 5.4 collective-permute-start.48
  507.2 2.9 constant_dynamic-slice_fusion
  512.5 10.0 %first_grads.3 = bf16[1280,1280]{1,0:T(8,128)(2,1)} custom-call(bf16[1536,1280]{1,0:T(8,128)(2,1)} %copy-done.7, bf16[1536,1280]{1,0:T(8,128)(2,1)} %get-tuple-element.230.g_ref.refs_3_, bf16[960,1536]{1,0:T(8,128)(2,1)S(1)} %bitcast.159, bf16[320,1536]{1,0:T(8,128)(2,1)S(1)} %copy-done.16), custom_call_target="tpu_custom_call" | custom-call | tf_op jit(solution)/shard_map/first_grads/pallas_call | solution.py:587
  523.4 2.7 constant_dynamic-slice_fusion.2
  527.2 2.9 select_bitcast_fusion.3
  534.4 2.5 collective-permute-start.60
  537.0 10.5 %norm_back.1 = (bf16[1536,1280]{1,0:T(8,128)(2,1)S(1)}, f32[1,1280]{1,0:T(1,128)S(1)}, f32[1,1280]{1,0:T(1,128)S(1)}) custom-call(bf16[1536,1280]{1,0:T(8,128)(2,1)} %qkv_back.1.refs_0_, bf16[1536,1280]{1,0:T(8,128)(2,1)} %collective-permute-done.48.refs_1_, bf16[1536,1280]{1,0:T(8,128)(2,1)} %copy-done.8, ...), custom_call_target="tpu_custom_call" | custom-call | tf_op jit(solution)/shard_map/norm_back/pallas_call | solution.py:468
  547.5 13.0 %collective-permute-done.53 = bf16[2,1,320,1280]{3,2,1,0:T(8,128)(2,1)} collective-permute-done((bf16[2,1,320,1280]{3,2,1,0:T(8,128)(2,1)}, bf16[2,1,320,1280]{3,2,1,0:T(8,128)(2,1)}, u32[]{:S(2)}, u32[]{:S(2)}) %collective-permute-start.53) | collective-permute-done | bytes 1638432 | tf_op jit(solution)/shard_map/sq/ppermute | solution.py:71
  571.3 4.7 fusion.5
  576.0 6.4 collective-permute-done.54
  582.4 3.4 collective-permute-done.52
  585.8 8.9 %collective-permute-start.50 = (bf16[384,1280]{1,0:T(8,128)(2,1)}, bf16[384,1280]{1,0:T(8,128)(2,1)}, u32[]{:S(2)}, u32[]{:S(2)}) collective-permute-start(bf16[384,1280]{1,0:T(8,128)(2,1)} %get-tuple-element.329), channel_id=1, source_target_pairs={{0,0},{1,1},{4,2},{5,3},{2,4},{3,5},{6,6},{7,7},{8,8},{9,9},{12,10... | collective-permute-start | bytes 2949128 | tf_op jit(solution)/shard_map/rows_dx/ppermute | solution.py:191
  596.4 3.1 pad_maximum_fusion.12
  601.9 2.5 collective-permute-done.65
  605.4 2.8 collective-permute-done.49
  608.3 18.7 %collective-permute-start.63 = (bf16[160,640]{1,0:T(8,128)(2,1)S(1)}, bf16[160,640]{1,0:T(8,128)(2,1)S(1)}, u32[]{:S(2)}, u32[]{:S(2)}) collective-permute-start(bf16[160,640]{1,0:T(8,128)(2,1)S(1)} %select_convert_fusion), channel_id=1, source_target_pairs={{0,4},{4,0},{1,5},{5,1},{2,6},{6,2},{3,7},{7,3},{8,12},{12,8},{9,1... | collective-permute-start | bytes 614408 | tf_op jit(solution)/shard_map/sd/ppermute | solution.py:71
  630.7 2.8 collective-permute-start.56
  637.7 13.2 %collective-permute-done.67 = f32[13,1280]{1,0:T(8,128)S(1)} collective-permute-done((f32[13,1280]{1,0:T(8,128)S(1)}, f32[13,1280]{1,0:T(8,128)S(1)}, u32[]{:S(2)}, u32[]{:S(2)}) %collective-permute-start.67) | collective-permute-done | bytes 66592 | tf_op jit(solution)/shard_map/vectors/ppermute | solution.py:243
  650.9 3.6 collective-permute-start.68
  657.5 15.6 %collective-permute-done.68 = f32[13,1280]{1,0:T(8,128)S(1)} collective-permute-done((f32[13,1280]{1,0:T(8,128)S(1)}, f32[13,1280]{1,0:T(8,128)S(1)}, u32[]{:S(2)}, u32[]{:S(2)}) %collective-permute-start.68) | collective-permute-done | bytes 66592 | tf_op jit(solution)/shard_map/vectors/ppermute | solution.py:243
  681.9 4.9 multiply_subtract_fusion.1
  (465 shorter events, 180.6 us)
Async XLA Ops:
  3.5 17.8 %collective-permute-start = (f32[1,3424]{1,0:T(1,128)S(1)}, f32[1,3424]{1,0:T(1,128)S(1)}, u32[]{:S(2)}, u32[]{:S(2)}) collective-permute-start(f32[1,3424]{1,0:T(1,128)S(1)} %broadcast_in_dim.29), channel_id=1, source_target_pairs={{0,1},{1,0},{2,3},{3,2},{4,5},{5,4},{6,7},{7,6},{8,9},{9,8},{10,11... | collective-permute-start | bytes 41096 | tf_op jit(solution)/shard_map/small/ppermute | solution.py:672
  6.6 12.7 %collective-permute-start.1 = (f32[1,3424]{1,0:T(1,128)S(1)}, f32[1,3424]{1,0:T(1,128)S(1)}, u32[]{:S(2)}, u32[]{:S(2)}) collective-permute-start(f32[1,3424]{1,0:T(1,128)S(1)} %broadcast_in_dim.29), channel_id=1, source_target_pairs={{0,2},{1,3},{2,0},{3,1},{4,6},{5,7},{6,4},{7,5},{8,10},{9,11},{10,... | collective-permute-start | bytes 41096 | tf_op jit(solution)/shard_map/small/ppermute | solution.py:672
  9.2 11.8 %collective-permute-start.2 = (f32[1,3424]{1,0:T(1,128)S(1)}, f32[1,3424]{1,0:T(1,128)S(1)}, u32[]{:S(2)}, u32[]{:S(2)}) collective-permute-start(f32[1,3424]{1,0:T(1,128)S(1)} %broadcast_in_dim.29), channel_id=1, source_target_pairs={{0,3},{1,2},{2,1},{3,0},{4,7},{5,6},{6,5},{7,4},{8,11},{9,10},{10,... | collective-permute-start | bytes 41096 | tf_op jit(solution)/shard_map/small/ppermute | solution.py:672
  11.9 57.8 %collective-permute-start.4 = (bf16[384,1280]{1,0:T(8,128)(2,1)}, bf16[384,1280]{1,0:T(8,128)(2,1)S(1)}, u32[]{:S(2)}, u32[]{:S(2)}) collective-permute-start(bf16[384,1280]{1,0:T(8,128)(2,1)} %get-tuple-element.366), channel_id=1, source_target_pairs={{0,1},{1,0},{2,5},{3,4},{4,3},{5,2},{6,7},{7,6},{8,9},{9,8},{10,13... | collective-permute-start | bytes 2949128 | tf_op jit(solution)/shard_map/rows_x/ppermute | solution.py:71
  19.3 52.3 %collective-permute-start.7 = (bf16[384,1280]{1,0:T(8,128)(2,1)S(1)}, bf16[384,1280]{1,0:T(8,128)(2,1)}, u32[]{:S(2)}, u32[]{:S(2)}) collective-permute-start(bf16[384,1280]{1,0:T(8,128)(2,1)S(1)} %get-tuple-element.367), channel_id=1, source_target_pairs={{0,0},{1,1},{2,4},{3,5},{4,2},{5,3},{6,6},{7,7},{8,8},{9,9},{10,12... | collective-permute-start | bytes 2949128 | tf_op jit(solution)/shard_map/rows_x/ppermute | solution.py:71
  25.8 33.3 %collective-permute-start.9 = (bf16[320,640]{1,0:T(8,128)(2,1)S(1)}, bf16[320,640]{1,0:T(8,128)(2,1)S(1)}, u32[]{:S(2)}, u32[]{:S(2)}) collective-permute-start(bf16[320,640]{1,0:T(8,128)(2,1)S(1)} %get-tuple-element.153), channel_id=1, source_target_pairs={{0,1},{1,0},{2,3},{3,2},{4,5},{5,4},{6,7},{7,6},{8,9},{9,8},{10,11... | collective-permute-start | bytes 1228808 | tf_op jit(solution)/shard_map/near/ppermute | solution.py:71
  26.6 41.0 %collective-permute-start.6 = (bf16[320,640]{1,0:T(8,128)(2,1)S(1)}, bf16[320,640]{1,0:T(8,128)(2,1)S(1)}, u32[]{:S(2)}, u32[]{:S(2)}) collective-permute-start(bf16[320,640]{1,0:T(8,128)(2,1)S(1)} %get-tuple-element.381), channel_id=1, source_target_pairs={{0,1},{1,0},{2,3},{3,2},{4,5},{5,4},{6,7},{7,6},{8,9},{9,8},{10,11... | collective-permute-start | bytes 1228808 | tf_op jit(solution)/shard_map/near/ppermute | solution.py:71
  59.1 17.4 %collective-permute-start.14 = (bf16[320,640]{1,0:T(8,128)(2,1)S(1)}, bf16[320,640]{1,0:T(8,128)(2,1)S(1)}, u32[]{:S(2)}, u32[]{:S(2)}) collective-permute-start(bf16[320,640]{1,0:T(8,128)(2,1)S(1)} %get-tuple-element.150), channel_id=1, source_target_pairs={{0,1},{1,0},{2,3},{3,2},{4,5},{5,4},{6,7},{7,6},{8,9},{9,8},{10,11... | collective-permute-start | bytes 1228808 | tf_op jit(solution)/shard_map/near/ppermute | solution.py:71
  59.2 20.4 %collective-permute-start.10 = (bf16[1,1,320,1280]{3,2,1,0:T(8,128)(2,1)S(1)}, bf16[1,1,320,1280]{3,2,1,0:T(8,128)(2,1)S(1)}, u32[]{:S(2)}, u32[]{:S(2)}) collective-permute-start(bf16[1,1,320,1280]{3,2,1,0:T(8,128)(2,1)S(1)} %maximum_bitcast_fusion), channel_id=1, source_target_pairs={{0,8},{8,0},{16,24},{24,16},{1,9},{9,1},{17,25},{25,17},{2,10},{10... | collective-permute-start | bytes 2457608 | tf_op jit(solution)/shard_map/gx/ppermute | solution.py:71
  67.8 19.0 %collective-permute-start.11 = (bf16[1,1,320,1280]{3,2,1,0:T(8,128)(2,1)S(1)}, bf16[1,1,320,1280]{3,2,1,0:T(8,128)(2,1)S(1)}, u32[]{:S(2)}, u32[]{:S(2)}) collective-permute-start(bf16[1,1,320,1280]{3,2,1,0:T(8,128)(2,1)S(1)} %get-tuple-element.400), channel_id=1, source_target_pairs={{0,16},{8,24},{16,0},{24,8},{1,17},{9,25},{17,1},{25,9},{2,18},{10... | collective-permute-start | bytes 2457608 | tf_op jit(solution)/shard_map/gy/ppermute | solution.py:71
  69.7 31.0 %collective-permute-start.13 = (bf16[320,640]{1,0:T(8,128)(2,1)S(1)}, bf16[320,640]{1,0:T(8,128)(2,1)S(1)}, u32[]{:S(2)}, u32[]{:S(2)}) collective-permute-start(bf16[320,640]{1,0:T(8,128)(2,1)S(1)} %get-tuple-element.153), channel_id=1, source_target_pairs={{0,2},{1,3},{2,0},{3,1},{4,6},{5,7},{6,4},{7,5},{8,10},{9,11},{10,... | collective-permute-start | bytes 1228808 | tf_op jit(solution)/shard_map/far/ppermute | solution.py:71
  73.1 33.9 %collective-permute-start.8 = (bf16[768,1280]{1,0:T(8,128)(2,1)S(1)}, bf16[768,1280]{1,0:T(8,128)(2,1)S(1)}, u32[]{:S(2)}, u32[]{:S(2)}) collective-permute-start(bf16[768,1280]{1,0:T(8,128)(2,1)S(1)} %pad_maximum_fusion.10), channel_id=1, source_target_pairs={{0,4},{4,0},{1,5},{5,1},{2,6},{6,2},{3,7},{7,3},{8,12},{12,8},{9,1... | collective-permute-start | bytes 5898248 | tf_op jit(solution)/shard_map/rows_x/ppermute | solution.py:71
  76.5 14.9 %collective-permute-start.16 = (bf16[320,640]{1,0:T(8,128)(2,1)S(1)}, bf16[320,640]{1,0:T(8,128)(2,1)S(1)}, u32[]{:S(2)}, u32[]{:S(2)}) collective-permute-start(bf16[320,640]{1,0:T(8,128)(2,1)S(1)} %get-tuple-element.153), channel_id=1, source_target_pairs={{0,3},{1,2},{2,1},{3,0},{4,7},{5,6},{6,5},{7,4},{8,11},{9,10},{10,... | collective-permute-start | bytes 1228808 | tf_op jit(solution)/shard_map/far/ppermute | solution.py:71
  79.5 21.3 %collective-permute-start.15 = (bf16[1,1,320,1280]{3,2,1,0:T(8,128)(2,1)S(1)}, bf16[1,1,320,1280]{3,2,1,0:T(8,128)(2,1)S(1)}, u32[]{:S(2)}, u32[]{:S(2)}) collective-permute-start(bf16[1,1,320,1280]{3,2,1,0:T(8,128)(2,1)S(1)} %get-tuple-element.151), channel_id=1, source_target_pairs={{0,8},{8,0},{16,24},{24,16},{1,9},{9,1},{17,25},{25,17},{2,10},{10... | collective-permute-start | bytes 2457608 | tf_op jit(solution)/shard_map/gx/ppermute | solution.py:71
  86.8 35.6 %collective-permute-start.12 = (bf16[1,2,320,1280]{3,2,1,0:T(8,128)(2,1)S(1)}, bf16[1,2,320,1280]{3,2,1,0:T(8,128)(2,1)S(1)}, u32[]{:S(2)}, u32[]{:S(2)}) collective-permute-start(bf16[1,2,320,1280]{3,2,1,0:T(8,128)(2,1)S(1)} %pad_maximum_fusion.13), channel_id=1, source_target_pairs={{0,16},{8,24},{16,0},{24,8},{1,17},{9,25},{17,1},{25,9},{2,18},{10... | collective-permute-start | bytes 4915208 | tf_op jit(solution)/shard_map/gy/ppermute | solution.py:71
  100.8 16.9 %collective-permute-start.17 = (bf16[320,1280]{1,0:T(8,128)(2,1)S(1)}, bf16[320,1280]{1,0:T(8,128)(2,1)}, u32[]{:S(2)}, u32[]{:S(2)}) collective-permute-start(bf16[320,1280]{1,0:T(8,128)(2,1)S(1)} %get-tuple-element.155), channel_id=1, source_target_pairs={{1,2},{2,1},{5,6},{6,5},{9,10},{10,9},{13,14},{14,13},{17,18},{18,... | collective-permute-start | bytes 2457608 | tf_op jit(solution)/shard_map/far/ppermute | solution.py:71
  102.3 52.2 %collective-permute-start.19 = (bf16[2,1,320,1280]{3,2,1,0:T(8,128)(2,1)}, bf16[2,1,320,1280]{3,2,1,0:T(8,128)(2,1)}, u32[]{:S(2)}, u32[]{:S(2)}) collective-permute-start(bf16[2,1,320,1280]{3,2,1,0:T(8,128)(2,1)} %pad_maximum_fusion.15), channel_id=1, source_target_pairs={{0,8},{8,0},{16,24},{24,16},{1,9},{9,1},{17,25},{25,17},{2,10},{10... | collective-permute-start | bytes 4915208 | tf_op jit(solution)/shard_map/gx/ppermute | solution.py:71
  122.3 27.6 %collective-permute-start.23 = (bf16[320,1280]{1,0:T(8,128)(2,1)}, bf16[320,1280]{1,0:T(8,128)(2,1)}, u32[]{:S(2)}, u32[]{:S(2)}) collective-permute-start(bf16[320,1280]{1,0:T(8,128)(2,1)} %get-tuple-element.169), channel_id=1, source_target_pairs={{1,2},{2,1},{5,6},{6,5},{9,10},{10,9},{13,14},{14,13},{17,18},{18,... | collective-permute-start | bytes 2457608 | tf_op jit(solution)/shard_map/far/ppermute | solution.py:71
  123.9 26.0 %collective-permute-start.24 = (bf16[320,1280]{1,0:T(8,128)(2,1)}, bf16[320,1280]{1,0:T(8,128)(2,1)}, u32[]{:S(2)}, u32[]{:S(2)}) collective-permute-start(bf16[320,1280]{1,0:T(8,128)(2,1)} %collective-permute-done.17), channel_id=1, source_target_pairs={{1,0},{2,3},{5,4},{6,7},{9,8},{10,11},{13,12},{14,15},{17,16},{18,... | collective-permute-start | bytes 2457608 | tf_op jit(solution)/shard_map/far/ppermute | solution.py:71
  125.4 24.6 %collective-permute-start.18 = (bf16[1,1,320,1280]{3,2,1,0:T(8,128)(2,1)}, bf16[1,1,320,1280]{3,2,1,0:T(8,128)(2,1)}, u32[]{:S(2)}, u32[]{:S(2)}) collective-permute-start(bf16[1,1,320,1280]{3,2,1,0:T(8,128)(2,1)} %maximum_select_fusion), channel_id=1, source_target_pairs={{0,16},{8,24},{16,0},{24,8},{1,17},{9,25},{17,1},{25,9},{2,18},{10... | collective-permute-start | bytes 2457608 | tf_op jit(solution)/shard_map/gy/ppermute | solution.py:71
  150.0 25.4 %collective-permute-start.25 = (bf16[320,1280]{1,0:T(8,128)(2,1)}, bf16[320,1280]{1,0:T(8,128)(2,1)S(1)}, u32[]{:S(2)}, u32[]{:S(2)}) collective-permute-start(bf16[320,1280]{1,0:T(8,128)(2,1)} %collective-permute-done.23), channel_id=1, source_target_pairs={{1,0},{2,3},{5,4},{6,7},{9,8},{10,11},{13,12},{14,15},{17,16},{18,... | collective-permute-start | bytes 2457608 | tf_op jit(solution)/shard_map/far/ppermute | solution.py:71
  151.4 35.5 %collective-permute-start.21 = (bf16[1,2,320,1280]{3,2,1,0:T(8,128)(2,1)S(1)}, bf16[1,2,320,1280]{3,2,1,0:T(8,128)(2,1)S(1)}, u32[]{:S(2)}, u32[]{:S(2)}) collective-permute-start(bf16[1,2,320,1280]{3,2,1,0:T(8,128)(2,1)S(1)} %copy-done.71), channel_id=1, source_target_pairs={{0,16},{8,24},{16,0},{24,8},{1,17},{9,25},{17,1},{25,9},{2,18},{10... | collective-permute-start | bytes 4915208 | tf_op jit(solution)/shard_map/gy/ppermute | solution.py:71
  154.6 34.3 %collective-permute-start.20 = (bf16[2,1,320,1280]{3,2,1,0:T(8,128)(2,1)S(1)}, bf16[2,1,320,1280]{3,2,1,0:T(8,128)(2,1)S(1)}, u32[]{:S(2)}, u32[]{:S(2)}) collective-permute-start(bf16[2,1,320,1280]{3,2,1,0:T(8,128)(2,1)S(1)} %pad_maximum_fusion.14), channel_id=1, source_target_pairs={{0,8},{8,0},{16,24},{24,16},{1,9},{9,1},{17,25},{25,17},{2,10},{10... | collective-permute-start | bytes 4915208 | tf_op jit(solution)/shard_map/gx/ppermute | solution.py:71
  175.4 50.4 %collective-permute-start.29 = (bf16[384,1280]{1,0:T(8,128)(2,1)}, bf16[384,1280]{1,0:T(8,128)(2,1)}, u32[]{:S(2)}, u32[]{:S(2)}) collective-permute-start(bf16[384,1280]{1,0:T(8,128)(2,1)} %get-tuple-element.176), channel_id=1, source_target_pairs={{0,0},{1,1},{2,4},{3,5},{4,2},{5,3},{6,6},{7,7},{8,8},{9,9},{10,12... | collective-permute-start | bytes 2949128 | tf_op jit(solution)/shard_map/rows_g/ppermute | solution.py:71
  184.4 41.4 %collective-permute-start.26 = (bf16[384,1280]{1,0:T(8,128)(2,1)}, bf16[384,1280]{1,0:T(8,128)(2,1)}, u32[]{:S(2)}, u32[]{:S(2)}) collective-permute-start(bf16[384,1280]{1,0:T(8,128)(2,1)} %get-tuple-element.172), channel_id=1, source_target_pairs={{0,1},{1,0},{2,5},{3,4},{4,3},{5,2},{6,7},{7,6},{8,9},{9,8},{10,13... | collective-permute-start | bytes 2949128 | tf_op jit(solution)/shard_map/rows_g/ppermute | solution.py:71
  186.9 38.9 %collective-permute-start.28 = (bf16[1,1,320,1280]{3,2,1,0:T(8,128)(2,1)}, bf16[1,1,320,1280]{3,2,1,0:T(8,128)(2,1)}, u32[]{:S(2)}, u32[]{:S(2)}) collective-permute-start(bf16[1,1,320,1280]{3,2,1,0:T(8,128)(2,1)} %select_bitcast_fusion.8), channel_id=1, source_target_pairs={{0,16},{8,24},{16,0},{24,8},{1,17},{9,25},{17,1},{25,9},{2,18},{10... | collective-permute-start | bytes 2457608 | tf_op jit(solution)/shard_map/gy/ppermute | solution.py:71
  193.2 32.6 %collective-permute-start.27 = (bf16[1,1,320,1280]{3,2,1,0:T(8,128)(2,1)}, bf16[1,1,320,1280]{3,2,1,0:T(8,128)(2,1)}, u32[]{:S(2)}, u32[]{:S(2)}) collective-permute-start(bf16[1,1,320,1280]{3,2,1,0:T(8,128)(2,1)} %select_bitcast_fusion.9), channel_id=1, source_target_pairs={{0,8},{8,0},{16,24},{24,16},{1,9},{9,1},{17,25},{25,17},{2,10},{10... | collective-permute-start | bytes 2457608 | tf_op jit(solution)/shard_map/gx/ppermute | solution.py:71
  223.6 22.7 %collective-permute-start.22 = (bf16[1536,1280]{1,0:T(8,128)(2,1)}, bf16[1536,1280]{1,0:T(8,128)(2,1)}, u32[]{:S(2)}, u32[]{:S(2)}) collective-permute-start(bf16[1536,1280]{1,0:T(8,128)(2,1)} %out_product.1.refs_1_), channel_id=1, source_target_pairs={{0,4},{4,0},{1,5},{5,1},{2,6},{6,2},{3,7},{7,3},{8,12},{12,8},{9,1... | collective-permute-start | bytes 11796488 | tf_op jit(solution)/shard_map/ppermute | solution.py:71
  228.7 10.1 %collective-permute-start.30 = (bf16[768,1280]{1,0:T(8,128)(2,1)S(1)}, bf16[768,1280]{1,0:T(8,128)(2,1)S(1)}, u32[]{:S(2)}, u32[]{:S(2)}) collective-permute-start(bf16[768,1280]{1,0:T(8,128)(2,1)S(1)} %pad_maximum_fusion.11), channel_id=1, source_target_pairs={{0,4},{4,0},{1,5},{5,1},{2,6},{6,2},{3,7},{7,3},{8,12},{12,8},{9,1... | collective-permute-start | bytes 5898248 | tf_op jit(solution)/shard_map/rows_g/ppermute | solution.py:71
  231.6 44.3 %collective-permute-start.31 = (bf16[1,2,320,1280]{3,2,1,0:T(8,128)(2,1)}, bf16[1,2,320,1280]{3,2,1,0:T(8,128)(2,1)}, u32[]{:S(2)}, u32[]{:S(2)}) collective-permute-start(bf16[1,2,320,1280]{3,2,1,0:T(8,128)(2,1)} %pad_maximum_fusion.17), channel_id=1, source_target_pairs={{0,16},{8,24},{16,0},{24,8},{1,17},{9,25},{17,1},{25,9},{2,18},{10... | collective-permute-start | bytes 4915208 | tf_op jit(solution)/shard_map/gy/ppermute | solution.py:71
  237.8 62.5 %collective-permute-start.32 = (bf16[2,1,320,1280]{3,2,1,0:T(8,128)(2,1)}, bf16[2,1,320,1280]{3,2,1,0:T(8,128)(2,1)}, u32[]{:S(2)}, u32[]{:S(2)}) collective-permute-start(bf16[2,1,320,1280]{3,2,1,0:T(8,128)(2,1)} %pad_maximum_fusion.18), channel_id=1, source_target_pairs={{0,8},{8,0},{16,24},{24,16},{1,9},{9,1},{17,25},{25,17},{2,10},{10... | collective-permute-start | bytes 4915208 | tf_op jit(solution)/shard_map/gx/ppermute | solution.py:71
  300.3 52.4 %collective-permute-start.34 = (bf16[1,2,320,1280]{3,2,1,0:T(8,128)(2,1)}, bf16[1,2,320,1280]{3,2,1,0:T(8,128)(2,1)}, u32[]{:S(2)}, u32[]{:S(2)}) collective-permute-start(bf16[1,2,320,1280]{3,2,1,0:T(8,128)(2,1)} %constant_dynamic-slice_fusion.5), channel_id=1, source_target_pairs={{0,16},{8,24},{16,0},{24,8},{1,17},{9,25},{17,1},{25,9},{2,18},{10... | collective-permute-start | bytes 4915208 | tf_op jit(solution)/shard_map/sd/ppermute | solution.py:71
  303.4 49.4 %collective-permute-start.33 = (bf16[2,1,320,1280]{3,2,1,0:T(8,128)(2,1)}, bf16[2,1,320,1280]{3,2,1,0:T(8,128)(2,1)}, u32[]{:S(2)}, u32[]{:S(2)}) collective-permute-start(bf16[2,1,320,1280]{3,2,1,0:T(8,128)(2,1)} %constant_dynamic-slice_fusion.6), channel_id=1, source_target_pairs={{0,8},{8,0},{16,24},{24,16},{1,9},{9,1},{17,25},{25,17},{2,10},{10... | collective-permute-start | bytes 4915208 | tf_op jit(solution)/shard_map/sd/ppermute | solution.py:71
  367.9 17.7 %collective-permute-start.36 = (bf16[1536,1280]{1,0:T(8,128)(2,1)}, bf16[1536,1280]{1,0:T(8,128)(2,1)}, u32[]{:S(2)}, u32[]{:S(2)}) collective-permute-start(bf16[1536,1280]{1,0:T(8,128)(2,1)} %down_product.1.refs_1_), channel_id=1, source_target_pairs={{0,4},{4,0},{1,5},{5,1},{2,6},{6,2},{3,7},{7,3},{8,12},{12,8},{9,1... | collective-permute-start | bytes 11796488 | tf_op jit(solution)/shard_map/ppermute | solution.py:71
  367.9 17.7 %collective-permute-start.35 = (bf16[1536,1280]{1,0:T(8,128)(2,1)}, bf16[1536,1280]{1,0:T(8,128)(2,1)}, u32[]{:S(2)}, u32[]{:S(2)}) collective-permute-start(bf16[1536,1280]{1,0:T(8,128)(2,1)} %get-tuple-element.196.p_ref), channel_id=1, source_target_pairs={{0,4},{4,0},{1,5},{5,1},{2,6},{6,2},{3,7},{7,3},{8,12},{12,8},{9,1... | collective-permute-start | bytes 11796488 | tf_op jit(solution)/shard_map/ppermute | solution.py:71
  370.0 31.1 %collective-permute-start.38 = (bf16[1,1,320,1280]{3,2,1,0:T(8,128)(2,1)S(1)}, bf16[1,1,320,1280]{3,2,1,0:T(8,128)(2,1)S(1)}, u32[]{:S(2)}, u32[]{:S(2)}) collective-permute-start(bf16[1,1,320,1280]{3,2,1,0:T(8,128)(2,1)S(1)} %add_convert_fusion.7), channel_id=1, source_target_pairs={{0,8},{8,0},{16,24},{24,16},{1,9},{9,1},{17,25},{25,17},{2,10},{10... | collective-permute-start | bytes 2457608 | tf_op jit(solution)/shard_map/sd/ppermute | solution.py:71
  372.8 28.4 %collective-permute-start.37 = (bf16[1,1,320,1280]{3,2,1,0:T(8,128)(2,1)S(1)}, bf16[1,1,320,1280]{3,2,1,0:T(8,128)(2,1)S(1)}, u32[]{:S(2)}, u32[]{:S(2)}) collective-permute-start(bf16[1,1,320,1280]{3,2,1,0:T(8,128)(2,1)S(1)} %add_convert_fusion.8), channel_id=1, source_target_pairs={{0,16},{8,24},{16,0},{24,8},{1,17},{9,25},{17,1},{25,9},{2,18},{10... | collective-permute-start | bytes 2457608 | tf_op jit(solution)/shard_map/sd/ppermute | solution.py:71
  401.1 61.7 %collective-permute-start.45 = (bf16[1,2,320,1280]{3,2,1,0:T(8,128)(2,1)}, bf16[1,2,320,1280]{3,2,1,0:T(8,128)(2,1)}, u32[]{:S(2)}, u32[]{:S(2)}) collective-permute-start(bf16[1,2,320,1280]{3,2,1,0:T(8,128)(2,1)} %constant_dynamic-slice_fusion.3), channel_id=1, source_target_pairs={{0,16},{8,24},{16,0},{24,8},{1,17},{9,25},{17,1},{25,9},{2,18},{10... | collective-permute-start | bytes 4915208 | tf_op jit(solution)/shard_map/su/ppermute | solution.py:71
  402.4 63.9 %collective-permute-start.44 = (bf16[2,1,320,1280]{3,2,1,0:T(8,128)(2,1)}, bf16[2,1,320,1280]{3,2,1,0:T(8,128)(2,1)}, u32[]{:S(2)}, u32[]{:S(2)}) collective-permute-start(bf16[2,1,320,1280]{3,2,1,0:T(8,128)(2,1)} %constant_dynamic-slice_fusion.4), channel_id=1, source_target_pairs={{0,8},{8,0},{16,24},{24,16},{1,9},{9,1},{17,25},{25,17},{2,10},{10... | collective-permute-start | bytes 4915208 | tf_op jit(solution)/shard_map/su/ppermute | solution.py:71
  405.9 51.5 %collective-permute-start.41 = (bf16[320,640]{1,0:T(8,128)(2,1)}, bf16[320,640]{1,0:T(8,128)(2,1)}, u32[]{:S(2)}, u32[]{:S(2)}) collective-permute-start(bf16[320,640]{1,0:T(8,128)(2,1)} %slice.472), channel_id=1, source_target_pairs={{0,1},{1,0},{2,3},{3,2},{4,5},{5,4},{6,7},{7,6},{8,9},{9,8},{10,11... | collective-permute-start | bytes 1228808 | tf_op jit(solution)/shard_map/sd/ppermute | solution.py:71
  417.3 40.2 %collective-permute-start.39 = (bf16[320,640]{1,0:T(8,128)(2,1)}, bf16[320,640]{1,0:T(8,128)(2,1)}, u32[]{:S(2)}, u32[]{:S(2)}) collective-permute-start(bf16[320,640]{1,0:T(8,128)(2,1)} %get-tuple-element.396), channel_id=1, source_target_pairs={{0,2},{1,3},{2,0},{3,1},{4,6},{5,7},{6,4},{7,5},{8,10},{9,11},{10,... | collective-permute-start | bytes 1228808 | tf_op jit(solution)/shard_map/sd/ppermute | solution.py:71
  418.5 39.0 %collective-permute-start.40 = (bf16[320,640]{1,0:T(8,128)(2,1)}, bf16[320,640]{1,0:T(8,128)(2,1)}, u32[]{:S(2)}, u32[]{:S(2)}) collective-permute-start(bf16[320,640]{1,0:T(8,128)(2,1)} %get-tuple-element.395), channel_id=1, source_target_pairs={{0,3},{1,2},{2,1},{3,0},{4,7},{5,6},{6,5},{7,4},{8,11},{9,10},{10,... | collective-permute-start | bytes 1228808 | tf_op jit(solution)/shard_map/sd/ppermute | solution.py:71
  460.4 40.3 %collective-permute-start.42 = (bf16[384,1280]{1,0:T(8,128)(2,1)S(1)}, bf16[384,1280]{1,0:T(8,128)(2,1)}, u32[]{:S(2)}, u32[]{:S(2)}) collective-permute-start(bf16[384,1280]{1,0:T(8,128)(2,1)S(1)} %get-tuple-element.330), channel_id=1, source_target_pairs={{1,0},{0,1},{5,2},{4,3},{3,4},{2,5},{7,6},{6,7},{9,8},{8,9},{13,10... | collective-permute-start | bytes 2949128 | tf_op jit(solution)/shard_map/rows_out/ppermute | solution.py:191
  461.3 39.4 %collective-permute-start.43 = (bf16[384,1280]{1,0:T(8,128)(2,1)S(1)}, bf16[384,1280]{1,0:T(8,128)(2,1)}, u32[]{:S(2)}, u32[]{:S(2)}) collective-permute-start(bf16[384,1280]{1,0:T(8,128)(2,1)S(1)} %get-tuple-element.331), channel_id=1, source_target_pairs={{0,0},{1,1},{4,2},{5,3},{2,4},{3,5},{6,6},{7,7},{8,8},{9,9},{12,10... | collective-permute-start | bytes 2949128 | tf_op jit(solution)/shard_map/rows_out/ppermute | solution.py:191
  465.4 22.1 %collective-permute-start.47 = (bf16[1,1,320,1280]{3,2,1,0:T(8,128)(2,1)}, bf16[1,1,320,1280]{3,2,1,0:T(8,128)(2,1)}, u32[]{:S(2)}, u32[]{:S(2)}) collective-permute-start(bf16[1,1,320,1280]{3,2,1,0:T(8,128)(2,1)} %add_convert_fusion.4), channel_id=1, source_target_pairs={{0,8},{8,0},{16,24},{24,16},{1,9},{9,1},{17,25},{25,17},{2,10},{10... | collective-permute-start | bytes 2457608 | tf_op jit(solution)/shard_map/su/ppermute | solution.py:71
  468.5 20.7 %collective-permute-start.46 = (bf16[1,1,320,1280]{3,2,1,0:T(8,128)(2,1)}, bf16[1,1,320,1280]{3,2,1,0:T(8,128)(2,1)}, u32[]{:S(2)}, u32[]{:S(2)}) collective-permute-start(bf16[1,1,320,1280]{3,2,1,0:T(8,128)(2,1)} %add_convert_fusion.5), channel_id=1, source_target_pairs={{0,16},{8,24},{16,0},{24,8},{1,17},{9,25},{17,1},{25,9},{2,18},{10... | collective-permute-start | bytes 2457608 | tf_op jit(solution)/shard_map/su/ppermute | solution.py:71
  500.6 36.3 %collective-permute-start.48 = (bf16[1536,1280]{1,0:T(8,128)(2,1)}, bf16[1536,1280]{1,0:T(8,128)(2,1)}, u32[]{:S(2)}, u32[]{:S(2)}) collective-permute-start(bf16[1536,1280]{1,0:T(8,128)(2,1)} %qkv_back.1.refs_0_), channel_id=1, source_target_pairs={{0,4},{4,0},{1,5},{5,1},{2,6},{6,2},{3,7},{7,3},{8,12},{12,8},{9,1... | collective-permute-start | bytes 11796488 | tf_op jit(solution)/shard_map/ppermute | solution.py:71
  522.5 38.0 %collective-permute-start.53 = (bf16[2,1,320,1280]{3,2,1,0:T(8,128)(2,1)}, bf16[2,1,320,1280]{3,2,1,0:T(8,128)(2,1)}, u32[]{:S(2)}, u32[]{:S(2)}) collective-permute-start(bf16[2,1,320,1280]{3,2,1,0:T(8,128)(2,1)} %constant_dynamic-slice_fusion), channel_id=1, source_target_pairs={{0,8},{8,0},{16,24},{24,16},{1,9},{9,1},{17,25},{25,17},{2,10},{10... | collective-permute-start | bytes 4915208 | tf_op jit(solution)/shard_map/sq/ppermute | solution.py:71
  526.1 37.9 %collective-permute-start.51 = (bf16[1,2,320,1280]{3,2,1,0:T(8,128)(2,1)}, bf16[1,2,320,1280]{3,2,1,0:T(8,128)(2,1)}, u32[]{:S(2)}, u32[]{:S(2)}) collective-permute-start(bf16[1,2,320,1280]{3,2,1,0:T(8,128)(2,1)} %constant_dynamic-slice_fusion.2), channel_id=1, source_target_pairs={{0,16},{8,24},{16,0},{24,8},{1,17},{9,25},{17,1},{25,9},{2,18},{10... | collective-permute-start | bytes 4915208 | tf_op jit(solution)/shard_map/sq/ppermute | solution.py:71
  534.4 61.8 %collective-permute-start.59 = (bf16[320,640]{1,0:T(8,128)(2,1)}, bf16[320,640]{1,0:T(8,128)(2,1)}, u32[]{:S(2)}, u32[]{:S(2)}) collective-permute-start(bf16[320,640]{1,0:T(8,128)(2,1)} %get-tuple-element.391), channel_id=1, source_target_pairs={{0,2},{1,3},{2,0},{3,1},{4,6},{5,7},{6,4},{7,5},{8,10},{9,11},{10,... | collective-permute-start | bytes 1228808 | tf_op jit(solution)/shard_map/su/ppermute | solution.py:71
  534.4 65.0 %collective-permute-start.60 = (bf16[320,640]{1,0:T(8,128)(2,1)}, bf16[320,640]{1,0:T(8,128)(2,1)}, u32[]{:S(2)}, u32[]{:S(2)}) collective-permute-start(bf16[320,640]{1,0:T(8,128)(2,1)} %get-tuple-element.392), channel_id=1, source_target_pairs={{0,3},{1,2},{2,1},{3,0},{4,7},{5,6},{6,5},{7,4},{8,11},{9,10},{10,... | collective-permute-start | bytes 1228808 | tf_op jit(solution)/shard_map/su/ppermute | solution.py:71
  562.7 19.6 %collective-permute-start.54 = (bf16[1,1,320,1280]{3,2,1,0:T(8,128)(2,1)}, bf16[1,1,320,1280]{3,2,1,0:T(8,128)(2,1)}, u32[]{:S(2)}, u32[]{:S(2)}) collective-permute-start(bf16[1,1,320,1280]{3,2,1,0:T(8,128)(2,1)} %add_convert_fusion.2), channel_id=1, source_target_pairs={{0,16},{8,24},{16,0},{24,8},{1,17},{9,25},{17,1},{25,9},{2,18},{10... | collective-permute-start | bytes 2457608 | tf_op jit(solution)/shard_map/sq/ppermute | solution.py:71
  566.4 19.4 %collective-permute-start.52 = (bf16[1,1,320,1280]{3,2,1,0:T(8,128)(2,1)}, bf16[1,1,320,1280]{3,2,1,0:T(8,128)(2,1)}, u32[]{:S(2)}, u32[]{:S(2)}) collective-permute-start(bf16[1,1,320,1280]{3,2,1,0:T(8,128)(2,1)} %add_convert_fusion.3), channel_id=1, source_target_pairs={{0,8},{8,0},{16,24},{24,16},{1,9},{9,1},{17,25},{25,17},{2,10},{10... | collective-permute-start | bytes 2457608 | tf_op jit(solution)/shard_map/sq/ppermute | solution.py:71
  570.2 29.3 %collective-permute-start.61 = (bf16[320,640]{1,0:T(8,128)(2,1)}, bf16[320,640]{1,0:T(8,128)(2,1)}, u32[]{:S(2)}, u32[]{:S(2)}) collective-permute-start(bf16[320,640]{1,0:T(8,128)(2,1)} %slice.470), channel_id=1, source_target_pairs={{0,1},{1,0},{2,3},{3,2},{4,5},{5,4},{6,7},{7,6},{8,9},{9,8},{10,11... | collective-permute-start | bytes 1228808 | tf_op jit(solution)/shard_map/su/ppermute | solution.py:71
  582.4 25.9 %collective-permute-start.49 = (bf16[384,1280]{1,0:T(8,128)(2,1)}, bf16[384,1280]{1,0:T(8,128)(2,1)}, u32[]{:S(2)}, u32[]{:S(2)}) collective-permute-start(bf16[384,1280]{1,0:T(8,128)(2,1)} %get-tuple-element.328), channel_id=1, source_target_pairs={{1,0},{0,1},{5,2},{4,3},{3,4},{2,5},{7,6},{6,7},{9,8},{8,9},{13,10... | collective-permute-start | bytes 2949128 | tf_op jit(solution)/shard_map/rows_dx/ppermute | solution.py:191
  585.8 22.5 %collective-permute-start.50 = (bf16[384,1280]{1,0:T(8,128)(2,1)}, bf16[384,1280]{1,0:T(8,128)(2,1)}, u32[]{:S(2)}, u32[]{:S(2)}) collective-permute-start(bf16[384,1280]{1,0:T(8,128)(2,1)} %get-tuple-element.329), channel_id=1, source_target_pairs={{0,0},{1,1},{4,2},{5,3},{2,4},{3,5},{6,6},{7,7},{8,8},{9,9},{12,10... | collective-permute-start | bytes 2949128 | tf_op jit(solution)/shard_map/rows_dx/ppermute | solution.py:191
  604.4 30.7 %collective-permute-start.66 = (f32[13,1280]{1,0:T(8,128)S(1)}, f32[13,1280]{1,0:T(8,128)S(1)}, u32[]{:S(2)}, u32[]{:S(2)}) collective-permute-start(f32[13,1280]{1,0:T(8,128)S(1)} %add.444), channel_id=1, source_target_pairs={{0,16},{8,24},{16,0},{24,8},{1,17},{9,25},{17,1},{25,9},{2,18},{10... | collective-permute-start | bytes 199688 | tf_op jit(solution)/shard_map/vectors/ppermute | solution.py:71
  608.3 66.2 %collective-permute-start.63 = (bf16[160,640]{1,0:T(8,128)(2,1)S(1)}, bf16[160,640]{1,0:T(8,128)(2,1)S(1)}, u32[]{:S(2)}, u32[]{:S(2)}) collective-permute-start(bf16[160,640]{1,0:T(8,128)(2,1)S(1)} %select_convert_fusion), channel_id=1, source_target_pairs={{0,4},{4,0},{1,5},{5,1},{2,6},{6,2},{3,7},{7,3},{8,12},{12,8},{9,1... | collective-permute-start | bytes 614408 | tf_op jit(solution)/shard_map/sd/ppermute | solution.py:71
  627.8 50.4 %collective-permute-start.62 = (bf16[160,640]{1,0:T(8,128)(2,1)}, bf16[160,640]{1,0:T(8,128)(2,1)}, u32[]{:S(2)}, u32[]{:S(2)}) collective-permute-start(bf16[160,640]{1,0:T(8,128)(2,1)} %select_convert_fusion.1), channel_id=1, source_target_pairs={{0,4},{4,0},{1,5},{5,1},{2,6},{6,2},{3,7},{7,3},{8,12},{12,8},{9,1... | collective-permute-start | bytes 614408 | tf_op jit(solution)/shard_map/su/ppermute | solution.py:71
  630.4 56.3 %collective-permute-start.55 = (bf16[320,640]{1,0:T(8,128)(2,1)}, bf16[320,640]{1,0:T(8,128)(2,1)}, u32[]{:S(2)}, u32[]{:S(2)}) collective-permute-start(bf16[320,640]{1,0:T(8,128)(2,1)} %get-tuple-element.393), channel_id=1, source_target_pairs={{0,2},{1,3},{2,0},{3,1},{4,6},{5,7},{6,4},{7,5},{8,10},{9,11},{10,... | collective-permute-start | bytes 1228808 | tf_op jit(solution)/shard_map/sq/ppermute | solution.py:71
  630.7 56.1 %collective-permute-start.56 = (bf16[320,640]{1,0:T(8,128)(2,1)}, bf16[320,640]{1,0:T(8,128)(2,1)}, u32[]{:S(2)}, u32[]{:S(2)}) collective-permute-start(bf16[320,640]{1,0:T(8,128)(2,1)} %get-tuple-element.394), channel_id=1, source_target_pairs={{0,3},{1,2},{2,1},{3,0},{4,7},{5,6},{6,5},{7,4},{8,11},{9,10},{10,... | collective-permute-start | bytes 1228808 | tf_op jit(solution)/shard_map/sq/ppermute | solution.py:71
  635.1 15.8 %collective-permute-start.67 = (f32[13,1280]{1,0:T(8,128)S(1)}, f32[13,1280]{1,0:T(8,128)S(1)}, u32[]{:S(2)}, u32[]{:S(2)}) collective-permute-start(f32[13,1280]{1,0:T(8,128)S(1)} %add.445), channel_id=1, source_target_pairs={{0,1},{1,0},{2,3},{3,2},{4,5},{5,4},{6,7},{7,6},{8,9},{9,8},{10,11... | collective-permute-start | bytes 199688 | tf_op jit(solution)/shard_map/vectors/ppermute | solution.py:243
  650.9 22.3 %collective-permute-start.68 = (f32[13,1280]{1,0:T(8,128)S(1)}, f32[13,1280]{1,0:T(8,128)S(1)}, u32[]{:S(2)}, u32[]{:S(2)}) collective-permute-start(f32[13,1280]{1,0:T(8,128)S(1)} %add.446), channel_id=1, source_target_pairs={{0,2},{1,3},{2,0},{3,1},{4,6},{5,7},{6,4},{7,5},{8,10},{9,11},{10,... | collective-permute-start | bytes 199688 | tf_op jit(solution)/shard_map/vectors/ppermute | solution.py:243
  673.2 13.6 %collective-permute-start.57 = (bf16[320,640]{1,0:T(8,128)(2,1)}, bf16[320,640]{1,0:T(8,128)(2,1)}, u32[]{:S(2)}, u32[]{:S(2)}) collective-permute-start(bf16[320,640]{1,0:T(8,128)(2,1)} %slice.471), channel_id=1, source_target_pairs={{0,1},{1,0},{2,3},{3,2},{4,5},{5,4},{6,7},{7,6},{8,9},{9,8},{10,11... | collective-permute-start | bytes 1228808 | tf_op jit(solution)/shard_map/sq/ppermute | solution.py:71
  (98 other events, 1210.9 us)

commit v3 on v2

--- a/solution.py
+++ b/solution.py
@@ -57,12 +57,6 @@
     return (weight - rate * (ratio + decay * weight), first_new, second_new)
 
 
-NEAR = [(0, 1), (1, 0), (2, 3), (3, 2)]
-MIDS = [(1, 2), (2, 1)]
-OUTER = [(1, 0), (2, 3)]
-INNER = [(0, 1), (3, 2)]
-
-
 def after(value, *earlier):
     return lax.optimization_barrier((value, *earlier))[0]
 
@@ -139,6 +133,7 @@
         mine = (self.g >> bit) & 1
         sent = self.total(self.sliced(1 - mine, axis)).astype(BF)
         self.kept = self.sliced(mine, axis)
+        self.sent = sent
         self.got = swap_bit(sent, bit, self.count, *earlier)
         return self.got
 
@@ -157,40 +152,44 @@
     for c in range(2):
         for z in range(4):
             moves.append((c * 4 + z, (z >> 1) * 4 + 2 * c + ((z & 1) ^ step)))
-    return moves
+    return [(a, b) for a, b in moves if a != b]
 
 
 class RowsIn:
-    def __init__(self, local, z):
-        self.local, self.odd = local, (z & 1) == 1
+    def __init__(self, local, c, z):
+        self.local, self.odd, self.stays = local, (z & 1) == 1, (z >> 1) == c
         self.pieces = []
 
     def send(self, *earlier):
         step = len(self.pieces)
         sent = jnp.where(self.odd, self.local[1 - step], self.local[step])
         self.sent = sent
+        self.first = sent if step == 0 else self.first
         self.pieces.append(move(sent, ("c", "z"), row_moves(step), *earlier))
         return self.pieces[-1]
 
     def half(self, *earlier):
         first, second = [after(v, *earlier) if earlier else v for v in self.pieces]
+        first = jnp.where(self.stays, self.first, first)
         return jnp.concatenate(
             [jnp.where(self.odd, second, first), jnp.where(self.odd, first, second)], axis=0
         )
 
 
-def rows_out(turned, start, c, z):
+def rows_out(turned, start, c, z, chained=False):
     rows, width = turned.shape
     part = rows // 4
     odd = z & 1
     longer = jnp.concatenate([turned, turned[:part]], axis=0)
-    pieces = []
+    pieces, sents = [], []
     for step in range(2):
         first = lax.rem((2 * c + (odd ^ step)) * part - start + rows, rows)
         sent = lax.dynamic_slice(longer, (first, 0), (part, width))
-        pieces.append(lax.ppermute(sent, ("c", "z"), [(b, a) for a, b in row_moves(step)]))
-    first, second = pieces
-    return jnp.stack([jnp.where(odd == 1, second, first), jnp.where(odd == 1, first, second)]), pieces
+        sents.append(sent)
+        back = [(b, a) for a, b in row_moves(step)]
+        pieces.append(move(sent, ("c", "z"), back, *(pieces if chained else [])))
+    first, second = jnp.where((z >> 1) == c, sents[0], pieces[0]), pieces[1]
+    return jnp.stack([jnp.where(odd == 1, second, first), jnp.where(odd == 1, first, second)]), pieces, sents
 
 
 def turn_rows(start, upper, lower, vectors=None):
@@ -235,10 +234,11 @@
     )(start[None], upper, lower, *extra)
 
 
-def add_up(value, count):
-    value = value + swap_core(value)
+def add_up(value, count, first, then):
+    value = value + swap_core(value, *first)
     for bit in range(count.bit_length() - 1):
         value = value + swap_bit(value, bit, count)
+    value = after(value, *then)
     for distance in (1, 2):
         value = value + lax.ppermute(value, "z", [(i, i ^ distance) for i in range(4)])
     return value
@@ -653,7 +653,6 @@
     count = lax.axis_size("g")
     bits = count.bit_length() - 1
     g, c, z = lax.axis_index("g"), lax.axis_index("c"), lax.axis_index("z")
-    is_mid = (z == 1) | (z == 2)
     low_core = c == 0
     d_local = qkv_weight.shape[0]
     width = tokens_in.shape[2]
@@ -673,14 +672,14 @@
         relative = jnp.concatenate([small] + smalls, axis=0)
         biases = relative[:, :1120]
         bias_near = biases[:2]
-        bias_far = jnp.where(is_mid, biases[2:][::-1], biases[2:])
+        bias_far = biases[2:]
         counted = relative[:, 1120:].reshape(4, 3, 2, part_rows)
         counted = jnp.where((z & 1) == 0, counted[:, :, 0], counted[:, :, 1])
         counted = jnp.concatenate([lax.dynamic_slice_in_dim(counted, k ^ z, 1, 0) for k in range(4)], axis=0)
         counted = jnp.where((z >> 1) == c, counted, swap_core(counted))
         counted = jnp.moveaxis(counted, 1, 0).reshape(3, 4 * part_rows)
 
-    rows_x, rows_g = RowsIn(tokens_in, z), RowsIn(cotangent, z)
+    rows_x, rows_g = RowsIn(tokens_in, c, z), RowsIn(cotangent, c, z)
     with jax.named_scope("rows_x"):
         r0, r1 = rows_x.send(), rows_x.send()
 
@@ -709,9 +708,6 @@
     def far_of(two, three):
         return jnp.where(is_mid, pair(three, two), pair(two, three))
 
-    def far_of(mid, end):
-        return jnp.where(is_mid, mid, end)
-
     start = jnp.sum((counted[0] == 1).astype(jnp.int32))
 
     def halves_of(rows_half, *earlier):
@@ -720,13 +716,13 @@
         return jnp.where(low_core, own, other), jnp.where(low_core, other, own)
 
     with jax.named_scope("near"):
-        near_q = along(shard_q, 1)
-        near_u = along(shard_u, 1)
-        near_d = along(shard_d, 1, near_q)
+        near_q = pair(shard_q, along(shard_q, 1))
+        near_u = pair(shard_u, along(shard_u, 1))
+        near_d = pair(shard_d, along(shard_d, 1, near_q))
     with jax.named_scope("far"):
-        two_q = along(shard_q, 2, near_u)
-        three_q = along(shard_q, 3, near_d)
-    qa, ua, da = gather(pair(shard_q, near_q), forth), gather(pair(shard_u, near_u), back), gather(pair(shard_d, near_d), forth)
+        far_q = along(near_q, 2)
+        far_u = along(near_u, 2)
+    qa, ua, da = gather(near_q, forth), gather(near_u, back), gather(near_d, forth)
     with jax.named_scope("gx"):
         qax = qa.step()
         dax = da.step(qax)
@@ -735,21 +731,20 @@
         qay = qa.finish(uay)
     with jax.named_scope("gx"):
         uax = ua.finish(dax)
-    two_q, three_q = after(two_q, dax, qax, uay), after(three_q, dax, qax, uay)
-    qb = gather(jnp.where(is_mid, pair(three_q, two_q), pair(two_q, three_q)), back)
     with jax.named_scope("rows_x"):
-        source, a_one = turn_rows(start, *halves_of(rows_x, near_u), norm_vectors)
+        source, a_one = turn_rows(start, *halves_of(rows_x, near_d), norm_vectors)
     qa.take(a_one)
-    with jax.named_scope("far"):
-        mid_u = move(pair(shard_u, near_u), "z", MIDS, two_q, three_q, dax, uay)
-        end_u = move(mid_u, "z", OUTER, qay)
-        mid_d = move(pair(shard_d, near_d), "z", MIDS, mid_u, qay)
+    qb = gather(after(far_q, a_one), back)
     with jax.named_scope("gy"):
         qby = qb.step(qay)
+    with jax.named_scope("far"):
+        far_d = along(near_d, 2, qay, uax)
+    with jax.named_scope("gx"):
+        qbx = qb.finish(uax)
+    with jax.named_scope("gy"):
+        day = da.finish(qby)
 
     first_wa = qa.whole()
-
-    rows = source.shape[0]
     counted = jnp.roll(counted, -start, axis=1)
     ids = counted[0, MIDDLE:]
     mask = jnp.where(ids[:, None] == ids[None, :], 0.0, -1e30).astype(F32)
@@ -757,32 +752,27 @@
     inverse = jnp.power(10000.0, -powers)
     angles = jnp.concatenate([inverse[:, None] * counted[1][None], inverse[:, None] * counted[2][None]], axis=0)
     cosine, sine = jnp.cos(angles), jnp.sin(angles)
+    rows = source.shape[0]
 
     def qkv_bias(pair):
         zero = jnp.zeros((160,), F32)
         return jnp.concatenate([pair[0, :480], zero, pair[1, :480], zero])
 
-    mixed = dot(after(first_wa, mid_u), a_one, 0, 1) + qkv_bias(bias_near)[:, None]
+    mixed = dot(after(first_wa, qby), a_one, 0, 1) + qkv_bias(bias_near)[:, None]
     saved = [attend(mixed, cosine, sine, mask)]
     done = saved[0][3]
     qb.take(done)
-    ua.take(done)
-    with jax.named_scope("far"):
-        end_d = move(mid_d, "z", OUTER, end_u, qby, done)
-    with jax.named_scope("gx"):
-        qbx = qb.finish(uax)
-    with jax.named_scope("gy"):
-        day = da.finish(qby)
+    ub = gather(after(far_u, done), forth)
     with jax.named_scope("rows_g"):
-        rows_g.send(end_d, qby)
-        rows_g.send(end_d, qby)
-    ub, db = gather(far_of(mid_u, end_u), forth), gather(far_of(mid_d, end_d), back)
+        rows_g.send(far_u, done)
+        rows_g.send(far_u, done)
     with jax.named_scope("gx"):
         ubx = ub.step(qbx)
+    db = gather(after(far_d, done, qbx), back)
     with jax.named_scope("gy"):
         dby = db.step(day)
     first_wb = qb.whole()
-    mixed = dot(after(first_wb, day), a_one, 0, 1) + qkv_bias(bias_far)[:, None]
+    mixed = dot(after(first_wb, day, far_d), a_one, 0, 1) + qkv_bias(bias_far)[:, None]
     saved.append(attend(mixed, cosine, sine, mask))
     done = saved[1][3]
     ub.take(done)
@@ -805,7 +795,7 @@
     same = lambda total: (total,)
     (branch,) = product(
         "out_product",
-        [(saved[0][3], 0, out_wa, 1), (saved[1][3], 0, out_wb, 1)],
+        [(saved[0][3], 0, out_wa, 1), (after(saved[1][3], ubx, dby), 0, out_wb, 1)],
         [(width, BF)],
         same,
     )
@@ -846,20 +836,17 @@
 
     class SumZ:
         def __init__(self, near, far, *earlier):
-            low_part, high_part = far[:, :inner].astype(BF), far[:, inner:].astype(BF)
-            two, three = jnp.where(is_mid, high_part, low_part), jnp.where(is_mid, low_part, high_part)
-            self.own = near[:, :inner]
-            self.moved = [
-                along(value, distance, *earlier)
-                for distance, value in ((2, two), (3, three), (1, near[:, inner:].astype(BF)))
-            ]
-
-        def take(self, *earlier):
-            for value in self.moved:
-                self.own = self.own + (after(value, *earlier) if earlier else value).astype(F32)
+            self.near = pair(near[:, :inner], far[:, :inner])
+            self.moved = along(pair(near[:, inner:], far[:, inner:]).astype(BF), 1, *earlier)
+
+        def step(self, *earlier):
+            self.near = self.near + (after(self.moved, *earlier) if earlier else self.moved).astype(F32)
+            self.moved = along(self.near[:, inner:].astype(BF), 2)
+            return self.moved
 
         def whole(self, *earlier):
-            return both_halves(after(self.own, *earlier) if earlier else self.own)
+            moved = after(self.moved, *earlier) if earlier else self.moved
+            return both_halves(self.near[:, :inner] + moved.astype(F32))
 
     grads_d = [grads_d_near, grads_d_far]
     with jax.named_scope("sd"):
@@ -873,63 +860,73 @@
     def up_grads(value, *earlier):
         return product("up_grads", [(after(a_two, *earlier), 0, value, 0)], [(2 * inner, BF)], same)[0]
 
-    grads_u_far = up_grads(grad_hidden[1], part_u)
+    part_u_other = swap_core(part_u, *one_d)
     with jax.named_scope("sd"):
-        far_d.add(grads_u_far)
-        near_d.add(grads_u_far)
-        sent_d = [far_d.send(), near_d.send()]
-    part_u_other = swap_core(part_u, *one_d, grads_u_far)
+        far_d.add(part_u)
+        near_d.add(part_u)
+        sent_d = [far_d.send(*one_d), near_d.send(*one_d)]
+    grads_u_far = up_grads(grad_hidden[1], far_d.sent, near_d.sent)
+    grads_u_near = up_grads(grad_hidden[0], grads_u_far)
+    with jax.named_scope("sd"):
+        far_d.add(grads_u_near)
+        near_d.add(grads_u_near)
+        line_d = SumZ(near_d.whole(), far_d.whole())
+        line_d_moved = line_d.moved
+    with jax.named_scope("su"):
+        near_u, far_u = Scatter(grads_u_near, back, g, count), Scatter(grads_u_far, forth, g, count)
+        one_u = [far_u.send(*sent_d), near_u.send(*sent_d)]
+    grad_branch, *grad_atts, sums_0, sums_1, sums_2, sums_3 = second_norm_back(
+        part_u,
+        part_u_other,
+        after(middle, grads_u_near, *sent_d),
+        grad_rows,
+        norm_vectors,
+        (out_wa, out_wb),
+    )
+    sums_two = [sums_0, sums_1, sums_2, sums_3]
     (feed,) = product(
         "down_product",
-        [(active[0], 1, down_wa, 1), (after(active[1], grads_u_far, *one_d), 1, down_wb, 1)],
+        [(active[0], 1, down_wa, 1), (after(active[1], grad_branch), 1, down_wb, 1)],
         [(width, BF)],
         same,
     )
-    feed_other = swap_core(feed)
-    grads_u_near = up_grads(grad_hidden[0], feed)
-    grad_branch, *grad_atts, sums_0, sums_1, sums_2, sums_3 = second_norm_back(
-        part_u, part_u_other, after(middle, grads_u_near, feed_other), grad_rows, norm_vectors, (out_wa, out_wb)
-    )
-    sums_two = [sums_0, sums_1, sums_2, sums_3]
-    with jax.named_scope("sd"):
-        far_d.add(grad_branch)
-        near_d.add(grad_branch)
-    with jax.named_scope("su"):
-        near_u, far_u = Scatter(grads_u_near, back, g, count), Scatter(grads_u_far, forth, g, count)
-        one_u = [far_u.send(*sent_d, grad_branch), near_u.send(*sent_d, grad_branch)]
+    feed_other = jnp.concatenate(
+        [swap_core(feed[i * rows // 3 : (i + 1) * rows // 3], line_d_moved) for i in range(3)], axis=0
+    )
 
     def attention_back(i, *earlier):
         dq, dk, dv = attend_back(saved[i], after(grad_atts[i], *earlier), cosine, sine, mask)
         return jnp.stack([v.reshape(2, 160, rows) for v in (dq, dk, dv)], axis=1).reshape(960, rows)
 
-    with jax.named_scope("sd"):
-        line_d = SumZ(near_d.whole(), far_d.whole())
-    mixed_far = attention_back(1, *sent_d)
+    mixed_far = attention_back(1, feed)
+    with jax.named_scope("su"):
+        far_u.add(mixed_far)
+        near_u.add(mixed_far)
+        sent_u = [far_u.send(), near_u.send()]
     (result,) = by_rows(
         "result", [after(middle, mixed_far), feed, feed_other, norm_vectors], [(width, BF)], result_step
     )
-    with jax.named_scope("sd"):
-        line_d.take(result)
     with jax.named_scope("rows_out"):
-        block_out, out_pieces = rows_out(after(result, *line_d.moved), start, c, z)
-    grads_far = first_grads(a_one, after(grad_branch, result), mixed_far, saved[1][3], inner)
+        block_out, out_pieces, out_sents = rows_out(result, start, c, z)
+    grads_far = first_grads(a_one, after(grad_branch, *out_sents, *one_u), mixed_far, saved[1][3], inner)
+    mixed_near = attention_back(0, grads_far)
     with jax.named_scope("su"):
         far_u.add(grads_far)
         near_u.add(grads_far)
-        sent_u = [far_u.send(), near_u.send()]
-    mixed_near = attention_back(0, *one_u, grads_far)
-    with jax.named_scope("su"):
-        far_u.add(mixed_near)
-        near_u.add(mixed_near)
         line_u = SumZ(near_u.whole(), far_u.whole())
+        line_u_moved = line_u.moved
+    with jax.named_scope("sd"):
+        line_d.step(mixed_near)
     (part,) = product(
         "qkv_back",
         [(after(mixed_near, *sent_u), 0, qkv_wa, 1), (mixed_far, 0, qkv_wb, 1)],
         [(width, BF)],
         same,
     )
-    part_other = swap_core(part, *out_pieces)
-    grads_near = first_grads(a_one, after(grad_branch, part, *out_pieces), mixed_near, saved[0][3], inner)
+    part_other = jnp.concatenate(
+        [swap_core(part[i * rows // 3 : (i + 1) * rows // 3], *out_pieces, line_u_moved) for i in range(3)], axis=0
+    )
+    grads_near = first_grads(a_one, after(grad_branch, part), mixed_near, saved[0][3], inner)
     with jax.named_scope("sq"):
         near_q, far_q = Scatter(grads_near, back, g, count), Scatter(grads_far, forth, g, count)
         one_q = [far_q.send(grads_near), near_q.send(grads_near)]
@@ -941,37 +938,35 @@
         first_back_step,
     )
     with jax.named_scope("su"):
-        line_u.take(grad_source)
+        line_u.step(grad_source)
     with jax.named_scope("rows_dx"):
-        input_grad, dx_pieces = rows_out(grad_source, start, c, z)
+        input_grad, dx_pieces, _ = rows_out(after(grad_source, line_u_moved), start, c, z, True)
         input_grad = input_grad.astype(F32)
     with jax.named_scope("sq"):
         far_q.add(grad_source)
         near_q.add(grad_source)
         sent_q = [far_q.send(), near_q.send()]
-        far_q.add(*dx_pieces)
-        near_q.add(*dx_pieces)
+        far_q.add(dx_pieces[0])
+        near_q.add(dx_pieces[0])
         line_q = SumZ(near_q.whole(), far_q.whole())
-        line_q.take()
+        moved_q = [line_q.moved, line_q.step()]
         grad_first = line_q.whole()
     with jax.named_scope("sd"):
-        grad_down = line_d.whole(*dx_pieces)
+        grad_down = after(line_d.whole(grad_source), *one_q)
     with jax.named_scope("su"):
-        grad_up = line_u.whole(*dx_pieces)
+        grad_up = after(line_u.whole(dx_pieces[0]), *one_q)
 
     vector_grad = 0.5 * jnp.concatenate(sums_one + sums_two, axis=0)
     bias_up = [after(v, *sent_q) for v in bias_up]
-    far_zero = jnp.where(z < 2, 2, 1)
-    far_one = jnp.where(z < 2, 3, 0)
     placed = jnp.zeros((7, 4, 320), F32)
-    for index, place in enumerate((z, z ^ 1, far_zero, far_one)):
+    for index, place in enumerate((z, z ^ 1, z ^ 2, z ^ 3)):
         qkv_sum = bias_qkv[index // 2].reshape(2, 3, 1, 160)[index % 2]
         up_sum = bias_up[index // 2].reshape(2, 2, 1, 320)[index % 2]
         placed = lax.dynamic_update_slice(placed, qkv_sum, (0, place, c * 160))
         placed = lax.dynamic_update_slice(placed, up_sum, (3 + 2 * c, place, 0))
     with jax.named_scope("vectors"):
         summed = add_up(
-            after(jnp.concatenate([placed.reshape(7, 4 * 320), vector_grad], axis=0), *sent_q), count
+            jnp.concatenate([placed.reshape(7, 4 * 320), vector_grad], axis=0), count, moved_q[:1], moved_q + dx_pieces[1:]
         )
     grad_bias = lax.dynamic_slice(summed, (0, z * 320), (7, 320))
     grad_vector = summed[7:]

time: 711 us -> 696 us (0.979)
  starting transfers between devices: 121 us -> 86.8 us
  waiting for transfers between devices: 137 us -> 158 us
    ppermute x60 -> x62, waiting for transfers between devices: 106 us -> 152 us  [move(): lax.ppermute(after(value, *earlier) if earlier else value, axis, pairs)]
    ppermute x60 -> x62, starting transfers between devices: 99.2 us -> 75.7 us  [move(): lax.ppermute(after(value, *earlier) if earlier else value, axis, pairs)]
    ppermute x2, waiting for transfers between devices: 28.9 us -> 6.34 us  [add_up(): lax.ppermute(value, 'z', [(i, i ^ distance) for i in range(4)])]
    ppermute x4 -> x0, starting transfers between devices: 11.4 us -> none  [rows_out(): lax.ppermute(sent, ('c', 'z'), [(b, a) for a, b in row_moves(step)])]
    concatenate x0 -> x2, other arithmetic: none -> 7.18 us  [the longest x1 3.63 us: body(): jnp.concatenate([swap_core(feed[i * rows // 3:(i + 1) * rows // 3], line_...]
    unnamed x190 -> x193, local copies, waits for them, and re-layouts: 16.6 us -> 17.7 us
  transfers between devices with their start and end apart: 69 -> 67, of which waited for: 20 -> 22; matrix products, arithmetic and copies ran while one was open for 21% -> 21% of each run, Pallas kernels for 35% -> 38%
where the time goes in v3:
time: 696 us; the launch traced here: 687 us
  Pallas kernels  260 us (37%)
  waiting for transfers between devices  158 us (23%)
  other arithmetic  116 us (17%)
  starting transfers between devices  86.8 us (12%)
  local copies, waits for them, and re-layouts  49.1 us (7%)
  matrix products  12.2 us (2%)
    ppermute x62, waiting for transfers between devices, move(): lax.ppermute(after(value, *earlier) if earlier else value, axis, pairs)  152 us
    pallas_call x9, Pallas kernels, product(): pl.pallas_call(kernel, grid=(size // block,), in_specs=in_specs, out_spec...  88 us
    ppermute x62, starting transfers between devices, move(): lax.ppermute(after(value, *earlier) if earlier else value, axis, pairs)  75.7 us
    pallas_call x1, Pallas kernels, feed_back(): pl.pallas_call(kernel, grid=(size // 512,), in_specs=[rows_of(width, 512)...  34.5 us
    pallas_call x2, Pallas kernels, attend_back(): pl.pallas_call(functools.partial(attend_back_kernel, block=256), grid=(he...  31.6 us
    pallas_call x2, Pallas kernels, attend(): pl.pallas_call(functools.partial(attend_kernel, block=256), grid=(heads,)...  30.4 us
    pallas_call x3, Pallas kernels, by_rows(): pl.pallas_call(kernel, grid=(size // block,), in_specs=in_specs, out_spec...  25.4 us
    pallas_call x2, Pallas kernels, first_grads(): pl.pallas_call(kernel, grid=(width // BLOCK,), in_specs=[columns_of(rows)...  20.3 us
  transfers between devices with their start and end apart: 67, of which 22 were waited for; matrix products, arithmetic and copies ran while one was open for 21% of the time, Pallas kernels for 38%

profile of v3, /device:TPU:0, one launch (start us, length us, event | category | flops | bytes accessed | tf_op | source)
XLA Modules:
  0.0 687.3 jit_solution(13596461520669825185)
XLA Ops:
  3.5 5.1 collective-permute-start.2
  9.3 2.7 select_bitcast_fusion.6
  15.3 2.5 collective-permute-start.5
  26.5 33.5 %collective-permute-done.6 = bf16[320,640]{1,0:T(8,128)(2,1)S(1)} collective-permute-done((bf16[320,640]{1,0:T(8,128)(2,1)S(1)}, bf16[320,640]{1,0:T(8,128)(2,1)S(1)}, u32[]{:S(2)}, u32[]{:S(2)}) %collective-permute-start.6) | collective-permute-done | bytes 409632 | tf_op jit(solution)/shard_map/near/ppermute | solution.py:65
  63.1 2.5 collective-permute-done.11
  65.6 3.0 collective-permute-start.14
  69.6 10.0 %collective-permute-done.7 = bf16[320,640]{1,0:T(8,128)(2,1)S(1)} collective-permute-done((bf16[320,640]{1,0:T(8,128)(2,1)S(1)}, bf16[320,640]{1,0:T(8,128)(2,1)S(1)}, u32[]{:S(2)}, u32[]{:S(2)}) %collective-permute-start.7) | collective-permute-done | bytes 409632 | tf_op jit(solution)/shard_map/near/ppermute | solution.py:65
  84.5 17.4 %collective-permute-done.16 = bf16[1,1,320,1280]{3,2,1,0:T(8,128)(2,1)S(1)} collective-permute-done((bf16[1,1,320,1280]{3,2,1,0:T(8,128)(2,1)S(1)}, bf16[1,1,320,1280]{3,2,1,0:T(8,128)(2,1)S(1)}, u32[]{:S(2)}, u32[]{:S(2)}) %collective-permute-start.16) | collective-permute-done | bytes 819232 | tf_op jit(solution)/shard_map/gx/ppermute | solution.py:65
  106.6 8.0 %turn_rows.2 = (bf16[1536,1280]{1,0:T(8,128)(2,1)S(1)}, bf16[1536,1280]{1,0:T(8,128)(2,1)S(1)}) custom-call(s32[1]{0:T(128)} %bitcast.6.start_ref, bf16[768,1280]{1,0:T(8,128)(2,1)S(1)} %get-tuple-element.347.up_ref, bf16[768,1280]{1,0:T(8,128)(2,1)S(1)} %get-tuple-element.346.low_ref, f32[6,1280]{1,0:T(8,128)S(1)} %copy-done.32), custom_call_target="tpu_custom_call" | custom-call | tf_op jit(solution)/shard_map/rows_x/turn_rows/pallas_call | solution.py:224
  116.6 6.3 collective-permute-done.14
  123.7 15.4 %collective-permute-done.13 = bf16[1,2,320,1280]{3,2,1,0:T(8,128)(2,1)} collective-permute-done((bf16[1,2,320,1280]{3,2,1,0:T(8,128)(2,1)S(1)}, bf16[1,2,320,1280]{3,2,1,0:T(8,128)(2,1)}, u32[]{:S(2)}, u32[]{:S(2)}) %collective-permute-start.13) | collective-permute-done | bytes 1638432 | tf_op jit(solution)/shard_map/gy/ppermute | solution.py:65
  144.2 2.5 pad_maximum_fusion.10.refs_1_
  148.4 10.5 %collective-permute-done.15 = bf16[1,1,320,1280]{3,2,1,0:T(8,128)(2,1)S(1)} collective-permute-done((bf16[1,1,320,1280]{3,2,1,0:T(8,128)(2,1)S(1)}, bf16[1,1,320,1280]{3,2,1,0:T(8,128)(2,1)S(1)}, u32[]{:S(2)}, u32[]{:S(2)}) %collective-permute-start.15) | collective-permute-done | bytes 819232 | tf_op jit(solution)/shard_map/gy/ppermute | solution.py:65
  162.9 6.1 convolution_add_fusion.1.q_ref.k_ref.v_ref
  169.0 15.1 %attend.2 = (bf16[4,80,1536]{2,1,0:T(8,128)(2,1)S(1)}, bf16[4,80,1536]{2,1,0:T(8,128)(2,1)S(1)}, bf16[4,80,1536]{2,1,0:T(8,128)(2,1)S(1)}, bf16[320,1536]{1,0:T(8,128)(2,1)S(1)}, f32[4,1,1536]{2,1,0:T(1,128)S(1)}) custom-call(f32[1280,1536]{1,0:T(8,128)S(1)} %convolution_add_fusion.1.q_ref.k_ref.v_ref, ...), custom_call_target="tpu_custom_call" | custom-call | tf_op jit(solution)/shard_map/attend/pallas_call | solution.py:325
  184.2 4.9 collective-permute-start.25
  190.7 4.6 collective-permute-done.18
  199.3 6.1 convolution_add_fusion.q_ref.k_ref.v_ref
  206.0 15.3 %attend.3 = (bf16[4,80,1536]{2,1,0:T(8,128)(2,1)S(1)}, bf16[4,80,1536]{2,1,0:T(8,128)(2,1)S(1)}, bf16[4,80,1536]{2,1,0:T(8,128)(2,1)S(1)}, bf16[320,1536]{1,0:T(8,128)(2,1)S(1)}, f32[4,1,1536]{2,1,0:T(1,128)S(1)}) custom-call(f32[1280,1536]{1,0:T(8,128)S(1)} %convolution_add_fusion.q_ref.k_ref.v_ref, f32[1280,1536]{1,0:T(8,128)S(1)} %convolution_add_fusion.q_ref.k_ref.v_ref, ...), custom_call_target="tpu_custom_call" | custom-call | tf_op jit(solution)/shard_map/attend/pallas_call | solution.py:325
  223.0 5.9 out_product.1.refs_1_
  237.5 2.5 pad_maximum_fusion.11.refs_3_
  244.0 4.8 turn_rows.3.refs_0_.g_ref
  250.7 8.9 %norm_two.1 = (bf16[1536,1280]{1,0:T(8,128)(2,1)S(1)}, bf16[1536,1280]{1,0:T(8,128)(2,1)}) custom-call(bf16[1536,1280]{1,0:T(8,128)(2,1)} %copy-done.8, bf16[1536,1280]{1,0:T(8,128)(2,1)} %out_product.1.refs_1_, bf16[1536,1280]{1,0:T(8,128)(2,1)} %collective-permute-done.24.refs_2_, f32[6,1280]{1,0:T(8,128)S(1)} %copy-done.32), custom_call_target="tpu_custom_call" | custom-call | tf_op jit(solution)/shard_map/norm_two/pallas_call | solution.py:468
  261.6 10.4 %up_product.2 = (bf16[1536,1280]{1,0:T(8,128)(2,1)}, bf16[1536,1280]{1,0:T(8,128)(2,1)}) custom-call(bf16[1536,1280]{1,0:T(8,128)(2,1)} %get-tuple-element.198.refs_0_, bf16[1280,1280]{1,0:T(8,128)(2,1)S(1)} %bitcast.151, f32[1,1280]{1,0:T(1,128)S(1)} %bitcast.183), custom_call_target="tpu_custom_call" | custom-call | tf_op jit(solution)/shard_map/up_product/pallas_call | solution.py:424
  272.0 8.4 %down_grads.2 = bf16[1280,1280]{1,0:T(8,128)(2,1)S(1)} custom-call(bf16[1536,1280]{1,0:T(8,128)(2,1)} %copy-done, bf16[1536,1280]{1,0:T(8,128)(2,1)} %get-tuple-element.179.refs_1_.refs_0_), custom_call_target="tpu_custom_call" | custom-call | tf_op jit(solution)/shard_map/down_grads/pallas_call | solution.py:424
  280.4 2.8 broadcast_select_fusion.13
  283.6 11.4 %up_product.3 = (bf16[1536,1280]{1,0:T(8,128)(2,1)}, bf16[1536,1280]{1,0:T(8,128)(2,1)}) custom-call(bf16[1536,1280]{1,0:T(8,128)(2,1)} %get-tuple-element.198.refs_0_, bf16[1280,1280]{1,0:T(8,128)(2,1)S(1)} %bitcast.153, f32[1,1280]{1,0:T(1,128)S(1)} %bitcast.182), custom_call_target="tpu_custom_call" | custom-call | tf_op jit(solution)/shard_map/up_product/pallas_call | solution.py:424
  295.0 8.2 %down_grads.3 = bf16[1280,1280]{1,0:T(8,128)(2,1)S(1)} custom-call(bf16[1536,1280]{1,0:T(8,128)(2,1)} %copy-done, bf16[1536,1280]{1,0:T(8,128)(2,1)} %get-tuple-element.205.refs_1_.refs_2_), custom_call_target="tpu_custom_call" | custom-call | tf_op jit(solution)/shard_map/down_grads/pallas_call | solution.py:424
  315.4 34.5 %feed_back.1 = (bf16[1536,1280]{1,0:T(8,128)(2,1)}, bf16[1536,1280]{1,0:T(8,128)(2,1)}, bf16[1536,1280]{1,0:T(8,128)(2,1)}, f32[1,1280]{1,0:T(1,128)}, f32[1,1280]{1,0:T(1,128)}) custom-call(bf16[1536,1280]{1,0:T(8,128)(2,1)} %copy-done, bf16[1280,1280]{1,0:T(8,128)(2,1)} %bitcast.155, bf16[1280,1280]{1,0:T(8,128)(2,1)} %bitcast.184, ...), custom_call_target="tpu_custom_call" | custom-call | tf_op jit(solution)/shard_map/feed_back/pallas_call | solution.py:538
  355.0 8.3 %up_grads.2 = bf16[1280,1280]{1,0:T(8,128)(2,1)S(1)} custom-call(bf16[1536,1280]{1,0:T(8,128)(2,1)} %get-tuple-element.198.refs_0_, bf16[1536,1280]{1,0:T(8,128)(2,1)} %get-tuple-element.197.refs_1_), custom_call_target="tpu_custom_call" | custom-call | tf_op jit(solution)/shard_map/up_grads/pallas_call | solution.py:424
  364.0 8.6 %up_grads.3 = bf16[1280,1280]{1,0:T(8,128)(2,1)S(1)} custom-call(bf16[1536,1280]{1,0:T(8,128)(2,1)} %get-tuple-element.198.refs_0_, bf16[1536,1280]{1,0:T(8,128)(2,1)} %get-tuple-element.199.refs_1_), custom_call_target="tpu_custom_call" | custom-call | tf_op jit(solution)/shard_map/up_grads/pallas_call | solution.py:424
  375.9 7.8 %collective-permute-done.34 = bf16[1,1,320,1280]{3,2,1,0:T(8,128)(2,1)S(1)} collective-permute-done((bf16[1,1,320,1280]{3,2,1,0:T(8,128)(2,1)S(1)}, bf16[1,1,320,1280]{3,2,1,0:T(8,128)(2,1)S(1)}, u32[]{:S(2)}, u32[]{:S(2)}) %collective-permute-start.34) | collective-permute-done | bytes 819232 | tf_op jit(solution)/shard_map/sd/ppermute | solution.py:65
  385.4 4.8 collective-permute-start.35
  392.7 15.5 %norm_two_back.1 = (bf16[1536,1280]{1,0:T(8,128)(2,1)}, bf16[320,1536]{1,0:T(8,128)(2,1)S(1)}, bf16[320,1536]{1,0:T(8,128)(2,1)S(1)}, f32[1,1280]{1,0:T(1,128)S(...) custom-call(bf16[1536,1280]{1,0:T(8,128)(2,1)} %get-tuple-element.193.p_ref, ...), custom_call_target="tpu_custom_call" | custom-call | tf_op jit(solution)/shard_map/norm_two_back/pallas_call | solution.py:564
  408.3 15.3 %down_product.1.refs_1_ = bf16[1536,1280]{1,0:T(8,128)(2,1)} custom-call(bf16[1536,1280]{1,0:T(8,128)(2,1)} %get-tuple-element.179.refs_1_.refs_0_, bf16[1280,1280]{1,0:T(8,128)(2,1)S(1)} %bitcast.156, bf16[1536,1280]{1,0:T(8,128)(2,1)} %get-tuple-element.205.refs_1_.refs_2_, bf16[1280,1280]{1,0:T(8,128)(2,1)} %bitcast.185), custom_call_target="tpu_custom_call" | custom-call | tf_op jit(solution)/shard_map/down_product/pallas_call | solution.py:424
  423.6 4.2 fusion.43
  431.4 15.8 %attend_back.2 = (bf16[4,80,1536]{2,1,0:T(8,128)(2,1)S(1)}, bf16[4,80,1536]{2,1,0:T(8,128)(2,1)S(1)}, bf16[4,80,1536]{2,1,0:T(8,128)(2,1)S(1)}) custom-call(bf16[4,80,1536]{2,1,0:T(8,128)(2,1)} %copy-done.39, bf16[4,80,1536]{2,1,0:T(8,128)(2,1)} %copy-done.40, bf16[4,80,1536]{2,1,0:T(8,128)(2,1)} %copy-done.41, bf16[320,1536]{1,0:T(8,128)(2,1)} %copy-done.18, ...), custom_call_target="tpu_custom_call" | custom-call | tf_op jit(solution)/shard_map/attend_back/pallas_call | solution.py:353
  458.7 3.6 pad_maximum_fusion.refs_2_
  462.3 6.2 result.1
  468.6 4.0 fusion.6
  474.4 10.2 %first_grads.2 = bf16[1280,1280]{1,0:T(8,128)(2,1)} custom-call(bf16[1536,1280]{1,0:T(8,128)(2,1)} %copy-done.7, bf16[1536,1280]{1,0:T(8,128)(2,1)} %get-tuple-element.237.g_ref.refs_3_, bf16[960,1536]{1,0:T(8,128)(2,1)S(1)} %bitcast.157, bf16[320,1536]{1,0:T(8,128)(2,1)S(1)} %copy-done.19), custom_call_target="tpu_custom_call" | custom-call | tf_op jit(solution)/shard_map/first_grads/pallas_call | solution.py:587
  492.9 15.8 %attend_back.3 = (bf16[4,80,1536]{2,1,0:T(8,128)(2,1)S(1)}, bf16[4,80,1536]{2,1,0:T(8,128)(2,1)S(1)}, bf16[4,80,1536]{2,1,0:T(8,128)(2,1)S(1)}) custom-call(bf16[4,80,1536]{2,1,0:T(8,128)(2,1)} %copy-done.36, bf16[4,80,1536]{2,1,0:T(8,128)(2,1)} %copy-done.37, bf16[4,80,1536]{2,1,0:T(8,128)(2,1)} %copy-done.38, bf16[320,1536]{1,0:T(8,128)(2,1)} %copy-done.16, ...), custom_call_target="tpu_custom_call" | custom-call | tf_op jit(solution)/shard_map/attend_back/pallas_call | solution.py:353
  512.3 11.5 %qkv_back.1.refs_0_ = bf16[1536,1280]{1,0:T(8,128)(2,1)} custom-call(bf16[960,1536]{1,0:T(8,128)(2,1)} %bitcast.159, bf16[1280,960]{1,0:T(8,128)(2,1)S(1)} %copy-done.14, bf16[960,1536]{1,0:T(8,128)(2,1)} %bitcast.158, bf16[1280,960]{1,0:T(8,128)(2,1)S(1)} %copy-done.15), custom_call_target="tpu_custom_call" | custom-call | tf_op jit(solution)/shard_map/qkv_back/pallas_call | solution.py:424
  523.9 10.1 %first_grads.3 = bf16[1280,1280]{1,0:T(8,128)(2,1)} custom-call(bf16[1536,1280]{1,0:T(8,128)(2,1)} %copy-done.7, bf16[1536,1280]{1,0:T(8,128)(2,1)} %get-tuple-element.237.g_ref.refs_3_, bf16[960,1536]{1,0:T(8,128)(2,1)S(1)} %bitcast.160, bf16[320,1536]{1,0:T(8,128)(2,1)S(1)} %copy-done.17), custom_call_target="tpu_custom_call" | custom-call | tf_op jit(solution)/shard_map/first_grads/pallas_call | solution.py:587
  534.4 2.8 constant_dynamic-slice_fusion.1
  548.4 3.5 pad_maximum_fusion.1.refs_1_
  552.0 10.3 %norm_back.1 = (bf16[1536,1280]{1,0:T(8,128)(2,1)S(1)}, f32[1,1280]{1,0:T(1,128)S(1)}, f32[1,1280]{1,0:T(1,128)S(1)}) custom-call(bf16[1536,1280]{1,0:T(8,128)(2,1)} %qkv_back.1.refs_0_, bf16[1536,1280]{1,0:T(8,128)(2,1)} %pad_maximum_fusion.1.refs_1_, bf16[1536,1280]{1,0:T(8,128)(2,1)} %copy-done.8, bf16[1536,1280]{1,0:T(8,128)(2,1)} %get-tuple-element.237.g_ref.refs_3_, ...), custom_call_target="tpu_custom_call" | custom-call | tf_op jit(solution)/shard_map/norm_back/pallas_call | solution.py:468
  562.3 4.1 fusion.4
  568.0 3.9 collective-permute-done.53
  571.9 2.5 add_convert_fusion
  585.2 3.6 multiply_subtract_fusion
  588.8 6.8 collective-permute-done.54
  595.6 3.6 collective-permute-done.52
  602.9 2.5 add_bitcast_fusion.1
  607.5 4.3 collective-permute-done.58
  618.0 7.3 %collective-permute-done.55 = bf16[320,1280]{1,0:T(8,128)(2,1)} collective-permute-done((bf16[320,1280]{1,0:T(8,128)(2,1)}, bf16[320,1280]{1,0:T(8,128)(2,1)}, u32[]{:S(2)}, u32[]{:S(2)}) %collective-permute-start.55) | collective-permute-done | bytes 819232 | tf_op jit(solution)/shard_map/sq/ppermute | solution.py:65
  625.3 9.2 %collective-permute-start.62 = (f32[13,1280]{1,0:T(8,128)S(1)}, f32[13,1280]{1,0:T(8,128)S(1)}, u32[]{:S(2)}, u32[]{:S(2)}) collective-permute-start(f32[13,1280]{1,0:T(8,128)S(1)} %pad_maximum_fusion.34), channel_id=1, source_target_pairs={{0,4},{4,0},{1,5},{5,1},{2,6},{6,2},{3,7},{7,3},{8,12},{12,8},{9,1... | collective-permute-start | bytes 199688 | tf_op jit(solution)/shard_map/vectors/ppermute | solution.py:65
  634.5 4.5 multiply_subtract_fusion.1
  645.1 5.3 collective-permute-done.50
  654.4 10.3 %collective-permute-done.56 = bf16[320,640]{1,0:T(8,128)(2,1)S(1)} collective-permute-done((bf16[320,640]{1,0:T(8,128)(2,1)S(1)}, bf16[320,640]{1,0:T(8,128)(2,1)S(1)}, u32[]{:S(2)}, u32[]{:S(2)}) %collective-permute-start.56) | collective-permute-done | bytes 409632 | tf_op jit(solution)/shard_map/sq/ppermute | solution.py:65
  666.6 2.6 collective-permute-done.65
  669.2 3.4 collective-permute-start.66
  672.7 3.8 collective-permute-done.66
  682.8 3.1 multiply_subtract_fusion.2
  (485 shorter events, 174.2 us)
Async XLA Ops:
  3.5 15.8 %collective-permute-start.2 = (f32[1,3424]{1,0:T(1,128)S(1)}, f32[1,3424]{1,0:T(1,128)S(1)}, u32[]{:S(2)}, u32[]{:S(2)}) collective-permute-start(f32[1,3424]{1,0:T(1,128)S(1)} %broadcast_in_dim.29), channel_id=1, source_target_pairs={{0,3},{1,2},{2,1},{3,0},{4,7},{5,6},{6,5},{7,4},{8,11},{9,10},{10,... | collective-permute-start | bytes 41096 | tf_op jit(solution)/shard_map/small/ppermute | solution.py:671
  8.6 12.3 %collective-permute-start.1 = (f32[1,3424]{1,0:T(1,128)S(1)}, f32[1,3424]{1,0:T(1,128)S(1)}, u32[]{:S(2)}, u32[]{:S(2)}) collective-permute-start(f32[1,3424]{1,0:T(1,128)S(1)} %broadcast_in_dim.29), channel_id=1, source_target_pairs={{0,2},{1,3},{2,0},{3,1},{4,6},{5,7},{6,4},{7,5},{8,10},{9,11},{10,... | collective-permute-start | bytes 41096 | tf_op jit(solution)/shard_map/small/ppermute | solution.py:671
  8.6 12.3 %collective-permute-start = (f32[1,3424]{1,0:T(1,128)S(1)}, f32[1,3424]{1,0:T(1,128)S(1)}, u32[]{:S(2)}, u32[]{:S(2)}) collective-permute-start(f32[1,3424]{1,0:T(1,128)S(1)} %broadcast_in_dim.29), channel_id=1, source_target_pairs={{0,1},{1,0},{2,3},{3,2},{4,5},{5,4},{6,7},{7,6},{8,9},{9,8},{10,11... | collective-permute-start | bytes 41096 | tf_op jit(solution)/shard_map/small/ppermute | solution.py:671
  12.0 70.2 %collective-permute-start.4 = (bf16[384,1280]{1,0:T(8,128)(2,1)}, bf16[384,1280]{1,0:T(8,128)(2,1)}, u32[]{:S(2)}, u32[]{:S(2)}) collective-permute-start(bf16[384,1280]{1,0:T(8,128)(2,1)} %get-tuple-element.379), channel_id=1, source_target_pairs={{0,1},{1,0},{2,5},{3,4},{4,3},{5,2},{6,7},{7,6},{8,9},{9,8},{10,13... | collective-permute-start | bytes 2949128 | tf_op jit(solution)/shard_map/rows_x/ppermute | solution.py:65
  15.3 8.7 %collective-permute-start.5 = (bf16[160,1920]{1,0:T(8,128)(2,1)S(1)}, bf16[160,1920]{1,0:T(8,128)(2,1)S(1)}, u32[]{:S(2)}, u32[]{:S(2)}) collective-permute-start(bf16[160,1920]{1,0:T(8,128)(2,1)S(1)} %get-tuple-element.145), channel_id=1, source_target_pairs={{0,4},{4,0},{1,5},{5,1},{2,6},{6,2},{3,7},{7,3},{8,12},{12,8},{9,1... | collective-permute-start | bytes 1843208 | tf_op jit(solution)/shard_map/pack/ppermute | solution.py:65
  19.3 62.9 %collective-permute-start.8 = (bf16[384,1280]{1,0:T(8,128)(2,1)S(1)}, bf16[384,1280]{1,0:T(8,128)(2,1)}, u32[]{:S(2)}, u32[]{:S(2)}) collective-permute-start(bf16[384,1280]{1,0:T(8,128)(2,1)S(1)} %get-tuple-element.378), channel_id=1, source_target_pairs={{2,4},{3,5},{4,2},{5,3},{10,12},{11,13},{12,10},{13,11},{18,20},{1... | collective-permute-start | bytes 2949128 | tf_op jit(solution)/shard_map/rows_x/ppermute | solution.py:65
  24.3 35.7 %collective-permute-start.6 = (bf16[320,640]{1,0:T(8,128)(2,1)S(1)}, bf16[320,640]{1,0:T(8,128)(2,1)S(1)}, u32[]{:S(2)}, u32[]{:S(2)}) collective-permute-start(bf16[320,640]{1,0:T(8,128)(2,1)S(1)} %get-tuple-element.394), channel_id=1, source_target_pairs={{0,1},{1,0},{2,3},{3,2},{4,5},{5,4},{6,7},{7,6},{8,9},{9,8},{10,11... | collective-permute-start | bytes 1228808 | tf_op jit(solution)/shard_map/near/ppermute | solution.py:65
  25.0 40.6 %collective-permute-start.11 = (bf16[320,640]{1,0:T(8,128)(2,1)S(1)}, bf16[320,640]{1,0:T(8,128)(2,1)S(1)}, u32[]{:S(2)}, u32[]{:S(2)}) collective-permute-start(bf16[320,640]{1,0:T(8,128)(2,1)S(1)} %get-tuple-element.392), channel_id=1, source_target_pairs={{0,1},{1,0},{2,3},{3,2},{4,5},{5,4},{6,7},{7,6},{8,9},{9,8},{10,11... | collective-permute-start | bytes 1228808 | tf_op jit(solution)/shard_map/near/ppermute | solution.py:65
  60.1 22.2 %collective-permute-start.10 = (bf16[1,1,320,1280]{3,2,1,0:T(8,128)(2,1)S(1)}, bf16[1,1,320,1280]{3,2,1,0:T(8,128)(2,1)S(1)}, u32[]{:S(2)}, u32[]{:S(2)}) collective-permute-start(bf16[1,1,320,1280]{3,2,1,0:T(8,128)(2,1)S(1)} %get-tuple-element.407), channel_id=1, source_target_pairs={{0,8},{8,0},{16,24},{24,16},{1,9},{9,1},{17,25},{25,17},{2,10},{10... | collective-permute-start | bytes 2457608 | tf_op jit(solution)/shard_map/gx/ppermute | solution.py:65
  62.1 17.5 %collective-permute-start.7 = (bf16[320,640]{1,0:T(8,128)(2,1)S(1)}, bf16[320,640]{1,0:T(8,128)(2,1)S(1)}, u32[]{:S(2)}, u32[]{:S(2)}) collective-permute-start(bf16[320,640]{1,0:T(8,128)(2,1)S(1)} %get-tuple-element.146), channel_id=1, source_target_pairs={{0,1},{1,0},{2,3},{3,2},{4,5},{5,4},{6,7},{7,6},{8,9},{9,8},{10,11... | collective-permute-start | bytes 1228808 | tf_op jit(solution)/shard_map/near/ppermute | solution.py:65
  65.6 57.2 %collective-permute-start.14 = (bf16[320,1280]{1,0:T(8,128)(2,1)S(1)}, bf16[320,1280]{1,0:T(8,128)(2,1)S(1)}, u32[]{:S(2)}, u32[]{:S(2)}) collective-permute-start(bf16[320,1280]{1,0:T(8,128)(2,1)S(1)} %get-tuple-element.408), channel_id=1, source_target_pairs={{0,2},{1,3},{2,0},{3,1},{4,6},{5,7},{6,4},{7,5},{8,10},{9,11},{10,... | collective-permute-start | bytes 2457608 | tf_op jit(solution)/shard_map/far/ppermute | solution.py:65
  79.5 23.2 %collective-permute-start.12 = (bf16[1,1,320,1280]{3,2,1,0:T(8,128)(2,1)S(1)}, bf16[1,1,320,1280]{3,2,1,0:T(8,128)(2,1)S(1)}, u32[]{:S(2)}, u32[]{:S(2)}) collective-permute-start(bf16[1,1,320,1280]{3,2,1,0:T(8,128)(2,1)S(1)} %get-tuple-element.404), channel_id=1, source_target_pairs={{0,16},{8,24},{16,0},{24,8},{1,17},{9,25},{17,1},{25,9},{2,18},{10... | collective-permute-start | bytes 2457608 | tf_op jit(solution)/shard_map/gy/ppermute | solution.py:65
  82.3 101.9 %collective-permute-start.21 = (bf16[320,1280]{1,0:T(8,128)(2,1)}, bf16[320,1280]{1,0:T(8,128)(2,1)}, u32[]{:S(2)}, u32[]{:S(2)}) collective-permute-start(bf16[320,1280]{1,0:T(8,128)(2,1)} %get-tuple-element.403), channel_id=1, source_target_pairs={{0,2},{1,3},{2,0},{3,1},{4,6},{5,7},{6,4},{7,5},{8,10},{9,11},{10,... | collective-permute-start | bytes 2457608 | tf_op jit(solution)/shard_map/far/ppermute | solution.py:65
  82.3 19.6 %collective-permute-start.16 = (bf16[1,1,320,1280]{3,2,1,0:T(8,128)(2,1)S(1)}, bf16[1,1,320,1280]{3,2,1,0:T(8,128)(2,1)S(1)}, u32[]{:S(2)}, u32[]{:S(2)}) collective-permute-start(bf16[1,1,320,1280]{3,2,1,0:T(8,128)(2,1)S(1)} %get-tuple-element.157), channel_id=1, source_target_pairs={{0,8},{8,0},{16,24},{24,16},{1,9},{9,1},{17,25},{25,17},{2,10},{10... | collective-permute-start | bytes 2457608 | tf_op jit(solution)/shard_map/gx/ppermute | solution.py:65
  84.4 21.3 %collective-permute-start.9 = (bf16[768,1280]{1,0:T(8,128)(2,1)S(1)}, bf16[768,1280]{1,0:T(8,128)(2,1)S(1)}, u32[]{:S(2)}, u32[]{:S(2)}) collective-permute-start(bf16[768,1280]{1,0:T(8,128)(2,1)S(1)} %pad_maximum_fusion.12), channel_id=1, source_target_pairs={{0,4},{4,0},{1,5},{5,1},{2,6},{6,2},{3,7},{7,3},{8,12},{12,8},{9,1... | collective-permute-start | bytes 5898248 | tf_op jit(solution)/shard_map/rows_x/ppermute | solution.py:65
  102.8 36.4 %collective-permute-start.13 = (bf16[1,2,320,1280]{3,2,1,0:T(8,128)(2,1)S(1)}, bf16[1,2,320,1280]{3,2,1,0:T(8,128)(2,1)}, u32[]{:S(2)}, u32[]{:S(2)}) collective-permute-start(bf16[1,2,320,1280]{3,2,1,0:T(8,128)(2,1)S(1)} %pad_maximum_fusion.15), channel_id=1, source_target_pairs={{0,16},{8,24},{16,0},{24,8},{1,17},{9,25},{17,1},{25,9},{2,18},{10... | collective-permute-start | bytes 4915208 | tf_op jit(solution)/shard_map/gy/ppermute | solution.py:65
  103.8 39.1 %collective-permute-start.17 = (bf16[2,1,320,1280]{3,2,1,0:T(8,128)(2,1)S(1)}, bf16[2,1,320,1280]{3,2,1,0:T(8,128)(2,1)}, u32[]{:S(2)}, u32[]{:S(2)}) collective-permute-start(bf16[2,1,320,1280]{3,2,1,0:T(8,128)(2,1)S(1)} %pad_maximum_fusion.17), channel_id=1, source_target_pairs={{0,8},{8,0},{16,24},{24,16},{1,9},{9,1},{17,25},{25,17},{2,10},{10... | collective-permute-start | bytes 4915208 | tf_op jit(solution)/shard_map/gx/ppermute | solution.py:65
  141.1 17.8 %collective-permute-start.15 = (bf16[1,1,320,1280]{3,2,1,0:T(8,128)(2,1)S(1)}, bf16[1,1,320,1280]{3,2,1,0:T(8,128)(2,1)S(1)}, u32[]{:S(2)}, u32[]{:S(2)}) collective-permute-start(bf16[1,1,320,1280]{3,2,1,0:T(8,128)(2,1)S(1)} %bitcast.198), channel_id=1, source_target_pairs={{0,16},{8,24},{16,0},{24,8},{1,17},{9,25},{17,1},{25,9},{2,18},{10... | collective-permute-start | bytes 2457608 | tf_op jit(solution)/shard_map/gy/ppermute | solution.py:65
  142.9 54.4 %collective-permute-start.20 = (bf16[320,1280]{1,0:T(8,128)(2,1)}, bf16[320,1280]{1,0:T(8,128)(2,1)}, u32[]{:S(2)}, u32[]{:S(2)}) collective-permute-start(bf16[320,1280]{1,0:T(8,128)(2,1)} %get-tuple-element.162), channel_id=1, source_target_pairs={{0,2},{1,3},{2,0},{3,1},{4,6},{5,7},{6,4},{7,5},{8,10},{9,11},{10,... | collective-permute-start | bytes 2457608 | tf_op jit(solution)/shard_map/far/ppermute | solution.py:65
  160.5 34.8 %collective-permute-start.18 = (bf16[2,1,320,1280]{3,2,1,0:T(8,128)(2,1)}, bf16[2,1,320,1280]{3,2,1,0:T(8,128)(2,1)}, u32[]{:S(2)}, u32[]{:S(2)}) collective-permute-start(bf16[2,1,320,1280]{3,2,1,0:T(8,128)(2,1)} %pad_maximum_fusion.16), channel_id=1, source_target_pairs={{0,8},{8,0},{16,24},{24,16},{1,9},{9,1},{17,25},{25,17},{2,10},{10... | collective-permute-start | bytes 4915208 | tf_op jit(solution)/shard_map/gx/ppermute | solution.py:65
  161.7 35.5 %collective-permute-start.19 = (bf16[1,2,320,1280]{3,2,1,0:T(8,128)(2,1)}, bf16[1,2,320,1280]{3,2,1,0:T(8,128)(2,1)}, u32[]{:S(2)}, u32[]{:S(2)}) collective-permute-start(bf16[1,2,320,1280]{3,2,1,0:T(8,128)(2,1)} %pad_maximum_fusion.18), channel_id=1, source_target_pairs={{0,16},{8,24},{16,0},{24,8},{1,17},{9,25},{17,1},{25,9},{2,18},{10... | collective-permute-start | bytes 4915208 | tf_op jit(solution)/shard_map/gy/ppermute | solution.py:65
  184.2 45.1 %collective-permute-start.25 = (bf16[384,1280]{1,0:T(8,128)(2,1)}, bf16[384,1280]{1,0:T(8,128)(2,1)}, u32[]{:S(2)}, u32[]{:S(2)}) collective-permute-start(bf16[384,1280]{1,0:T(8,128)(2,1)} %get-tuple-element.174), channel_id=1, source_target_pairs={{0,1},{1,0},{2,5},{3,4},{4,3},{5,2},{6,7},{7,6},{8,9},{9,8},{10,13... | collective-permute-start | bytes 2949128 | tf_op jit(solution)/shard_map/rows_g/ppermute | solution.py:65
  189.1 40.2 %collective-permute-start.26 = (bf16[384,1280]{1,0:T(8,128)(2,1)}, bf16[384,1280]{1,0:T(8,128)(2,1)}, u32[]{:S(2)}, u32[]{:S(2)}) collective-permute-start(bf16[384,1280]{1,0:T(8,128)(2,1)} %get-tuple-element.176), channel_id=1, source_target_pairs={{2,4},{3,5},{4,2},{5,3},{10,12},{11,13},{12,10},{13,11},{18,20},{1... | collective-permute-start | bytes 2949128 | tf_op jit(solution)/shard_map/rows_g/ppermute | solution.py:65
  197.3 24.5 %collective-permute-start.22 = (bf16[1,1,320,1280]{3,2,1,0:T(8,128)(2,1)}, bf16[1,1,320,1280]{3,2,1,0:T(8,128)(2,1)}, u32[]{:S(2)}, u32[]{:S(2)}) collective-permute-start(bf16[1,1,320,1280]{3,2,1,0:T(8,128)(2,1)} %bitcast.24), channel_id=1, source_target_pairs={{0,8},{8,0},{16,24},{24,16},{1,9},{9,1},{17,25},{25,17},{2,10},{10... | collective-permute-start | bytes 2457608 | tf_op jit(solution)/shard_map/gx/ppermute | solution.py:65
  197.9 23.9 %collective-permute-start.23 = (bf16[1,1,320,1280]{3,2,1,0:T(8,128)(2,1)}, bf16[1,1,320,1280]{3,2,1,0:T(8,128)(2,1)S(1)}, u32[]{:S(2)}, u32[]{:S(2)}) collective-permute-start(bf16[1,1,320,1280]{3,2,1,0:T(8,128)(2,1)} %bitcast.25), channel_id=1, source_target_pairs={{0,16},{8,24},{16,0},{24,8},{1,17},{9,25},{17,1},{25,9},{2,18},{10... | collective-permute-start | bytes 2457608 | tf_op jit(solution)/shard_map/gy/ppermute | solution.py:65
  229.0 21.7 %collective-permute-start.24 = (bf16[1536,1280]{1,0:T(8,128)(2,1)}, bf16[1536,1280]{1,0:T(8,128)(2,1)}, u32[]{:S(2)}, u32[]{:S(2)}) collective-permute-start(bf16[1536,1280]{1,0:T(8,128)(2,1)} %out_product.1.refs_1_), channel_id=1, source_target_pairs={{0,4},{4,0},{1,5},{5,1},{2,6},{6,2},{3,7},{7,3},{8,12},{12,8},{9,1... | collective-permute-start | bytes 11796488 | tf_op jit(solution)/shard_map/ppermute | solution.py:65
  231.8 11.5 %collective-permute-start.27 = (bf16[768,1280]{1,0:T(8,128)(2,1)S(1)}, bf16[768,1280]{1,0:T(8,128)(2,1)S(1)}, u32[]{:S(2)}, u32[]{:S(2)}) collective-permute-start(bf16[768,1280]{1,0:T(8,128)(2,1)S(1)} %pad_maximum_fusion.13), channel_id=1, source_target_pairs={{0,4},{4,0},{1,5},{5,1},{2,6},{6,2},{3,7},{7,3},{8,12},{12,8},{9,1... | collective-permute-start | bytes 5898248 | tf_op jit(solution)/shard_map/rows_g/ppermute | solution.py:65
  236.3 44.2 %collective-permute-start.28 = (bf16[1,2,320,1280]{3,2,1,0:T(8,128)(2,1)}, bf16[1,2,320,1280]{3,2,1,0:T(8,128)(2,1)}, u32[]{:S(2)}, u32[]{:S(2)}) collective-permute-start(bf16[1,2,320,1280]{3,2,1,0:T(8,128)(2,1)} %pad_maximum_fusion.19), channel_id=1, source_target_pairs={{0,16},{8,24},{16,0},{24,8},{1,17},{9,25},{17,1},{25,9},{2,18},{10... | collective-permute-start | bytes 4915208 | tf_op jit(solution)/shard_map/gy/ppermute | solution.py:65
  242.5 62.1 %collective-permute-start.29 = (bf16[2,1,320,1280]{3,2,1,0:T(8,128)(2,1)}, bf16[2,1,320,1280]{3,2,1,0:T(8,128)(2,1)}, u32[]{:S(2)}, u32[]{:S(2)}) collective-permute-start(bf16[2,1,320,1280]{3,2,1,0:T(8,128)(2,1)} %pad_maximum_fusion.20), channel_id=1, source_target_pairs={{0,8},{8,0},{16,24},{24,16},{1,9},{9,1},{17,25},{25,17},{2,10},{10... | collective-permute-start | bytes 4915208 | tf_op jit(solution)/shard_map/gx/ppermute | solution.py:65
  304.6 45.2 %collective-permute-start.30 = (bf16[2,1,320,1280]{3,2,1,0:T(8,128)(2,1)}, bf16[2,1,320,1280]{3,2,1,0:T(8,128)(2,1)}, u32[]{:S(2)}, u32[]{:S(2)}) collective-permute-start(bf16[2,1,320,1280]{3,2,1,0:T(8,128)(2,1)} %constant_dynamic-slice_fusion.6), channel_id=1, source_target_pairs={{0,8},{8,0},{16,24},{24,16},{1,9},{9,1},{17,25},{25,17},{2,10},{10... | collective-permute-start | bytes 4915208 | tf_op jit(solution)/shard_map/sd/ppermute | solution.py:65
  307.3 42.6 %collective-permute-start.31 = (bf16[1,2,320,1280]{3,2,1,0:T(8,128)(2,1)}, bf16[1,2,320,1280]{3,2,1,0:T(8,128)(2,1)}, u32[]{:S(2)}, u32[]{:S(2)}) collective-permute-start(bf16[1,2,320,1280]{3,2,1,0:T(8,128)(2,1)} %constant_dynamic-slice_fusion.5), channel_id=1, source_target_pairs={{0,16},{8,24},{16,0},{24,8},{1,17},{9,25},{17,1},{25,9},{2,18},{10... | collective-permute-start | bytes 4915208 | tf_op jit(solution)/shard_map/sd/ppermute | solution.py:65
  349.9 42.7 %collective-permute-start.32 = (bf16[1536,1280]{1,0:T(8,128)(2,1)}, bf16[1536,1280]{1,0:T(8,128)(2,1)}, u32[]{:S(2)}, u32[]{:S(2)}) collective-permute-start(bf16[1536,1280]{1,0:T(8,128)(2,1)} %get-tuple-element.193.p_ref), channel_id=1, source_target_pairs={{0,4},{4,0},{1,5},{5,1},{2,6},{6,2},{3,7},{7,3},{8,12},{12,8},{9,1... | collective-permute-start | bytes 11796488 | tf_op jit(solution)/shard_map/ppermute | solution.py:65
  352.2 21.7 %collective-permute-start.33 = (bf16[1,1,320,1280]{3,2,1,0:T(8,128)(2,1)}, bf16[1,1,320,1280]{3,2,1,0:T(8,128)(2,1)}, u32[]{:S(2)}, u32[]{:S(2)}) collective-permute-start(bf16[1,1,320,1280]{3,2,1,0:T(8,128)(2,1)} %add_convert_fusion.5), channel_id=1, source_target_pairs={{0,16},{8,24},{16,0},{24,8},{1,17},{9,25},{17,1},{25,9},{2,18},{10... | collective-permute-start | bytes 2457608 | tf_op jit(solution)/shard_map/sd/ppermute | solution.py:65
  363.2 20.4 %collective-permute-start.34 = (bf16[1,1,320,1280]{3,2,1,0:T(8,128)(2,1)S(1)}, bf16[1,1,320,1280]{3,2,1,0:T(8,128)(2,1)S(1)}, u32[]{:S(2)}, u32[]{:S(2)}) collective-permute-start(bf16[1,1,320,1280]{3,2,1,0:T(8,128)(2,1)S(1)} %add_convert_fusion.4), channel_id=1, source_target_pairs={{0,8},{8,0},{16,24},{24,16},{1,9},{9,1},{17,25},{25,17},{2,10},{10... | collective-permute-start | bytes 2457608 | tf_op jit(solution)/shard_map/sd/ppermute | solution.py:65
  385.4 42.3 %collective-permute-start.35 = (bf16[320,1280]{1,0:T(8,128)(2,1)S(1)}, bf16[320,1280]{1,0:T(8,128)(2,1)S(1)}, u32[]{:S(2)}, u32[]{:S(2)}) collective-permute-start(bf16[320,1280]{1,0:T(8,128)(2,1)S(1)} %pad_maximum_fusion.26), channel_id=1, source_target_pairs={{0,1},{1,0},{2,3},{3,2},{4,5},{5,4},{6,7},{7,6},{8,9},{9,8},{10,11... | collective-permute-start | bytes 2457608 | tf_op jit(solution)/shard_map/sd/ppermute | solution.py:65
  390.2 57.6 %collective-permute-start.41 = (bf16[2,1,320,1280]{3,2,1,0:T(8,128)(2,1)}, bf16[2,1,320,1280]{3,2,1,0:T(8,128)(2,1)}, u32[]{:S(2)}, u32[]{:S(2)}) collective-permute-start(bf16[2,1,320,1280]{3,2,1,0:T(8,128)(2,1)} %constant_dynamic-slice_fusion.4), channel_id=1, source_target_pairs={{0,8},{8,0},{16,24},{24,16},{1,9},{9,1},{17,25},{25,17},{2,10},{10... | collective-permute-start | bytes 4915208 | tf_op jit(solution)/shard_map/su/ppermute | solution.py:65
  392.0 61.6 %collective-permute-start.42 = (bf16[1,2,320,1280]{3,2,1,0:T(8,128)(2,1)}, bf16[1,2,320,1280]{3,2,1,0:T(8,128)(2,1)}, u32[]{:S(2)}, u32[]{:S(2)}) collective-permute-start(bf16[1,2,320,1280]{3,2,1,0:T(8,128)(2,1)} %constant_dynamic-slice_fusion.3), channel_id=1, source_target_pairs={{0,16},{8,24},{16,0},{24,8},{1,17},{9,25},{17,1},{25,9},{2,18},{10... | collective-permute-start | bytes 4915208 | tf_op jit(solution)/shard_map/su/ppermute | solution.py:65
  428.6 30.0 %collective-permute-start.38 = (bf16[512,1280]{1,0:T(8,128)(2,1)}, bf16[512,1280]{1,0:T(8,128)(2,1)}, u32[]{:S(2)}, u32[]{:S(2)}) collective-permute-start(bf16[512,1280]{1,0:T(8,128)(2,1)} %get-tuple-element.216), channel_id=1, source_target_pairs={{0,4},{4,0},{1,5},{5,1},{2,6},{6,2},{3,7},{7,3},{8,12},{12,8},{9,1... | collective-permute-start | bytes 3932168 | tf_op jit(solution)/shard_map/ppermute | solution.py:65
  428.6 30.0 %collective-permute-start.37 = (bf16[512,1280]{1,0:T(8,128)(2,1)}, bf16[512,1280]{1,0:T(8,128)(2,1)}, u32[]{:S(2)}, u32[]{:S(2)}) collective-permute-start(bf16[512,1280]{1,0:T(8,128)(2,1)} %get-tuple-element.215), channel_id=1, source_target_pairs={{0,4},{4,0},{1,5},{5,1},{2,6},{6,2},{3,7},{7,3},{8,12},{12,8},{9,1... | collective-permute-start | bytes 3932168 | tf_op jit(solution)/shard_map/ppermute | solution.py:65
  429.1 29.5 %collective-permute-start.36 = (bf16[512,1280]{1,0:T(8,128)(2,1)}, bf16[512,1280]{1,0:T(8,128)(2,1)}, u32[]{:S(2)}, u32[]{:S(2)}) collective-permute-start(bf16[512,1280]{1,0:T(8,128)(2,1)} %get-tuple-element.214), channel_id=1, source_target_pairs={{0,4},{4,0},{1,5},{5,1},{2,6},{6,2},{3,7},{7,3},{8,12},{12,8},{9,1... | collective-permute-start | bytes 3932168 | tf_op jit(solution)/shard_map/ppermute | solution.py:65
  452.3 32.3 %collective-permute-start.43 = (bf16[1,1,320,1280]{3,2,1,0:T(8,128)(2,1)}, bf16[1,1,320,1280]{3,2,1,0:T(8,128)(2,1)}, u32[]{:S(2)}, u32[]{:S(2)}) collective-permute-start(bf16[1,1,320,1280]{3,2,1,0:T(8,128)(2,1)} %add_convert_fusion.3), channel_id=1, source_target_pairs={{0,16},{8,24},{16,0},{24,8},{1,17},{9,25},{17,1},{25,9},{2,18},{10... | collective-permute-start | bytes 2457608 | tf_op jit(solution)/shard_map/su/ppermute | solution.py:65
  455.9 30.5 %collective-permute-start.44 = (bf16[1,1,320,1280]{3,2,1,0:T(8,128)(2,1)}, bf16[1,1,320,1280]{3,2,1,0:T(8,128)(2,1)}, u32[]{:S(2)}, u32[]{:S(2)}) collective-permute-start(bf16[1,1,320,1280]{3,2,1,0:T(8,128)(2,1)} %add_convert_fusion.2), channel_id=1, source_target_pairs={{0,8},{8,0},{16,24},{24,16},{1,9},{9,1},{17,25},{25,17},{2,10},{10... | collective-permute-start | bytes 2457608 | tf_op jit(solution)/shard_map/su/ppermute | solution.py:65
  472.6 67.1 %collective-permute-start.39 = (bf16[384,1280]{1,0:T(8,128)(2,1)}, bf16[384,1280]{1,0:T(8,128)(2,1)}, u32[]{:S(2)}, u32[]{:S(2)}) collective-permute-start(bf16[384,1280]{1,0:T(8,128)(2,1)} %get-tuple-element.337), channel_id=1, source_target_pairs={{1,0},{0,1},{5,2},{4,3},{3,4},{2,5},{7,6},{6,7},{9,8},{8,9},{13,10... | collective-permute-start | bytes 2949128 | tf_op jit(solution)/shard_map/rows_out/ppermute | solution.py:65
  472.8 67.0 %collective-permute-start.40 = (bf16[384,1280]{1,0:T(8,128)(2,1)}, bf16[384,1280]{1,0:T(8,128)(2,1)}, u32[]{:S(2)}, u32[]{:S(2)}) collective-permute-start(bf16[384,1280]{1,0:T(8,128)(2,1)} %get-tuple-element.336), channel_id=1, source_target_pairs={{4,2},{5,3},{2,4},{3,5},{12,10},{13,11},{10,12},{11,13},{20,18},{2... | collective-permute-start | bytes 2949128 | tf_op jit(solution)/shard_map/rows_out/ppermute | solution.py:65
  489.7 50.0 %collective-permute-start.45 = (bf16[320,1280]{1,0:T(8,128)(2,1)S(1)}, bf16[320,1280]{1,0:T(8,128)(2,1)S(1)}, u32[]{:S(2)}, u32[]{:S(2)}) collective-permute-start(bf16[320,1280]{1,0:T(8,128)(2,1)S(1)} %pad_maximum_fusion.27), channel_id=1, source_target_pairs={{0,1},{1,0},{2,3},{3,2},{4,5},{5,4},{6,7},{7,6},{8,9},{9,8},{10,11... | collective-permute-start | bytes 2457608 | tf_op jit(solution)/shard_map/su/ppermute | solution.py:65
  534.0 37.9 %collective-permute-start.53 = (bf16[2,1,320,1280]{3,2,1,0:T(8,128)(2,1)}, bf16[2,1,320,1280]{3,2,1,0:T(8,128)(2,1)}, u32[]{:S(2)}, u32[]{:S(2)}) collective-permute-start(bf16[2,1,320,1280]{3,2,1,0:T(8,128)(2,1)} %constant_dynamic-slice_fusion), channel_id=1, source_target_pairs={{0,8},{8,0},{16,24},{24,16},{1,9},{9,1},{17,25},{25,17},{2,10},{10... | collective-permute-start | bytes 4915208 | tf_op jit(solution)/shard_map/sq/ppermute | solution.py:65
  537.2 38.2 %collective-permute-start.51 = (bf16[1,2,320,1280]{3,2,1,0:T(8,128)(2,1)}, bf16[1,2,320,1280]{3,2,1,0:T(8,128)(2,1)}, u32[]{:S(2)}, u32[]{:S(2)}) collective-permute-start(bf16[1,2,320,1280]{3,2,1,0:T(8,128)(2,1)} %constant_dynamic-slice_fusion.1), channel_id=1, source_target_pairs={{0,16},{8,24},{16,0},{24,8},{1,17},{9,25},{17,1},{25,9},{2,18},{10... | collective-permute-start | bytes 4915208 | tf_op jit(solution)/shard_map/sq/ppermute | solution.py:65
  539.8 7.8 %collective-permute-start.48 = (bf16[512,1280]{1,0:T(8,128)(2,1)}, bf16[512,1280]{1,0:T(8,128)(2,1)}, u32[]{:S(2)}, u32[]{:S(2)}) collective-permute-start(bf16[512,1280]{1,0:T(8,128)(2,1)} %get-tuple-element.236), channel_id=1, source_target_pairs={{0,4},{4,0},{1,5},{5,1},{2,6},{6,2},{3,7},{7,3},{8,12},{12,8},{9,1... | collective-permute-start | bytes 3932168 | tf_op jit(solution)/shard_map/ppermute | solution.py:65
  541.3 7.1 %collective-permute-start.47 = (bf16[512,1280]{1,0:T(8,128)(2,1)}, bf16[512,1280]{1,0:T(8,128)(2,1)}, u32[]{:S(2)}, u32[]{:S(2)}) collective-permute-start(bf16[512,1280]{1,0:T(8,128)(2,1)} %get-tuple-element.235), channel_id=1, source_target_pairs={{0,4},{4,0},{1,5},{5,1},{2,6},{6,2},{3,7},{7,3},{8,12},{12,8},{9,1... | collective-permute-start | bytes 3932168 | tf_op jit(solution)/shard_map/ppermute | solution.py:65
  541.4 7.0 %collective-permute-start.46 = (bf16[512,1280]{1,0:T(8,128)(2,1)S(1)}, bf16[512,1280]{1,0:T(8,128)(2,1)}, u32[]{:S(2)}, u32[]{:S(2)}) collective-permute-start(bf16[512,1280]{1,0:T(8,128)(2,1)S(1)} %get-tuple-element.234), channel_id=1, source_target_pairs={{0,4},{4,0},{1,5},{5,1},{2,6},{6,2},{3,7},{7,3},{8,12},{12,8},{9,1... | collective-permute-start | bytes 3932168 | tf_op jit(solution)/shard_map/ppermute | solution.py:65
  547.6 33.0 %collective-permute-start.60 = (bf16[320,640]{1,0:T(8,128)(2,1)}, bf16[320,640]{1,0:T(8,128)(2,1)S(1)}, u32[]{:S(2)}, u32[]{:S(2)}) collective-permute-start(bf16[320,640]{1,0:T(8,128)(2,1)} %slice.516), channel_id=1, source_target_pairs={{0,2},{1,3},{2,0},{3,1},{4,6},{5,7},{6,4},{7,5},{8,10},{9,11},{10,... | collective-permute-start | bytes 1228808 | tf_op jit(solution)/shard_map/sd/ppermute | solution.py:65
  566.4 34.5 %collective-permute-start.49 = (bf16[384,1280]{1,0:T(8,128)(2,1)}, bf16[384,1280]{1,0:T(8,128)(2,1)}, u32[]{:S(2)}, u32[]{:S(2)}) collective-permute-start(bf16[384,1280]{1,0:T(8,128)(2,1)} %get-tuple-element.334), channel_id=1, source_target_pairs={{4,2},{5,3},{2,4},{3,5},{12,10},{13,11},{10,12},{11,13},{20,18},{2... | collective-permute-start | bytes 2949128 | tf_op jit(solution)/shard_map/rows_dx/ppermute | solution.py:65
  574.4 21.2 %collective-permute-start.54 = (bf16[1,1,320,1280]{3,2,1,0:T(8,128)(2,1)}, bf16[1,1,320,1280]{3,2,1,0:T(8,128)(2,1)}, u32[]{:S(2)}, u32[]{:S(2)}) collective-permute-start(bf16[1,1,320,1280]{3,2,1,0:T(8,128)(2,1)} %add_convert_fusion), channel_id=1, source_target_pairs={{0,16},{8,24},{16,0},{24,8},{1,17},{9,25},{17,1},{25,9},{2,18},{10... | collective-permute-start | bytes 2457608 | tf_op jit(solution)/shard_map/sq/ppermute | solution.py:65
  577.9 21.3 %collective-permute-start.52 = (bf16[1,1,320,1280]{3,2,1,0:T(8,128)(2,1)}, bf16[1,1,320,1280]{3,2,1,0:T(8,128)(2,1)}, u32[]{:S(2)}, u32[]{:S(2)}) collective-permute-start(bf16[1,1,320,1280]{3,2,1,0:T(8,128)(2,1)} %add_convert_fusion.1), channel_id=1, source_target_pairs={{0,8},{8,0},{16,24},{24,16},{1,9},{9,1},{17,25},{25,17},{2,10},{10... | collective-permute-start | bytes 2457608 | tf_op jit(solution)/shard_map/sq/ppermute | solution.py:65
  580.5 31.3 %collective-permute-start.58 = (bf16[320,640]{1,0:T(8,128)(2,1)}, bf16[320,640]{1,0:T(8,128)(2,1)}, u32[]{:S(2)}, u32[]{:S(2)}) collective-permute-start(bf16[320,640]{1,0:T(8,128)(2,1)} %slice.517), channel_id=1, source_target_pairs={{0,2},{1,3},{2,0},{3,1},{4,6},{5,7},{6,4},{7,5},{8,10},{9,11},{10,... | collective-permute-start | bytes 1228808 | tf_op jit(solution)/shard_map/su/ppermute | solution.py:65
  606.4 18.9 %collective-permute-start.55 = (bf16[320,1280]{1,0:T(8,128)(2,1)}, bf16[320,1280]{1,0:T(8,128)(2,1)}, u32[]{:S(2)}, u32[]{:S(2)}) collective-permute-start(bf16[320,1280]{1,0:T(8,128)(2,1)} %pad_maximum_fusion.28), channel_id=1, source_target_pairs={{0,1},{1,0},{2,3},{3,2},{4,5},{5,4},{6,7},{7,6},{8,9},{9,8},{10,11... | collective-permute-start | bytes 2457608 | tf_op jit(solution)/shard_map/sq/ppermute | solution.py:65
  615.1 35.3 %collective-permute-start.50 = (bf16[384,1280]{1,0:T(8,128)(2,1)}, bf16[384,1280]{1,0:T(8,128)(2,1)}, u32[]{:S(2)}, u32[]{:S(2)}) collective-permute-start(bf16[384,1280]{1,0:T(8,128)(2,1)} %get-tuple-element.241), channel_id=1, source_target_pairs={{1,0},{0,1},{5,2},{4,3},{3,4},{2,5},{7,6},{6,7},{9,8},{8,9},{13,10... | collective-permute-start | bytes 2949128 | tf_op jit(solution)/shard_map/rows_dx/ppermute | solution.py:65
  625.3 13.7 %collective-permute-start.62 = (f32[13,1280]{1,0:T(8,128)S(1)}, f32[13,1280]{1,0:T(8,128)S(1)}, u32[]{:S(2)}, u32[]{:S(2)}) collective-permute-start(f32[13,1280]{1,0:T(8,128)S(1)} %pad_maximum_fusion.34), channel_id=1, source_target_pairs={{0,4},{4,0},{1,5},{5,1},{2,6},{6,2},{3,7},{7,3},{8,12},{12,8},{9,1... | collective-permute-start | bytes 199688 | tf_op jit(solution)/shard_map/vectors/ppermute | solution.py:65
  639.1 4.6 collective-permute-start.63
  642.2 22.5 %collective-permute-start.56 = (bf16[320,640]{1,0:T(8,128)(2,1)S(1)}, bf16[320,640]{1,0:T(8,128)(2,1)S(1)}, u32[]{:S(2)}, u32[]{:S(2)}) collective-permute-start(bf16[320,640]{1,0:T(8,128)(2,1)S(1)} %slice.518), channel_id=1, source_target_pairs={{0,2},{1,3},{2,0},{3,1},{4,6},{5,7},{6,4},{7,5},{8,10},{9,11},{10,... | collective-permute-start | bytes 1228808 | tf_op jit(solution)/shard_map/sq/ppermute | solution.py:65
  643.7 10.6 %collective-permute-start.64 = (f32[13,1280]{1,0:T(8,128)S(1)}, f32[13,1280]{1,0:T(8,128)S(1)}, u32[]{:S(2)}, u32[]{:S(2)}) collective-permute-start(f32[13,1280]{1,0:T(8,128)S(1)} %add.432), channel_id=1, source_target_pairs={{0,16},{8,24},{16,0},{24,8},{1,17},{9,25},{17,1},{25,9},{2,18},{10... | collective-permute-start | bytes 199688 | tf_op jit(solution)/shard_map/vectors/ppermute | solution.py:65
  664.6 4.5 collective-permute-start.65
  669.2 7.3 %collective-permute-start.66 = (f32[13,1280]{1,0:T(8,128)S(1)}, f32[13,1280]{1,0:T(8,128)S(1)}, u32[]{:S(2)}, u32[]{:S(2)}) collective-permute-start(f32[13,1280]{1,0:T(8,128)S(1)} %add.434), channel_id=1, source_target_pairs={{0,2},{1,3},{2,0},{3,1},{4,6},{5,7},{6,4},{7,5},{8,10},{9,11},{10,... | collective-permute-start | bytes 199688 | tf_op jit(solution)/shard_map/vectors/ppermute | solution.py:243
  672.7 5.3 collective-permute-start.57
  (104 other events, 1373.3 us)

commit v4 on v3

--- a/solution.py
+++ b/solution.py
@@ -433,6 +433,40 @@
     )(*operands)
 
 
+def product_in_thirds(name, pairs):
+    size = pairs[0][0].shape[1 - pairs[0][1]]
+    width = pairs[0][2].shape[1 - pairs[0][3]]
+    block = size // 3
+    in_specs, operands = [], []
+    for left, left_dim, right, _ in pairs:
+        in_specs.append(rows_of(left.shape[1], block) if left_dim == 1 else columns_of(left.shape[0], block))
+        in_specs.append(whole(right.shape))
+        operands.extend([left, right])
+
+    def kernel(*refs):
+        total = None
+        for i, (_, left_dim, _, right_dim) in enumerate(pairs):
+            term = dot(refs[2 * i][...], refs[2 * i + 1][...], left_dim, right_dim)
+            total = term if total is None else total + term
+        value = total.astype(BF)
+        for k, ref in enumerate(refs[2 * len(pairs) :]):
+
+            @pl.when(pl.program_id(0) == k)
+            def _(ref=ref):
+                ref[...] = value
+
+    return pl.pallas_call(
+        kernel,
+        grid=(3,),
+        in_specs=in_specs,
+        out_specs=[whole((block, width))] * 3,
+        out_shape=[jax.ShapeDtypeStruct((block, width), BF)] * 3,
+        compiler_params=params(),
+        cost_estimate=FREE,
+        name=name,
+    )(*operands)
+
+
 def store(values, refs, outs):
     for value, ref, out in zip(values, refs, outs):
         if len(out) == 2:
@@ -450,8 +484,22 @@
 
 
 def by_rows(name, inputs, outs, step, block=256):
-    size = inputs[0].shape[0]
-    in_specs = [rows_of(v.shape[1], block) if v.shape[0] == size else whole(v.shape) for v in inputs]
+    size = inputs[0].shape[0] if not isinstance(inputs[0], (list, tuple)) else 3 * inputs[0][0].shape[0]
+    count = size // block
+    each = count // 3
+    in_specs, operands = [], []
+    for value in inputs:
+        if isinstance(value, (list, tuple)):
+            for k, third in enumerate(value):
+                operands.append(third)
+                in_specs.append(
+                    pl.BlockSpec(
+                        (block, third.shape[1]), lambda i, k=k: (jnp.clip(i - each * k, 0, each - 1), 0)
+                    )
+                )
+        else:
+            operands.append(value)
+            in_specs.append(rows_of(value.shape[1], block) if value.shape[0] == size else whole(value.shape))
     out_specs, out_shape = [], []
     for out in outs:
         if len(out) == 2:
@@ -462,19 +510,28 @@
             out_shape.append(jax.ShapeDtypeStruct((1, out[0]), F32))
 
     def kernel(*refs):
-        values = step(*[r[...] for r in refs[: len(inputs)]])
-        store(values, refs[len(inputs) :], outs)
+        place = pl.program_id(0)
+        values, at = [], 0
+        for value in inputs:
+            if isinstance(value, (list, tuple)):
+                one, two, three = [r[...] for r in refs[at : at + 3]]
+                values.append(jnp.where(place < each, one, jnp.where(place < 2 * each, two, three)))
+                at += 3
+            else:
+                values.append(refs[at][...])
+                at += 1
+        store(step(*values), refs[at:], outs)
 
     return pl.pallas_call(
         kernel,
-        grid=(size // block,),
+        grid=(count,),
         in_specs=in_specs,
         out_specs=out_specs,
         out_shape=out_shape,
         compiler_params=params(),
         cost_estimate=FREE,
         name=name,
-    )(*inputs)
+    )(*operands)
 
 
 def first_norm_step(source, vectors):
@@ -884,21 +941,16 @@
         (out_wa, out_wb),
     )
     sums_two = [sums_0, sums_1, sums_2, sums_3]
-    (feed,) = product(
-        "down_product",
-        [(active[0], 1, down_wa, 1), (after(active[1], grad_branch), 1, down_wb, 1)],
-        [(width, BF)],
-        same,
+    feed = product_in_thirds(
+        "down_product", [(active[0], 1, down_wa, 1), (after(active[1], grad_branch), 1, down_wb, 1)]
     )
-    feed_other = jnp.concatenate(
-        [swap_core(feed[i * rows // 3 : (i + 1) * rows // 3], line_d_moved) for i in range(3)], axis=0
-    )
+    feed_other = [swap_core(v, line_d_moved) for v in feed]
 
     def attention_back(i, *earlier):
         dq, dk, dv = attend_back(saved[i], after(grad_atts[i], *earlier), cosine, sine, mask)
         return jnp.stack([v.reshape(2, 160, rows) for v in (dq, dk, dv)], axis=1).reshape(960, rows)
 
-    mixed_far = attention_back(1, feed)
+    mixed_far = attention_back(1, *feed)
     with jax.named_scope("su"):
         far_u.add(mixed_far)
         near_u.add(mixed_far)
@@ -917,16 +969,11 @@
         line_u_moved = line_u.moved
     with jax.named_scope("sd"):
         line_d.step(mixed_near)
-    (part,) = product(
-        "qkv_back",
-        [(after(mixed_near, *sent_u), 0, qkv_wa, 1), (mixed_far, 0, qkv_wb, 1)],
-        [(width, BF)],
-        same,
+    part = product_in_thirds(
+        "qkv_back", [(after(mixed_near, *sent_u), 0, qkv_wa, 1), (mixed_far, 0, qkv_wb, 1)]
     )
-    part_other = jnp.concatenate(
-        [swap_core(part[i * rows // 3 : (i + 1) * rows // 3], *out_pieces, line_u_moved) for i in range(3)], axis=0
-    )
-    grads_near = first_grads(a_one, after(grad_branch, part), mixed_near, saved[0][3], inner)
+    part_other = [swap_core(v, *out_pieces, line_u_moved) for v in part]
+    grads_near = first_grads(a_one, after(grad_branch, *part), mixed_near, saved[0][3], inner)
     with jax.named_scope("sq"):
         near_q, far_q = Scatter(grads_near, back, g, count), Scatter(grads_far, forth, g, count)
         one_q = [far_q.send(grads_near), near_q.send(grads_near)]

time: 696 us -> 689 us (0.990)
  Pallas kernels: 260 us -> 268 us
    pallas_call x3 -> x5, Pallas kernels: 25.4 us -> 59.9 us  [the longest x2 30.4 us: product_in_thirds(): pl.pallas_call(kernel, grid=(3,), in_specs=in_specs, out_specs=[whole((bl...]
    pallas_call x9 -> x7, Pallas kernels: 88 us -> 61.6 us  [product(): pl.pallas_call(kernel, grid=(size // block,), in_specs=in_specs, out_spec...]
    concatenate x2 -> x0, other arithmetic: 7.18 us -> none  [the longest x1 3.63 us: body(): jnp.concatenate([swap_core(feed[i * rows // 3:(i + 1) * rows // 3], line_...]
    unnamed x193 -> x173, local copies, waits for them, and re-layouts: 17.7 us -> 15.1 us
  transfers between devices with their start and end apart: 67 -> 67, of which waited for: 22 -> 22; matrix products, arithmetic and copies ran while one was open for 21% -> 21% of each run, Pallas kernels for 38% -> 39%
where the time goes in v4:
time: 689 us; the launch traced here: 680 us
  Pallas kernels  268 us (39%)
  waiting for transfers between devices  154 us (22%)
  other arithmetic  115 us (17%)
  starting transfers between devices  83.4 us (12%)
  local copies, waits for them, and re-layouts  42.2 us (6%)
  matrix products  12.1 us (2%)
    ppermute x62, waiting for transfers between devices, move(): lax.ppermute(after(value, *earlier) if earlier else value, axis, pairs)  150 us
    ppermute x62, starting transfers between devices, move(): lax.ppermute(after(value, *earlier) if earlier else value, axis, pairs)  71.3 us
    pallas_call x7, Pallas kernels, product(): pl.pallas_call(kernel, grid=(size // block,), in_specs=in_specs, out_spec...  61.6 us
    pallas_call x1, Pallas kernels, feed_back(): pl.pallas_call(kernel, grid=(size // 512,), in_specs=[rows_of(width, 512)...  34.5 us
    pallas_call x2, Pallas kernels, attend_back(): pl.pallas_call(functools.partial(attend_back_kernel, block=256), grid=(he...  31.6 us
    pallas_call x2, Pallas kernels, product_in_thirds(): pl.pallas_call(kernel, grid=(3,), in_specs=in_specs, out_specs=[whole((bl...  30.4 us
    pallas_call x2, Pallas kernels, attend(): pl.pallas_call(functools.partial(attend_kernel, block=256), grid=(heads,)...  30.3 us
    pallas_call x3, Pallas kernels, by_rows(): pl.pallas_call(kernel, grid=(count,), in_specs=in_specs, out_specs=out_sp...  29.5 us
  transfers between devices with their start and end apart: 67, of which 22 were waited for; matrix products, arithmetic and copies ran while one was open for 21% of the time, Pallas kernels for 39%

profile of v4, /device:TPU:0, one launch (start us, length us, event | category | flops | bytes accessed | tf_op | source)
XLA Modules:
  0.0 679.8 jit_solution(11693224336034576056)
XLA Ops:
  3.5 5.1 collective-permute-start.2
  9.3 2.7 select_bitcast_fusion.6
  15.3 2.5 collective-permute-start.5
  28.6 30.5 %collective-permute-done.6 = bf16[320,640]{1,0:T(8,128)(2,1)S(1)} collective-permute-done((bf16[320,640]{1,0:T(8,128)(2,1)S(1)}, bf16[320,640]{1,0:T(8,128)(2,1)S(1)}, u32[]{:S(2)}, u32[]{:S(2)}) %collective-permute-start.6) | collective-permute-done | bytes 409632 | tf_op jit(solution)/shard_map/near/ppermute | solution.py:65
  64.9 3.8 collective-permute-start.14
  69.7 9.4 %collective-permute-done.7 = bf16[320,640]{1,0:T(8,128)(2,1)S(1)} collective-permute-done((bf16[320,640]{1,0:T(8,128)(2,1)S(1)}, bf16[320,640]{1,0:T(8,128)(2,1)S(1)}, u32[]{:S(2)}, u32[]{:S(2)}) %collective-permute-start.7) | collective-permute-done | bytes 409632 | tf_op jit(solution)/shard_map/near/ppermute | solution.py:65
  84.3 17.8 %collective-permute-done.16 = bf16[1,1,320,1280]{3,2,1,0:T(8,128)(2,1)S(1)} collective-permute-done((bf16[1,1,320,1280]{3,2,1,0:T(8,128)(2,1)S(1)}, bf16[1,1,320,1280]{3,2,1,0:T(8,128)(2,1)S(1)}, u32[]{:S(2)}, u32[]{:S(2)}) %collective-permute-start.16) | collective-permute-done | bytes 819232 | tf_op jit(solution)/shard_map/gx/ppermute | solution.py:65
  109.4 8.0 %turn_rows.2 = (bf16[1536,1280]{1,0:T(8,128)(2,1)S(1)}, bf16[1536,1280]{1,0:T(8,128)(2,1)S(1)}) custom-call(s32[1]{0:T(128)} %bitcast.6.start_ref, bf16[768,1280]{1,0:T(8,128)(2,1)S(1)} %get-tuple-element.353.up_ref, bf16[768,1280]{1,0:T(8,128)(2,1)S(1)} %get-tuple-element.352.low_ref, f32[6,1280]{1,0:T(8,128)S(1)} %copy-done.28), custom_call_target="tpu_custom_call" | custom-call | tf_op jit(solution)/shard_map/rows_x/turn_rows/pallas_call | solution.py:224
  119.4 3.9 collective-permute-done.14
  123.3 17.4 %collective-permute-done.13 = bf16[1,2,320,1280]{3,2,1,0:T(8,128)(2,1)} collective-permute-done((bf16[1,2,320,1280]{3,2,1,0:T(8,128)(2,1)}, bf16[1,2,320,1280]{3,2,1,0:T(8,128)(2,1)}, u32[]{:S(2)}, u32[]{:S(2)}) %collective-permute-start.13) | collective-permute-done | bytes 1638432 | tf_op jit(solution)/shard_map/gy/ppermute | solution.py:65
  145.9 2.5 pad_maximum_fusion.8.refs_1_
  150.3 10.3 %collective-permute-done.15 = bf16[1,1,320,1280]{3,2,1,0:T(8,128)(2,1)S(1)} collective-permute-done((bf16[1,1,320,1280]{3,2,1,0:T(8,128)(2,1)}, bf16[1,1,320,1280]{3,2,1,0:T(8,128)(2,1)S(1)}, u32[]{:S(2)}, u32[]{:S(2)}) %collective-permute-start.15) | collective-permute-done | bytes 819232 | tf_op jit(solution)/shard_map/gy/ppermute | solution.py:65
  163.1 2.4 collective-permute-start.18
  166.6 6.1 convolution_add_fusion.1.q_ref.k_ref.v_ref
  172.7 15.1 %attend.2 = (bf16[4,80,1536]{2,1,0:T(8,128)(2,1)S(1)}, bf16[4,80,1536]{2,1,0:T(8,128)(2,1)S(1)}, bf16[4,80,1536]{2,1,0:T(8,128)(2,1)S(1)}, bf16[320,1536]{1,0:T(8,128)(2,1)S(1)}, f32[4,1,1536]{2,1,0:T(1,128)S(1)}) custom-call(f32[1280,1536]{1,0:T(8,128)S(1)} %convolution_add_fusion.1.q_ref.k_ref.v_ref, ...), custom_call_target="tpu_custom_call" | custom-call | tf_op jit(solution)/shard_map/attend/pallas_call | solution.py:325
  187.8 3.0 collective-permute-start.25
  192.5 6.9 %collective-permute-done.18 = bf16[2,1,320,1280]{3,2,1,0:T(8,128)(2,1)} collective-permute-done((bf16[2,1,320,1280]{3,2,1,0:T(8,128)(2,1)}, bf16[2,1,320,1280]{3,2,1,0:T(8,128)(2,1)}, u32[]{:S(2)}, u32[]{:S(2)}) %collective-permute-start.18) | collective-permute-done | bytes 1638432 | tf_op jit(solution)/shard_map/gx/ppermute | solution.py:65
  203.5 6.1 convolution_add_fusion.q_ref.k_ref.v_ref
  210.2 15.3 %attend.3 = (bf16[4,80,1536]{2,1,0:T(8,128)(2,1)S(1)}, bf16[4,80,1536]{2,1,0:T(8,128)(2,1)S(1)}, bf16[4,80,1536]{2,1,0:T(8,128)(2,1)S(1)}, bf16[320,1536]{1,0:T(8,128)(2,1)S(1)}, f32[4,1,1536]{2,1,0:T(1,128)S(1)}) custom-call(f32[1280,1536]{1,0:T(8,128)S(1)} %convolution_add_fusion.q_ref.k_ref.v_ref, f32[1280,1536]{1,0:T(8,128)S(1)} %convolution_add_fusion.q_ref.k_ref.v_ref, ...), custom_call_target="tpu_custom_call" | custom-call | tf_op jit(solution)/shard_map/attend/pallas_call | solution.py:325
  227.8 5.9 out_product.1.refs_1_
  241.0 2.5 pad_maximum_fusion.9.refs_3_
  247.5 4.8 turn_rows.3.refs_0_.g_ref
  254.2 8.9 %norm_two.1 = (bf16[1536,1280]{1,0:T(8,128)(2,1)S(1)}, bf16[1536,1280]{1,0:T(8,128)(2,1)}) custom-call(bf16[1536,1280]{1,0:T(8,128)(2,1)} %copy-done.7, bf16[1536,1280]{1,0:T(8,128)(2,1)} %out_product.1.refs_1_, bf16[1536,1280]{1,0:T(8,128)(2,1)} %collective-permute-done.24.refs_2_, f32[6,1280]{1,0:T(8,128)S(1)} %copy-done.28), custom_call_target="tpu_custom_call" | custom-call | tf_op jit(solution)/shard_map/norm_two/pallas_call | solution.py:525
  265.2 10.4 %up_product.2 = (bf16[1536,1280]{1,0:T(8,128)(2,1)}, bf16[1536,1280]{1,0:T(8,128)(2,1)}) custom-call(bf16[1536,1280]{1,0:T(8,128)(2,1)} %get-tuple-element.204.refs_0_, bf16[1280,1280]{1,0:T(8,128)(2,1)S(1)} %bitcast.151, f32[1,1280]{1,0:T(1,128)S(1)} %bitcast.181), custom_call_target="tpu_custom_call" | custom-call | tf_op jit(solution)/shard_map/up_product/pallas_call | solution.py:424
  275.5 8.4 %down_grads.2 = bf16[1280,1280]{1,0:T(8,128)(2,1)S(1)} custom-call(bf16[1536,1280]{1,0:T(8,128)(2,1)} %copy-done, bf16[1536,1280]{1,0:T(8,128)(2,1)} %get-tuple-element.185.refs_1_.refs_0_), custom_call_target="tpu_custom_call" | custom-call | tf_op jit(solution)/shard_map/down_grads/pallas_call | solution.py:424
  285.9 11.5 %up_product.3 = (bf16[1536,1280]{1,0:T(8,128)(2,1)}, bf16[1536,1280]{1,0:T(8,128)(2,1)}) custom-call(bf16[1536,1280]{1,0:T(8,128)(2,1)} %get-tuple-element.204.refs_0_, bf16[1280,1280]{1,0:T(8,128)(2,1)S(1)} %bitcast.153, f32[1,1280]{1,0:T(1,128)S(1)} %bitcast.180), custom_call_target="tpu_custom_call" | custom-call | tf_op jit(solution)/shard_map/up_product/pallas_call | solution.py:424
  297.4 8.2 %down_grads.3 = bf16[1280,1280]{1,0:T(8,128)(2,1)S(1)} custom-call(bf16[1536,1280]{1,0:T(8,128)(2,1)} %copy-done, bf16[1536,1280]{1,0:T(8,128)(2,1)} %get-tuple-element.211.refs_1_.refs_2_), custom_call_target="tpu_custom_call" | custom-call | tf_op jit(solution)/shard_map/down_grads/pallas_call | solution.py:424
  318.7 34.5 %feed_back.1 = (bf16[1536,1280]{1,0:T(8,128)(2,1)}, bf16[1536,1280]{1,0:T(8,128)(2,1)}, bf16[1536,1280]{1,0:T(8,128)(2,1)}, f32[1,1280]{1,0:T(1,128)}, f32[1,1280]{1,0:T(1,128)}) custom-call(bf16[1536,1280]{1,0:T(8,128)(2,1)} %copy-done, bf16[1280,1280]{1,0:T(8,128)(2,1)} %bitcast.182, bf16[1280,1280]{1,0:T(8,128)(2,1)} %bitcast.184, ...), custom_call_target="tpu_custom_call" | custom-call | tf_op jit(solution)/shard_map/feed_back/pallas_call | solution.py:595
  353.3 2.5 add_convert_fusion.5
  358.5 8.3 %up_grads.2 = bf16[1280,1280]{1,0:T(8,128)(2,1)S(1)} custom-call(bf16[1536,1280]{1,0:T(8,128)(2,1)} %get-tuple-element.204.refs_0_, bf16[1536,1280]{1,0:T(8,128)(2,1)} %get-tuple-element.203.refs_1_), custom_call_target="tpu_custom_call" | custom-call | tf_op jit(solution)/shard_map/up_grads/pallas_call | solution.py:424
  367.2 8.9 %up_grads.3 = bf16[1280,1280]{1,0:T(8,128)(2,1)S(1)} custom-call(bf16[1536,1280]{1,0:T(8,128)(2,1)} %get-tuple-element.204.refs_0_, bf16[1536,1280]{1,0:T(8,128)(2,1)} %get-tuple-element.205.refs_1_), custom_call_target="tpu_custom_call" | custom-call | tf_op jit(solution)/shard_map/up_grads/pallas_call | solution.py:424
  379.8 7.4 %collective-permute-done.34 = bf16[1,1,320,1280]{3,2,1,0:T(8,128)(2,1)S(1)} collective-permute-done((bf16[1,1,320,1280]{3,2,1,0:T(8,128)(2,1)S(1)}, bf16[1,1,320,1280]{3,2,1,0:T(8,128)(2,1)S(1)}, u32[]{:S(2)}, u32[]{:S(2)}) %collective-permute-start.34) | collective-permute-done | bytes 819232 | tf_op jit(solution)/shard_map/sd/ppermute | solution.py:65
  389.2 3.3 collective-permute-start.35
  394.5 14.9 %norm_two_back.1 = (bf16[1536,1280]{1,0:T(8,128)(2,1)}, bf16[320,1536]{1,0:T(8,128)(2,1)S(1)}, bf16[320,1536]{1,0:T(8,128)(2,1)S(1)}, f32[1,1280]{1,0:T(1,128)S(...) custom-call(bf16[1536,1280]{1,0:T(8,128)(2,1)} %get-tuple-element.199.p_ref, ...), custom_call_target="tpu_custom_call" | custom-call | tf_op jit(solution)/shard_map/norm_two_back/pallas_call | solution.py:621
  411.9 16.8 %down_product.1 = (bf16[512,1280]{1,0:T(8,128)(2,1)}, bf16[512,1280]{1,0:T(8,128)(2,1)}, bf16[512,1280]{1,0:T(8,128)(2,1)}) custom-call(bf16[1536,1280]{1,0:T(8,128)(2,1)} %get-tuple-element.185.refs_1_.refs_0_, bf16[1280,1280]{1,0:T(8,128)(2,1)} %bitcast.183, bf16[1536,1280]{1,0:T(8,128)(2,1)} %get-tuple-element.211.refs_1_.refs_2_, ...), custom_call_target="tpu_custom_call" | custom-call | tf_op jit(solution)/shard_map/down_product/pallas_call | solution.py:458
  429.5 15.8 %attend_back.2 = (bf16[4,80,1536]{2,1,0:T(8,128)(2,1)S(1)}, bf16[4,80,1536]{2,1,0:T(8,128)(2,1)S(1)}, bf16[4,80,1536]{2,1,0:T(8,128)(2,1)S(1)}) custom-call(bf16[4,80,1536]{2,1,0:T(8,128)(2,1)} %copy-done.33, bf16[4,80,1536]{2,1,0:T(8,128)(2,1)} %copy-done.34, bf16[4,80,1536]{2,1,0:T(8,128)(2,1)} %copy-done.35, bf16[320,1536]{1,0:T(8,128)(2,1)} %copy-done.14, ...), custom_call_target="tpu_custom_call" | custom-call | tf_op jit(solution)/shard_map/attend_back/pallas_call | solution.py:353
  453.2 8.4 %result.1 = bf16[1536,1280]{1,0:T(8,128)(2,1)} custom-call(bf16[1536,1280]{1,0:T(8,128)(2,1)} %copy-done.8, bf16[512,1280]{1,0:T(8,128)(2,1)} %get-tuple-element.223.refs_1_, bf16[512,1280]{1,0:T(8,128)(2,1)} %get-tuple-element.224.refs_2_, bf16[512,1280]{1,0:T(8,128)(2,1)} %get-tuple-element.225.refs_3_, bf16[512,1280]{1,0:T(8,128)(2,1)} %collective-permute-done.36.refs_4_, ...), custom_call_target="tpu_custom_call" | custom-call | tf_op jit(solution)/shard_map/result/pallas_call | solution.py:525
  462.9 4.8 fusion.6
  469.4 10.1 %first_grads.2 = bf16[1280,1280]{1,0:T(8,128)(2,1)} custom-call(bf16[1536,1280]{1,0:T(8,128)(2,1)} %copy-done.6, bf16[1536,1280]{1,0:T(8,128)(2,1)} %get-tuple-element.249.g_ref.refs_7_, bf16[960,1536]{1,0:T(8,128)(2,1)S(1)} %bitcast.155, bf16[320,1536]{1,0:T(8,128)(2,1)S(1)} %copy-done.15), custom_call_target="tpu_custom_call" | custom-call | tf_op jit(solution)/shard_map/first_grads/pallas_call | solution.py:644
  487.8 15.8 %attend_back.3 = (bf16[4,80,1536]{2,1,0:T(8,128)(2,1)S(1)}, bf16[4,80,1536]{2,1,0:T(8,128)(2,1)S(1)}, bf16[4,80,1536]{2,1,0:T(8,128)(2,1)S(1)}) custom-call(bf16[4,80,1536]{2,1,0:T(8,128)(2,1)} %copy-done.30, bf16[4,80,1536]{2,1,0:T(8,128)(2,1)} %copy-done.31, bf16[4,80,1536]{2,1,0:T(8,128)(2,1)} %copy-done.32, bf16[320,1536]{1,0:T(8,128)(2,1)} %copy-done.12, ...), custom_call_target="tpu_custom_call" | custom-call | tf_op jit(solution)/shard_map/attend_back/pallas_call | solution.py:353
  505.5 13.6 %qkv_back.1 = (bf16[512,1280]{1,0:T(8,128)(2,1)S(1)}, bf16[512,1280]{1,0:T(8,128)(2,1)S(1)}, bf16[512,1280]{1,0:T(8,128)(2,1)}) custom-call(bf16[960,1536]{1,0:T(8,128)(2,1)} %bitcast.157, bf16[1280,960]{1,0:T(8,128)(2,1)} %pad_maximum_fusion.8.refs_1_, bf16[960,1536]{1,0:T(8,128)(2,1)} %bitcast.156, bf16[1280,960]{1,0:T(8,128)(2,1)} %pad_maximum_fusion.9.refs_3_), custom_call_target="tpu_custom_call" | custom-call | tf_op jit(solution)/shard_map/qkv_back/pallas_call | solution.py:458
  519.0 10.1 %first_grads.3 = bf16[1280,1280]{1,0:T(8,128)(2,1)} custom-call(bf16[1536,1280]{1,0:T(8,128)(2,1)} %copy-done.6, bf16[1536,1280]{1,0:T(8,128)(2,1)} %get-tuple-element.249.g_ref.refs_7_, bf16[960,1536]{1,0:T(8,128)(2,1)S(1)} %bitcast.158, bf16[320,1536]{1,0:T(8,128)(2,1)S(1)} %copy-done.13), custom_call_target="tpu_custom_call" | custom-call | tf_op jit(solution)/shard_map/first_grads/pallas_call | solution.py:644
  542.4 12.1 %norm_back.1 = (bf16[1536,1280]{1,0:T(8,128)(2,1)}, f32[1,1280]{1,0:T(1,128)S(1)}, f32[1,1280]{1,0:T(1,128)S(1)}) custom-call(bf16[512,1280]{1,0:T(8,128)(2,1)S(1)} %get-tuple-element.246.refs_0_, bf16[512,1280]{1,0:T(8,128)(2,1)S(1)} %get-tuple-element.247.refs_1_, bf16[512,1280]{1,0:T(8,128)(2,1)} %get-tuple-element.248.refs_2_, ...), custom_call_target="tpu_custom_call" | custom-call | tf_op jit(solution)/shard_map/norm_back/pallas_call | solution.py:525
  555.8 5.0 fusion.4
  562.4 6.0 collective-permute-done.53
  568.4 2.5 add_convert_fusion
  571.5 2.6 add_convert_fusion.1
  581.1 3.6 multiply_subtract_fusion
  584.7 7.5 %collective-permute-done.54 = bf16[1,1,320,1280]{3,2,1,0:T(8,128)(2,1)} collective-permute-done((bf16[1,1,320,1280]{3,2,1,0:T(8,128)(2,1)}, bf16[1,1,320,1280]{3,2,1,0:T(8,128)(2,1)}, u32[]{:S(2)}, u32[]{:S(2)}) %collective-permute-start.54) | collective-permute-done | bytes 819232 | tf_op jit(solution)/shard_map/sq/ppermute | solution.py:65
  592.1 3.3 collective-permute-done.52
  599.2 2.5 add_bitcast_fusion.1
  602.7 3.4 collective-permute-done.58
  607.3 2.3 collective-permute-start.59
  613.4 7.3 %collective-permute-done.55 = bf16[320,1280]{1,0:T(8,128)(2,1)} collective-permute-done((bf16[320,1280]{1,0:T(8,128)(2,1)}, bf16[320,1280]{1,0:T(8,128)(2,1)}, u32[]{:S(2)}, u32[]{:S(2)}) %collective-permute-start.55) | collective-permute-done | bytes 819232 | tf_op jit(solution)/shard_map/sq/ppermute | solution.py:65
  620.7 9.9 %collective-permute-start.62 = (f32[13,1280]{1,0:T(8,128)S(1)}, f32[13,1280]{1,0:T(8,128)S(1)}, u32[]{:S(2)}, u32[]{:S(2)}) collective-permute-start(f32[13,1280]{1,0:T(8,128)S(1)} %pad_maximum_fusion.32), channel_id=1, source_target_pairs={{0,4},{4,0},{1,5},{5,1},{2,6},{6,2},{3,7},{7,3},{8,12},{12,8},{9,1... | collective-permute-start | bytes 199688 | tf_op jit(solution)/shard_map/vectors/ppermute | solution.py:65
  630.6 4.8 multiply_subtract_fusion.1
  637.7 2.2 collective-permute-done.63
  641.1 4.3 collective-permute-done.50
  649.3 8.3 %collective-permute-done.56 = bf16[320,640]{1,0:T(8,128)(2,1)S(1)} collective-permute-done((bf16[320,640]{1,0:T(8,128)(2,1)S(1)}, bf16[320,640]{1,0:T(8,128)(2,1)S(1)}, u32[]{:S(2)}, u32[]{:S(2)}) %collective-permute-start.56) | collective-permute-done | bytes 409632 | tf_op jit(solution)/shard_map/sq/ppermute | solution.py:65
  657.5 2.8 collective-permute-start.65
  660.4 2.3 collective-permute-done.65
  662.8 3.4 collective-permute-start.66
  666.4 2.6 collective-permute-done.66
  675.3 3.1 multiply_subtract_fusion.2
  (462 shorter events, 168.8 us)
Async XLA Ops:
  3.5 15.8 %collective-permute-start.2 = (f32[1,3424]{1,0:T(1,128)S(1)}, f32[1,3424]{1,0:T(1,128)S(1)}, u32[]{:S(2)}, u32[]{:S(2)}) collective-permute-start(f32[1,3424]{1,0:T(1,128)S(1)} %broadcast_in_dim.29), channel_id=1, source_target_pairs={{0,3},{1,2},{2,1},{3,0},{4,7},{5,6},{6,5},{7,4},{8,11},{9,10},{10,... | collective-permute-start | bytes 41096 | tf_op jit(solution)/shard_map/small/ppermute | solution.py:728
  8.6 12.3 %collective-permute-start.1 = (f32[1,3424]{1,0:T(1,128)S(1)}, f32[1,3424]{1,0:T(1,128)S(1)}, u32[]{:S(2)}, u32[]{:S(2)}) collective-permute-start(f32[1,3424]{1,0:T(1,128)S(1)} %broadcast_in_dim.29), channel_id=1, source_target_pairs={{0,2},{1,3},{2,0},{3,1},{4,6},{5,7},{6,4},{7,5},{8,10},{9,11},{10,... | collective-permute-start | bytes 41096 | tf_op jit(solution)/shard_map/small/ppermute | solution.py:728
  8.6 12.3 %collective-permute-start = (f32[1,3424]{1,0:T(1,128)S(1)}, f32[1,3424]{1,0:T(1,128)S(1)}, u32[]{:S(2)}, u32[]{:S(2)}) collective-permute-start(f32[1,3424]{1,0:T(1,128)S(1)} %broadcast_in_dim.29), channel_id=1, source_target_pairs={{0,1},{1,0},{2,3},{3,2},{4,5},{5,4},{6,7},{7,6},{8,9},{9,8},{10,11... | collective-permute-start | bytes 41096 | tf_op jit(solution)/shard_map/small/ppermute | solution.py:728
  12.0 69.7 %collective-permute-start.4 = (bf16[384,1280]{1,0:T(8,128)(2,1)}, bf16[384,1280]{1,0:T(8,128)(2,1)}, u32[]{:S(2)}, u32[]{:S(2)}) collective-permute-start(bf16[384,1280]{1,0:T(8,128)(2,1)} %get-tuple-element.385), channel_id=1, source_target_pairs={{0,1},{1,0},{2,5},{3,4},{4,3},{5,2},{6,7},{7,6},{8,9},{9,8},{10,13... | collective-permute-start | bytes 2949128 | tf_op jit(solution)/shard_map/rows_x/ppermute | solution.py:65
  15.3 8.9 %collective-permute-start.5 = (bf16[160,1920]{1,0:T(8,128)(2,1)S(1)}, bf16[160,1920]{1,0:T(8,128)(2,1)S(1)}, u32[]{:S(2)}, u32[]{:S(2)}) collective-permute-start(bf16[160,1920]{1,0:T(8,128)(2,1)S(1)} %get-tuple-element.151), channel_id=1, source_target_pairs={{0,4},{4,0},{1,5},{5,1},{2,6},{6,2},{3,7},{7,3},{8,12},{12,8},{9,1... | collective-permute-start | bytes 1843208 | tf_op jit(solution)/shard_map/pack/ppermute | solution.py:65
  19.3 63.3 %collective-permute-start.8 = (bf16[384,1280]{1,0:T(8,128)(2,1)S(1)}, bf16[384,1280]{1,0:T(8,128)(2,1)}, u32[]{:S(2)}, u32[]{:S(2)}) collective-permute-start(bf16[384,1280]{1,0:T(8,128)(2,1)S(1)} %get-tuple-element.384), channel_id=1, source_target_pairs={{2,4},{3,5},{4,2},{5,3},{10,12},{11,13},{12,10},{13,11},{18,20},{1... | collective-permute-start | bytes 2949128 | tf_op jit(solution)/shard_map/rows_x/ppermute | solution.py:65
  26.3 32.7 %collective-permute-start.6 = (bf16[320,640]{1,0:T(8,128)(2,1)S(1)}, bf16[320,640]{1,0:T(8,128)(2,1)S(1)}, u32[]{:S(2)}, u32[]{:S(2)}) collective-permute-start(bf16[320,640]{1,0:T(8,128)(2,1)S(1)} %get-tuple-element.400), channel_id=1, source_target_pairs={{0,1},{1,0},{2,3},{3,2},{4,5},{5,4},{6,7},{7,6},{8,9},{9,8},{10,11... | collective-permute-start | bytes 1228808 | tf_op jit(solution)/shard_map/near/ppermute | solution.py:65
  27.0 37.9 %collective-permute-start.11 = (bf16[320,640]{1,0:T(8,128)(2,1)S(1)}, bf16[320,640]{1,0:T(8,128)(2,1)S(1)}, u32[]{:S(2)}, u32[]{:S(2)}) collective-permute-start(bf16[320,640]{1,0:T(8,128)(2,1)S(1)} %get-tuple-element.398), channel_id=1, source_target_pairs={{0,1},{1,0},{2,3},{3,2},{4,5},{5,4},{6,7},{7,6},{8,9},{9,8},{10,11... | collective-permute-start | bytes 1228808 | tf_op jit(solution)/shard_map/near/ppermute | solution.py:65
  60.0 22.6 %collective-permute-start.10 = (bf16[1,1,320,1280]{3,2,1,0:T(8,128)(2,1)S(1)}, bf16[1,1,320,1280]{3,2,1,0:T(8,128)(2,1)S(1)}, u32[]{:S(2)}, u32[]{:S(2)}) collective-permute-start(bf16[1,1,320,1280]{3,2,1,0:T(8,128)(2,1)S(1)} %get-tuple-element.413), channel_id=1, source_target_pairs={{0,8},{8,0},{16,24},{24,16},{1,9},{9,1},{17,25},{25,17},{2,10},{10... | collective-permute-start | bytes 2457608 | tf_op jit(solution)/shard_map/gx/ppermute | solution.py:65
  62.0 17.1 %collective-permute-start.7 = (bf16[320,640]{1,0:T(8,128)(2,1)S(1)}, bf16[320,640]{1,0:T(8,128)(2,1)S(1)}, u32[]{:S(2)}, u32[]{:S(2)}) collective-permute-start(bf16[320,640]{1,0:T(8,128)(2,1)S(1)} %get-tuple-element.152), channel_id=1, source_target_pairs={{0,1},{1,0},{2,3},{3,2},{4,5},{5,4},{6,7},{7,6},{8,9},{9,8},{10,11... | collective-permute-start | bytes 1228808 | tf_op jit(solution)/shard_map/near/ppermute | solution.py:65
  64.9 58.3 %collective-permute-start.14 = (bf16[320,1280]{1,0:T(8,128)(2,1)}, bf16[320,1280]{1,0:T(8,128)(2,1)}, u32[]{:S(2)}, u32[]{:S(2)}) collective-permute-start(bf16[320,1280]{1,0:T(8,128)(2,1)} %get-tuple-element.414), channel_id=1, source_target_pairs={{0,2},{1,3},{2,0},{3,1},{4,6},{5,7},{6,4},{7,5},{8,10},{9,11},{10,... | collective-permute-start | bytes 2457608 | tf_op jit(solution)/shard_map/far/ppermute | solution.py:65
  79.1 25.1 %collective-permute-start.12 = (bf16[1,1,320,1280]{3,2,1,0:T(8,128)(2,1)S(1)}, bf16[1,1,320,1280]{3,2,1,0:T(8,128)(2,1)S(1)}, u32[]{:S(2)}, u32[]{:S(2)}) collective-permute-start(bf16[1,1,320,1280]{3,2,1,0:T(8,128)(2,1)S(1)} %get-tuple-element.410), channel_id=1, source_target_pairs={{0,16},{8,24},{16,0},{24,8},{1,17},{9,25},{17,1},{25,9},{2,18},{10... | collective-permute-start | bytes 2457608 | tf_op jit(solution)/shard_map/gy/ppermute | solution.py:65
  81.7 106.1 %collective-permute-start.21 = (bf16[320,1280]{1,0:T(8,128)(2,1)}, bf16[320,1280]{1,0:T(8,128)(2,1)}, u32[]{:S(2)}, u32[]{:S(2)}) collective-permute-start(bf16[320,1280]{1,0:T(8,128)(2,1)} %get-tuple-element.409), channel_id=1, source_target_pairs={{0,2},{1,3},{2,0},{3,1},{4,6},{5,7},{6,4},{7,5},{8,10},{9,11},{10,... | collective-permute-start | bytes 2457608 | tf_op jit(solution)/shard_map/far/ppermute | solution.py:65
  82.6 19.5 %collective-permute-start.16 = (bf16[1,1,320,1280]{3,2,1,0:T(8,128)(2,1)S(1)}, bf16[1,1,320,1280]{3,2,1,0:T(8,128)(2,1)S(1)}, u32[]{:S(2)}, u32[]{:S(2)}) collective-permute-start(bf16[1,1,320,1280]{3,2,1,0:T(8,128)(2,1)S(1)} %get-tuple-element.163), channel_id=1, source_target_pairs={{0,8},{8,0},{16,24},{24,16},{1,9},{9,1},{17,25},{25,17},{2,10},{10... | collective-permute-start | bytes 2457608 | tf_op jit(solution)/shard_map/gx/ppermute | solution.py:65
  84.2 24.4 %collective-permute-start.9 = (bf16[768,1280]{1,0:T(8,128)(2,1)S(1)}, bf16[768,1280]{1,0:T(8,128)(2,1)S(1)}, u32[]{:S(2)}, u32[]{:S(2)}) collective-permute-start(bf16[768,1280]{1,0:T(8,128)(2,1)S(1)} %pad_maximum_fusion.10), channel_id=1, source_target_pairs={{0,4},{4,0},{1,5},{5,1},{2,6},{6,2},{3,7},{7,3},{8,12},{12,8},{9,1... | collective-permute-start | bytes 5898248 | tf_op jit(solution)/shard_map/rows_x/ppermute | solution.py:65
  104.2 36.5 %collective-permute-start.13 = (bf16[1,2,320,1280]{3,2,1,0:T(8,128)(2,1)}, bf16[1,2,320,1280]{3,2,1,0:T(8,128)(2,1)}, u32[]{:S(2)}, u32[]{:S(2)}) collective-permute-start(bf16[1,2,320,1280]{3,2,1,0:T(8,128)(2,1)} %pad_maximum_fusion.13), channel_id=1, source_target_pairs={{0,16},{8,24},{16,0},{24,8},{1,17},{9,25},{17,1},{25,9},{2,18},{10... | collective-permute-start | bytes 4915208 | tf_op jit(solution)/shard_map/gy/ppermute | solution.py:65
  106.4 37.8 %collective-permute-start.17 = (bf16[2,1,320,1280]{3,2,1,0:T(8,128)(2,1)}, bf16[2,1,320,1280]{3,2,1,0:T(8,128)(2,1)}, u32[]{:S(2)}, u32[]{:S(2)}) collective-permute-start(bf16[2,1,320,1280]{3,2,1,0:T(8,128)(2,1)} %pad_maximum_fusion.15), channel_id=1, source_target_pairs={{0,8},{8,0},{16,24},{24,16},{1,9},{9,1},{17,25},{25,17},{2,10},{10... | collective-permute-start | bytes 4915208 | tf_op jit(solution)/shard_map/gx/ppermute | solution.py:65
  142.6 18.0 %collective-permute-start.15 = (bf16[1,1,320,1280]{3,2,1,0:T(8,128)(2,1)}, bf16[1,1,320,1280]{3,2,1,0:T(8,128)(2,1)S(1)}, u32[]{:S(2)}, u32[]{:S(2)}) collective-permute-start(bf16[1,1,320,1280]{3,2,1,0:T(8,128)(2,1)} %bitcast.16), channel_id=1, source_target_pairs={{0,16},{8,24},{16,0},{24,8},{1,17},{9,25},{17,1},{25,9},{2,18},{10... | collective-permute-start | bytes 2457608 | tf_op jit(solution)/shard_map/gy/ppermute | solution.py:65
  144.2 57.2 %collective-permute-start.20 = (bf16[320,1280]{1,0:T(8,128)(2,1)}, bf16[320,1280]{1,0:T(8,128)(2,1)}, u32[]{:S(2)}, u32[]{:S(2)}) collective-permute-start(bf16[320,1280]{1,0:T(8,128)(2,1)} %get-tuple-element.168), channel_id=1, source_target_pairs={{0,2},{1,3},{2,0},{3,1},{4,6},{5,7},{6,4},{7,5},{8,10},{9,11},{10,... | collective-permute-start | bytes 2457608 | tf_op jit(solution)/shard_map/far/ppermute | solution.py:65
  163.1 36.2 %collective-permute-start.18 = (bf16[2,1,320,1280]{3,2,1,0:T(8,128)(2,1)}, bf16[2,1,320,1280]{3,2,1,0:T(8,128)(2,1)}, u32[]{:S(2)}, u32[]{:S(2)}) collective-permute-start(bf16[2,1,320,1280]{3,2,1,0:T(8,128)(2,1)} %pad_maximum_fusion.14), channel_id=1, source_target_pairs={{0,8},{8,0},{16,24},{24,16},{1,9},{9,1},{17,25},{25,17},{2,10},{10... | collective-permute-start | bytes 4915208 | tf_op jit(solution)/shard_map/gx/ppermute | solution.py:65
  166.3 35.3 %collective-permute-start.19 = (bf16[1,2,320,1280]{3,2,1,0:T(8,128)(2,1)}, bf16[1,2,320,1280]{3,2,1,0:T(8,128)(2,1)}, u32[]{:S(2)}, u32[]{:S(2)}) collective-permute-start(bf16[1,2,320,1280]{3,2,1,0:T(8,128)(2,1)} %pad_maximum_fusion.16), channel_id=1, source_target_pairs={{0,16},{8,24},{16,0},{24,8},{1,17},{9,25},{17,1},{25,9},{2,18},{10... | collective-permute-start | bytes 4915208 | tf_op jit(solution)/shard_map/gy/ppermute | solution.py:65
  187.8 46.2 %collective-permute-start.25 = (bf16[384,1280]{1,0:T(8,128)(2,1)}, bf16[384,1280]{1,0:T(8,128)(2,1)}, u32[]{:S(2)}, u32[]{:S(2)}) collective-permute-start(bf16[384,1280]{1,0:T(8,128)(2,1)} %get-tuple-element.180), channel_id=1, source_target_pairs={{0,1},{1,0},{2,5},{3,4},{4,3},{5,2},{6,7},{7,6},{8,9},{9,8},{10,13... | collective-permute-start | bytes 2949128 | tf_op jit(solution)/shard_map/rows_g/ppermute | solution.py:65
  190.9 43.2 %collective-permute-start.26 = (bf16[384,1280]{1,0:T(8,128)(2,1)}, bf16[384,1280]{1,0:T(8,128)(2,1)}, u32[]{:S(2)}, u32[]{:S(2)}) collective-permute-start(bf16[384,1280]{1,0:T(8,128)(2,1)} %get-tuple-element.182), channel_id=1, source_target_pairs={{2,4},{3,5},{4,2},{5,3},{10,12},{11,13},{12,10},{13,11},{18,20},{1... | collective-permute-start | bytes 2949128 | tf_op jit(solution)/shard_map/rows_g/ppermute | solution.py:65
  201.6 26.2 %collective-permute-start.22 = (bf16[1,1,320,1280]{3,2,1,0:T(8,128)(2,1)}, bf16[1,1,320,1280]{3,2,1,0:T(8,128)(2,1)}, u32[]{:S(2)}, u32[]{:S(2)}) collective-permute-start(bf16[1,1,320,1280]{3,2,1,0:T(8,128)(2,1)} %bitcast.24), channel_id=1, source_target_pairs={{0,8},{8,0},{16,24},{24,16},{1,9},{9,1},{17,25},{25,17},{2,10},{10... | collective-permute-start | bytes 2457608 | tf_op jit(solution)/shard_map/gx/ppermute | solution.py:65
  203.2 24.6 %collective-permute-start.23 = (bf16[1,1,320,1280]{3,2,1,0:T(8,128)(2,1)}, bf16[1,1,320,1280]{3,2,1,0:T(8,128)(2,1)}, u32[]{:S(2)}, u32[]{:S(2)}) collective-permute-start(bf16[1,1,320,1280]{3,2,1,0:T(8,128)(2,1)} %bitcast.25), channel_id=1, source_target_pairs={{0,16},{8,24},{16,0},{24,8},{1,17},{9,25},{17,1},{25,9},{2,18},{10... | collective-permute-start | bytes 2457608 | tf_op jit(solution)/shard_map/gy/ppermute | solution.py:65
  233.8 20.5 %collective-permute-start.24 = (bf16[1536,1280]{1,0:T(8,128)(2,1)}, bf16[1536,1280]{1,0:T(8,128)(2,1)}, u32[]{:S(2)}, u32[]{:S(2)}) collective-permute-start(bf16[1536,1280]{1,0:T(8,128)(2,1)} %out_product.1.refs_1_), channel_id=1, source_target_pairs={{0,4},{4,0},{1,5},{5,1},{2,6},{6,2},{3,7},{7,3},{8,12},{12,8},{9,1... | collective-permute-start | bytes 11796488 | tf_op jit(solution)/shard_map/ppermute | solution.py:65
  235.9 10.8 %collective-permute-start.27 = (bf16[768,1280]{1,0:T(8,128)(2,1)S(1)}, bf16[768,1280]{1,0:T(8,128)(2,1)S(1)}, u32[]{:S(2)}, u32[]{:S(2)}) collective-permute-start(bf16[768,1280]{1,0:T(8,128)(2,1)S(1)} %pad_maximum_fusion.11), channel_id=1, source_target_pairs={{0,4},{4,0},{1,5},{5,1},{2,6},{6,2},{3,7},{7,3},{8,12},{12,8},{9,1... | collective-permute-start | bytes 5898248 | tf_op jit(solution)/shard_map/rows_g/ppermute | solution.py:65
  239.3 44.7 %collective-permute-start.28 = (bf16[1,2,320,1280]{3,2,1,0:T(8,128)(2,1)}, bf16[1,2,320,1280]{3,2,1,0:T(8,128)(2,1)}, u32[]{:S(2)}, u32[]{:S(2)}) collective-permute-start(bf16[1,2,320,1280]{3,2,1,0:T(8,128)(2,1)} %pad_maximum_fusion.17), channel_id=1, source_target_pairs={{0,16},{8,24},{16,0},{24,8},{1,17},{9,25},{17,1},{25,9},{2,18},{10... | collective-permute-start | bytes 4915208 | tf_op jit(solution)/shard_map/gy/ppermute | solution.py:65
  246.3 61.6 %collective-permute-start.29 = (bf16[2,1,320,1280]{3,2,1,0:T(8,128)(2,1)}, bf16[2,1,320,1280]{3,2,1,0:T(8,128)(2,1)}, u32[]{:S(2)}, u32[]{:S(2)}) collective-permute-start(bf16[2,1,320,1280]{3,2,1,0:T(8,128)(2,1)} %pad_maximum_fusion.18), channel_id=1, source_target_pairs={{0,8},{8,0},{16,24},{24,16},{1,9},{9,1},{17,25},{25,17},{2,10},{10... | collective-permute-start | bytes 4915208 | tf_op jit(solution)/shard_map/gx/ppermute | solution.py:65
  307.9 45.3 %collective-permute-start.30 = (bf16[2,1,320,1280]{3,2,1,0:T(8,128)(2,1)}, bf16[2,1,320,1280]{3,2,1,0:T(8,128)(2,1)}, u32[]{:S(2)}, u32[]{:S(2)}) collective-permute-start(bf16[2,1,320,1280]{3,2,1,0:T(8,128)(2,1)} %constant_dynamic-slice_fusion.6), channel_id=1, source_target_pairs={{0,8},{8,0},{16,24},{24,16},{1,9},{9,1},{17,25},{25,17},{2,10},{10... | collective-permute-start | bytes 4915208 | tf_op jit(solution)/shard_map/sd/ppermute | solution.py:65
  310.8 42.4 %collective-permute-start.31 = (bf16[1,2,320,1280]{3,2,1,0:T(8,128)(2,1)}, bf16[1,2,320,1280]{3,2,1,0:T(8,128)(2,1)}, u32[]{:S(2)}, u32[]{:S(2)}) collective-permute-start(bf16[1,2,320,1280]{3,2,1,0:T(8,128)(2,1)} %constant_dynamic-slice_fusion.5), channel_id=1, source_target_pairs={{0,16},{8,24},{16,0},{24,8},{1,17},{9,25},{17,1},{25,9},{2,18},{10... | collective-permute-start | bytes 4915208 | tf_op jit(solution)/shard_map/sd/ppermute | solution.py:65
  353.2 41.2 %collective-permute-start.32 = (bf16[1536,1280]{1,0:T(8,128)(2,1)}, bf16[1536,1280]{1,0:T(8,128)(2,1)}, u32[]{:S(2)}, u32[]{:S(2)}) collective-permute-start(bf16[1536,1280]{1,0:T(8,128)(2,1)} %get-tuple-element.199.p_ref), channel_id=1, source_target_pairs={{0,4},{4,0},{1,5},{5,1},{2,6},{6,2},{3,7},{7,3},{8,12},{12,8},{9,1... | collective-permute-start | bytes 11796488 | tf_op jit(solution)/shard_map/ppermute | solution.py:65
  355.8 21.7 %collective-permute-start.33 = (bf16[1,1,320,1280]{3,2,1,0:T(8,128)(2,1)}, bf16[1,1,320,1280]{3,2,1,0:T(8,128)(2,1)}, u32[]{:S(2)}, u32[]{:S(2)}) collective-permute-start(bf16[1,1,320,1280]{3,2,1,0:T(8,128)(2,1)} %add_convert_fusion.5), channel_id=1, source_target_pairs={{0,16},{8,24},{16,0},{24,8},{1,17},{9,25},{17,1},{25,9},{2,18},{10... | collective-permute-start | bytes 2457608 | tf_op jit(solution)/shard_map/sd/ppermute | solution.py:65
  366.8 20.4 %collective-permute-start.34 = (bf16[1,1,320,1280]{3,2,1,0:T(8,128)(2,1)S(1)}, bf16[1,1,320,1280]{3,2,1,0:T(8,128)(2,1)S(1)}, u32[]{:S(2)}, u32[]{:S(2)}) collective-permute-start(bf16[1,1,320,1280]{3,2,1,0:T(8,128)(2,1)S(1)} %add_convert_fusion.4), channel_id=1, source_target_pairs={{0,8},{8,0},{16,24},{24,16},{1,9},{9,1},{17,25},{25,17},{2,10},{10... | collective-permute-start | bytes 2457608 | tf_op jit(solution)/shard_map/sd/ppermute | solution.py:65
  388.7 57.2 %collective-permute-start.41 = (bf16[2,1,320,1280]{3,2,1,0:T(8,128)(2,1)}, bf16[2,1,320,1280]{3,2,1,0:T(8,128)(2,1)S(1)}, u32[]{:S(2)}, u32[]{:S(2)}) collective-permute-start(bf16[2,1,320,1280]{3,2,1,0:T(8,128)(2,1)} %constant_dynamic-slice_fusion.4), channel_id=1, source_target_pairs={{0,8},{8,0},{16,24},{24,16},{1,9},{9,1},{17,25},{25,17},{2,10},{10... | collective-permute-start | bytes 4915208 | tf_op jit(solution)/shard_map/su/ppermute | solution.py:65
  389.2 39.6 %collective-permute-start.35 = (bf16[320,1280]{1,0:T(8,128)(2,1)S(1)}, bf16[320,1280]{1,0:T(8,128)(2,1)S(1)}, u32[]{:S(2)}, u32[]{:S(2)}) collective-permute-start(bf16[320,1280]{1,0:T(8,128)(2,1)S(1)} %pad_maximum_fusion.24), channel_id=1, source_target_pairs={{0,1},{1,0},{2,3},{3,2},{4,5},{5,4},{6,7},{7,6},{8,9},{9,8},{10,11... | collective-permute-start | bytes 2457608 | tf_op jit(solution)/shard_map/sd/ppermute | solution.py:65
  393.7 56.2 %collective-permute-start.42 = (bf16[1,2,320,1280]{3,2,1,0:T(8,128)(2,1)}, bf16[1,2,320,1280]{3,2,1,0:T(8,128)(2,1)}, u32[]{:S(2)}, u32[]{:S(2)}) collective-permute-start(bf16[1,2,320,1280]{3,2,1,0:T(8,128)(2,1)} %constant_dynamic-slice_fusion.3), channel_id=1, source_target_pairs={{0,16},{8,24},{16,0},{24,8},{1,17},{9,25},{17,1},{25,9},{2,18},{10... | collective-permute-start | bytes 4915208 | tf_op jit(solution)/shard_map/su/ppermute | solution.py:65
  428.8 24.4 %collective-permute-start.36 = (bf16[512,1280]{1,0:T(8,128)(2,1)}, bf16[512,1280]{1,0:T(8,128)(2,1)}, u32[]{:S(2)}, u32[]{:S(2)}) collective-permute-start(bf16[512,1280]{1,0:T(8,128)(2,1)} %get-tuple-element.223.refs_1_), channel_id=1, source_target_pairs={{0,4},{4,0},{1,5},{5,1},{2,6},{6,2},{3,7},{7,3},{8,12},{12,8},{9,1... | collective-permute-start | bytes 3932168 | tf_op jit(solution)/shard_map/ppermute | solution.py:65
  428.9 24.3 %collective-permute-start.37 = (bf16[512,1280]{1,0:T(8,128)(2,1)}, bf16[512,1280]{1,0:T(8,128)(2,1)}, u32[]{:S(2)}, u32[]{:S(2)}) collective-permute-start(bf16[512,1280]{1,0:T(8,128)(2,1)} %get-tuple-element.224.refs_2_), channel_id=1, source_target_pairs={{0,4},{4,0},{1,5},{5,1},{2,6},{6,2},{3,7},{7,3},{8,12},{12,8},{9,1... | collective-permute-start | bytes 3932168 | tf_op jit(solution)/shard_map/ppermute | solution.py:65
  429.4 23.9 %collective-permute-start.38 = (bf16[512,1280]{1,0:T(8,128)(2,1)}, bf16[512,1280]{1,0:T(8,128)(2,1)}, u32[]{:S(2)}, u32[]{:S(2)}) collective-permute-start(bf16[512,1280]{1,0:T(8,128)(2,1)} %get-tuple-element.225.refs_3_), channel_id=1, source_target_pairs={{0,4},{4,0},{1,5},{5,1},{2,6},{6,2},{3,7},{7,3},{8,12},{12,8},{9,1... | collective-permute-start | bytes 3932168 | tf_op jit(solution)/shard_map/ppermute | solution.py:65
  447.3 32.2 %collective-permute-start.43 = (bf16[1,1,320,1280]{3,2,1,0:T(8,128)(2,1)}, bf16[1,1,320,1280]{3,2,1,0:T(8,128)(2,1)}, u32[]{:S(2)}, u32[]{:S(2)}) collective-permute-start(bf16[1,1,320,1280]{3,2,1,0:T(8,128)(2,1)} %add_convert_fusion.3), channel_id=1, source_target_pairs={{0,16},{8,24},{16,0},{24,8},{1,17},{9,25},{17,1},{25,9},{2,18},{10... | collective-permute-start | bytes 2457608 | tf_op jit(solution)/shard_map/su/ppermute | solution.py:65
  451.5 29.7 %collective-permute-start.44 = (bf16[1,1,320,1280]{3,2,1,0:T(8,128)(2,1)S(1)}, bf16[1,1,320,1280]{3,2,1,0:T(8,128)(2,1)S(1)}, u32[]{:S(2)}, u32[]{:S(2)}) collective-permute-start(bf16[1,1,320,1280]{3,2,1,0:T(8,128)(2,1)S(1)} %add_convert_fusion.2), channel_id=1, source_target_pairs={{0,8},{8,0},{16,24},{24,16},{1,9},{9,1},{17,25},{25,17},{2,10},{10... | collective-permute-start | bytes 2457608 | tf_op jit(solution)/shard_map/su/ppermute | solution.py:65
  467.6 66.0 %collective-permute-start.39 = (bf16[384,1280]{1,0:T(8,128)(2,1)}, bf16[384,1280]{1,0:T(8,128)(2,1)}, u32[]{:S(2)}, u32[]{:S(2)}) collective-permute-start(bf16[384,1280]{1,0:T(8,128)(2,1)} %get-tuple-element.349), channel_id=1, source_target_pairs={{1,0},{0,1},{5,2},{4,3},{3,4},{2,5},{7,6},{6,7},{9,8},{8,9},{13,10... | collective-permute-start | bytes 2949128 | tf_op jit(solution)/shard_map/rows_out/ppermute | solution.py:65
  467.6 66.0 %collective-permute-start.40 = (bf16[384,1280]{1,0:T(8,128)(2,1)S(1)}, bf16[384,1280]{1,0:T(8,128)(2,1)}, u32[]{:S(2)}, u32[]{:S(2)}) collective-permute-start(bf16[384,1280]{1,0:T(8,128)(2,1)S(1)} %get-tuple-element.348), channel_id=1, source_target_pairs={{4,2},{5,3},{2,4},{3,5},{12,10},{13,11},{10,12},{11,13},{20,18},{2... | collective-permute-start | bytes 2949128 | tf_op jit(solution)/shard_map/rows_out/ppermute | solution.py:65
  484.6 49.1 %collective-permute-start.45 = (bf16[320,1280]{1,0:T(8,128)(2,1)}, bf16[320,1280]{1,0:T(8,128)(2,1)S(1)}, u32[]{:S(2)}, u32[]{:S(2)}) collective-permute-start(bf16[320,1280]{1,0:T(8,128)(2,1)} %pad_maximum_fusion.25), channel_id=1, source_target_pairs={{0,1},{1,0},{2,3},{3,2},{4,5},{5,4},{6,7},{7,6},{8,9},{9,8},{10,11... | collective-permute-start | bytes 2457608 | tf_op jit(solution)/shard_map/su/ppermute | solution.py:65
  530.5 37.9 %collective-permute-start.53 = (bf16[2,1,320,1280]{3,2,1,0:T(8,128)(2,1)}, bf16[2,1,320,1280]{3,2,1,0:T(8,128)(2,1)}, u32[]{:S(2)}, u32[]{:S(2)}) collective-permute-start(bf16[2,1,320,1280]{3,2,1,0:T(8,128)(2,1)} %constant_dynamic-slice_fusion), channel_id=1, source_target_pairs={{0,8},{8,0},{16,24},{24,16},{1,9},{9,1},{17,25},{25,17},{2,10},{10... | collective-permute-start | bytes 4915208 | tf_op jit(solution)/shard_map/sq/ppermute | solution.py:65
  533.0 38.5 %collective-permute-start.51 = (bf16[1,2,320,1280]{3,2,1,0:T(8,128)(2,1)}, bf16[1,2,320,1280]{3,2,1,0:T(8,128)(2,1)}, u32[]{:S(2)}, u32[]{:S(2)}) collective-permute-start(bf16[1,2,320,1280]{3,2,1,0:T(8,128)(2,1)} %constant_dynamic-slice_fusion.1), channel_id=1, source_target_pairs={{0,16},{8,24},{16,0},{24,8},{1,17},{9,25},{17,1},{25,9},{2,18},{10... | collective-permute-start | bytes 4915208 | tf_op jit(solution)/shard_map/sq/ppermute | solution.py:65
  533.7 7.8 %collective-permute-start.46 = (bf16[512,1280]{1,0:T(8,128)(2,1)S(1)}, bf16[512,1280]{1,0:T(8,128)(2,1)}, u32[]{:S(2)}, u32[]{:S(2)}) collective-permute-start(bf16[512,1280]{1,0:T(8,128)(2,1)S(1)} %get-tuple-element.246.refs_0_), channel_id=1, source_target_pairs={{0,4},{4,0},{1,5},{5,1},{2,6},{6,2},{3,7},{7,3},{8,12},{12,8},{9,1... | collective-permute-start | bytes 3932168 | tf_op jit(solution)/shard_map/ppermute | solution.py:65
  535.5 6.9 %collective-permute-start.47 = (bf16[512,1280]{1,0:T(8,128)(2,1)S(1)}, bf16[512,1280]{1,0:T(8,128)(2,1)}, u32[]{:S(2)}, u32[]{:S(2)}) collective-permute-start(bf16[512,1280]{1,0:T(8,128)(2,1)S(1)} %get-tuple-element.247.refs_1_), channel_id=1, source_target_pairs={{0,4},{4,0},{1,5},{5,1},{2,6},{6,2},{3,7},{7,3},{8,12},{12,8},{9,1... | collective-permute-start | bytes 3932168 | tf_op jit(solution)/shard_map/ppermute | solution.py:65
  535.6 6.8 %collective-permute-start.48 = (bf16[512,1280]{1,0:T(8,128)(2,1)}, bf16[512,1280]{1,0:T(8,128)(2,1)}, u32[]{:S(2)}, u32[]{:S(2)}) collective-permute-start(bf16[512,1280]{1,0:T(8,128)(2,1)} %get-tuple-element.248.refs_2_), channel_id=1, source_target_pairs={{0,4},{4,0},{1,5},{5,1},{2,6},{6,2},{3,7},{7,3},{8,12},{12,8},{9,1... | collective-permute-start | bytes 3932168 | tf_op jit(solution)/shard_map/ppermute | solution.py:65
  541.5 34.7 %collective-permute-start.60 = (bf16[320,640]{1,0:T(8,128)(2,1)S(1)}, bf16[320,640]{1,0:T(8,128)(2,1)S(1)}, u32[]{:S(2)}, u32[]{:S(2)}) collective-permute-start(bf16[320,640]{1,0:T(8,128)(2,1)S(1)} %slice.486), channel_id=1, source_target_pairs={{0,2},{1,3},{2,0},{3,1},{4,6},{5,7},{6,4},{7,5},{8,10},{9,11},{10,... | collective-permute-start | bytes 1228808 | tf_op jit(solution)/shard_map/sd/ppermute | solution.py:65
  560.8 36.4 %collective-permute-start.49 = (bf16[384,1280]{1,0:T(8,128)(2,1)}, bf16[384,1280]{1,0:T(8,128)(2,1)}, u32[]{:S(2)}, u32[]{:S(2)}) collective-permute-start(bf16[384,1280]{1,0:T(8,128)(2,1)} %get-tuple-element.346), channel_id=1, source_target_pairs={{4,2},{5,3},{2,4},{3,5},{12,10},{13,11},{10,12},{11,13},{20,18},{2... | collective-permute-start | bytes 2949128 | tf_op jit(solution)/shard_map/rows_dx/ppermute | solution.py:65
  570.9 21.2 %collective-permute-start.54 = (bf16[1,1,320,1280]{3,2,1,0:T(8,128)(2,1)}, bf16[1,1,320,1280]{3,2,1,0:T(8,128)(2,1)}, u32[]{:S(2)}, u32[]{:S(2)}) collective-permute-start(bf16[1,1,320,1280]{3,2,1,0:T(8,128)(2,1)} %add_convert_fusion), channel_id=1, source_target_pairs={{0,16},{8,24},{16,0},{24,8},{1,17},{9,25},{17,1},{25,9},{2,18},{10... | collective-permute-start | bytes 2457608 | tf_op jit(solution)/shard_map/sq/ppermute | solution.py:65
  574.1 21.4 %collective-permute-start.52 = (bf16[1,1,320,1280]{3,2,1,0:T(8,128)(2,1)}, bf16[1,1,320,1280]{3,2,1,0:T(8,128)(2,1)}, u32[]{:S(2)}, u32[]{:S(2)}) collective-permute-start(bf16[1,1,320,1280]{3,2,1,0:T(8,128)(2,1)} %add_convert_fusion.1), channel_id=1, source_target_pairs={{0,8},{8,0},{16,24},{24,16},{1,9},{9,1},{17,25},{25,17},{2,10},{10... | collective-permute-start | bytes 2457608 | tf_op jit(solution)/shard_map/sq/ppermute | solution.py:65
  575.6 30.6 %collective-permute-start.58 = (bf16[320,640]{1,0:T(8,128)(2,1)}, bf16[320,640]{1,0:T(8,128)(2,1)}, u32[]{:S(2)}, u32[]{:S(2)}) collective-permute-start(bf16[320,640]{1,0:T(8,128)(2,1)} %slice.487), channel_id=1, source_target_pairs={{0,2},{1,3},{2,0},{3,1},{4,6},{5,7},{6,4},{7,5},{8,10},{9,11},{10,... | collective-permute-start | bytes 1228808 | tf_op jit(solution)/shard_map/su/ppermute | solution.py:65
  602.7 18.0 %collective-permute-start.55 = (bf16[320,1280]{1,0:T(8,128)(2,1)}, bf16[320,1280]{1,0:T(8,128)(2,1)}, u32[]{:S(2)}, u32[]{:S(2)}) collective-permute-start(bf16[320,1280]{1,0:T(8,128)(2,1)} %pad_maximum_fusion.26), channel_id=1, source_target_pairs={{0,1},{1,0},{2,3},{3,2},{4,5},{5,4},{6,7},{7,6},{8,9},{9,8},{10,11... | collective-permute-start | bytes 2457608 | tf_op jit(solution)/shard_map/sq/ppermute | solution.py:65
  609.6 35.8 %collective-permute-start.50 = (bf16[384,1280]{1,0:T(8,128)(2,1)}, bf16[384,1280]{1,0:T(8,128)(2,1)}, u32[]{:S(2)}, u32[]{:S(2)}) collective-permute-start(bf16[384,1280]{1,0:T(8,128)(2,1)} %get-tuple-element.253), channel_id=1, source_target_pairs={{1,0},{0,1},{5,2},{4,3},{3,4},{2,5},{7,6},{6,7},{9,8},{8,9},{13,10... | collective-permute-start | bytes 2949128 | tf_op jit(solution)/shard_map/rows_dx/ppermute | solution.py:65
  620.7 14.7 %collective-permute-start.62 = (f32[13,1280]{1,0:T(8,128)S(1)}, f32[13,1280]{1,0:T(8,128)S(1)}, u32[]{:S(2)}, u32[]{:S(2)}) collective-permute-start(f32[13,1280]{1,0:T(8,128)S(1)} %pad_maximum_fusion.32), channel_id=1, source_target_pairs={{0,4},{4,0},{1,5},{5,1},{2,6},{6,2},{3,7},{7,3},{8,12},{12,8},{9,1... | collective-permute-start | bytes 199688 | tf_op jit(solution)/shard_map/vectors/ppermute | solution.py:65
  635.4 4.5 collective-permute-start.63
  637.6 19.9 %collective-permute-start.56 = (bf16[320,640]{1,0:T(8,128)(2,1)S(1)}, bf16[320,640]{1,0:T(8,128)(2,1)S(1)}, u32[]{:S(2)}, u32[]{:S(2)}) collective-permute-start(bf16[320,640]{1,0:T(8,128)(2,1)S(1)} %slice.488), channel_id=1, source_target_pairs={{0,2},{1,3},{2,0},{3,1},{4,6},{5,7},{6,4},{7,5},{8,10},{9,11},{10,... | collective-permute-start | bytes 1228808 | tf_op jit(solution)/shard_map/sq/ppermute | solution.py:65
  639.9 9.3 %collective-permute-start.64 = (f32[13,1280]{1,0:T(8,128)S(1)}, f32[13,1280]{1,0:T(8,128)S(1)}, u32[]{:S(2)}, u32[]{:S(2)}) collective-permute-start(f32[13,1280]{1,0:T(8,128)S(1)} %add.432), channel_id=1, source_target_pairs={{0,16},{8,24},{16,0},{24,8},{1,17},{9,25},{17,1},{25,9},{2,18},{10... | collective-permute-start | bytes 199688 | tf_op jit(solution)/shard_map/vectors/ppermute | solution.py:65
  657.5 5.2 collective-permute-start.65
  662.8 6.1 collective-permute-start.66
  666.3 4.1 collective-permute-start.57
  (95 other events, 1319.8 us)

commit v5 on v4

--- a/solution.py
+++ b/solution.py
@@ -565,7 +565,7 @@
 
 def hidden_step(total, bias):
     hidden = total + bias
-    gate = 1.0 / (1.0 + jnp.exp(-GELU_SLOPE * hidden))
+    gate = 0.5 + 0.5 * jnp.tanh((0.5 * GELU_SLOPE) * hidden)
     return hidden * gate, gate + GELU_SLOPE * hidden * gate * (1.0 - gate)
 
 

time: 689 us -> 688 us (level)
  no operation moved by 1% of the time
where the time goes in v5:
time: 688 us; the launch traced here: 679 us
  Pallas kernels  267 us (39%)
  waiting for transfers between devices  154 us (22%)
  other arithmetic  115 us (17%)
  starting transfers between devices  84.2 us (12%)
  local copies, waits for them, and re-layouts  42.2 us (6%)
  matrix products  12.1 us (2%)
    ppermute x62, waiting for transfers between devices, move(): lax.ppermute(after(value, *earlier) if earlier else value, axis, pairs)  149 us
    ppermute x62, starting transfers between devices, move(): lax.ppermute(after(value, *earlier) if earlier else value, axis, pairs)  72.2 us
    pallas_call x7, Pallas kernels, product(): pl.pallas_call(kernel, grid=(size // block,), in_specs=in_specs, out_spec...  61 us
    pallas_call x1, Pallas kernels, feed_back(): pl.pallas_call(kernel, grid=(size // 512,), in_specs=[rows_of(width, 512)...  34.5 us
    pallas_call x2, Pallas kernels, attend_back(): pl.pallas_call(functools.partial(attend_back_kernel, block=256), grid=(he...  31.6 us
    pallas_call x2, Pallas kernels, product_in_thirds(): pl.pallas_call(kernel, grid=(3,), in_specs=in_specs, out_specs=[whole((bl...  30.4 us
    pallas_call x2, Pallas kernels, attend(): pl.pallas_call(functools.partial(attend_kernel, block=256), grid=(heads,)...  30.3 us
    pallas_call x3, Pallas kernels, by_rows(): pl.pallas_call(kernel, grid=(count,), in_specs=in_specs, out_specs=out_sp...  29.4 us
  transfers between devices with their start and end apart: 67, of which 22 were waited for; matrix products, arithmetic and copies ran while one was open for 21% of the time, Pallas kernels for 39%

profile of v5, /device:TPU:0, one launch (start us, length us, event | category | flops | bytes accessed | tf_op | source)
XLA Modules:
  0.0 679.2 jit_solution(17067454835940595096)
XLA Ops:
  3.5 5.1 collective-permute-start.2
  9.3 2.7 select_bitcast_fusion.6
  15.3 2.5 collective-permute-start.5
  28.6 30.5 %collective-permute-done.6 = bf16[320,640]{1,0:T(8,128)(2,1)S(1)} collective-permute-done((bf16[320,640]{1,0:T(8,128)(2,1)S(1)}, bf16[320,640]{1,0:T(8,128)(2,1)S(1)}, u32[]{:S(2)}, u32[]{:S(2)}) %collective-permute-start.6) | collective-permute-done | bytes 409632 | tf_op jit(solution)/shard_map/near/ppermute | solution.py:65
  64.9 3.8 collective-permute-start.14
  69.7 9.4 %collective-permute-done.7 = bf16[320,640]{1,0:T(8,128)(2,1)S(1)} collective-permute-done((bf16[320,640]{1,0:T(8,128)(2,1)S(1)}, bf16[320,640]{1,0:T(8,128)(2,1)S(1)}, u32[]{:S(2)}, u32[]{:S(2)}) %collective-permute-start.7) | collective-permute-done | bytes 409632 | tf_op jit(solution)/shard_map/near/ppermute | solution.py:65
  84.3 17.8 %collective-permute-done.16 = bf16[1,1,320,1280]{3,2,1,0:T(8,128)(2,1)S(1)} collective-permute-done((bf16[1,1,320,1280]{3,2,1,0:T(8,128)(2,1)S(1)}, bf16[1,1,320,1280]{3,2,1,0:T(8,128)(2,1)S(1)}, u32[]{:S(2)}, u32[]{:S(2)}) %collective-permute-start.16) | collective-permute-done | bytes 819232 | tf_op jit(solution)/shard_map/gx/ppermute | solution.py:65
  109.4 8.0 %turn_rows.2 = (bf16[1536,1280]{1,0:T(8,128)(2,1)S(1)}, bf16[1536,1280]{1,0:T(8,128)(2,1)S(1)}) custom-call(s32[1]{0:T(128)} %bitcast.6.start_ref, bf16[768,1280]{1,0:T(8,128)(2,1)S(1)} %get-tuple-element.353.up_ref, bf16[768,1280]{1,0:T(8,128)(2,1)S(1)} %get-tuple-element.352.low_ref, f32[6,1280]{1,0:T(8,128)S(1)} %copy-done.28), custom_call_target="tpu_custom_call" | custom-call | tf_op jit(solution)/shard_map/rows_x/turn_rows/pallas_call | solution.py:224
  119.4 3.9 collective-permute-done.14
  123.3 17.4 %collective-permute-done.13 = bf16[1,2,320,1280]{3,2,1,0:T(8,128)(2,1)} collective-permute-done((bf16[1,2,320,1280]{3,2,1,0:T(8,128)(2,1)}, bf16[1,2,320,1280]{3,2,1,0:T(8,128)(2,1)}, u32[]{:S(2)}, u32[]{:S(2)}) %collective-permute-start.13) | collective-permute-done | bytes 1638432 | tf_op jit(solution)/shard_map/gy/ppermute | solution.py:65
  145.9 2.5 pad_maximum_fusion.8.refs_1_
  150.3 10.3 %collective-permute-done.15 = bf16[1,1,320,1280]{3,2,1,0:T(8,128)(2,1)S(1)} collective-permute-done((bf16[1,1,320,1280]{3,2,1,0:T(8,128)(2,1)}, bf16[1,1,320,1280]{3,2,1,0:T(8,128)(2,1)S(1)}, u32[]{:S(2)}, u32[]{:S(2)}) %collective-permute-start.15) | collective-permute-done | bytes 819232 | tf_op jit(solution)/shard_map/gy/ppermute | solution.py:65
  163.1 2.4 collective-permute-start.18
  166.6 6.1 convolution_add_fusion.1.q_ref.k_ref.v_ref
  172.7 15.1 %attend.2 = (bf16[4,80,1536]{2,1,0:T(8,128)(2,1)S(1)}, bf16[4,80,1536]{2,1,0:T(8,128)(2,1)S(1)}, bf16[4,80,1536]{2,1,0:T(8,128)(2,1)S(1)}, bf16[320,1536]{1,0:T(8,128)(2,1)S(1)}, f32[4,1,1536]{2,1,0:T(1,128)S(1)}) custom-call(f32[1280,1536]{1,0:T(8,128)S(1)} %convolution_add_fusion.1.q_ref.k_ref.v_ref, ...), custom_call_target="tpu_custom_call" | custom-call | tf_op jit(solution)/shard_map/attend/pallas_call | solution.py:325
  187.8 3.0 collective-permute-start.25
  192.5 6.9 %collective-permute-done.18 = bf16[2,1,320,1280]{3,2,1,0:T(8,128)(2,1)} collective-permute-done((bf16[2,1,320,1280]{3,2,1,0:T(8,128)(2,1)}, bf16[2,1,320,1280]{3,2,1,0:T(8,128)(2,1)}, u32[]{:S(2)}, u32[]{:S(2)}) %collective-permute-start.18) | collective-permute-done | bytes 1638432 | tf_op jit(solution)/shard_map/gx/ppermute | solution.py:65
  203.5 6.1 convolution_add_fusion.q_ref.k_ref.v_ref
  210.2 15.3 %attend.3 = (bf16[4,80,1536]{2,1,0:T(8,128)(2,1)S(1)}, bf16[4,80,1536]{2,1,0:T(8,128)(2,1)S(1)}, bf16[4,80,1536]{2,1,0:T(8,128)(2,1)S(1)}, bf16[320,1536]{1,0:T(8,128)(2,1)S(1)}, f32[4,1,1536]{2,1,0:T(1,128)S(1)}) custom-call(f32[1280,1536]{1,0:T(8,128)S(1)} %convolution_add_fusion.q_ref.k_ref.v_ref, f32[1280,1536]{1,0:T(8,128)S(1)} %convolution_add_fusion.q_ref.k_ref.v_ref, ...), custom_call_target="tpu_custom_call" | custom-call | tf_op jit(solution)/shard_map/attend/pallas_call | solution.py:325
  227.8 5.9 out_product.1.refs_1_
  241.0 2.5 pad_maximum_fusion.9.refs_3_
  247.5 4.8 turn_rows.3.refs_0_.g_ref
  254.2 8.9 %norm_two.1 = (bf16[1536,1280]{1,0:T(8,128)(2,1)S(1)}, bf16[1536,1280]{1,0:T(8,128)(2,1)}) custom-call(bf16[1536,1280]{1,0:T(8,128)(2,1)} %copy-done.7, bf16[1536,1280]{1,0:T(8,128)(2,1)} %out_product.1.refs_1_, bf16[1536,1280]{1,0:T(8,128)(2,1)} %collective-permute-done.24.refs_2_, f32[6,1280]{1,0:T(8,128)S(1)} %copy-done.28), custom_call_target="tpu_custom_call" | custom-call | tf_op jit(solution)/shard_map/norm_two/pallas_call | solution.py:525
  265.2 10.1 %up_product.2 = (bf16[1536,1280]{1,0:T(8,128)(2,1)}, bf16[1536,1280]{1,0:T(8,128)(2,1)}) custom-call(bf16[1536,1280]{1,0:T(8,128)(2,1)} %get-tuple-element.204.refs_0_, bf16[1280,1280]{1,0:T(8,128)(2,1)S(1)} %bitcast.151, f32[1,1280]{1,0:T(1,128)S(1)} %bitcast.181), custom_call_target="tpu_custom_call" | custom-call | tf_op jit(solution)/shard_map/up_product/pallas_call | solution.py:424
  275.3 8.4 %down_grads.2 = bf16[1280,1280]{1,0:T(8,128)(2,1)S(1)} custom-call(bf16[1536,1280]{1,0:T(8,128)(2,1)} %copy-done, bf16[1536,1280]{1,0:T(8,128)(2,1)} %get-tuple-element.185.refs_1_.refs_0_), custom_call_target="tpu_custom_call" | custom-call | tf_op jit(solution)/shard_map/down_grads/pallas_call | solution.py:424
  285.6 11.2 %up_product.3 = (bf16[1536,1280]{1,0:T(8,128)(2,1)}, bf16[1536,1280]{1,0:T(8,128)(2,1)}) custom-call(bf16[1536,1280]{1,0:T(8,128)(2,1)} %get-tuple-element.204.refs_0_, bf16[1280,1280]{1,0:T(8,128)(2,1)S(1)} %bitcast.153, f32[1,1280]{1,0:T(1,128)S(1)} %bitcast.180), custom_call_target="tpu_custom_call" | custom-call | tf_op jit(solution)/shard_map/up_product/pallas_call | solution.py:424
  296.8 8.2 %down_grads.3 = bf16[1280,1280]{1,0:T(8,128)(2,1)S(1)} custom-call(bf16[1536,1280]{1,0:T(8,128)(2,1)} %copy-done, bf16[1536,1280]{1,0:T(8,128)(2,1)} %get-tuple-element.211.refs_1_.refs_2_), custom_call_target="tpu_custom_call" | custom-call | tf_op jit(solution)/shard_map/down_grads/pallas_call | solution.py:424
  318.2 34.5 %feed_back.1 = (bf16[1536,1280]{1,0:T(8,128)(2,1)}, bf16[1536,1280]{1,0:T(8,128)(2,1)}, bf16[1536,1280]{1,0:T(8,128)(2,1)}, f32[1,1280]{1,0:T(1,128)}, f32[1,1280]{1,0:T(1,128)}) custom-call(bf16[1536,1280]{1,0:T(8,128)(2,1)} %copy-done, bf16[1280,1280]{1,0:T(8,128)(2,1)} %bitcast.182, bf16[1280,1280]{1,0:T(8,128)(2,1)} %bitcast.184, ...), custom_call_target="tpu_custom_call" | custom-call | tf_op jit(solution)/shard_map/feed_back/pallas_call | solution.py:595
  352.8 2.5 add_convert_fusion.5
  357.9 8.3 %up_grads.2 = bf16[1280,1280]{1,0:T(8,128)(2,1)S(1)} custom-call(bf16[1536,1280]{1,0:T(8,128)(2,1)} %get-tuple-element.204.refs_0_, bf16[1536,1280]{1,0:T(8,128)(2,1)} %get-tuple-element.203.refs_1_), custom_call_target="tpu_custom_call" | custom-call | tf_op jit(solution)/shard_map/up_grads/pallas_call | solution.py:424
  366.7 8.9 %up_grads.3 = bf16[1280,1280]{1,0:T(8,128)(2,1)S(1)} custom-call(bf16[1536,1280]{1,0:T(8,128)(2,1)} %get-tuple-element.204.refs_0_, bf16[1536,1280]{1,0:T(8,128)(2,1)} %get-tuple-element.205.refs_1_), custom_call_target="tpu_custom_call" | custom-call | tf_op jit(solution)/shard_map/up_grads/pallas_call | solution.py:424
  377.0 2.2 add_bitcast_fusion.4
  379.2 7.4 %collective-permute-done.34 = bf16[1,1,320,1280]{3,2,1,0:T(8,128)(2,1)S(1)} collective-permute-done((bf16[1,1,320,1280]{3,2,1,0:T(8,128)(2,1)S(1)}, bf16[1,1,320,1280]{3,2,1,0:T(8,128)(2,1)S(1)}, u32[]{:S(2)}, u32[]{:S(2)}) %collective-permute-start.34) | collective-permute-done | bytes 819232 | tf_op jit(solution)/shard_map/sd/ppermute | solution.py:65
  388.7 3.3 collective-permute-start.35
  394.0 14.9 %norm_two_back.1 = (bf16[1536,1280]{1,0:T(8,128)(2,1)}, bf16[320,1536]{1,0:T(8,128)(2,1)S(1)}, bf16[320,1536]{1,0:T(8,128)(2,1)S(1)}, f32[1,1280]{1,0:T(1,128)S(...) custom-call(bf16[1536,1280]{1,0:T(8,128)(2,1)} %get-tuple-element.199.p_ref, ...), custom_call_target="tpu_custom_call" | custom-call | tf_op jit(solution)/shard_map/norm_two_back/pallas_call | solution.py:621
  411.4 16.8 %down_product.1 = (bf16[512,1280]{1,0:T(8,128)(2,1)}, bf16[512,1280]{1,0:T(8,128)(2,1)}, bf16[512,1280]{1,0:T(8,128)(2,1)}) custom-call(bf16[1536,1280]{1,0:T(8,128)(2,1)} %get-tuple-element.185.refs_1_.refs_0_, bf16[1280,1280]{1,0:T(8,128)(2,1)} %bitcast.183, bf16[1536,1280]{1,0:T(8,128)(2,1)} %get-tuple-element.211.refs_1_.refs_2_, ...), custom_call_target="tpu_custom_call" | custom-call | tf_op jit(solution)/shard_map/down_product/pallas_call | solution.py:458
  428.9 15.8 %attend_back.2 = (bf16[4,80,1536]{2,1,0:T(8,128)(2,1)S(1)}, bf16[4,80,1536]{2,1,0:T(8,128)(2,1)S(1)}, bf16[4,80,1536]{2,1,0:T(8,128)(2,1)S(1)}) custom-call(bf16[4,80,1536]{2,1,0:T(8,128)(2,1)} %copy-done.33, bf16[4,80,1536]{2,1,0:T(8,128)(2,1)} %copy-done.34, bf16[4,80,1536]{2,1,0:T(8,128)(2,1)} %copy-done.35, bf16[320,1536]{1,0:T(8,128)(2,1)} %copy-done.14, ...), custom_call_target="tpu_custom_call" | custom-call | tf_op jit(solution)/shard_map/attend_back/pallas_call | solution.py:353
  452.7 8.4 %result.1 = bf16[1536,1280]{1,0:T(8,128)(2,1)} custom-call(bf16[1536,1280]{1,0:T(8,128)(2,1)} %copy-done.8, bf16[512,1280]{1,0:T(8,128)(2,1)} %get-tuple-element.223.refs_1_, bf16[512,1280]{1,0:T(8,128)(2,1)} %get-tuple-element.224.refs_2_, bf16[512,1280]{1,0:T(8,128)(2,1)} %get-tuple-element.225.refs_3_, bf16[512,1280]{1,0:T(8,128)(2,1)} %collective-permute-done.36.refs_4_, ...), custom_call_target="tpu_custom_call" | custom-call | tf_op jit(solution)/shard_map/result/pallas_call | solution.py:525
  462.3 4.7 fusion.6
  468.9 10.1 %first_grads.2 = bf16[1280,1280]{1,0:T(8,128)(2,1)} custom-call(bf16[1536,1280]{1,0:T(8,128)(2,1)} %copy-done.6, bf16[1536,1280]{1,0:T(8,128)(2,1)} %get-tuple-element.249.g_ref.refs_7_, bf16[960,1536]{1,0:T(8,128)(2,1)S(1)} %bitcast.155, bf16[320,1536]{1,0:T(8,128)(2,1)S(1)} %copy-done.15), custom_call_target="tpu_custom_call" | custom-call | tf_op jit(solution)/shard_map/first_grads/pallas_call | solution.py:644
  487.2 15.8 %attend_back.3 = (bf16[4,80,1536]{2,1,0:T(8,128)(2,1)S(1)}, bf16[4,80,1536]{2,1,0:T(8,128)(2,1)S(1)}, bf16[4,80,1536]{2,1,0:T(8,128)(2,1)S(1)}) custom-call(bf16[4,80,1536]{2,1,0:T(8,128)(2,1)} %copy-done.30, bf16[4,80,1536]{2,1,0:T(8,128)(2,1)} %copy-done.31, bf16[4,80,1536]{2,1,0:T(8,128)(2,1)} %copy-done.32, bf16[320,1536]{1,0:T(8,128)(2,1)} %copy-done.12, ...), custom_call_target="tpu_custom_call" | custom-call | tf_op jit(solution)/shard_map/attend_back/pallas_call | solution.py:353
  504.8 13.6 %qkv_back.1 = (bf16[512,1280]{1,0:T(8,128)(2,1)S(1)}, bf16[512,1280]{1,0:T(8,128)(2,1)S(1)}, bf16[512,1280]{1,0:T(8,128)(2,1)}) custom-call(bf16[960,1536]{1,0:T(8,128)(2,1)} %bitcast.157, bf16[1280,960]{1,0:T(8,128)(2,1)} %pad_maximum_fusion.8.refs_1_, bf16[960,1536]{1,0:T(8,128)(2,1)} %bitcast.156, bf16[1280,960]{1,0:T(8,128)(2,1)} %pad_maximum_fusion.9.refs_3_), custom_call_target="tpu_custom_call" | custom-call | tf_op jit(solution)/shard_map/qkv_back/pallas_call | solution.py:458
  518.4 10.1 %first_grads.3 = bf16[1280,1280]{1,0:T(8,128)(2,1)} custom-call(bf16[1536,1280]{1,0:T(8,128)(2,1)} %copy-done.6, bf16[1536,1280]{1,0:T(8,128)(2,1)} %get-tuple-element.249.g_ref.refs_7_, bf16[960,1536]{1,0:T(8,128)(2,1)S(1)} %bitcast.158, bf16[320,1536]{1,0:T(8,128)(2,1)S(1)} %copy-done.13), custom_call_target="tpu_custom_call" | custom-call | tf_op jit(solution)/shard_map/first_grads/pallas_call | solution.py:644
  541.8 12.1 %norm_back.1 = (bf16[1536,1280]{1,0:T(8,128)(2,1)}, f32[1,1280]{1,0:T(1,128)S(1)}, f32[1,1280]{1,0:T(1,128)S(1)}) custom-call(bf16[512,1280]{1,0:T(8,128)(2,1)S(1)} %get-tuple-element.246.refs_0_, bf16[512,1280]{1,0:T(8,128)(2,1)S(1)} %get-tuple-element.247.refs_1_, bf16[512,1280]{1,0:T(8,128)(2,1)} %get-tuple-element.248.refs_2_, ...), custom_call_target="tpu_custom_call" | custom-call | tf_op jit(solution)/shard_map/norm_back/pallas_call | solution.py:525
  555.1 4.9 fusion.4
  561.7 6.0 collective-permute-done.53
  567.7 2.5 add_convert_fusion
  570.9 2.5 add_convert_fusion.1
  580.5 3.6 multiply_subtract_fusion
  584.1 7.3 %collective-permute-done.54 = bf16[1,1,320,1280]{3,2,1,0:T(8,128)(2,1)} collective-permute-done((bf16[1,1,320,1280]{3,2,1,0:T(8,128)(2,1)}, bf16[1,1,320,1280]{3,2,1,0:T(8,128)(2,1)}, u32[]{:S(2)}, u32[]{:S(2)}) %collective-permute-start.54) | collective-permute-done | bytes 819232 | tf_op jit(solution)/shard_map/sq/ppermute | solution.py:65
  591.4 3.3 collective-permute-done.52
  598.3 2.5 add_bitcast_fusion.1
  601.9 3.5 collective-permute-done.58
  606.6 2.3 collective-permute-start.59
  612.7 7.0 %collective-permute-done.55 = bf16[320,1280]{1,0:T(8,128)(2,1)} collective-permute-done((bf16[320,1280]{1,0:T(8,128)(2,1)}, bf16[320,1280]{1,0:T(8,128)(2,1)}, u32[]{:S(2)}, u32[]{:S(2)}) %collective-permute-start.55) | collective-permute-done | bytes 819232 | tf_op jit(solution)/shard_map/sq/ppermute | solution.py:65
  619.7 10.0 %collective-permute-start.62 = (f32[13,1280]{1,0:T(8,128)S(1)}, f32[13,1280]{1,0:T(8,128)S(1)}, u32[]{:S(2)}, u32[]{:S(2)}) collective-permute-start(f32[13,1280]{1,0:T(8,128)S(1)} %pad_maximum_fusion.32), channel_id=1, source_target_pairs={{0,4},{4,0},{1,5},{5,1},{2,6},{6,2},{3,7},{7,3},{8,12},{12,8},{9,1... | collective-permute-start | bytes 199688 | tf_op jit(solution)/shard_map/vectors/ppermute | solution.py:65
  629.7 4.8 multiply_subtract_fusion.1
  640.5 4.0 collective-permute-done.50
  648.4 8.5 %collective-permute-done.56 = bf16[320,640]{1,0:T(8,128)(2,1)S(1)} collective-permute-done((bf16[320,640]{1,0:T(8,128)(2,1)S(1)}, bf16[320,640]{1,0:T(8,128)(2,1)S(1)}, u32[]{:S(2)}, u32[]{:S(2)}) %collective-permute-start.56) | collective-permute-done | bytes 409632 | tf_op jit(solution)/shard_map/sq/ppermute | solution.py:65
  657.0 2.8 collective-permute-start.65
  659.8 2.3 collective-permute-done.65
  662.2 3.4 collective-permute-start.66
  665.8 2.6 collective-permute-done.66
  674.7 3.1 multiply_subtract_fusion.2
  (462 shorter events, 169.4 us)
Async XLA Ops:
  3.5 15.8 %collective-permute-start.2 = (f32[1,3424]{1,0:T(1,128)S(1)}, f32[1,3424]{1,0:T(1,128)S(1)}, u32[]{:S(2)}, u32[]{:S(2)}) collective-permute-start(f32[1,3424]{1,0:T(1,128)S(1)} %broadcast_in_dim.29), channel_id=1, source_target_pairs={{0,3},{1,2},{2,1},{3,0},{4,7},{5,6},{6,5},{7,4},{8,11},{9,10},{10,... | collective-permute-start | bytes 41096 | tf_op jit(solution)/shard_map/small/ppermute | solution.py:728
  8.6 12.3 %collective-permute-start.1 = (f32[1,3424]{1,0:T(1,128)S(1)}, f32[1,3424]{1,0:T(1,128)S(1)}, u32[]{:S(2)}, u32[]{:S(2)}) collective-permute-start(f32[1,3424]{1,0:T(1,128)S(1)} %broadcast_in_dim.29), channel_id=1, source_target_pairs={{0,2},{1,3},{2,0},{3,1},{4,6},{5,7},{6,4},{7,5},{8,10},{9,11},{10,... | collective-permute-start | bytes 41096 | tf_op jit(solution)/shard_map/small/ppermute | solution.py:728
  8.6 12.3 %collective-permute-start = (f32[1,3424]{1,0:T(1,128)S(1)}, f32[1,3424]{1,0:T(1,128)S(1)}, u32[]{:S(2)}, u32[]{:S(2)}) collective-permute-start(f32[1,3424]{1,0:T(1,128)S(1)} %broadcast_in_dim.29), channel_id=1, source_target_pairs={{0,1},{1,0},{2,3},{3,2},{4,5},{5,4},{6,7},{7,6},{8,9},{9,8},{10,11... | collective-permute-start | bytes 41096 | tf_op jit(solution)/shard_map/small/ppermute | solution.py:728
  12.0 69.7 %collective-permute-start.4 = (bf16[384,1280]{1,0:T(8,128)(2,1)}, bf16[384,1280]{1,0:T(8,128)(2,1)}, u32[]{:S(2)}, u32[]{:S(2)}) collective-permute-start(bf16[384,1280]{1,0:T(8,128)(2,1)} %get-tuple-element.385), channel_id=1, source_target_pairs={{0,1},{1,0},{2,5},{3,4},{4,3},{5,2},{6,7},{7,6},{8,9},{9,8},{10,13... | collective-permute-start | bytes 2949128 | tf_op jit(solution)/shard_map/rows_x/ppermute | solution.py:65
  15.3 8.9 %collective-permute-start.5 = (bf16[160,1920]{1,0:T(8,128)(2,1)S(1)}, bf16[160,1920]{1,0:T(8,128)(2,1)S(1)}, u32[]{:S(2)}, u32[]{:S(2)}) collective-permute-start(bf16[160,1920]{1,0:T(8,128)(2,1)S(1)} %get-tuple-element.151), channel_id=1, source_target_pairs={{0,4},{4,0},{1,5},{5,1},{2,6},{6,2},{3,7},{7,3},{8,12},{12,8},{9,1... | collective-permute-start | bytes 1843208 | tf_op jit(solution)/shard_map/pack/ppermute | solution.py:65
  19.3 63.3 %collective-permute-start.8 = (bf16[384,1280]{1,0:T(8,128)(2,1)S(1)}, bf16[384,1280]{1,0:T(8,128)(2,1)}, u32[]{:S(2)}, u32[]{:S(2)}) collective-permute-start(bf16[384,1280]{1,0:T(8,128)(2,1)S(1)} %get-tuple-element.384), channel_id=1, source_target_pairs={{2,4},{3,5},{4,2},{5,3},{10,12},{11,13},{12,10},{13,11},{18,20},{1... | collective-permute-start | bytes 2949128 | tf_op jit(solution)/shard_map/rows_x/ppermute | solution.py:65
  26.3 32.7 %collective-permute-start.6 = (bf16[320,640]{1,0:T(8,128)(2,1)S(1)}, bf16[320,640]{1,0:T(8,128)(2,1)S(1)}, u32[]{:S(2)}, u32[]{:S(2)}) collective-permute-start(bf16[320,640]{1,0:T(8,128)(2,1)S(1)} %get-tuple-element.400), channel_id=1, source_target_pairs={{0,1},{1,0},{2,3},{3,2},{4,5},{5,4},{6,7},{7,6},{8,9},{9,8},{10,11... | collective-permute-start | bytes 1228808 | tf_op jit(solution)/shard_map/near/ppermute | solution.py:65
  27.0 37.9 %collective-permute-start.11 = (bf16[320,640]{1,0:T(8,128)(2,1)S(1)}, bf16[320,640]{1,0:T(8,128)(2,1)S(1)}, u32[]{:S(2)}, u32[]{:S(2)}) collective-permute-start(bf16[320,640]{1,0:T(8,128)(2,1)S(1)} %get-tuple-element.398), channel_id=1, source_target_pairs={{0,1},{1,0},{2,3},{3,2},{4,5},{5,4},{6,7},{7,6},{8,9},{9,8},{10,11... | collective-permute-start | bytes 1228808 | tf_op jit(solution)/shard_map/near/ppermute | solution.py:65
  60.0 22.6 %collective-permute-start.10 = (bf16[1,1,320,1280]{3,2,1,0:T(8,128)(2,1)S(1)}, bf16[1,1,320,1280]{3,2,1,0:T(8,128)(2,1)S(1)}, u32[]{:S(2)}, u32[]{:S(2)}) collective-permute-start(bf16[1,1,320,1280]{3,2,1,0:T(8,128)(2,1)S(1)} %get-tuple-element.413), channel_id=1, source_target_pairs={{0,8},{8,0},{16,24},{24,16},{1,9},{9,1},{17,25},{25,17},{2,10},{10... | collective-permute-start | bytes 2457608 | tf_op jit(solution)/shard_map/gx/ppermute | solution.py:65
  62.0 17.1 %collective-permute-start.7 = (bf16[320,640]{1,0:T(8,128)(2,1)S(1)}, bf16[320,640]{1,0:T(8,128)(2,1)S(1)}, u32[]{:S(2)}, u32[]{:S(2)}) collective-permute-start(bf16[320,640]{1,0:T(8,128)(2,1)S(1)} %get-tuple-element.152), channel_id=1, source_target_pairs={{0,1},{1,0},{2,3},{3,2},{4,5},{5,4},{6,7},{7,6},{8,9},{9,8},{10,11... | collective-permute-start | bytes 1228808 | tf_op jit(solution)/shard_map/near/ppermute | solution.py:65
  64.9 58.3 %collective-permute-start.14 = (bf16[320,1280]{1,0:T(8,128)(2,1)}, bf16[320,1280]{1,0:T(8,128)(2,1)}, u32[]{:S(2)}, u32[]{:S(2)}) collective-permute-start(bf16[320,1280]{1,0:T(8,128)(2,1)} %get-tuple-element.414), channel_id=1, source_target_pairs={{0,2},{1,3},{2,0},{3,1},{4,6},{5,7},{6,4},{7,5},{8,10},{9,11},{10,... | collective-permute-start | bytes 2457608 | tf_op jit(solution)/shard_map/far/ppermute | solution.py:65
  79.1 25.1 %collective-permute-start.12 = (bf16[1,1,320,1280]{3,2,1,0:T(8,128)(2,1)S(1)}, bf16[1,1,320,1280]{3,2,1,0:T(8,128)(2,1)S(1)}, u32[]{:S(2)}, u32[]{:S(2)}) collective-permute-start(bf16[1,1,320,1280]{3,2,1,0:T(8,128)(2,1)S(1)} %get-tuple-element.410), channel_id=1, source_target_pairs={{0,16},{8,24},{16,0},{24,8},{1,17},{9,25},{17,1},{25,9},{2,18},{10... | collective-permute-start | bytes 2457608 | tf_op jit(solution)/shard_map/gy/ppermute | solution.py:65
  81.7 106.1 %collective-permute-start.21 = (bf16[320,1280]{1,0:T(8,128)(2,1)}, bf16[320,1280]{1,0:T(8,128)(2,1)}, u32[]{:S(2)}, u32[]{:S(2)}) collective-permute-start(bf16[320,1280]{1,0:T(8,128)(2,1)} %get-tuple-element.409), channel_id=1, source_target_pairs={{0,2},{1,3},{2,0},{3,1},{4,6},{5,7},{6,4},{7,5},{8,10},{9,11},{10,... | collective-permute-start | bytes 2457608 | tf_op jit(solution)/shard_map/far/ppermute | solution.py:65
  82.6 19.5 %collective-permute-start.16 = (bf16[1,1,320,1280]{3,2,1,0:T(8,128)(2,1)S(1)}, bf16[1,1,320,1280]{3,2,1,0:T(8,128)(2,1)S(1)}, u32[]{:S(2)}, u32[]{:S(2)}) collective-permute-start(bf16[1,1,320,1280]{3,2,1,0:T(8,128)(2,1)S(1)} %get-tuple-element.163), channel_id=1, source_target_pairs={{0,8},{8,0},{16,24},{24,16},{1,9},{9,1},{17,25},{25,17},{2,10},{10... | collective-permute-start | bytes 2457608 | tf_op jit(solution)/shard_map/gx/ppermute | solution.py:65
  84.2 24.4 %collective-permute-start.9 = (bf16[768,1280]{1,0:T(8,128)(2,1)S(1)}, bf16[768,1280]{1,0:T(8,128)(2,1)S(1)}, u32[]{:S(2)}, u32[]{:S(2)}) collective-permute-start(bf16[768,1280]{1,0:T(8,128)(2,1)S(1)} %pad_maximum_fusion.10), channel_id=1, source_target_pairs={{0,4},{4,0},{1,5},{5,1},{2,6},{6,2},{3,7},{7,3},{8,12},{12,8},{9,1... | collective-permute-start | bytes 5898248 | tf_op jit(solution)/shard_map/rows_x/ppermute | solution.py:65
  104.2 36.5 %collective-permute-start.13 = (bf16[1,2,320,1280]{3,2,1,0:T(8,128)(2,1)}, bf16[1,2,320,1280]{3,2,1,0:T(8,128)(2,1)}, u32[]{:S(2)}, u32[]{:S(2)}) collective-permute-start(bf16[1,2,320,1280]{3,2,1,0:T(8,128)(2,1)} %pad_maximum_fusion.13), channel_id=1, source_target_pairs={{0,16},{8,24},{16,0},{24,8},{1,17},{9,25},{17,1},{25,9},{2,18},{10... | collective-permute-start | bytes 4915208 | tf_op jit(solution)/shard_map/gy/ppermute | solution.py:65
  106.4 37.8 %collective-permute-start.17 = (bf16[2,1,320,1280]{3,2,1,0:T(8,128)(2,1)}, bf16[2,1,320,1280]{3,2,1,0:T(8,128)(2,1)}, u32[]{:S(2)}, u32[]{:S(2)}) collective-permute-start(bf16[2,1,320,1280]{3,2,1,0:T(8,128)(2,1)} %pad_maximum_fusion.15), channel_id=1, source_target_pairs={{0,8},{8,0},{16,24},{24,16},{1,9},{9,1},{17,25},{25,17},{2,10},{10... | collective-permute-start | bytes 4915208 | tf_op jit(solution)/shard_map/gx/ppermute | solution.py:65
  142.6 18.0 %collective-permute-start.15 = (bf16[1,1,320,1280]{3,2,1,0:T(8,128)(2,1)}, bf16[1,1,320,1280]{3,2,1,0:T(8,128)(2,1)S(1)}, u32[]{:S(2)}, u32[]{:S(2)}) collective-permute-start(bf16[1,1,320,1280]{3,2,1,0:T(8,128)(2,1)} %bitcast.16), channel_id=1, source_target_pairs={{0,16},{8,24},{16,0},{24,8},{1,17},{9,25},{17,1},{25,9},{2,18},{10... | collective-permute-start | bytes 2457608 | tf_op jit(solution)/shard_map/gy/ppermute | solution.py:65
  144.2 57.2 %collective-permute-start.20 = (bf16[320,1280]{1,0:T(8,128)(2,1)}, bf16[320,1280]{1,0:T(8,128)(2,1)}, u32[]{:S(2)}, u32[]{:S(2)}) collective-permute-start(bf16[320,1280]{1,0:T(8,128)(2,1)} %get-tuple-element.168), channel_id=1, source_target_pairs={{0,2},{1,3},{2,0},{3,1},{4,6},{5,7},{6,4},{7,5},{8,10},{9,11},{10,... | collective-permute-start | bytes 2457608 | tf_op jit(solution)/shard_map/far/ppermute | solution.py:65
  163.1 36.2 %collective-permute-start.18 = (bf16[2,1,320,1280]{3,2,1,0:T(8,128)(2,1)}, bf16[2,1,320,1280]{3,2,1,0:T(8,128)(2,1)}, u32[]{:S(2)}, u32[]{:S(2)}) collective-permute-start(bf16[2,1,320,1280]{3,2,1,0:T(8,128)(2,1)} %pad_maximum_fusion.14), channel_id=1, source_target_pairs={{0,8},{8,0},{16,24},{24,16},{1,9},{9,1},{17,25},{25,17},{2,10},{10... | collective-permute-start | bytes 4915208 | tf_op jit(solution)/shard_map/gx/ppermute | solution.py:65
  166.3 35.3 %collective-permute-start.19 = (bf16[1,2,320,1280]{3,2,1,0:T(8,128)(2,1)}, bf16[1,2,320,1280]{3,2,1,0:T(8,128)(2,1)}, u32[]{:S(2)}, u32[]{:S(2)}) collective-permute-start(bf16[1,2,320,1280]{3,2,1,0:T(8,128)(2,1)} %pad_maximum_fusion.16), channel_id=1, source_target_pairs={{0,16},{8,24},{16,0},{24,8},{1,17},{9,25},{17,1},{25,9},{2,18},{10... | collective-permute-start | bytes 4915208 | tf_op jit(solution)/shard_map/gy/ppermute | solution.py:65
  187.8 46.2 %collective-permute-start.25 = (bf16[384,1280]{1,0:T(8,128)(2,1)}, bf16[384,1280]{1,0:T(8,128)(2,1)}, u32[]{:S(2)}, u32[]{:S(2)}) collective-permute-start(bf16[384,1280]{1,0:T(8,128)(2,1)} %get-tuple-element.180), channel_id=1, source_target_pairs={{0,1},{1,0},{2,5},{3,4},{4,3},{5,2},{6,7},{7,6},{8,9},{9,8},{10,13... | collective-permute-start | bytes 2949128 | tf_op jit(solution)/shard_map/rows_g/ppermute | solution.py:65
  190.9 43.2 %collective-permute-start.26 = (bf16[384,1280]{1,0:T(8,128)(2,1)}, bf16[384,1280]{1,0:T(8,128)(2,1)}, u32[]{:S(2)}, u32[]{:S(2)}) collective-permute-start(bf16[384,1280]{1,0:T(8,128)(2,1)} %get-tuple-element.182), channel_id=1, source_target_pairs={{2,4},{3,5},{4,2},{5,3},{10,12},{11,13},{12,10},{13,11},{18,20},{1... | collective-permute-start | bytes 2949128 | tf_op jit(solution)/shard_map/rows_g/ppermute | solution.py:65
  201.6 26.2 %collective-permute-start.22 = (bf16[1,1,320,1280]{3,2,1,0:T(8,128)(2,1)}, bf16[1,1,320,1280]{3,2,1,0:T(8,128)(2,1)}, u32[]{:S(2)}, u32[]{:S(2)}) collective-permute-start(bf16[1,1,320,1280]{3,2,1,0:T(8,128)(2,1)} %bitcast.24), channel_id=1, source_target_pairs={{0,8},{8,0},{16,24},{24,16},{1,9},{9,1},{17,25},{25,17},{2,10},{10... | collective-permute-start | bytes 2457608 | tf_op jit(solution)/shard_map/gx/ppermute | solution.py:65
  203.2 24.6 %collective-permute-start.23 = (bf16[1,1,320,1280]{3,2,1,0:T(8,128)(2,1)}, bf16[1,1,320,1280]{3,2,1,0:T(8,128)(2,1)}, u32[]{:S(2)}, u32[]{:S(2)}) collective-permute-start(bf16[1,1,320,1280]{3,2,1,0:T(8,128)(2,1)} %bitcast.25), channel_id=1, source_target_pairs={{0,16},{8,24},{16,0},{24,8},{1,17},{9,25},{17,1},{25,9},{2,18},{10... | collective-permute-start | bytes 2457608 | tf_op jit(solution)/shard_map/gy/ppermute | solution.py:65
  233.8 20.5 %collective-permute-start.24 = (bf16[1536,1280]{1,0:T(8,128)(2,1)}, bf16[1536,1280]{1,0:T(8,128)(2,1)}, u32[]{:S(2)}, u32[]{:S(2)}) collective-permute-start(bf16[1536,1280]{1,0:T(8,128)(2,1)} %out_product.1.refs_1_), channel_id=1, source_target_pairs={{0,4},{4,0},{1,5},{5,1},{2,6},{6,2},{3,7},{7,3},{8,12},{12,8},{9,1... | collective-permute-start | bytes 11796488 | tf_op jit(solution)/shard_map/ppermute | solution.py:65
  235.9 10.8 %collective-permute-start.27 = (bf16[768,1280]{1,0:T(8,128)(2,1)S(1)}, bf16[768,1280]{1,0:T(8,128)(2,1)S(1)}, u32[]{:S(2)}, u32[]{:S(2)}) collective-permute-start(bf16[768,1280]{1,0:T(8,128)(2,1)S(1)} %pad_maximum_fusion.11), channel_id=1, source_target_pairs={{0,4},{4,0},{1,5},{5,1},{2,6},{6,2},{3,7},{7,3},{8,12},{12,8},{9,1... | collective-permute-start | bytes 5898248 | tf_op jit(solution)/shard_map/rows_g/ppermute | solution.py:65
  239.3 44.4 %collective-permute-start.28 = (bf16[1,2,320,1280]{3,2,1,0:T(8,128)(2,1)}, bf16[1,2,320,1280]{3,2,1,0:T(8,128)(2,1)}, u32[]{:S(2)}, u32[]{:S(2)}) collective-permute-start(bf16[1,2,320,1280]{3,2,1,0:T(8,128)(2,1)} %pad_maximum_fusion.17), channel_id=1, source_target_pairs={{0,16},{8,24},{16,0},{24,8},{1,17},{9,25},{17,1},{25,9},{2,18},{10... | collective-permute-start | bytes 4915208 | tf_op jit(solution)/shard_map/gy/ppermute | solution.py:65
  246.3 61.0 %collective-permute-start.29 = (bf16[2,1,320,1280]{3,2,1,0:T(8,128)(2,1)}, bf16[2,1,320,1280]{3,2,1,0:T(8,128)(2,1)}, u32[]{:S(2)}, u32[]{:S(2)}) collective-permute-start(bf16[2,1,320,1280]{3,2,1,0:T(8,128)(2,1)} %pad_maximum_fusion.18), channel_id=1, source_target_pairs={{0,8},{8,0},{16,24},{24,16},{1,9},{9,1},{17,25},{25,17},{2,10},{10... | collective-permute-start | bytes 4915208 | tf_op jit(solution)/shard_map/gx/ppermute | solution.py:65
  307.3 45.3 %collective-permute-start.30 = (bf16[2,1,320,1280]{3,2,1,0:T(8,128)(2,1)}, bf16[2,1,320,1280]{3,2,1,0:T(8,128)(2,1)}, u32[]{:S(2)}, u32[]{:S(2)}) collective-permute-start(bf16[2,1,320,1280]{3,2,1,0:T(8,128)(2,1)} %constant_dynamic-slice_fusion.6), channel_id=1, source_target_pairs={{0,8},{8,0},{16,24},{24,16},{1,9},{9,1},{17,25},{25,17},{2,10},{10... | collective-permute-start | bytes 4915208 | tf_op jit(solution)/shard_map/sd/ppermute | solution.py:65
  310.2 42.4 %collective-permute-start.31 = (bf16[1,2,320,1280]{3,2,1,0:T(8,128)(2,1)}, bf16[1,2,320,1280]{3,2,1,0:T(8,128)(2,1)}, u32[]{:S(2)}, u32[]{:S(2)}) collective-permute-start(bf16[1,2,320,1280]{3,2,1,0:T(8,128)(2,1)} %constant_dynamic-slice_fusion.5), channel_id=1, source_target_pairs={{0,16},{8,24},{16,0},{24,8},{1,17},{9,25},{17,1},{25,9},{2,18},{10... | collective-permute-start | bytes 4915208 | tf_op jit(solution)/shard_map/sd/ppermute | solution.py:65
  352.7 41.2 %collective-permute-start.32 = (bf16[1536,1280]{1,0:T(8,128)(2,1)}, bf16[1536,1280]{1,0:T(8,128)(2,1)}, u32[]{:S(2)}, u32[]{:S(2)}) collective-permute-start(bf16[1536,1280]{1,0:T(8,128)(2,1)} %get-tuple-element.199.p_ref), channel_id=1, source_target_pairs={{0,4},{4,0},{1,5},{5,1},{2,6},{6,2},{3,7},{7,3},{8,12},{12,8},{9,1... | collective-permute-start | bytes 11796488 | tf_op jit(solution)/shard_map/ppermute | solution.py:65
  355.3 21.7 %collective-permute-start.33 = (bf16[1,1,320,1280]{3,2,1,0:T(8,128)(2,1)}, bf16[1,1,320,1280]{3,2,1,0:T(8,128)(2,1)}, u32[]{:S(2)}, u32[]{:S(2)}) collective-permute-start(bf16[1,1,320,1280]{3,2,1,0:T(8,128)(2,1)} %add_convert_fusion.5), channel_id=1, source_target_pairs={{0,16},{8,24},{16,0},{24,8},{1,17},{9,25},{17,1},{25,9},{2,18},{10... | collective-permute-start | bytes 2457608 | tf_op jit(solution)/shard_map/sd/ppermute | solution.py:65
  366.2 20.4 %collective-permute-start.34 = (bf16[1,1,320,1280]{3,2,1,0:T(8,128)(2,1)S(1)}, bf16[1,1,320,1280]{3,2,1,0:T(8,128)(2,1)S(1)}, u32[]{:S(2)}, u32[]{:S(2)}) collective-permute-start(bf16[1,1,320,1280]{3,2,1,0:T(8,128)(2,1)S(1)} %add_convert_fusion.4), channel_id=1, source_target_pairs={{0,8},{8,0},{16,24},{24,16},{1,9},{9,1},{17,25},{25,17},{2,10},{10... | collective-permute-start | bytes 2457608 | tf_op jit(solution)/shard_map/sd/ppermute | solution.py:65
  388.1 57.3 %collective-permute-start.41 = (bf16[2,1,320,1280]{3,2,1,0:T(8,128)(2,1)}, bf16[2,1,320,1280]{3,2,1,0:T(8,128)(2,1)S(1)}, u32[]{:S(2)}, u32[]{:S(2)}) collective-permute-start(bf16[2,1,320,1280]{3,2,1,0:T(8,128)(2,1)} %constant_dynamic-slice_fusion.4), channel_id=1, source_target_pairs={{0,8},{8,0},{16,24},{24,16},{1,9},{9,1},{17,25},{25,17},{2,10},{10... | collective-permute-start | bytes 4915208 | tf_op jit(solution)/shard_map/su/ppermute | solution.py:65
  388.7 39.6 %collective-permute-start.35 = (bf16[320,1280]{1,0:T(8,128)(2,1)S(1)}, bf16[320,1280]{1,0:T(8,128)(2,1)S(1)}, u32[]{:S(2)}, u32[]{:S(2)}) collective-permute-start(bf16[320,1280]{1,0:T(8,128)(2,1)S(1)} %pad_maximum_fusion.24), channel_id=1, source_target_pairs={{0,1},{1,0},{2,3},{3,2},{4,5},{5,4},{6,7},{7,6},{8,9},{9,8},{10,11... | collective-permute-start | bytes 2457608 | tf_op jit(solution)/shard_map/sd/ppermute | solution.py:65
  393.2 56.2 %collective-permute-start.42 = (bf16[1,2,320,1280]{3,2,1,0:T(8,128)(2,1)}, bf16[1,2,320,1280]{3,2,1,0:T(8,128)(2,1)}, u32[]{:S(2)}, u32[]{:S(2)}) collective-permute-start(bf16[1,2,320,1280]{3,2,1,0:T(8,128)(2,1)} %constant_dynamic-slice_fusion.3), channel_id=1, source_target_pairs={{0,16},{8,24},{16,0},{24,8},{1,17},{9,25},{17,1},{25,9},{2,18},{10... | collective-permute-start | bytes 4915208 | tf_op jit(solution)/shard_map/su/ppermute | solution.py:65
  428.3 24.4 %collective-permute-start.36 = (bf16[512,1280]{1,0:T(8,128)(2,1)}, bf16[512,1280]{1,0:T(8,128)(2,1)}, u32[]{:S(2)}, u32[]{:S(2)}) collective-permute-start(bf16[512,1280]{1,0:T(8,128)(2,1)} %get-tuple-element.223.refs_1_), channel_id=1, source_target_pairs={{0,4},{4,0},{1,5},{5,1},{2,6},{6,2},{3,7},{7,3},{8,12},{12,8},{9,1... | collective-permute-start | bytes 3932168 | tf_op jit(solution)/shard_map/ppermute | solution.py:65
  428.4 24.3 %collective-permute-start.37 = (bf16[512,1280]{1,0:T(8,128)(2,1)}, bf16[512,1280]{1,0:T(8,128)(2,1)}, u32[]{:S(2)}, u32[]{:S(2)}) collective-permute-start(bf16[512,1280]{1,0:T(8,128)(2,1)} %get-tuple-element.224.refs_2_), channel_id=1, source_target_pairs={{0,4},{4,0},{1,5},{5,1},{2,6},{6,2},{3,7},{7,3},{8,12},{12,8},{9,1... | collective-permute-start | bytes 3932168 | tf_op jit(solution)/shard_map/ppermute | solution.py:65
  428.8 23.8 %collective-permute-start.38 = (bf16[512,1280]{1,0:T(8,128)(2,1)}, bf16[512,1280]{1,0:T(8,128)(2,1)}, u32[]{:S(2)}, u32[]{:S(2)}) collective-permute-start(bf16[512,1280]{1,0:T(8,128)(2,1)} %get-tuple-element.225.refs_3_), channel_id=1, source_target_pairs={{0,4},{4,0},{1,5},{5,1},{2,6},{6,2},{3,7},{7,3},{8,12},{12,8},{9,1... | collective-permute-start | bytes 3932168 | tf_op jit(solution)/shard_map/ppermute | solution.py:65
  446.8 32.2 %collective-permute-start.43 = (bf16[1,1,320,1280]{3,2,1,0:T(8,128)(2,1)}, bf16[1,1,320,1280]{3,2,1,0:T(8,128)(2,1)}, u32[]{:S(2)}, u32[]{:S(2)}) collective-permute-start(bf16[1,1,320,1280]{3,2,1,0:T(8,128)(2,1)} %add_convert_fusion.3), channel_id=1, source_target_pairs={{0,16},{8,24},{16,0},{24,8},{1,17},{9,25},{17,1},{25,9},{2,18},{10... | collective-permute-start | bytes 2457608 | tf_op jit(solution)/shard_map/su/ppermute | solution.py:65
  451.0 29.7 %collective-permute-start.44 = (bf16[1,1,320,1280]{3,2,1,0:T(8,128)(2,1)S(1)}, bf16[1,1,320,1280]{3,2,1,0:T(8,128)(2,1)S(1)}, u32[]{:S(2)}, u32[]{:S(2)}) collective-permute-start(bf16[1,1,320,1280]{3,2,1,0:T(8,128)(2,1)S(1)} %add_convert_fusion.2), channel_id=1, source_target_pairs={{0,8},{8,0},{16,24},{24,16},{1,9},{9,1},{17,25},{25,17},{2,10},{10... | collective-permute-start | bytes 2457608 | tf_op jit(solution)/shard_map/su/ppermute | solution.py:65
  467.0 66.1 %collective-permute-start.39 = (bf16[384,1280]{1,0:T(8,128)(2,1)}, bf16[384,1280]{1,0:T(8,128)(2,1)}, u32[]{:S(2)}, u32[]{:S(2)}) collective-permute-start(bf16[384,1280]{1,0:T(8,128)(2,1)} %get-tuple-element.349), channel_id=1, source_target_pairs={{1,0},{0,1},{5,2},{4,3},{3,4},{2,5},{7,6},{6,7},{9,8},{8,9},{13,10... | collective-permute-start | bytes 2949128 | tf_op jit(solution)/shard_map/rows_out/ppermute | solution.py:65
  467.1 66.0 %collective-permute-start.40 = (bf16[384,1280]{1,0:T(8,128)(2,1)S(1)}, bf16[384,1280]{1,0:T(8,128)(2,1)}, u32[]{:S(2)}, u32[]{:S(2)}) collective-permute-start(bf16[384,1280]{1,0:T(8,128)(2,1)S(1)} %get-tuple-element.348), channel_id=1, source_target_pairs={{4,2},{5,3},{2,4},{3,5},{12,10},{13,11},{10,12},{11,13},{20,18},{2... | collective-permute-start | bytes 2949128 | tf_op jit(solution)/shard_map/rows_out/ppermute | solution.py:65
  484.1 49.0 %collective-permute-start.45 = (bf16[320,1280]{1,0:T(8,128)(2,1)}, bf16[320,1280]{1,0:T(8,128)(2,1)S(1)}, u32[]{:S(2)}, u32[]{:S(2)}) collective-permute-start(bf16[320,1280]{1,0:T(8,128)(2,1)} %pad_maximum_fusion.25), channel_id=1, source_target_pairs={{0,1},{1,0},{2,3},{3,2},{4,5},{5,4},{6,7},{7,6},{8,9},{9,8},{10,11... | collective-permute-start | bytes 2457608 | tf_op jit(solution)/shard_map/su/ppermute | solution.py:65
  529.9 37.9 %collective-permute-start.53 = (bf16[2,1,320,1280]{3,2,1,0:T(8,128)(2,1)}, bf16[2,1,320,1280]{3,2,1,0:T(8,128)(2,1)}, u32[]{:S(2)}, u32[]{:S(2)}) collective-permute-start(bf16[2,1,320,1280]{3,2,1,0:T(8,128)(2,1)} %constant_dynamic-slice_fusion), channel_id=1, source_target_pairs={{0,8},{8,0},{16,24},{24,16},{1,9},{9,1},{17,25},{25,17},{2,10},{10... | collective-permute-start | bytes 4915208 | tf_op jit(solution)/shard_map/sq/ppermute | solution.py:65
  532.4 38.6 %collective-permute-start.51 = (bf16[1,2,320,1280]{3,2,1,0:T(8,128)(2,1)}, bf16[1,2,320,1280]{3,2,1,0:T(8,128)(2,1)}, u32[]{:S(2)}, u32[]{:S(2)}) collective-permute-start(bf16[1,2,320,1280]{3,2,1,0:T(8,128)(2,1)} %constant_dynamic-slice_fusion.1), channel_id=1, source_target_pairs={{0,16},{8,24},{16,0},{24,8},{1,17},{9,25},{17,1},{25,9},{2,18},{10... | collective-permute-start | bytes 4915208 | tf_op jit(solution)/shard_map/sq/ppermute | solution.py:65
  533.1 7.8 %collective-permute-start.46 = (bf16[512,1280]{1,0:T(8,128)(2,1)S(1)}, bf16[512,1280]{1,0:T(8,128)(2,1)}, u32[]{:S(2)}, u32[]{:S(2)}) collective-permute-start(bf16[512,1280]{1,0:T(8,128)(2,1)S(1)} %get-tuple-element.246.refs_0_), channel_id=1, source_target_pairs={{0,4},{4,0},{1,5},{5,1},{2,6},{6,2},{3,7},{7,3},{8,12},{12,8},{9,1... | collective-permute-start | bytes 3932168 | tf_op jit(solution)/shard_map/ppermute | solution.py:65
  535.0 6.7 collective-permute-start.47
  535.1 6.7 collective-permute-start.48
  540.9 34.7 %collective-permute-start.60 = (bf16[320,640]{1,0:T(8,128)(2,1)S(1)}, bf16[320,640]{1,0:T(8,128)(2,1)S(1)}, u32[]{:S(2)}, u32[]{:S(2)}) collective-permute-start(bf16[320,640]{1,0:T(8,128)(2,1)S(1)} %slice.486), channel_id=1, source_target_pairs={{0,2},{1,3},{2,0},{3,1},{4,6},{5,7},{6,4},{7,5},{8,10},{9,11},{10,... | collective-permute-start | bytes 1228808 | tf_op jit(solution)/shard_map/sd/ppermute | solution.py:65
  560.0 36.3 %collective-permute-start.49 = (bf16[384,1280]{1,0:T(8,128)(2,1)}, bf16[384,1280]{1,0:T(8,128)(2,1)}, u32[]{:S(2)}, u32[]{:S(2)}) collective-permute-start(bf16[384,1280]{1,0:T(8,128)(2,1)} %get-tuple-element.346), channel_id=1, source_target_pairs={{4,2},{5,3},{2,4},{3,5},{12,10},{13,11},{10,12},{11,13},{20,18},{2... | collective-permute-start | bytes 2949128 | tf_op jit(solution)/shard_map/rows_dx/ppermute | solution.py:65
  570.2 21.2 %collective-permute-start.54 = (bf16[1,1,320,1280]{3,2,1,0:T(8,128)(2,1)}, bf16[1,1,320,1280]{3,2,1,0:T(8,128)(2,1)}, u32[]{:S(2)}, u32[]{:S(2)}) collective-permute-start(bf16[1,1,320,1280]{3,2,1,0:T(8,128)(2,1)} %add_convert_fusion), channel_id=1, source_target_pairs={{0,16},{8,24},{16,0},{24,8},{1,17},{9,25},{17,1},{25,9},{2,18},{10... | collective-permute-start | bytes 2457608 | tf_op jit(solution)/shard_map/sq/ppermute | solution.py:65
  573.4 21.2 %collective-permute-start.52 = (bf16[1,1,320,1280]{3,2,1,0:T(8,128)(2,1)}, bf16[1,1,320,1280]{3,2,1,0:T(8,128)(2,1)}, u32[]{:S(2)}, u32[]{:S(2)}) collective-permute-start(bf16[1,1,320,1280]{3,2,1,0:T(8,128)(2,1)} %add_convert_fusion.1), channel_id=1, source_target_pairs={{0,8},{8,0},{16,24},{24,16},{1,9},{9,1},{17,25},{25,17},{2,10},{10... | collective-permute-start | bytes 2457608 | tf_op jit(solution)/shard_map/sq/ppermute | solution.py:65
  574.9 30.6 %collective-permute-start.58 = (bf16[320,640]{1,0:T(8,128)(2,1)}, bf16[320,640]{1,0:T(8,128)(2,1)}, u32[]{:S(2)}, u32[]{:S(2)}) collective-permute-start(bf16[320,640]{1,0:T(8,128)(2,1)} %slice.487), channel_id=1, source_target_pairs={{0,2},{1,3},{2,0},{3,1},{4,6},{5,7},{6,4},{7,5},{8,10},{9,11},{10,... | collective-permute-start | bytes 1228808 | tf_op jit(solution)/shard_map/su/ppermute | solution.py:65
  601.9 17.8 %collective-permute-start.55 = (bf16[320,1280]{1,0:T(8,128)(2,1)}, bf16[320,1280]{1,0:T(8,128)(2,1)}, u32[]{:S(2)}, u32[]{:S(2)}) collective-permute-start(bf16[320,1280]{1,0:T(8,128)(2,1)} %pad_maximum_fusion.26), channel_id=1, source_target_pairs={{0,1},{1,0},{2,3},{3,2},{4,5},{5,4},{6,7},{7,6},{8,9},{9,8},{10,11... | collective-permute-start | bytes 2457608 | tf_op jit(solution)/shard_map/sq/ppermute | solution.py:65
  608.9 35.6 %collective-permute-start.50 = (bf16[384,1280]{1,0:T(8,128)(2,1)}, bf16[384,1280]{1,0:T(8,128)(2,1)}, u32[]{:S(2)}, u32[]{:S(2)}) collective-permute-start(bf16[384,1280]{1,0:T(8,128)(2,1)} %get-tuple-element.253), channel_id=1, source_target_pairs={{1,0},{0,1},{5,2},{4,3},{3,4},{2,5},{7,6},{6,7},{9,8},{8,9},{13,10... | collective-permute-start | bytes 2949128 | tf_op jit(solution)/shard_map/rows_dx/ppermute | solution.py:65
  619.7 14.8 %collective-permute-start.62 = (f32[13,1280]{1,0:T(8,128)S(1)}, f32[13,1280]{1,0:T(8,128)S(1)}, u32[]{:S(2)}, u32[]{:S(2)}) collective-permute-start(f32[13,1280]{1,0:T(8,128)S(1)} %pad_maximum_fusion.32), channel_id=1, source_target_pairs={{0,4},{4,0},{1,5},{5,1},{2,6},{6,2},{3,7},{7,3},{8,12},{12,8},{9,1... | collective-permute-start | bytes 199688 | tf_op jit(solution)/shard_map/vectors/ppermute | solution.py:65
  634.6 4.5 collective-permute-start.63
  637.0 20.0 %collective-permute-start.56 = (bf16[320,640]{1,0:T(8,128)(2,1)S(1)}, bf16[320,640]{1,0:T(8,128)(2,1)S(1)}, u32[]{:S(2)}, u32[]{:S(2)}) collective-permute-start(bf16[320,640]{1,0:T(8,128)(2,1)S(1)} %slice.488), channel_id=1, source_target_pairs={{0,2},{1,3},{2,0},{3,1},{4,6},{5,7},{6,4},{7,5},{8,10},{9,11},{10,... | collective-permute-start | bytes 1228808 | tf_op jit(solution)/shard_map/sq/ppermute | solution.py:65
  639.1 9.3 %collective-permute-start.64 = (f32[13,1280]{1,0:T(8,128)S(1)}, f32[13,1280]{1,0:T(8,128)S(1)}, u32[]{:S(2)}, u32[]{:S(2)}) collective-permute-start(f32[13,1280]{1,0:T(8,128)S(1)} %add.432), channel_id=1, source_target_pairs={{0,16},{8,24},{16,0},{24,8},{1,17},{9,25},{17,1},{25,9},{2,18},{10... | collective-permute-start | bytes 199688 | tf_op jit(solution)/shard_map/vectors/ppermute | solution.py:65
  657.0 5.2 collective-permute-start.65
  662.2 6.1 collective-permute-start.66
  665.7 4.1 collective-permute-start.57
  (95 other events, 1320.8 us)
